TPU v7x, 32 devices: a whole 2x2x4 slice. The times are simulated.
32 devices in a mesh: region: 4 (over z), tile: 8 (over y, x, core).
Axes of the slice: x: 2, y: 2, z: 4, core: 2. Of those that a mesh axis runs over, the one named last changes fastest.
Arguments:
- global_deriv: bfloat16 [6144, 32, 128], P(('region', 'tile')), may hold values from -0.15625 to 0.15625
- local_deriv: bfloat16 [6144, 5, 32], P(('region', 'tile')), may hold values from -4 to 4
- hit_weight: bfloat16 [6144, 32], P(('region', 'tile')), may hold values from 0.25 to 4
- hit_resid: bfloat16 [6144, 32], P(('region', 'tile')), may hold values from -6 to 6
- block_ids: int32 [6144, 32], P(('region', 'tile')), may hold values from 0 to 7
- hit_count: int32 [6144], P(('region', 'tile')), may hold values from 4 to 32
- track_region: int32 [6144, 1], P(('region', 'tile')), may hold values from 0 to 3; in each aligned block of 192 rows (0 to 191, 192 to 383, ...) at most 96 rows name the same one
- block_place: int32 [8], replicated, may hold values from 0 to 7, each once
Outputs:
- normal_matrix: float32 [4, 1024, 1024], P('region', 'tile')
- right_side: float32 [4, 1024], P('region', 'tile')
Inputs may be any that keep to these rules, and one draw needn't show every extreme that they name: `track_region`: among the tracks of one device at most 96 share a region, and in every draw some device has exactly 96 tracks in some region. `block_place`: each position appears once.
All inputs are finite; a program needn't handle non-finite values.
Results may differ from a plain program's by a relative error of at most 0.0029.
Values may be sent and summed in bfloat16 or wider, within the bound.
No kernel may reach another device: no remote copies, remote signals or barrier semaphores. Data moves between devices by JAX's collectives and lax.ppermute only.
A program may use at most 128 MiB of HBM per device.

v0:
```python
import jax
import jax.numpy as jnp
from jax import lax
from jax.sharding import PartitionSpec as P


def cholesky_fit(local_slopes, weight, misfit, live_hits):
    masked_w = live_hits * weight
    weighted_l = local_slopes * masked_w[:, None, :]
    gamma_mat = [
        [
            jnp.sum(weighted_l[:, a, :] * local_slopes[:, b, :], axis=1) + (1.0 if a == b else 0.0)
            for b in range(5)
        ]
        for a in range(5)
    ]
    beta_vec = [jnp.sum(weighted_l[:, a, :] * misfit, axis=1) for a in range(5)]
    factor = [[None for b in range(5)] for a in range(5)]
    for j in range(5):
        center = gamma_mat[j][j]
        for k in range(j):
            center = center - factor[j][k] * factor[j][k]
        factor[j][j] = jnp.sqrt(center)
        for i in range(j + 1, 5):
            offdiag = gamma_mat[i][j]
            for k in range(j):
                offdiag = offdiag - factor[i][k] * factor[j][k]
            factor[i][j] = offdiag / factor[j][j]
    solved = []
    solved_rhs = []
    for j in range(5):
        current = weighted_l[:, j, :]
        target = beta_vec[j]
        for k in range(j):
            current = current - factor[j][k][:, None] * solved[k]
            target = target - factor[j][k] * solved_rhs[k]
        solved.append(current / factor[j][j][:, None])
        solved_rhs.append(target / factor[j][j])
    scaled = jnp.stack(solved, axis=1)
    projection = solved[0] * solved_rhs[0][:, None]
    for k in range(1, 5):
        projection = projection + solved[k] * solved_rhs[k][:, None]
    hit_factor = masked_w * misfit - projection
    return (scaled, hit_factor, masked_w)


def fit_tracks(gderiv, packed, block_rows, counts, place):
    hit_slots = block_rows.shape[1]
    blocks = place.shape[0]
    live_hits = (jnp.arange(hit_slots)[None, :] < counts[:, None]).astype(jnp.float32)
    floats = packed.astype(jnp.float32)
    scaled, hit_factor, masked_w = cholesky_fit(
        floats[:, 0:5, :], floats[:, 5, :], floats[:, 6, :], live_hits
    )
    matches = (block_rows[:, :, None] == jnp.arange(blocks)[None, None, :]).astype(jnp.float32)
    placing = (place[:, None] == jnp.arange(blocks)[None, :]).astype(jnp.float32)
    onehot = jnp.einsum("nhb,bp->nhp", matches, placing, precision=lax.Precision.HIGHEST)
    gfloat = gderiv.astype(jnp.float32)
    expanded = scaled[:, :, :, None] * onehot[:, None, :, :]
    spread = jnp.einsum("nchp,nhi->ncpi", expanded, gfloat, precision=lax.Precision.HIGHEST).astype(
        jnp.bfloat16
    )
    weighted = (masked_w[:, :, None] * gfloat).astype(jnp.bfloat16)
    return (spread, weighted, hit_factor.astype(jnp.bfloat16), onehot)


def place_direct(weighted, gderiv, onehot):
    blocks = onehot.shape[2]
    block_size = gderiv.shape[2]
    flat_g = gderiv.reshape(-1, block_size)
    diagonal_part = jnp.zeros((blocks * block_size, blocks * block_size), jnp.float32)
    for column in range(blocks):
        picked = (weighted * onehot[:, :, column, None].astype(jnp.bfloat16)).reshape(
            -1, block_size
        )
        tile_sum = lax.dot_general(
            picked, flat_g, (((0,), (0,)), ((), ())), preferred_element_type=jnp.float32
        )
        diagonal_part = diagonal_part.at[
            column * block_size : (column + 1) * block_size,
            column * block_size : (column + 1) * block_size,
        ].set(tile_sum)
    return diagonal_part


def right_vector(hit_factor, gderiv, onehot):
    block_size = gderiv.shape[2]
    loads = (hit_factor[:, :, None] * onehot.astype(jnp.bfloat16)).reshape(-1, onehot.shape[2])
    summed = lax.dot_general(
        loads,
        gderiv.reshape(-1, block_size),
        (((0,), (0,)), ((), ())),
        preferred_element_type=jnp.float32,
    )
    return summed.reshape(-1)


def local(
    global_deriv,
    local_deriv,
    hit_weight,
    hit_resid,
    block_ids,
    hit_count,
    track_region,
    block_place,
):
    slab_width = block_place.shape[0] * global_deriv.shape[2]
    regions = lax.axis_size("region")
    owning = track_region[:, 0]
    packed = jnp.concatenate([local_deriv, hit_weight[:, None, :], hit_resid[:, None, :]], axis=1)
    spread, weighted, hit_factor, onehot = fit_tracks(
        global_deriv, packed, block_ids, hit_count, block_place
    )

    def region_term(index):
        keeper = (owning == index).astype(jnp.bfloat16)
        flat_spread = (spread * keeper[:, None, None, None]).reshape(-1, slab_width)
        schur = lax.dot_general(
            flat_spread, flat_spread, (((0,), (0,)), ((), ())), preferred_element_type=jnp.float32
        )
        diagonal_part = place_direct(weighted * keeper[:, None, None], global_deriv, onehot)
        return (
            diagonal_part - schur,
            right_vector(hit_factor * keeper[:, None], global_deriv, onehot),
        )

    partials, vectors = lax.map(region_term, jnp.arange(regions))
    matrix_rows, vector_rows = (
        lax.psum_scatter(
            partials.reshape(-1, slab_width), ("region", "tile"), scatter_dimension=0, tiled=True
        ),
        lax.psum_scatter(vectors.reshape(-1), ("region", "tile"), scatter_dimension=0, tiled=True),
    )
    return (matrix_rows.reshape(1, -1, slab_width), vector_rows.reshape(1, -1))


def solution(mesh):
    return jax.shard_map(
        local,
        mesh=mesh,
        in_specs=(
            P(("region", "tile"), None, None),
            P(("region", "tile"), None, None),
            P(("region", "tile"), None),
            P(("region", "tile"), None),
            P(("region", "tile"), None),
            P(("region", "tile")),
            P(("region", "tile"), None),
            P(),
        ),
        out_specs=(P("region", "tile", None), P("region", "tile")),
        check_vma=False,
    )
```

profile of v0, /device:TPU:0, one launch (start us, length us, event | category | flops | bytes accessed | tf_op | source)
XLA Modules:
  0.0 321.4 jit_solution(2999021492277848735)
XLA Ops:
  15.7 2.9 multiply_convert_fusion
  23.6 5.1 %fusion.81 = bf16[192,5,8,128]{3,2,1,0:T(8,128)(2,1)S(1)} fusion(f32[192,32,8]{1,2,0:T(8,128)} %copy.24, f32[192,5,32]{2,1,0:T(8,128)} %copy.23, bf16[192,32,128]{2,1,0:T(8,128)(2,1)} %param.26), kind=kOutput, calls=%fused_computation.55 | convolution fusion | flops 378716160 | bytes 3858432 | tf_op jit(solution)/shard_map/nchp,nhi->ncpi/dot_general | solution.py:60
  29.2 98.9 %while.24 = (s32[]{:T(128)}, f32[4,1024,1024]{2,1,0:T(8,128)}, f32[4,1024]{1,0:T(4,128)}, s32[4]{0:T(128)}, s32[192]{0:T(256)}, /*index=5*/bf16[192,32,128]{2,0,...) while((s32[]{:T(128)}, f32[4,1024,1024]{2,1,0:T(8,128)}, ...), condition=%wide.region_21.0_spmd, body=%wide.region_20.21_spmd.sunk | while | flops 3651131904 | bytes 53119696 | solution.py:128
  31.8 2.9 fusion.198
  36.2 1.5 fusion.199
  37.7 1.5 fusion.200
  39.3 1.5 fusion.201
  40.8 1.5 fusion.202
  42.4 1.5 fusion.203
  43.9 1.5 fusion.204
  45.4 1.5 fusion.205
  47.3 4.3 %bitcast_dynamic-update-slice_fusion.2 = f32[4,1024,1024]{2,1,0:T(8,128)} fusion(f32[4,1024,1024]{2,1,0:T(8,128)} %get-tuple-element.706, s32[]{:T(128)} %get-tuple-element.705, f32[1024,1024]{1,0:T(8,128)S(1)} %fusion.205, bf16[120,8,8,128]{3,2,1,0:T(8,128)(2,1)S(1)} %bitcast.314), kind=kOutput, calls=%fused_computation.clone.1 | convolution fusion | flops 2014314496 | bytes 10355200 | tf_op jit(solution)/shard_map/while/body/eval_jaxpr/dot_general | solution.py:119
  52.6 1.3 dynamic_update_slice.24
  55.2 1.3 compare_convert_fusion.2
  56.5 2.9 fusion.198
  60.9 1.5 fusion.199
  62.4 1.5 fusion.200
  63.9 1.5 fusion.201
  65.5 1.5 fusion.202
  67.0 1.5 fusion.203
  68.6 1.5 fusion.204
  70.1 1.5 fusion.205
  71.9 4.4 %bitcast_dynamic-update-slice_fusion.2 = f32[4,1024,1024]{2,1,0:T(8,128)} fusion(f32[4,1024,1024]{2,1,0:T(8,128)} %get-tuple-element.706, s32[]{:T(128)} %get-tuple-element.705, f32[1024,1024]{1,0:T(8,128)S(1)} %fusion.205, bf16[120,8,8,128]{3,2,1,0:T(8,128)(2,1)S(1)} %bitcast.314), kind=kOutput, calls=%fused_computation.clone.1 | convolution fusion | flops 2014314496 | bytes 10355200 | tf_op jit(solution)/shard_map/while/body/eval_jaxpr/dot_general | solution.py:119
  77.3 1.3 dynamic_update_slice.24
  79.9 1.3 compare_convert_fusion.2
  81.2 2.9 fusion.198
  85.6 1.5 fusion.199
  87.1 1.5 fusion.200
  88.7 1.5 fusion.201
  90.2 1.5 fusion.202
  91.8 1.5 fusion.203
  93.3 1.5 fusion.204
  94.8 1.5 fusion.205
  96.7 4.4 %bitcast_dynamic-update-slice_fusion.2 = f32[4,1024,1024]{2,1,0:T(8,128)} fusion(f32[4,1024,1024]{2,1,0:T(8,128)} %get-tuple-element.706, s32[]{:T(128)} %get-tuple-element.705, f32[1024,1024]{1,0:T(8,128)S(1)} %fusion.205, bf16[120,8,8,128]{3,2,1,0:T(8,128)(2,1)S(1)} %bitcast.314), kind=kOutput, calls=%fused_computation.clone.1 | convolution fusion | flops 2014314496 | bytes 10355200 | tf_op jit(solution)/shard_map/while/body/eval_jaxpr/dot_general | solution.py:119
  102.0 1.3 dynamic_update_slice.24
  104.6 1.3 compare_convert_fusion.2
  106.0 2.9 fusion.198
  110.3 1.5 fusion.199
  111.9 1.5 fusion.200
  113.4 1.5 fusion.201
  114.9 1.5 fusion.202
  116.5 1.5 fusion.203
  118.0 1.5 fusion.204
  119.6 1.5 fusion.205
  121.4 4.3 %bitcast_dynamic-update-slice_fusion.2 = f32[4,1024,1024]{2,1,0:T(8,128)} fusion(f32[4,1024,1024]{2,1,0:T(8,128)} %get-tuple-element.706, s32[]{:T(128)} %get-tuple-element.705, f32[1024,1024]{1,0:T(8,128)S(1)} %fusion.205, bf16[120,8,8,128]{3,2,1,0:T(8,128)(2,1)S(1)} %bitcast.314), kind=kOutput, calls=%fused_computation.clone.1 | convolution fusion | flops 2014314496 | bytes 10355200 | tf_op jit(solution)/shard_map/while/body/eval_jaxpr/dot_general | solution.py:119
  126.7 1.3 dynamic_update_slice.24
  128.8 47.1 %all-reduce.1 = f32[4096]{0:T(1024)S(1)} all-reduce(f32[4096]{0:T(1024)S(1)} %bitcast.317), channel_id=3, replica_groups=mesh['region'=4,'tile'=8] {'region','tile'}, use_global_device_ids=true, to_apply=%region_23.0.clone | all-reduce | flops 4096 | bytes 32768
  176.5 138.0 %reduce-scatter.2.cloned.1.call-done = f32[128,1024]{1,0:T(8,128)} async-done(((f32[4096,1024]{1,0:T(8,128)}), f32[128,1024]{1,0:T(8,128)}) %reduce-scatter.2.cloned.1.call-update) | async-done | bytes 524304 | tf_op jit(solution)/shard_map/reduce_scatter | solution.py:130
  (152 shorter events, 32.3 us)
Async XLA Ops:
  7.2 5.6 %copy-start.5 = (s32[192,32]{0,1:T(8,128)S(1)}, s32[192,32]{0,1:T(8,128)}, u32[]{:S(2)}) copy-start(s32[192,32]{0,1:T(8,128)} %param.30) | copy-start | bytes 73732
  7.2 5.5 %copy-start.20 = (s32[8]{0:T(128)S(1)}, s32[8]{0:T(128)}, u32[]{:S(2)}) copy-start(s32[8]{0:T(128)} %param.33) | copy-start | bytes 100
  7.2 307.3 %reduce-scatter.2.cloned.1.call-start = ((), (), s32[]{:S(2)}) async-start(), calls=%async_computation.1 | async-start | bytes 17301504 | tf_op jit(solution)/shard_map/reduce_scatter | solution.py:130
  8.2 4.7 %copy-start.3 = (f32[192,7,32]{0,2,1:T(8,128)}, f32[192,7,32]{0,2,1:T(8,128)S(1)}, u32[]{:S(2)}) copy-start(f32[192,7,32]{0,2,1:T(8,128)S(1)} %maximum_convert_fusion) | copy-start | bytes 516100
  10.8 3.3 %copy-start = (bf16[192,32,128]{2,1,0:T(8,128)(2,1)S(1)}, bf16[192,32,128]{2,1,0:T(8,128)(2,1)}, u32[]{:S(2)}) copy-start(bf16[192,32,128]{2,1,0:T(8,128)(2,1)} %param.26) | copy-start | bytes 4718596
  12.9 5.6 %copy-start.1 = (bf16[192,32,8]{0,2,1:T(8,128)(2,1)}, bf16[192,32,8]{0,2,1:T(8,128)(2,1)S(1)}, u32[]{:S(2)}) copy-start(bf16[192,32,8]{0,2,1:T(8,128)(2,1)S(1)} %get-tuple-element.701) | copy-start | bytes 294916
  14.1 0.7 copy-start.14
  14.1 0.7 copy-start.15
  14.1 0.7 copy-start.16
  14.1 0.7 copy-start.17
  14.1 0.7 copy-start.18
  34.8 1.4 copy-start.4
  34.8 1.4 copy-start.6
  36.2 1.5 copy-start.7
  37.7 1.5 copy-start.8
  39.3 1.5 copy-start.9
  40.8 1.5 copy-start.10
  42.3 1.5 copy-start.11
  43.9 1.5 copy-start.12
  47.2 4.3 %copy-start.2 = (bf16[192,32,8]{0,2,1:T(8,128)(2,1)S(1)}, bf16[192,32,8]{0,2,1:T(8,128)(2,1)}, u32[]{:S(2)}) copy-start(bf16[192,32,8]{0,2,1:T(8,128)(2,1)} %get-tuple-element.743) | copy-start | bytes 294916 | tf_op jit(solution)/shard_map/while
  59.4 1.4 copy-start.4
  59.5 1.4 copy-start.6
  60.9 1.5 copy-start.7
  62.4 1.5 copy-start.8
  63.9 1.5 copy-start.9
  65.5 1.5 copy-start.10
  67.0 1.5 copy-start.11
  68.6 1.5 copy-start.12
  71.9 4.4 %copy-start.2 = (bf16[192,32,8]{0,2,1:T(8,128)(2,1)S(1)}, bf16[192,32,8]{0,2,1:T(8,128)(2,1)}, u32[]{:S(2)}) copy-start(bf16[192,32,8]{0,2,1:T(8,128)(2,1)} %get-tuple-element.743) | copy-start | bytes 294916 | tf_op jit(solution)/shard_map/while
  84.2 1.4 copy-start.4
  84.2 1.4 copy-start.6
  85.6 1.5 copy-start.7
  87.1 1.5 copy-start.8
  88.7 1.5 copy-start.9
  90.2 1.5 copy-start.10
  91.8 1.5 copy-start.11
  93.3 1.5 copy-start.12
  96.7 4.4 %copy-start.2 = (bf16[192,32,8]{0,2,1:T(8,128)(2,1)S(1)}, bf16[192,32,8]{0,2,1:T(8,128)(2,1)}, u32[]{:S(2)}) copy-start(bf16[192,32,8]{0,2,1:T(8,128)(2,1)} %get-tuple-element.743) | copy-start | bytes 294916 | tf_op jit(solution)/shard_map/while
  108.9 1.4 copy-start.4
  108.9 1.4 copy-start.6
  110.3 1.5 copy-start.7
  111.8 1.5 copy-start.8
  113.4 1.5 copy-start.9
  114.9 1.5 copy-start.10
  116.5 1.5 copy-start.11
  118.0 1.5 copy-start.12
  121.4 4.4 %copy-start.2 = (bf16[192,32,8]{0,2,1:T(8,128)(2,1)S(1)}, bf16[192,32,8]{0,2,1:T(8,128)(2,1)}, u32[]{:S(2)}) copy-start(bf16[192,32,8]{0,2,1:T(8,128)(2,1)} %get-tuple-element.743) | copy-start | bytes 294916 | tf_op jit(solution)/shard_map/while
  128.1 0.7 copy-start.13
  (1 other events, 0.7 us)
Sparse Core Ops, SparseCore 0:
  128.2 186.2 reduce-scatter.1
where the time goes:
time: 324 us; the launch traced here: 321 us
  waiting for transfers between devices  138 us (43%)
  matrix products  80.8 us (25%)
  blocking collectives  47.1 us (15%)
  local copies, waits for them, and re-layouts  26.1 us (8%)
  other arithmetic  14.3 us (4%)
  between operations  14.2 us (4%)
    reduce_scatter x1, waiting for transfers between devices, local(): lax.psum_scatter(partials.reshape(-1, slab_width), ('region', 'tile'), sc...  138 us
    dot_general x32, matrix products, place_direct(): lax.dot_general(picked, flat_g, (((0,), (0,)), ((), ())), preferred_eleme...  54.3 us
    unnamed x1, blocking collectives  47.1 us
    dot_general x4, matrix products, region_term(): lax.dot_general(flat_spread, flat_spread, (((0,), (0,)), ((), ())), prefe...  17.4 us
  transfers between devices with their start and end apart: 1, of which 1 were waited for; matrix products, arithmetic and copies ran while one was open for 0% of the time, Pallas kernels for 0%

commit v1 on v0

v1 whole, which is shorter than its diff:
```python
import functools
import jax
import jax.numpy as jnp
from jax import lax
from jax.experimental import pallas as pl
from jax.experimental.pallas import tpu as pltpu
from jax.sharding import PartitionSpec as P

F32 = jnp.float32
BF16 = jnp.bfloat16
GROUP = 8
DEPTH = 256

NT = (((1,), (1,)), ((), ()))


def iota(shape, axis):
    return lax.broadcasted_iota(jnp.int32, shape, axis)


def fit(ld, weight, resid, counts):
    hits = weight.shape[0]
    live = iota(weight.shape, 0) < counts.astype(jnp.int32)
    masked_w = jnp.where(live, weight, 0.0)
    weighted_l = [v * masked_w for v in ld]
    gamma = [[None] * 5 for _ in range(5)]
    for a in range(5):
        for b in range(a + 1):
            gamma[a][b] = jnp.sum(weighted_l[a] * ld[b], axis=0, keepdims=True)
            if a == b:
                gamma[a][b] = gamma[a][b] + 1.0
    beta = [jnp.sum(weighted_l[a] * resid, axis=0, keepdims=True) for a in range(5)]
    factor = [[None] * 5 for _ in range(5)]
    inverse = [None] * 5
    for j in range(5):
        center = gamma[j][j]
        for k in range(j):
            center = center - factor[j][k] * factor[j][k]
        factor[j][j] = jnp.sqrt(center)
        inverse[j] = 1.0 / factor[j][j]
        for i in range(j + 1, 5):
            offdiag = gamma[i][j]
            for k in range(j):
                offdiag = offdiag - factor[i][k] * factor[j][k]
            factor[i][j] = offdiag * inverse[j]
    solved, rhs = [], []
    for j in range(5):
        current, target = weighted_l[j], beta[j]
        for k in range(j):
            current = current - factor[j][k] * solved[k]
            target = target - factor[j][k] * rhs[k]
        solved.append(current * inverse[j])
        rhs.append(target * inverse[j])
    projection = solved[0] * rhs[0]
    for k in range(1, 5):
        projection = projection + solved[k] * rhs[k]
    return solved, masked_w * resid - projection, masked_w


def prepare(place_ref, region_ref, packed_ref, scaled_s, lanes_s, table_v, table_s):
    tracks = packed_ref.shape[0]
    slots = scaled_s.shape[1]
    groups = slots // GROUP
    hits = DEPTH // GROUP
    blocks = place_ref.shape[0]
    rr = table_v.shape[0] - 8
    member = iota((rr, tracks), 0) == region_ref[...]
    member_f = member.astype(F32)
    before = (iota((tracks, tracks), 0) < iota((tracks, tracks), 1)).astype(F32).astype(BF16)
    rank = jnp.dot(member_f.astype(BF16), before, preferred_element_type=F32)
    count = jnp.sum(member_f, axis=1, keepdims=True)
    room = lax.shift_left(lax.shift_right_logical(count.astype(jnp.int32) + 7, 3), 3)
    room = jnp.broadcast_to(room.astype(F32), (rr, slots))
    lower = (iota((rr, rr), 1) < iota((rr, rr), 0)).astype(F32)
    start = jnp.zeros((rr, slots), F32)
    for g in range(rr):
        start = start + lower[:, g : g + 1] * room[g : g + 1, :]
    slot = jnp.sum(member_f * (rank + start[:, 0:1]), axis=0, keepdims=True)
    perm = (iota((slots, tracks), 0) == slot.astype(jnp.int32)).astype(F32).astype(BF16)
    numbers = iota((8, tracks), 1).astype(F32).astype(BF16)
    order = lax.dot_general(numbers, perm, NT, preferred_element_type=F32)
    table_v[0:8, :] = order.astype(jnp.int32)
    table_v[8:, :] = jnp.where(
        iota((rr, slots), 1) == 0, start.astype(jnp.int32), (start + room).astype(jnp.int32)
    )
    pltpu.sync_copy(table_v, table_s)
    rows = jnp.dot(perm, packed_ref[...], preferred_element_type=F32)
    flat = rows.T
    ld = [flat[c * hits : (c + 1) * hits] for c in range(5)]
    weight, resid, ids = (flat[c * hits : (c + 1) * hits] for c in range(5, 8))
    counts = flat[8 * hits : 8 * hits + 1]
    solved, hit_factor, masked_w = fit(ld, weight, resid, counts)
    position = jnp.zeros_like(ids)
    for b in range(blocks):
        position = jnp.where(ids == float(b), place_ref[b].astype(F32), position)
    own = (iota((DEPTH, slots), 0) // hits) == (iota((DEPTH, slots), 1) % GROUP)

    def spread_out(value):
        return jnp.where(own, jnp.concatenate([value] * GROUP, axis=0), 0.0)

    grouping = (iota((groups, slots), 1) // GROUP == iota((groups, slots), 0)).astype(F32)
    grouping = grouping.astype(BF16)
    for n, value in enumerate((masked_w, position, hit_factor)):
        lanes_s[n] = lax.dot_general(
            grouping, spread_out(value).astype(BF16), NT, preferred_element_type=F32
        )
    for c in range(5):
        scaled_s[c] = spread_out(solved[c]).T


def one_group(group, local, order_s, g_ref, scaled_s, lanes_s, g_s, direct_s, spread_s):
    hits, width = g_ref.shape[1:]
    blocks = spread_s.shape[0]
    for i in range(GROUP):
        g_s[i * hits : (i + 1) * hits, :] = g_ref[order_s[0, group * GROUP + i]]
    g = g_s[...]
    weight = lanes_s[0, pl.ds(group, 1), :]
    position = lanes_s[1, pl.ds(group, 1), :]
    hit_factor = lanes_s[2, pl.ds(group, 1), :]
    weighted = g.astype(F32).T * weight
    base = pl.multiple_of(group * GROUP, GROUP)
    scaled = jnp.concatenate([scaled_s[c, pl.ds(base, GROUP), :] for c in range(5)], axis=0)
    high = scaled.astype(BF16).astype(F32)
    low = scaled - high
    direct, highs, lows = [], [], []
    for p in range(blocks):
        here = position == float(p)
        direct.append(jnp.where(here, weighted, 0.0))
        highs.append(jnp.where(here, high, 0.0))
        lows.append(jnp.where(here, low, 0.0))
    sub = iota((16, DEPTH), 0).astype(F32)
    vector = jnp.where(sub == position, hit_factor, 0.0)
    total = jnp.dot(
        jnp.concatenate(direct + [vector], axis=0).astype(BF16), g, preferred_element_type=F32
    )
    direct_s[...] += total
    upper = jnp.dot(
        jnp.concatenate(highs, axis=0).astype(BF16), g, preferred_element_type=F32
    ) + jnp.dot(jnp.concatenate(lows, axis=0).astype(BF16), g, preferred_element_type=F32)
    step = 5 * GROUP
    at = pl.multiple_of(local * step, GROUP)
    for p in range(blocks):
        spread_s[p, pl.ds(at, step), :] = upper[p * step : (p + 1) * step]


def assemble_kernel(
    where_ref, place_ref, region_ref, packed_ref, g_ref,
    keep_a, send_a, keep_b, send_b,
    scaled_s, lanes_s, table_v, table_s, g_s, direct_s, spread_s, wide_s, turned_s, acc_s,
):
    k = pl.program_id(0)
    blocks, _, width = spread_s.shape

    @pl.when(k == 0)
    def _():
        prepare(place_ref, region_ref, packed_ref, scaled_s, lanes_s, table_v, table_s)

    region = where_ref[1] ^ k
    first = table_s[8 + region, 0] // GROUP
    groups = table_s[8 + region, 1] // GROUP - first
    direct_s[...] = jnp.zeros_like(direct_s)
    acc_s[...] = jnp.zeros_like(acc_s)

    def group_step(local, carry):
        one_group(
            first + local, local, table_s, g_ref, scaled_s, lanes_s, g_s, direct_s, spread_s
        )
        return carry

    lax.fori_loop(0, groups, group_step, 0)
    used = groups * 5
    depth_tiles = DEPTH // 8
    chunks = (used + depth_tiles - 1) // depth_tiles

    def clear(tile, carry):
        spread_s[:, pl.ds(pl.multiple_of(tile * 8, 8), 8), :] = jnp.zeros((blocks, 8, width), F32)
        return carry

    lax.fori_loop(used, chunks * depth_tiles, clear, 0)

    def chunk_step(chunk, carry):
        at = pl.multiple_of(chunk * DEPTH, DEPTH)
        for p in range(blocks):
            part = spread_s[p, pl.ds(at, DEPTH), :]
            narrow = part.astype(BF16)
            wide_s[:, p * width : (p + 1) * width] = narrow
            if p < blocks // 2:
                wide_s[:, (blocks + p) * width : (blocks + p + 1) * width] = narrow
            turned_s[p] = narrow.astype(F32).T.astype(BF16)
        for p in range(blocks):
            many = blocks // 2 + (1 if p < blocks // 2 else 0)
            acc_s[p, :, : many * width] += jnp.dot(
                turned_s[p],
                wide_s[:, p * width : (p + many) * width],
                preferred_element_type=F32,
            )
        return carry

    lax.fori_loop(0, chunks, chunk_step, 0)
    half = width // 2
    for j in range(blocks):
        p = where_ref[0] ^ j
        at = pl.multiple_of(p * width, width)
        d0 = direct_s[pl.ds(at, width), :] - acc_s[p, :, 0:width]
        d1, d2, d3 = (0.0 - acc_s[p, :, d * width : (d + 1) * width] for d in range(1, 4))
        upper = pl.multiple_of((p // (blocks // 2)) * half, half)
        ext = 0.0 - acc_s[p % (blocks // 2), pl.ds(upper, half), 4 * width : 5 * width]
        row = direct_s[pl.ds(blocks * width + p, 1), :]
        row_high = row.astype(BF16).astype(F32)
        sub = iota((16, width), 0)
        row_tile = jnp.where(sub == 0, row_high, jnp.where(sub == 1, row - row_high, 0.0))
        part_a = jnp.concatenate([d0, d1, ext[: half // 2], row_tile], axis=0).astype(BF16)
        part_b = jnp.concatenate([d2, d3, ext[half // 2 :]], axis=0).astype(BF16)
        (send_a if j & 1 else keep_a)[ORDER_A.index(j & 6), 0] = part_a
        (send_b if j & 1 else keep_b)[ORDER_B.index(j & 6), 0] = part_b


ORDER_A = (0, 4, 2, 6)
ORDER_B = (0, 2, 4, 6)


def assemble(where, place, region_row, packed, g, regions):
    tracks, hits, width = g.shape
    blocks = place.shape[0]
    rr = -(-regions // 8) * 8
    slots = -(-(tracks + regions * (GROUP - 1)) // 128) * 128
    rows_a, rows_b = width * 2 + width // 4 + 16, width * 2 + width // 4
    longest = -(-(-(-tracks // GROUP) * 5 * GROUP) // DEPTH) * DEPTH

    def out(rows):
        return jax.ShapeDtypeStruct((blocks // 2, regions, rows, width), BF16)

    def spec(rows):
        return pl.BlockSpec((blocks // 2, 1, rows, width), lambda k: (0, k, 0, 0))

    smem = pl.BlockSpec(memory_space=pltpu.SMEM)
    vmem = pl.BlockSpec(memory_space=pltpu.VMEM)
    return pl.pallas_call(
        assemble_kernel,
        grid=(regions,),
        in_specs=[smem, smem, vmem, vmem, vmem],
        out_specs=[spec(rows_a), spec(rows_a), spec(rows_b), spec(rows_b)],
        out_shape=[out(rows_a), out(rows_a), out(rows_b), out(rows_b)],
        scratch_shapes=[
            pltpu.VMEM((5, slots, DEPTH), F32),
            pltpu.VMEM((3, slots // GROUP, DEPTH), F32),
            pltpu.VMEM((8 + rr, slots), jnp.int32),
            pltpu.SMEM((8 + rr, slots), jnp.int32),
            pltpu.VMEM((DEPTH, width), BF16),
            pltpu.VMEM((blocks * width + 16, width), F32),
            pltpu.VMEM((blocks, longest, width), F32),
            pltpu.VMEM((DEPTH, (blocks + blocks // 2) * width), BF16),
            pltpu.VMEM((blocks, width, DEPTH), BF16),
            pltpu.VMEM((blocks, width, (blocks // 2 + 1) * width), F32),
        ],
        compiler_params=pltpu.CompilerParams(
            dimension_semantics=("arbitrary",), vmem_limit_bytes=48 * 1024 * 1024
        ),
        cost_estimate=pl.CostEstimate(
            flops=8 * 10**9, bytes_accessed=8 * 10**6, transcendentals=0
        ),
        name="assemble",
    )(where, place, region_row, packed, g)


def finish_kernel(where_ref, a_ref, b_ref, r1_ref, r2_ref, r3_ref, e_ref, out_ref, vec_ref):
    width = a_ref.shape[1]
    half = width // 2
    p = where_ref[0]
    blocks = out_ref.shape[1] // width

    def put(column, value):
        column = pl.multiple_of(((column + blocks) % blocks) * width, width)
        out_ref[:, pl.ds(column, width)] = value

    put(p, a_ref[0:width, :])
    put(p + 1, a_ref[width : 2 * width, :])
    put(p + 2, b_ref[0:width, :])
    put(p + 3, b_ref[width : 2 * width, :])
    for d, ref in ((1, r1_ref), (2, r2_ref), (3, r3_ref)):
        put(p - d, ref[...].astype(F32).T)
    mine = [a_ref[2 * width : 2 * width + half // 2, :], b_ref[2 * width :, :]]
    other = e_ref[...].astype(F32)

    @pl.when(p < blocks // 2)
    def _():
        put(p + blocks // 2, jnp.concatenate(mine + [other], axis=0))

    @pl.when(p >= blocks // 2)
    def _():
        put(p + blocks // 2, jnp.concatenate([other] + mine, axis=0).T)

    tail = 2 * width + half // 2
    vec_ref[...] = a_ref[tail : tail + 1, :] + a_ref[tail + 1 : tail + 2, :]


def finish(where, a, b, r1, r2, r3, ext, blocks):
    width = a.shape[1]
    smem = pl.BlockSpec(memory_space=pltpu.SMEM)
    vmem = pl.BlockSpec(memory_space=pltpu.VMEM)
    return pl.pallas_call(
        finish_kernel,
        in_specs=[smem] + [vmem] * 6,
        out_specs=[vmem, vmem],
        out_shape=[
            jax.ShapeDtypeStruct((width, blocks * width), F32),
            jax.ShapeDtypeStruct((1, width), F32),
        ],
        name="finish",
    )(where, a, b, r1, r2, r3, ext)


def local(
    tiles, global_deriv, local_deriv, hit_weight, hit_resid, block_ids, hit_count, track_region,
    block_place,
):
    regions = lax.axis_size("region")
    tracks, hits, width = global_deriv.shape
    blocks = block_place.shape[0]
    sub = tiles // blocks
    tile = lax.axis_index("tile")
    where = jnp.stack([tile // sub, lax.axis_index("region")]).astype(jnp.int32)
    packed = jnp.concatenate(
        [
            local_deriv.reshape(tracks, -1),
            hit_weight,
            hit_resid,
            block_ids.astype(BF16),
            jnp.broadcast_to(hit_count.astype(BF16)[:, None], (tracks, 32)),
        ],
        axis=1,
    )
    keep_a, send_a, keep_b, send_b = assemble(
        where, block_place, track_region.reshape(1, tracks), packed, global_deriv, regions
    )

    def swap(value, bit):
        return lax.ppermute(value, "tile", [(t, t ^ bit) for t in range(tiles)])

    def reduce_tile(keep, send, bits):
        bit = 1
        while bit < sub:
            keep, send = keep + swap(keep, bit), send + swap(send, bit)
            bit *= 2
        got = swap(send, sub * bits[0])
        total = keep.astype(F32) + got.astype(F32)
        got = swap(total[2:].astype(BF16), sub * bits[1])
        total = total[:2] + got.astype(F32)
        got = swap(total[1].astype(BF16), sub * bits[2])
        return total[0] + got.astype(F32)

    def reduce_region(total):
        narrow = total[1:].astype(BF16)
        result = total[0]
        for k in range(1, regions):
            result = result + lax.ppermute(
                narrow[k - 1], "region", [(r, r ^ k) for r in range(regions)]
            ).astype(F32)
        return result

    a = reduce_region(reduce_tile(keep_a, send_a, (1, 2, 4)))
    b = reduce_region(reduce_tile(keep_b, send_b, (1, 4, 2)))

    def onward(value, d):
        pairs = [
            (p * sub + s, ((p + d) % blocks) * sub + s) for p in range(blocks) for s in range(sub)
        ]
        return lax.ppermute(value.astype(BF16), "tile", pairs)

    ext = jnp.concatenate([a[2 * width : 2 * width + width // 4], b[2 * width :]], axis=0)
    matrix, vector = finish(
        where,
        a,
        b,
        onward(a[width : 2 * width], 1),
        onward(b[:width], 2),
        onward(b[width : 2 * width], 3),
        onward(ext, blocks // 2),
        blocks,
    )
    if sub > 1:
        part = tile % sub
        rows = width // sub
        matrix = lax.dynamic_slice(matrix, (part * rows, 0), (rows, blocks * width))
        vector = lax.dynamic_slice(vector, (0, part * rows), (1, rows))
    return matrix[None], vector


def solution(mesh):
    return jax.shard_map(
        functools.partial(local, mesh.shape["tile"]),
        mesh=mesh,
        in_specs=(
            P(("region", "tile"), None, None),
            P(("region", "tile"), None, None),
            P(("region", "tile"), None),
            P(("region", "tile"), None),
            P(("region", "tile"), None),
            P(("region", "tile")),
            P(("region", "tile"), None),
            P(),
        ),
        out_specs=(P("region", "tile", None), P("region", "tile")),
        check_vma=False,
    )
```

time: 324 us -> 86.3 us (0.27)
  waiting for transfers between devices: 138 us -> 33 us
  matrix products: 80.8 us -> 0 us
  blocking collectives: 47.1 us -> 0 us
  Pallas kernels: 0 us -> 22.2 us
  local copies, waits for them, and re-layouts: 26.1 us -> 5.27 us
  starting transfers between devices: 0.04 us -> 20.8 us
  between operations: 14.2 us -> 0.82 us
  other arithmetic: 14.3 us -> 3.9 us
    reduce_scatter x1 -> x0, waiting for transfers between devices: 138 us -> none  [local(): lax.psum_scatter(partials.reshape(-1, slab_width), ('region', 'tile'), sc...]
    dot_general x42 -> x0, matrix products: 80.8 us -> none  [the longest x32 54.3 us: place_direct(): lax.dot_general(picked, flat_g, (((0,), (0,)), ((), ())), preferred_eleme...]
    unnamed x1 -> x0, blocking collectives: 47.1 us -> none
    ppermute x0 -> x16, waiting for transfers between devices: none -> 33 us  [the longest x6 20.8 us: swap(): return lax.ppermute(value, 'tile', [(t, t ^ bit) for t in range(tiles)])]
    pallas_call x0 -> x2, Pallas kernels: none -> 22.2 us  [the longest x1 20.2 us: assemble(): pl.pallas_call(assemble_kernel, grid=(regions,), in_specs=[smem, smem, vm...]
    ppermute x0 -> x16, starting transfers between devices: none -> 20.8 us  [the longest x6 9.64 us: swap(): return lax.ppermute(value, 'tile', [(t, t ^ bit) for t in range(tiles)])]
    convert_element_type x7 -> x2, other arithmetic: 9.93 us -> 1.45 us  [the longest x1 0.76 us: local(): block_ids.astype(BF16)]
    while x80 -> x0, local copies, waits for them, and re-layouts: 8.42 us -> none  [the longest x8 4.82 us: local(): partials, vectors = lax.map(region_term, jnp.arange(regions))]
  transfers between devices with their start and end apart: 1 -> 16, of which waited for: 1 -> 11; matrix products, arithmetic and copies ran while one was open for 0% -> 3% of each run, Pallas kernels for 0% -> 0%
where the time goes in v1:
time: 86.3 us; the launch traced here: 85.9 us
  waiting for transfers between devices  33 us (38%)
  Pallas kernels  22.2 us (26%)
  starting transfers between devices  20.8 us (24%)
  local copies, waits for them, and re-layouts  5.27 us (6%)
  other arithmetic  3.9 us (5%)
    ppermute x6, waiting for transfers between devices, swap(): return lax.ppermute(value, 'tile', [(t, t ^ bit) for t in range(tiles)])  20.8 us
    pallas_call x1, Pallas kernels, assemble(): pl.pallas_call(assemble_kernel, grid=(regions,), in_specs=[smem, smem, vm...  20.2 us
    ppermute x6, starting transfers between devices, swap(): return lax.ppermute(value, 'tile', [(t, t ^ bit) for t in range(tiles)])  9.64 us
    ppermute x6, waiting for transfers between devices, reduce_region(): lax.ppermute(narrow[k - 1], 'region', [(r, r ^ k) for r in range(regions)])  9.16 us
    ppermute x6, starting transfers between devices, reduce_region(): lax.ppermute(narrow[k - 1], 'region', [(r, r ^ k) for r in range(regions)])  8.42 us
    unnamed x16, local copies, waits for them, and re-layouts  3.63 us
    ppermute x4, waiting for transfers between devices, onward(): return lax.ppermute(value.astype(BF16), 'tile', pairs)  2.98 us
    ppermute x4, starting transfers between devices, onward(): return lax.ppermute(value.astype(BF16), 'tile', pairs)  2.73 us
  transfers between devices with their start and end apart: 16, of which 11 were waited for; matrix products, arithmetic and copies ran while one was open for 3% of the time, Pallas kernels for 0%

profile of v1, /device:TPU:0, one launch (start us, length us, event | category | flops | bytes accessed | tf_op | source)
XLA Modules:
  0.0 85.9 jit_solution(9780070037166970406)
XLA Ops:
  0.6 0.7 convert_element_type.65
  1.3 0.8 convert_element_type.64
  2.1 0.1 copy.21
  2.2 0.8 copy.19
  3.0 0.8 copy.20
  3.9 1.0 %copy.18 = bf16[192,160]{1,0:T(8,128)(2,1)S(1)} copy(bf16[192,160]{0,1:T(8,128)(2,1)} %bitcast.50) | data formatting | bytes 122880 | tf_op jit(solution)/shard_map/reshape | solution.py:325
  4.9 0.1 pad_add_fusion.where_ref
  5.0 0.1 broadcast_in_dim.4
  5.1 0.1 concatenate.7.packed_ref
  5.2 0.7 copy-done.1
  5.9 0.7 copy-done.2
  6.5 20.2 %assemble.1 = (bf16[4,4,304,128]{3,2,1,0:T(8,128)(2,1)S(1)}, bf16[4,4,304,128]{3,2,1,0:T(8,128)(2,1)S(1)}, bf16[4,4,288,128]{3,2,1,0:T(8,128)(2,1)S(1)}, bf16[4,4,288,128]{3,2,1,0:T(8,128)(2,1)S(1)}) custom-call(s32[2]{0:T(128)S(1)} %pad_add_fusion.where_ref, s32[8]{0:T(128)S(1)} %copy-done.2, s32[1,192]{1,0:T(1,128)S(1)} %bitcast.49, ...), custom_call_target="tpu_custom_call" | custom-call | flops 8000000000 | bytes 8000000 | tf_op jit(solution)/shard_map/assemble/pallas_call | solution.py:238
  26.8 1.3 %collective-permute-start.6 = (bf16[4,4,288,128]{3,2,1,0:T(8,128)(2,1)S(1)}, bf16[4,4,288,128]{3,2,1,0:T(8,128)(2,1)S(1)}, u32[]{:S(2)}, u32[]{:S(2)}) collective-permute-start(bf16[4,4,288,128]{3,2,1,0:T(8,128)(2,1)S(1)} %get-tuple-element.11), channel_id=1, source_target_pairs={{0,1},{1,0},{2,3},{3,2},{4,5},{5,4},{6,7},{7,6},{8,9},{9,8},{10,11... | collective-permute-start | bytes 3538952 | tf_op jit(solution)/shard_map/ppermute | solution.py:338
  28.2 2.4 %collective-permute-done.6 = bf16[4,4,288,128]{3,2,1,0:T(8,128)(2,1)S(1)} collective-permute-done((bf16[4,4,288,128]{3,2,1,0:T(8,128)(2,1)S(1)}, bf16[4,4,288,128]{3,2,1,0:T(8,128)(2,1)S(1)}, u32[]{:S(2)}, u32[]{:S(2)}) %collective-permute-start.6) | collective-permute-done | bytes 1179680 | tf_op jit(solution)/shard_map/ppermute | solution.py:338
  30.6 0.3 convert_add_fusion.1
  30.9 0.1 slice.161
  30.9 2.6 %collective-permute-start.7 = (bf16[2,4,288,128]{3,2,1,0:T(8,128)(2,1)S(1)}, bf16[2,4,288,128]{3,2,1,0:T(8,128)(2,1)S(1)}, u32[]{:S(2)}, u32[]{:S(2)}) collective-permute-start(bf16[2,4,288,128]{3,2,1,0:T(8,128)(2,1)S(1)} %slice.161), channel_id=1, source_target_pairs={{0,4},{1,5},{2,6},{3,7},{4,0},{5,1},{6,2},{7,3},{8,12},{9,13},{10,... | collective-permute-start | bytes 1769480 | tf_op jit(solution)/shard_map/ppermute | solution.py:338
  33.5 0.3 convert_add_fusion
  33.8 0.1 slice.160
  33.9 2.2 %collective-permute-start.1 = (bf16[2,4,304,128]{3,2,1,0:T(8,128)(2,1)S(1)}, bf16[2,4,304,128]{3,2,1,0:T(8,128)(2,1)S(1)}, u32[]{:S(2)}, u32[]{:S(2)}) collective-permute-start(bf16[2,4,304,128]{3,2,1,0:T(8,128)(2,1)S(1)} %slice.160), channel_id=1, source_target_pairs={{0,2},{1,3},{2,0},{3,1},{4,6},{5,7},{6,4},{7,5},{8,10},{9,11},{10,... | collective-permute-start | bytes 1867784 | tf_op jit(solution)/shard_map/ppermute | solution.py:338
  36.1 11.1 %collective-permute-done.7 = bf16[2,4,288,128]{3,2,1,0:T(8,128)(2,1)S(1)} collective-permute-done((bf16[2,4,288,128]{3,2,1,0:T(8,128)(2,1)S(1)}, bf16[2,4,288,128]{3,2,1,0:T(8,128)(2,1)S(1)}, u32[]{:S(2)}, u32[]{:S(2)}) %collective-permute-start.7) | collective-permute-done | bytes 589856 | tf_op jit(solution)/shard_map/ppermute | solution.py:338
  47.2 0.1 slice_add_fusion.1
  47.3 2.6 %collective-permute-start.8 = (bf16[4,288,128]{2,1,0:T(8,128)(2,1)S(1)}, bf16[4,288,128]{2,1,0:T(8,128)(2,1)S(1)}, u32[]{:S(2)}, u32[]{:S(2)}) collective-permute-start(bf16[4,288,128]{2,1,0:T(8,128)(2,1)S(1)} %fusion.3), channel_id=1, source_target_pairs={{0,2},{1,3},{2,0},{3,1},{4,6},{5,7},{6,4},{7,5},{8,10},{9,11},{10,... | collective-permute-start | bytes 884744 | tf_op jit(solution)/shard_map/ppermute | solution.py:338
  49.9 0.8 collective-permute-done.1
  50.7 0.1 slice_add_fusion
  50.8 5.9 %collective-permute-done.8 = bf16[4,288,128]{2,1,0:T(8,128)(2,1)S(1)} collective-permute-done((bf16[4,288,128]{2,1,0:T(8,128)(2,1)S(1)}, bf16[4,288,128]{2,1,0:T(8,128)(2,1)S(1)}, u32[]{:S(2)}, u32[]{:S(2)}) %collective-permute-start.8) | collective-permute-done | bytes 294944 | tf_op jit(solution)/shard_map/ppermute | solution.py:338
  56.7 0.1 fusion.14
  56.8 1.1 %collective-permute-start.9 = (bf16[288,128]{1,0:T(8,128)(2,1)S(1)}, bf16[288,128]{1,0:T(8,128)(2,1)S(1)}, u32[]{:S(2)}, u32[]{:S(2)}) collective-permute-start(bf16[288,128]{1,0:T(8,128)(2,1)S(1)} %get-tuple-element.25), channel_id=1, source_target_pairs={{0,8},{8,0},{16,24},{24,16},{1,9},{9,1},{17,25},{25,17},{2,10},{10... | collective-permute-start | bytes 221192 | tf_op jit(solution)/shard_map/ppermute | solution.py:356
  57.9 2.9 %collective-permute-start.11 = (bf16[288,128]{1,0:T(8,128)(2,1)S(1)}, bf16[288,128]{1,0:T(8,128)(2,1)S(1)}, u32[]{:S(2)}, u32[]{:S(2)}) collective-permute-start(bf16[288,128]{1,0:T(8,128)(2,1)S(1)} %get-tuple-element.26), channel_id=1, source_target_pairs={{0,24},{8,16},{16,8},{24,0},{1,25},{9,17},{17,9},{25,1},{2,26},{10... | collective-permute-start | bytes 221192 | tf_op jit(solution)/shard_map/ppermute | solution.py:356
  60.8 0.5 collective-permute-start.10
  61.3 0.9 %collective-permute-start.2 = (bf16[4,304,128]{2,1,0:T(8,128)(2,1)S(1)}, bf16[4,304,128]{2,1,0:T(8,128)(2,1)S(1)}, u32[]{:S(2)}, u32[]{:S(2)}) collective-permute-start(bf16[4,304,128]{2,1,0:T(8,128)(2,1)S(1)} %fusion.2), channel_id=1, source_target_pairs={{0,4},{1,5},{2,6},{3,7},{4,0},{5,1},{6,2},{7,3},{8,12},{9,13},{10,... | collective-permute-start | bytes 933896 | tf_op jit(solution)/shard_map/ppermute | solution.py:338
  62.3 2.4 %collective-permute-done.11 = bf16[288,128]{1,0:T(8,128)(2,1)S(1)} collective-permute-done((bf16[288,128]{1,0:T(8,128)(2,1)S(1)}, bf16[288,128]{1,0:T(8,128)(2,1)S(1)}, u32[]{:S(2)}, u32[]{:S(2)}) %collective-permute-start.11) | collective-permute-done | bytes 73760 | tf_op jit(solution)/shard_map/ppermute | solution.py:356
  64.6 2.8 %collective-permute-done.10 = bf16[288,128]{1,0:T(8,128)(2,1)S(1)} collective-permute-done((bf16[288,128]{1,0:T(8,128)(2,1)S(1)}, bf16[288,128]{1,0:T(8,128)(2,1)S(1)}, u32[]{:S(2)}, u32[]{:S(2)}) %collective-permute-start.10) | collective-permute-done | bytes 73760 | tf_op jit(solution)/shard_map/ppermute | solution.py:356
  67.5 0.7 fusion.10
  68.2 0.7 collective-permute-done.2
  68.8 0.1 fusion.16
  69.0 0.8 collective-permute-start.3
  69.8 3.1 %collective-permute-start.5 = (bf16[304,128]{1,0:T(8,128)(2,1)S(1)}, bf16[304,128]{1,0:T(8,128)(2,1)S(1)}, u32[]{:S(2)}, u32[]{:S(2)}) collective-permute-start(bf16[304,128]{1,0:T(8,128)(2,1)S(1)} %get-tuple-element.23), channel_id=1, source_target_pairs={{0,24},{8,16},{16,8},{24,0},{1,25},{9,17},{17,9},{25,1},{2,26},{10... | collective-permute-start | bytes 233480 | tf_op jit(solution)/shard_map/ppermute | solution.py:356
  73.0 1.4 %collective-permute-start.13 = (bf16[128,128]{1,0:T(8,128)(2,1)S(1)}, bf16[128,128]{1,0:T(8,128)(2,1)S(1)}, u32[]{:S(2)}, u32[]{:S(2)}) collective-permute-start(bf16[128,128]{1,0:T(8,128)(2,1)S(1)} %get-tuple-element.29), channel_id=1, source_target_pairs={{0,2},{1,3},{2,4},{3,5},{4,6},{5,7},{6,0},{7,1},{8,10},{9,11},{10,... | collective-permute-start | bytes 98312 | tf_op jit(solution)/shard_map/ppermute | solution.py:368
  74.4 1.7 %collective-permute-done.5 = bf16[304,128]{1,0:T(8,128)(2,1)S(1)} collective-permute-done((bf16[304,128]{1,0:T(8,128)(2,1)S(1)}, bf16[304,128]{1,0:T(8,128)(2,1)S(1)}, u32[]{:S(2)}, u32[]{:S(2)}) %collective-permute-start.5) | collective-permute-done | bytes 77856 | tf_op jit(solution)/shard_map/ppermute | solution.py:356
  76.1 2.2 %collective-permute-done.4 = bf16[304,128]{1,0:T(8,128)(2,1)S(1)} collective-permute-done((bf16[304,128]{1,0:T(8,128)(2,1)S(1)}, bf16[304,128]{1,0:T(8,128)(2,1)S(1)}, u32[]{:S(2)}, u32[]{:S(2)}) %collective-permute-start.4) | collective-permute-done | bytes 77856 | tf_op jit(solution)/shard_map/ppermute | solution.py:356
  78.4 0.7 fusion.12
  79.1 1.3 %collective-permute-start.15 = (bf16[64,128]{1,0:T(8,128)(2,1)S(1)}, bf16[64,128]{1,0:T(8,128)(2,1)S(1)}, u32[]{:S(2)}, u32[]{:S(2)}) collective-permute-start(bf16[64,128]{1,0:T(8,128)(2,1)S(1)} %pad_maximum_fusion), channel_id=1, source_target_pairs={{0,4},{1,5},{2,6},{3,7},{4,0},{5,1},{6,2},{7,3},{8,12},{9,13},{10,... | collective-permute-start | bytes 49160 | tf_op jit(solution)/shard_map/ppermute | solution.py:368
  80.4 2.5 %collective-permute-done.15.e_ref = bf16[64,128]{1,0:T(8,128)(2,1)S(1)} collective-permute-done((bf16[64,128]{1,0:T(8,128)(2,1)S(1)}, bf16[64,128]{1,0:T(8,128)(2,1)S(1)}, u32[]{:S(2)}, u32[]{:S(2)}) %collective-permute-start.15) | collective-permute-done | bytes 16416 | tf_op jit(solution)/shard_map/ppermute | solution.py:368
  82.9 0.4 collective-permute-done.12.r1_ref
  83.3 0.1 copy-done.6
  83.5 0.5 copy-done.5
  84.0 1.9 %finish.1 = (f32[128,1024]{1,0:T(8,128)}, f32[1,128]{1,0:T(1,128)}) custom-call(s32[2]{0:T(128)} %copy-done, f32[304,128]{1,0:T(8,128)} %get-tuple-element.17.a_ref, f32[288,128]{1,0:T(8,128)} %get-tuple-element.15.b_ref, bf16[128,128]{1,0:T(8,128)(2,1)} %copy-done.5, bf16[128,128]{1,0:T(8,128)(2,1)} %copy-done.4, bf16[128,128]{1,0:T(8,128)(2,1)} %copy-done.3, ...), custom_call_target="tpu_custom_call" | custom-call | tf_op jit(solution)/shard_map/finish/pallas_call | solution.py:301
  (28 shorter events, 0.3 us)
Async XLA Ops:
  5.0 21.8 %copy-start = (s32[2]{0:T(128)}, s32[2]{0:T(128)S(1)}, u32[]{:S(2)}) copy-start(s32[2]{0:T(128)S(1)} %pad_add_fusion.where_ref) | copy-start | bytes 28
  5.2 0.7 copy-start.1
  5.9 0.7 copy-start.2
  26.8 3.8 %collective-permute-start.6 = (bf16[4,4,288,128]{3,2,1,0:T(8,128)(2,1)S(1)}, bf16[4,4,288,128]{3,2,1,0:T(8,128)(2,1)S(1)}, u32[]{:S(2)}, u32[]{:S(2)}) collective-permute-start(bf16[4,4,288,128]{3,2,1,0:T(8,128)(2,1)S(1)} %get-tuple-element.11), channel_id=1, source_target_pairs={{0,1},{1,0},{2,3},{3,2},{4,5},{5,4},{6,7},{7,6},{8,9},{9,8},{10,11... | collective-permute-start | bytes 3538952 | tf_op jit(solution)/shard_map/ppermute | solution.py:338
  28.1 5.5 %collective-permute-start = (bf16[4,4,304,128]{3,2,1,0:T(8,128)(2,1)S(1)}, bf16[4,4,304,128]{3,2,1,0:T(8,128)(2,1)S(1)}, u32[]{:S(2)}, u32[]{:S(2)}) collective-permute-start(bf16[4,4,304,128]{3,2,1,0:T(8,128)(2,1)S(1)} %get-tuple-element.9), channel_id=1, source_target_pairs={{0,1},{1,0},{2,3},{3,2},{4,5},{5,4},{6,7},{7,6},{8,9},{9,8},{10,11... | collective-permute-start | bytes 3735560 | tf_op jit(solution)/shard_map/ppermute | solution.py:338
  30.9 16.2 %collective-permute-start.7 = (bf16[2,4,288,128]{3,2,1,0:T(8,128)(2,1)S(1)}, bf16[2,4,288,128]{3,2,1,0:T(8,128)(2,1)S(1)}, u32[]{:S(2)}, u32[]{:S(2)}) collective-permute-start(bf16[2,4,288,128]{3,2,1,0:T(8,128)(2,1)S(1)} %slice.161), channel_id=1, source_target_pairs={{0,4},{1,5},{2,6},{3,7},{4,0},{5,1},{6,2},{7,3},{8,12},{9,13},{10,... | collective-permute-start | bytes 1769480 | tf_op jit(solution)/shard_map/ppermute | solution.py:338
  33.9 16.8 %collective-permute-start.1 = (bf16[2,4,304,128]{3,2,1,0:T(8,128)(2,1)S(1)}, bf16[2,4,304,128]{3,2,1,0:T(8,128)(2,1)S(1)}, u32[]{:S(2)}, u32[]{:S(2)}) collective-permute-start(bf16[2,4,304,128]{3,2,1,0:T(8,128)(2,1)S(1)} %slice.160), channel_id=1, source_target_pairs={{0,2},{1,3},{2,0},{3,1},{4,6},{5,7},{6,4},{7,5},{8,10},{9,11},{10,... | collective-permute-start | bytes 1867784 | tf_op jit(solution)/shard_map/ppermute | solution.py:338
  47.3 9.4 %collective-permute-start.8 = (bf16[4,288,128]{2,1,0:T(8,128)(2,1)S(1)}, bf16[4,288,128]{2,1,0:T(8,128)(2,1)S(1)}, u32[]{:S(2)}, u32[]{:S(2)}) collective-permute-start(bf16[4,288,128]{2,1,0:T(8,128)(2,1)S(1)} %fusion.3), channel_id=1, source_target_pairs={{0,2},{1,3},{2,0},{3,1},{4,6},{5,7},{6,4},{7,5},{8,10},{9,11},{10,... | collective-permute-start | bytes 884744 | tf_op jit(solution)/shard_map/ppermute | solution.py:338
  56.8 5.4 %collective-permute-start.9 = (bf16[288,128]{1,0:T(8,128)(2,1)S(1)}, bf16[288,128]{1,0:T(8,128)(2,1)S(1)}, u32[]{:S(2)}, u32[]{:S(2)}) collective-permute-start(bf16[288,128]{1,0:T(8,128)(2,1)S(1)} %get-tuple-element.25), channel_id=1, source_target_pairs={{0,8},{8,0},{16,24},{24,16},{1,9},{9,1},{17,25},{25,17},{2,10},{10... | collective-permute-start | bytes 221192 | tf_op jit(solution)/shard_map/ppermute | solution.py:356
  57.9 6.7 %collective-permute-start.11 = (bf16[288,128]{1,0:T(8,128)(2,1)S(1)}, bf16[288,128]{1,0:T(8,128)(2,1)S(1)}, u32[]{:S(2)}, u32[]{:S(2)}) collective-permute-start(bf16[288,128]{1,0:T(8,128)(2,1)S(1)} %get-tuple-element.26), channel_id=1, source_target_pairs={{0,24},{8,16},{16,8},{24,0},{1,25},{9,17},{17,9},{25,1},{2,26},{10... | collective-permute-start | bytes 221192 | tf_op jit(solution)/shard_map/ppermute | solution.py:356
  60.8 6.7 %collective-permute-start.10 = (bf16[288,128]{1,0:T(8,128)(2,1)S(1)}, bf16[288,128]{1,0:T(8,128)(2,1)S(1)}, u32[]{:S(2)}, u32[]{:S(2)}) collective-permute-start(bf16[288,128]{1,0:T(8,128)(2,1)S(1)} %get-tuple-element.27), channel_id=1, source_target_pairs={{0,16},{8,24},{16,0},{24,8},{1,17},{9,25},{17,1},{25,9},{2,18},{10... | collective-permute-start | bytes 221192 | tf_op jit(solution)/shard_map/ppermute | solution.py:356
  61.3 7.5 %collective-permute-start.2 = (bf16[4,304,128]{2,1,0:T(8,128)(2,1)S(1)}, bf16[4,304,128]{2,1,0:T(8,128)(2,1)S(1)}, u32[]{:S(2)}, u32[]{:S(2)}) collective-permute-start(bf16[4,304,128]{2,1,0:T(8,128)(2,1)S(1)} %fusion.2), channel_id=1, source_target_pairs={{0,4},{1,5},{2,6},{3,7},{4,0},{5,1},{6,2},{7,3},{8,12},{9,13},{10,... | collective-permute-start | bytes 933896 | tf_op jit(solution)/shard_map/ppermute | solution.py:338
  69.0 5.5 %collective-permute-start.3 = (bf16[304,128]{1,0:T(8,128)(2,1)S(1)}, bf16[304,128]{1,0:T(8,128)(2,1)S(1)}, u32[]{:S(2)}, u32[]{:S(2)}) collective-permute-start(bf16[304,128]{1,0:T(8,128)(2,1)S(1)} %get-tuple-element.22), channel_id=1, source_target_pairs={{0,8},{8,0},{16,24},{24,16},{1,9},{9,1},{17,25},{25,17},{2,10},{10... | collective-permute-start | bytes 233480 | tf_op jit(solution)/shard_map/ppermute | solution.py:356
  69.8 6.3 %collective-permute-start.5 = (bf16[304,128]{1,0:T(8,128)(2,1)S(1)}, bf16[304,128]{1,0:T(8,128)(2,1)S(1)}, u32[]{:S(2)}, u32[]{:S(2)}) collective-permute-start(bf16[304,128]{1,0:T(8,128)(2,1)S(1)} %get-tuple-element.23), channel_id=1, source_target_pairs={{0,24},{8,16},{16,8},{24,0},{1,25},{9,17},{17,9},{25,1},{2,26},{10... | collective-permute-start | bytes 233480 | tf_op jit(solution)/shard_map/ppermute | solution.py:356
  72.9 5.4 %collective-permute-start.4 = (bf16[304,128]{1,0:T(8,128)(2,1)S(1)}, bf16[304,128]{1,0:T(8,128)(2,1)S(1)}, u32[]{:S(2)}, u32[]{:S(2)}) collective-permute-start(bf16[304,128]{1,0:T(8,128)(2,1)S(1)} %get-tuple-element.24), channel_id=1, source_target_pairs={{0,16},{8,24},{16,0},{24,8},{1,17},{9,25},{17,1},{25,9},{2,18},{10... | collective-permute-start | bytes 233480 | tf_op jit(solution)/shard_map/ppermute | solution.py:356
  72.9 7.4 %collective-permute-start.14 = (bf16[128,128]{1,0:T(8,128)(2,1)S(1)}, bf16[128,128]{1,0:T(8,128)(2,1)S(1)}, u32[]{:S(2)}, u32[]{:S(2)}) collective-permute-start(bf16[128,128]{1,0:T(8,128)(2,1)S(1)} %get-tuple-element.28), channel_id=1, source_target_pairs={{0,3},{1,4},{2,5},{3,6},{4,7},{5,0},{6,1},{7,2},{8,11},{9,12},{10,... | collective-permute-start | bytes 98312 | tf_op jit(solution)/shard_map/ppermute | solution.py:368
  73.0 7.3 %collective-permute-start.13 = (bf16[128,128]{1,0:T(8,128)(2,1)S(1)}, bf16[128,128]{1,0:T(8,128)(2,1)S(1)}, u32[]{:S(2)}, u32[]{:S(2)}) collective-permute-start(bf16[128,128]{1,0:T(8,128)(2,1)S(1)} %get-tuple-element.29), channel_id=1, source_target_pairs={{0,2},{1,3},{2,4},{3,5},{4,6},{5,7},{6,0},{7,1},{8,10},{9,11},{10,... | collective-permute-start | bytes 98312 | tf_op jit(solution)/shard_map/ppermute | solution.py:368
  79.1 4.3 %collective-permute-start.12 = (bf16[128,128]{1,0:T(8,128)(2,1)S(1)}, bf16[128,128]{1,0:T(8,128)(2,1)S(1)}, u32[]{:S(2)}, u32[]{:S(2)}) collective-permute-start(bf16[128,128]{1,0:T(8,128)(2,1)S(1)} %slice.119), channel_id=1, source_target_pairs={{0,1},{1,2},{2,3},{3,4},{4,5},{5,6},{6,7},{7,0},{8,9},{9,10},{10,1... | collective-permute-start | bytes 98312 | tf_op jit(solution)/shard_map/ppermute | solution.py:368
  79.1 3.8 %collective-permute-start.15 = (bf16[64,128]{1,0:T(8,128)(2,1)S(1)}, bf16[64,128]{1,0:T(8,128)(2,1)S(1)}, u32[]{:S(2)}, u32[]{:S(2)}) collective-permute-start(bf16[64,128]{1,0:T(8,128)(2,1)S(1)} %pad_maximum_fusion), channel_id=1, source_target_pairs={{0,4},{1,5},{2,6},{3,7},{4,0},{5,1},{6,2},{7,3},{8,12},{9,13},{10,... | collective-permute-start | bytes 49160 | tf_op jit(solution)/shard_map/ppermute | solution.py:368
  80.3 3.0 %copy-start.3 = (bf16[128,128]{1,0:T(8,128)(2,1)}, bf16[128,128]{1,0:T(8,128)(2,1)S(1)}, u32[]{:S(2)}) copy-start(bf16[128,128]{1,0:T(8,128)(2,1)S(1)} %collective-permute-done.14.r3_ref) | copy-start | bytes 98308
  80.4 3.0 %copy-start.4 = (bf16[128,128]{1,0:T(8,128)(2,1)}, bf16[128,128]{1,0:T(8,128)(2,1)S(1)}, u32[]{:S(2)}) copy-start(bf16[128,128]{1,0:T(8,128)(2,1)S(1)} %collective-permute-done.13.r2_ref) | copy-start | bytes 98308
  82.9 0.6 copy-start.6
  83.3 0.6 copy-start.5

commit v2 on v1

v2 whole, which is shorter than its diff:
```python
import functools
import jax
import jax.numpy as jnp
from jax import lax
from jax.experimental import pallas as pl
from jax.experimental.pallas import tpu as pltpu
from jax.sharding import PartitionSpec as P

F32 = jnp.float32
BF16 = jnp.bfloat16
GROUP = 8
DEPTH = 256

NT = (((1,), (1,)), ((), ()))


def iota(shape, axis):
    return lax.broadcasted_iota(jnp.int32, shape, axis)


def fit(ld, weight, resid, counts):
    hits = weight.shape[0]
    live = iota(weight.shape, 0) < counts.astype(jnp.int32)
    masked_w = jnp.where(live, weight, 0.0)
    weighted_l = [v * masked_w for v in ld]
    gamma = [[None] * 5 for _ in range(5)]
    for a in range(5):
        for b in range(a + 1):
            gamma[a][b] = jnp.sum(weighted_l[a] * ld[b], axis=0, keepdims=True)
            if a == b:
                gamma[a][b] = gamma[a][b] + 1.0
    beta = [jnp.sum(weighted_l[a] * resid, axis=0, keepdims=True) for a in range(5)]
    factor = [[None] * 5 for _ in range(5)]
    inverse = [None] * 5
    for j in range(5):
        center = gamma[j][j]
        for k in range(j):
            center = center - factor[j][k] * factor[j][k]
        factor[j][j] = jnp.sqrt(center)
        inverse[j] = 1.0 / factor[j][j]
        for i in range(j + 1, 5):
            offdiag = gamma[i][j]
            for k in range(j):
                offdiag = offdiag - factor[i][k] * factor[j][k]
            factor[i][j] = offdiag * inverse[j]
    solved, rhs = [], []
    for j in range(5):
        current, target = weighted_l[j], beta[j]
        for k in range(j):
            current = current - factor[j][k] * solved[k]
            target = target - factor[j][k] * rhs[k]
        solved.append(current * inverse[j])
        rhs.append(target * inverse[j])
    projection = solved[0] * rhs[0]
    for k in range(1, 5):
        projection = projection + solved[k] * rhs[k]
    return solved, masked_w * resid - projection, masked_w


def prepare_kernel(
    place_ref, region_ref, count_ref, ld_ref, weight_ref, resid_ref, ids_ref,
    scaled_ref, lanes_ref, column_ref, table_ref,
):
    tracks = region_ref.shape[1]
    groups, _, depth = scaled_ref.shape
    slots = groups * GROUP
    hits = depth // GROUP
    blocks = place_ref.shape[0]
    rr = table_ref.shape[0] - 8
    member = (iota((rr, tracks), 0) == region_ref[...]).astype(F32)
    before = (iota((tracks, tracks), 0) < iota((tracks, tracks), 1)).astype(F32).astype(BF16)
    rank = jnp.dot(member.astype(BF16), before, preferred_element_type=F32)
    count = jnp.sum(member, axis=1, keepdims=True)
    room = lax.shift_left(lax.shift_right_logical(count.astype(jnp.int32) + 7, 3), 3)
    room = jnp.broadcast_to(room.astype(F32), (rr, slots))
    lower = (iota((rr, rr), 1) < iota((rr, rr), 0)).astype(F32)
    start = jnp.zeros((rr, slots), F32)
    for g in range(rr):
        start = start + lower[:, g : g + 1] * room[g : g + 1, :]
    slot = jnp.sum(member * (rank + start[:, 0:1]), axis=0, keepdims=True)
    perm = (iota((slots, tracks), 0) == slot.astype(jnp.int32)).astype(F32).astype(BF16)
    numbers = jnp.where(
        iota((8, tracks), 0) == 0, iota((8, tracks), 1), jnp.broadcast_to(count_ref[...], (8, tracks))
    )

    def sort(value):
        return lax.dot_general(value, perm, NT, preferred_element_type=F32)

    numbers = sort(numbers.astype(F32).astype(BF16))
    table_ref[0:8, :] = numbers.astype(jnp.int32)
    table_ref[8:, :] = jnp.where(
        iota((rr, slots), 1) == 0, start.astype(jnp.int32), (start + room).astype(jnp.int32)
    )
    flat = sort(ld_ref[...])
    ld = [flat[c * hits : (c + 1) * hits] for c in range(5)]
    solved, hit_factor, masked_w = fit(
        ld, sort(weight_ref[...]), sort(resid_ref[...]), numbers[1:2]
    )
    ids = sort(ids_ref[...].astype(F32).astype(BF16))
    position = jnp.zeros_like(ids)
    for b in range(blocks):
        position = jnp.where(ids == float(b), place_ref[b].astype(F32), position)
    own = (iota((depth, slots), 0) // hits) == (iota((depth, slots), 1) % GROUP)

    def spread_out(value):
        return jnp.where(own, jnp.concatenate([value] * GROUP, axis=0), 0.0)

    grouping = (iota((groups, slots), 1) // GROUP == iota((groups, slots), 0)).astype(F32)
    for n, value in enumerate((masked_w, hit_factor)):
        lanes_ref[n] = lax.dot_general(
            grouping.astype(BF16), spread_out(value).astype(BF16), NT, preferred_element_type=F32
        )
    columns = column_ref.shape[1]
    grouping = (iota((columns, slots), 1) // GROUP == iota((columns, slots), 0)).astype(F32)
    column_ref[...] = lax.dot_general(
        spread_out(position).astype(BF16), grouping.astype(BF16), NT, preferred_element_type=F32
    ).astype(BF16)
    for c in range(5):
        scaled_ref[:, c * GROUP : (c + 1) * GROUP, :] = spread_out(solved[c]).T.reshape(
            groups, GROUP, depth
        )


def prepare(place, region_row, count_row, ld, weight, resid, ids, regions):
    tracks = region_row.shape[1]
    hits = weight.shape[0]
    rr = -(-regions // 8) * 8
    slots = -(-(tracks + regions * (GROUP - 1)) // 128) * 128
    depth = GROUP * hits
    smem = pl.BlockSpec(memory_space=pltpu.SMEM)
    vmem = pl.BlockSpec(memory_space=pltpu.VMEM)
    return pl.pallas_call(
        prepare_kernel,
        in_specs=[smem] + [vmem] * 6,
        out_specs=[vmem] * 4,
        out_shape=[
            jax.ShapeDtypeStruct((slots // GROUP, 5 * GROUP, depth), F32),
            jax.ShapeDtypeStruct((2, slots // GROUP, depth), F32),
            jax.ShapeDtypeStruct((depth, 128), BF16),
            jax.ShapeDtypeStruct((8 + rr, slots), jnp.int32),
        ],
        compiler_params=pltpu.CompilerParams(vmem_limit_bytes=24 * 1024 * 1024),
        cost_estimate=pl.CostEstimate(flops=10**9, bytes_accessed=2 * 10**6, transcendentals=0),
        name="prepare",
    )(place, region_row, count_row, ld, weight, resid, ids)


def one_group(group, local, table_ref, g_ref, scaled_ref, lanes_ref, column_ref, g_s, direct_s, spread_s):
    hits, width = g_ref.shape[1:]
    depth = GROUP * hits
    blocks = spread_s.shape[1] // width
    for i in range(GROUP):
        g_s[i * hits : (i + 1) * hits, :] = g_ref[table_ref[0, group * GROUP + i]]
    g = g_s[...]
    chosen = (iota((128, width), 0) == group).astype(F32).astype(BF16)
    position = jnp.dot(column_ref[...], chosen, preferred_element_type=F32).astype(BF16)
    right = jnp.concatenate(
        [jnp.where(position == jnp.bfloat16(p), g, jnp.bfloat16(0)) for p in range(blocks)], axis=1
    )
    weighted = g.astype(F32).T * lanes_ref[0, pl.ds(group, 1), :]
    factor = jnp.where(iota((8, depth), 0) == 0, lanes_ref[1, pl.ds(group, 1), :], 0.0)
    scaled = scaled_ref[group]
    high = scaled.astype(BF16).astype(F32)
    left = jnp.concatenate(
        [weighted, factor, high, scaled - high, jnp.zeros((8, depth), F32)], axis=0
    )
    total = jnp.dot(left.astype(BF16), right, preferred_element_type=F32)
    head = width + 8
    step = 5 * GROUP
    direct_s[...] += total[:head]
    spread_s[pl.ds(pl.multiple_of(local * step, GROUP), step), :] = (
        total[head : head + step] + total[head + step : head + 2 * step]
    )


ODD = (0, 4, 2, 6)
EVEN = (0, 2, 4, 6)


def assemble_kernel(
    first_k, where_ref, table_ref, scaled_ref, lanes_ref, column_ref, g_ref,
    keep_ref, send_ref, g_s, direct_s, spread_s, wide_s, turned_s, acc_s,
):
    k = pl.program_id(0) + first_k
    width = g_ref.shape[2]
    blocks = spread_s.shape[1] // width
    many = blocks // 2
    region = where_ref[1] ^ k
    first = table_ref[8 + region, 0] // GROUP
    groups = table_ref[8 + region, 1] // GROUP - first
    direct_s[...] = jnp.zeros_like(direct_s)
    acc_s[...] = jnp.zeros_like(acc_s)

    def group_step(local, carry):
        one_group(
            first + local, local, table_ref, g_ref, scaled_ref, lanes_ref, column_ref,
            g_s, direct_s, spread_s,
        )
        return carry

    lax.fori_loop(0, groups, group_step, 0)
    used = groups * 5
    depth_tiles = DEPTH // 8
    chunks = (used + depth_tiles - 1) // depth_tiles

    def clear(tile, carry):
        spread_s[pl.ds(pl.multiple_of(tile * 8, 8), 8), :] = jnp.zeros((8, blocks * width), F32)
        return carry

    lax.fori_loop(used, chunks * depth_tiles, clear, 0)

    def chunk_step(chunk, carry):
        at = pl.multiple_of(chunk * DEPTH, DEPTH)
        narrow = spread_s[pl.ds(at, DEPTH), :].astype(BF16)
        wide_s[:, : blocks * width] = narrow
        wide_s[:, blocks * width :] = narrow[:, : many * width]
        turned_s[...] = narrow.astype(F32).T.astype(BF16)
        for p in range(blocks):
            columns = (many + (1 if p < many else 0)) * width
            acc_s[p, :, :columns] += jnp.dot(
                turned_s[p * width : (p + 1) * width],
                wide_s[:, p * width : p * width + columns],
                preferred_element_type=F32,
            )
        return carry

    lax.fori_loop(0, chunks, chunk_step, 0)
    half = width // 2
    for n in range(blocks // 2):
        for odd, out_ref in ((0, keep_ref), (1, send_ref)):
            p = where_ref[0] ^ (jnp.where(k % 2 == 1, ODD[n], EVEN[n]) + odd)
            columns = pl.ds(pl.multiple_of(p * width, width), width)
            parts = [direct_s[0:width, columns] - acc_s[p, :, 0:width]]
            parts += [0.0 - acc_s[p, :, d * width : (d + 1) * width] for d in range(1, many)]
            upper = pl.multiple_of((p // many) * half, half)
            parts.append(0.0 - acc_s[p % many, pl.ds(upper, half), many * width :])
            row = direct_s[width : width + 1, columns]
            high = row.astype(BF16).astype(F32)
            sub = iota((16, width), 0)
            parts.append(jnp.where(sub == 0, high, jnp.where(sub == 1, row - high, 0.0)))
            out_ref[n, 0] = jnp.concatenate(parts, axis=0).astype(BF16)


def assemble(first_k, number, where, table, scaled, lanes, column, g, blocks):
    tracks, hits, width = g.shape
    rows = width * (blocks // 2) + width // 2 + 16
    longest = -(-(-(-tracks // GROUP) * 5 * GROUP) // DEPTH) * DEPTH
    out = jax.ShapeDtypeStruct((blocks // 2, number, rows, width), BF16)
    spec = pl.BlockSpec((blocks // 2, 1, rows, width), lambda k: (0, k, 0, 0))
    smem = pl.BlockSpec(memory_space=pltpu.SMEM)
    vmem = pl.BlockSpec(memory_space=pltpu.VMEM)
    return pl.pallas_call(
        functools.partial(assemble_kernel, first_k),
        grid=(number,),
        in_specs=[smem, smem, vmem, vmem, vmem, vmem],
        out_specs=[spec, spec],
        out_shape=[out, out],
        scratch_shapes=[
            pltpu.VMEM((GROUP * hits, width), BF16),
            pltpu.VMEM((width + 8, blocks * width), F32),
            pltpu.VMEM((longest, blocks * width), F32),
            pltpu.VMEM((DEPTH, (blocks + blocks // 2) * width), BF16),
            pltpu.VMEM((blocks * width, DEPTH), BF16),
            pltpu.VMEM((blocks, width, (blocks // 2 + 1) * width), F32),
        ],
        compiler_params=pltpu.CompilerParams(
            dimension_semantics=("arbitrary",), vmem_limit_bytes=32 * 1024 * 1024
        ),
        cost_estimate=pl.CostEstimate(
            flops=3 * 10**9 * number // 2, bytes_accessed=4 * 10**6, transcendentals=0
        ),
        name="assemble",
    )(where, table, scaled, lanes, column, g)


def finish_kernel(where_ref, own_ref, r1_ref, r2_ref, r3_ref, e_ref, out_ref, vec_ref):
    width = own_ref.shape[1]
    p = where_ref[0]
    blocks = out_ref.shape[1] // width
    many = blocks // 2

    def put(column, value):
        column = pl.multiple_of(((column + blocks) % blocks) * width, width)
        out_ref[:, pl.ds(column, width)] = value

    for d in range(many):
        put(p + d, own_ref[d * width : (d + 1) * width, :])
    for d, ref in ((1, r1_ref), (2, r2_ref), (3, r3_ref)):
        put(p - d, ref[...].astype(F32).T)
    tail = many * width + width // 2
    mine = own_ref[many * width : tail, :]
    other = e_ref[...].astype(F32)

    @pl.when(p < many)
    def _():
        put(p + many, jnp.concatenate([mine, other], axis=0))

    @pl.when(p >= many)
    def _():
        put(p + many, jnp.concatenate([other, mine], axis=0).T)

    vec_ref[...] = own_ref[tail : tail + 1, :] + own_ref[tail + 1 : tail + 2, :]


def finish(where, own, r1, r2, r3, ext, blocks):
    width = own.shape[1]
    smem = pl.BlockSpec(memory_space=pltpu.SMEM)
    vmem = pl.BlockSpec(memory_space=pltpu.VMEM)
    return pl.pallas_call(
        finish_kernel,
        in_specs=[smem] + [vmem] * 5,
        out_specs=[vmem, vmem],
        out_shape=[
            jax.ShapeDtypeStruct((width, blocks * width), F32),
            jax.ShapeDtypeStruct((1, width), F32),
        ],
        name="finish",
    )(where, own, r1, r2, r3, ext)


def local(
    tiles, global_deriv, local_deriv, hit_weight, hit_resid, block_ids, hit_count, track_region,
    block_place,
):
    regions = lax.axis_size("region")
    tracks, hits, width = global_deriv.shape
    blocks = block_place.shape[0]
    sub = tiles // blocks
    tile = lax.axis_index("tile")
    where = jnp.stack([tile // sub, lax.axis_index("region")]).astype(jnp.int32)
    scaled, lanes, column, table = prepare(
        block_place,
        track_region.reshape(1, tracks),
        hit_count.reshape(1, tracks),
        local_deriv.transpose(1, 2, 0).reshape(-1, tracks),
        hit_weight.T,
        hit_resid.T,
        block_ids.T,
        regions,
    )

    def swap(value, bit):
        return lax.ppermute(value, "tile", [(t, t ^ bit) for t in range(tiles)])

    totals = [None] * regions
    for first in range(regions - 2, -1, -2):
        keep, send = assemble(first, 2, where, table, scaled, lanes, column, global_deriv, blocks)
        bit = 1
        while bit < sub:
            keep, send = keep + swap(keep, bit), send + swap(send, bit)
            bit *= 2
        got = swap(send, sub)
        for n in range(2):
            bits = ((4, 2), (2, 4))[n]
            total = keep[:, n].astype(F32) + got[:, n].astype(F32)
            more = swap(total[2:].astype(BF16), sub * bits[0])
            total = total[:2] + more.astype(F32)
            more = swap(total[1].astype(BF16), sub * bits[1])
            totals[first + n] = total[0] + more.astype(F32)
    own = totals[0]
    for k in range(regions - 1, 0, -1):
        pairs = [(r, r ^ k) for r in range(regions)]
        own = own + lax.ppermute(totals[k].astype(BF16), "region", pairs).astype(F32)

    def onward(value, d):
        pairs = [
            (p * sub + s, ((p + d) % blocks) * sub + s) for p in range(blocks) for s in range(sub)
        ]
        return lax.ppermute(value.astype(BF16), "tile", pairs)

    matrix, vector = finish(
        where,
        own,
        *(onward(own[d * width : (d + 1) * width], d) for d in range(1, blocks // 2)),
        onward(own[blocks // 2 * width : blocks // 2 * width + width // 2], blocks // 2),
        blocks,
    )
    if sub > 1:
        part = tile % sub
        rows = width // sub
        matrix = lax.dynamic_slice(matrix, (part * rows, 0), (rows, blocks * width))
        vector = lax.dynamic_slice(vector, (0, part * rows), (1, rows))
    return matrix[None], vector


def solution(mesh):
    return jax.shard_map(
        functools.partial(local, mesh.shape["tile"]),
        mesh=mesh,
        in_specs=(
            P(("region", "tile"), None, None),
            P(("region", "tile"), None, None),
            P(("region", "tile"), None),
            P(("region", "tile"), None),
            P(("region", "tile"), None),
            P(("region", "tile")),
            P(("region", "tile"), None),
            P(),
        ),
        out_specs=(P("region", "tile", None), P("region", "tile")),
        check_vma=False,
    )
```

time: 86.3 us -> 76.3 us (0.88)
  waiting for transfers between devices: 33 us -> 22.3 us
  starting transfers between devices: 20.8 us -> 23.8 us
  other arithmetic: 3.9 us -> 1.77 us
    ppermute x6 -> x10, waiting for transfers between devices: 20.8 us -> 8.46 us  [swap(): return lax.ppermute(value, 'tile', [(t, t ^ bit) for t in range(tiles)])]
    ppermute x6 -> x10, starting transfers between devices: 9.64 us -> 13.9 us  [swap(): return lax.ppermute(value, 'tile', [(t, t ^ bit) for t in range(tiles)])]
    ppermute x6 -> x3, starting transfers between devices: 8.42 us -> 5.19 us  [local(): lax.ppermute(totals[k].astype(BF16), 'region', pairs).astype(F32)]
    unnamed x16 -> x26, local copies, waits for them, and re-layouts: 3.63 us -> 5.71 us
    ppermute x4, starting transfers between devices: 2.73 us -> 4.64 us  [onward(): return lax.ppermute(value.astype(BF16), 'tile', pairs)]
    ppermute x6 -> x3, waiting for transfers between devices: 9.16 us -> 10.6 us  [local(): lax.ppermute(totals[k].astype(BF16), 'region', pairs).astype(F32)]
    convert_element_type x2 -> x3, other arithmetic: 1.45 us -> 0.12 us  [local(): totals[k].astype(BF16)]
    reshape x1 -> x0, local copies, waits for them, and re-layouts: 1 us -> none  [local(): local_deriv.reshape(tracks, -1)]
  transfers between devices with their start and end apart: 16 -> 17, of which waited for: 11 -> 6; matrix products, arithmetic and copies ran while one was open for 3% -> 2% of each run, Pallas kernels for 0% -> 10%
where the time goes in v2:
time: 76.3 us; the launch traced here: 76.4 us
  starting transfers between devices  23.8 us (31%)
  waiting for transfers between devices  22.3 us (29%)
  Pallas kernels  21.6 us (28%)
  local copies, waits for them, and re-layouts  6.12 us (8%)
  other arithmetic  1.77 us (2%)
  between operations  0.86 us (1%)
    pallas_call x2, Pallas kernels, assemble(): pl.pallas_call(functools.partial(assemble_kernel, first_k), grid=(number,...  18.1 us
    ppermute x10, starting transfers between devices, swap(): return lax.ppermute(value, 'tile', [(t, t ^ bit) for t in range(tiles)])  13.9 us
    ppermute x3, waiting for transfers between devices, local(): lax.ppermute(totals[k].astype(BF16), 'region', pairs).astype(F32)  10.6 us
    ppermute x10, waiting for transfers between devices, swap(): return lax.ppermute(value, 'tile', [(t, t ^ bit) for t in range(tiles)])  8.46 us
    unnamed x26, local copies, waits for them, and re-layouts  5.71 us
    ppermute x3, starting transfers between devices, local(): lax.ppermute(totals[k].astype(BF16), 'region', pairs).astype(F32)  5.19 us
    ppermute x4, starting transfers between devices, onward(): return lax.ppermute(value.astype(BF16), 'tile', pairs)  4.64 us
    ppermute x4, waiting for transfers between devices, onward(): return lax.ppermute(value.astype(BF16), 'tile', pairs)  3.24 us
  transfers between devices with their start and end apart: 17, of which 6 were waited for; matrix products, arithmetic and copies ran while one was open for 2% of the time, Pallas kernels for 10%

profile of v2, /device:TPU:0, one launch (start us, length us, event | category | flops | bytes accessed | tf_op | source)
XLA Modules:
  0.0 76.4 jit_solution(388012870033975743)
XLA Ops:
  0.6 0.1 pad_add_fusion.where_ref
  0.7 0.9 %copy-done.2 = bf16[192,5,32]{0,2,1:T(8,128)(2,1)S(1)} copy-done((bf16[192,5,32]{0,2,1:T(8,128)(2,1)S(1)}, bf16[192,5,32]{0,2,1:T(8,128)(2,1)}, u32[]{:S(2)}) %copy-start.2) | copy-done | bytes 61464
  1.6 0.8 copy-done.3
  2.4 0.7 copy-done.4
  3.1 0.7 copy-done.5
  3.8 0.7 copy-done.6
  4.5 0.7 copy-done.7
  5.2 0.7 copy-done.8
  5.8 1.5 %prepare.1 = (f32[32,40,256]{2,1,0:T(8,128)S(1)}, f32[2,32,256]{2,1,0:T(8,128)S(1)}, bf16[256,128]{1,0:T(8,128)(2,1)S(1)}, s32[16,256]{1,0:T(8,128)S(1)}) custom-call(s32[8]{0:T(128)S(1)} %copy-done.8, s32[1,192]{1,0:T(1,128)S(1)} %bitcast.76, s32[1,192]{1,0:T(1,128)S(1)} %bitcast.77, bf16[160,192]{1,0:T(8,128)(2,1)S(1)} %bitcast.72, ...), custom_call_target="tpu_custom_call" | custom-call | flops 1000000000 | bytes 2000000 | tf_op jit(solution)/shard_map/prepare/pallas_call | solution.py:132
  7.4 10.7 %assemble.3 = (bf16[4,2,592,128]{3,2,1,0:T(8,128)(2,1)S(1)}, bf16[4,2,592,128]{3,2,1,0:T(8,128)(2,1)S(1)}) custom-call(s32[2]{0:T(128)S(1)} %pad_add_fusion.where_ref, s32[16,256]{1,0:T(8,128)S(1)} %get-tuple-element.12.table_ref, f32[32,40,256]{2,1,0:T(8,128)S(1)} %get-tuple-element.13.scaled_ref, f32[2,32,256]{2,1,0:T(8,128)S(1)} %get-tuple-element.14.lanes_ref, ...), custom_call_target="tpu_custom_call" | custom-call | flops 3000000000 | bytes 4000000 | tf_op jit(solution)/shard_map/assemble/pallas_call | solution.py:252
  18.1 0.1 copy.13
  18.2 0.5 collective-permute-start.3
  18.7 7.4 %assemble.2 = (bf16[4,2,592,128]{3,2,1,0:T(8,128)(2,1)S(1)}, bf16[4,2,592,128]{3,2,1,0:T(8,128)(2,1)S(1)}) custom-call(s32[2]{0:T(128)S(1)} %pad_add_fusion.where_ref, s32[16,256]{1,0:T(8,128)S(1)} %get-tuple-element.12.table_ref, f32[32,40,256]{2,1,0:T(8,128)S(1)} %get-tuple-element.13.scaled_ref, f32[2,32,256]{2,1,0:T(8,128)S(1)} %get-tuple-element.14.lanes_ref, ...), custom_call_target="tpu_custom_call" | custom-call | flops 3000000000 | bytes 4000000 | tf_op jit(solution)/shard_map/assemble/pallas_call | solution.py:252
  26.1 0.1 copy.11
  26.2 0.1 collective-permute-start
  26.3 0.0 collective-permute-done.3
  26.3 0.2 convert_add_fusion.2
  26.6 2.6 %collective-permute-start.4 = (bf16[2,592,128]{2,1,0:T(8,128)(2,1)S(1)}, bf16[2,592,128]{2,1,0:T(8,128)(2,1)S(1)}, u32[]{:S(2)}, u32[]{:S(2)}) collective-permute-start(bf16[2,592,128]{2,1,0:T(8,128)(2,1)S(1)} %fusion.5), channel_id=1, source_target_pairs={{0,2},{1,3},{2,0},{3,1},{4,6},{5,7},{6,4},{7,5},{8,10},{9,11},{10,... | collective-permute-start | bytes 909320 | tf_op jit(solution)/shard_map/ppermute | solution.py:343
  29.3 1.4 %collective-permute-start.7 = (bf16[2,592,128]{2,1,0:T(8,128)(2,1)S(1)}, bf16[2,592,128]{2,1,0:T(8,128)(2,1)S(1)}, u32[]{:S(2)}, u32[]{:S(2)}) collective-permute-start(bf16[2,592,128]{2,1,0:T(8,128)(2,1)S(1)} %fusion.6), channel_id=1, source_target_pairs={{0,4},{1,5},{2,6},{3,7},{4,0},{5,1},{6,2},{7,3},{8,12},{9,13},{10,... | collective-permute-start | bytes 909320 | tf_op jit(solution)/shard_map/ppermute | solution.py:343
  30.6 0.3 convert_add_fusion.3
  31.0 2.0 %collective-permute-start.10 = (bf16[2,592,128]{2,1,0:T(8,128)(2,1)S(1)}, bf16[2,592,128]{2,1,0:T(8,128)(2,1)S(1)}, u32[]{:S(2)}, u32[]{:S(2)}) collective-permute-start(bf16[2,592,128]{2,1,0:T(8,128)(2,1)S(1)} %fusion.7), channel_id=1, source_target_pairs={{0,2},{1,3},{2,0},{3,1},{4,6},{5,7},{6,4},{7,5},{8,10},{9,11},{10,... | collective-permute-start | bytes 909320 | tf_op jit(solution)/shard_map/ppermute | solution.py:343
  33.0 0.5 collective-permute-start.1
  33.5 3.7 %collective-permute-done.4 = bf16[2,592,128]{2,1,0:T(8,128)(2,1)S(1)} collective-permute-done((bf16[2,592,128]{2,1,0:T(8,128)(2,1)S(1)}, bf16[2,592,128]{2,1,0:T(8,128)(2,1)S(1)}, u32[]{:S(2)}, u32[]{:S(2)}) %collective-permute-start.4) | collective-permute-done | bytes 303136 | tf_op jit(solution)/shard_map/ppermute | solution.py:343
  37.2 0.1 fusion.2
  37.3 3.3 %collective-permute-start.5 = (bf16[592,128]{1,0:T(8,128)(2,1)S(1)}, bf16[592,128]{1,0:T(8,128)(2,1)S(1)}, u32[]{:S(2)}, u32[]{:S(2)}) collective-permute-start(bf16[592,128]{1,0:T(8,128)(2,1)S(1)} %fusion.19), channel_id=1, source_target_pairs={{0,4},{1,5},{2,6},{3,7},{4,0},{5,1},{6,2},{7,3},{8,12},{9,13},{10,... | collective-permute-start | bytes 454664 | tf_op jit(solution)/shard_map/ppermute | solution.py:343
  40.6 0.1 fusion.1
  40.7 0.1 collective-permute-start.8
  40.8 2.9 %collective-permute-done.10 = bf16[2,592,128]{2,1,0:T(8,128)(2,1)S(1)} collective-permute-done((bf16[2,592,128]{2,1,0:T(8,128)(2,1)S(1)}, bf16[2,592,128]{2,1,0:T(8,128)(2,1)S(1)}, u32[]{:S(2)}, u32[]{:S(2)}) %collective-permute-start.10) | collective-permute-done | bytes 303136 | tf_op jit(solution)/shard_map/ppermute | solution.py:343
  43.7 0.1 fusion
  43.8 3.3 %collective-permute-start.11 = (bf16[592,128]{1,0:T(8,128)(2,1)S(1)}, bf16[592,128]{1,0:T(8,128)(2,1)S(1)}, u32[]{:S(2)}, u32[]{:S(2)}) collective-permute-start(bf16[592,128]{1,0:T(8,128)(2,1)S(1)} %fusion.21), channel_id=1, source_target_pairs={{0,4},{1,5},{2,6},{3,7},{4,0},{5,1},{6,2},{7,3},{8,12},{9,13},{10,... | collective-permute-start | bytes 454664 | tf_op jit(solution)/shard_map/ppermute | solution.py:343
  47.1 0.1 fusion.3
  47.2 0.1 collective-permute-start.2
  47.3 1.9 %collective-permute-done.5 = bf16[592,128]{1,0:T(8,128)(2,1)S(1)} collective-permute-done((bf16[592,128]{1,0:T(8,128)(2,1)S(1)}, bf16[592,128]{1,0:T(8,128)(2,1)S(1)}, u32[]{:S(2)}, u32[]{:S(2)}) %collective-permute-start.5) | collective-permute-done | bytes 151584 | tf_op jit(solution)/shard_map/ppermute | solution.py:343
  49.2 4.5 %collective-permute-start.6 = (bf16[592,128]{1,0:T(8,128)(2,1)S(1)}, bf16[592,128]{1,0:T(8,128)(2,1)S(1)}, u32[]{:S(2)}, u32[]{:S(2)}) collective-permute-start(bf16[592,128]{1,0:T(8,128)(2,1)S(1)} %fusion.13), channel_id=1, source_target_pairs={{0,24},{8,16},{16,8},{24,0},{1,25},{9,17},{17,9},{25,1},{2,26},{10... | collective-permute-start | bytes 454664 | tf_op jit(solution)/shard_map/ppermute | solution.py:363
  53.7 0.1 collective-permute-start.9
  53.9 0.6 collective-permute-start.12
  54.5 4.0 %collective-permute-done.6 = bf16[592,128]{1,0:T(8,128)(2,1)S(1)} collective-permute-done((bf16[592,128]{1,0:T(8,128)(2,1)S(1)}, bf16[592,128]{1,0:T(8,128)(2,1)S(1)}, u32[]{:S(2)}, u32[]{:S(2)}) %collective-permute-start.6) | collective-permute-done | bytes 151584 | tf_op jit(solution)/shard_map/ppermute | solution.py:363
  58.5 6.6 %collective-permute-done.9 = bf16[592,128]{1,0:T(8,128)(2,1)S(1)} collective-permute-done((bf16[592,128]{1,0:T(8,128)(2,1)S(1)}, bf16[592,128]{1,0:T(8,128)(2,1)S(1)}, u32[]{:S(2)}, u32[]{:S(2)}) %collective-permute-start.9) | collective-permute-done | bytes 151584 | tf_op jit(solution)/shard_map/ppermute | solution.py:363
  65.1 0.8 %fusion.22 = (bf16[592,128]{1,0:T(8,128)(2,1)S(1)}, f32[592,128]{1,0:T(8,128)}) fusion(bf16[592,128]{1,0:T(8,128)(2,1)S(1)} %collective-permute-done.12, bf16[592,128]{1,0:T(8,128)(2,1)S(1)} %collective-permute-done.9, bf16[592,128]{1,0:T(8,128)(2,1)S(1)} %collective-permute-done.6, bf16[592,128]{1,0:T(8,128)(2,1)S(1)} %collective-permute-done.2, ...), kind=kLoop, calls=%fused_computation.43 | loop fusion | flops 681984 | bytes 1363968 | tf_op jit(solution)/shard_map/convert.3
  65.9 0.1 collective-permute-start.13
  66.0 1.7 %collective-permute-start.14 = (bf16[128,128]{1,0:T(8,128)(2,1)S(1)}, bf16[128,128]{1,0:T(8,128)(2,1)S(1)}, u32[]{:S(2)}, u32[]{:S(2)}) collective-permute-start(bf16[128,128]{1,0:T(8,128)(2,1)S(1)} %get-tuple-element.29), channel_id=1, source_target_pairs={{0,2},{1,3},{2,4},{3,5},{4,6},{5,7},{6,0},{7,1},{8,10},{9,11},{10,... | collective-permute-start | bytes 98312 | tf_op jit(solution)/shard_map/ppermute | solution.py:369
  67.7 2.4 %collective-permute-start.15 = (bf16[128,128]{1,0:T(8,128)(2,1)S(1)}, bf16[128,128]{1,0:T(8,128)(2,1)S(1)}, u32[]{:S(2)}, u32[]{:S(2)}) collective-permute-start(bf16[128,128]{1,0:T(8,128)(2,1)S(1)} %get-tuple-element.28), channel_id=1, source_target_pairs={{0,3},{1,4},{2,5},{3,6},{4,7},{5,0},{6,1},{7,2},{8,11},{9,12},{10,... | collective-permute-start | bytes 98312 | tf_op jit(solution)/shard_map/ppermute | solution.py:369
  70.0 0.5 collective-permute-start.16
  70.6 3.2 %collective-permute-done.16.e_ref = bf16[64,128]{1,0:T(8,128)(2,1)S(1)} collective-permute-done((bf16[64,128]{1,0:T(8,128)(2,1)S(1)}, bf16[64,128]{1,0:T(8,128)(2,1)S(1)}, u32[]{:S(2)}, u32[]{:S(2)}) %collective-permute-start.16) | collective-permute-done | bytes 16416 | tf_op jit(solution)/shard_map/ppermute | solution.py:369
  73.8 0.6 copy-done.12
  74.4 0.0 copy-done.9
  74.4 0.0 copy-done.10
  74.4 1.9 %finish.1 = (f32[128,1024]{1,0:T(8,128)}, f32[1,128]{1,0:T(1,128)}) custom-call(s32[2]{0:T(128)} %copy-done, f32[592,128]{1,0:T(8,128)} %get-tuple-element.23.own_ref, bf16[128,128]{1,0:T(8,128)(2,1)} %copy-done.9, bf16[128,128]{1,0:T(8,128)(2,1)} %copy-done.10, bf16[128,128]{1,0:T(8,128)(2,1)} %copy-done.11, bf16[64,128]{1,0:T(8,128)(2,1)} %copy-done.12), custom_call_target="tpu_custom_call" | custom-call | tf_op jit(solution)/shard_map/finish/pallas_call | solution.py:309
  (39 shorter events, 0.4 us)
Async XLA Ops:
  0.7 18.0 %copy-start = (s32[2]{0:T(128)}, s32[2]{0:T(128)S(1)}, u32[]{:S(2)}) copy-start(s32[2]{0:T(128)S(1)} %pad_add_fusion.where_ref) | copy-start | bytes 28
  0.7 0.9 %copy-start.2 = (bf16[192,5,32]{0,2,1:T(8,128)(2,1)S(1)}, bf16[192,5,32]{0,2,1:T(8,128)(2,1)}, u32[]{:S(2)}) copy-start(bf16[192,5,32]{0,2,1:T(8,128)(2,1)} %param.9) | copy-start | bytes 184324
  1.6 0.8 copy-start.3
  2.4 0.7 copy-start.4
  3.1 0.7 copy-start.5
  3.8 0.7 copy-start.6
  4.5 0.7 copy-start.7
  5.2 0.7 copy-start.8
  5.8 1.5 %copy-start.1 = (bf16[192,32,128]{2,1,0:T(8,128)(2,1)S(1)}, bf16[192,32,128]{2,1,0:T(8,128)(2,1)}, u32[]{:S(2)}) copy-start(bf16[192,32,128]{2,1,0:T(8,128)(2,1)} %g_ref.3) | copy-start | bytes 4718596
  18.2 8.1 %collective-permute-start.3 = (bf16[4,2,592,128]{3,2,0,1:T(8,128)(2,1)S(1)}, bf16[4,2,592,128]{3,2,0,1:T(8,128)(2,1)S(1)}, u32[]{:S(2)}, u32[]{:S(2)}) collective-permute-start(bf16[4,2,592,128]{3,2,0,1:T(8,128)(2,1)S(1)} %copy.13), channel_id=1, source_target_pairs={{0,1},{1,0},{2,3},{3,2},{4,5},{5,4},{6,7},{7,6},{8,9},{9,8},{10,11... | collective-permute-start | bytes 3637256 | tf_op jit(solution)/shard_map/ppermute | solution.py:343
  26.2 4.4 %collective-permute-start = (bf16[4,2,592,128]{3,2,0,1:T(8,128)(2,1)S(1)}, bf16[4,2,592,128]{3,2,0,1:T(8,128)(2,1)S(1)}, u32[]{:S(2)}, u32[]{:S(2)}) collective-permute-start(bf16[4,2,592,128]{3,2,0,1:T(8,128)(2,1)S(1)} %copy.11), channel_id=1, source_target_pairs={{0,1},{1,0},{2,3},{3,2},{4,5},{5,4},{6,7},{7,6},{8,9},{9,8},{10,11... | collective-permute-start | bytes 3637256 | tf_op jit(solution)/shard_map/ppermute | solution.py:343
  26.6 10.6 %collective-permute-start.4 = (bf16[2,592,128]{2,1,0:T(8,128)(2,1)S(1)}, bf16[2,592,128]{2,1,0:T(8,128)(2,1)S(1)}, u32[]{:S(2)}, u32[]{:S(2)}) collective-permute-start(bf16[2,592,128]{2,1,0:T(8,128)(2,1)S(1)} %fusion.5), channel_id=1, source_target_pairs={{0,2},{1,3},{2,0},{3,1},{4,6},{5,7},{6,4},{7,5},{8,10},{9,11},{10,... | collective-permute-start | bytes 909320 | tf_op jit(solution)/shard_map/ppermute | solution.py:343
  29.3 11.3 %collective-permute-start.7 = (bf16[2,592,128]{2,1,0:T(8,128)(2,1)S(1)}, bf16[2,592,128]{2,1,0:T(8,128)(2,1)S(1)}, u32[]{:S(2)}, u32[]{:S(2)}) collective-permute-start(bf16[2,592,128]{2,1,0:T(8,128)(2,1)S(1)} %fusion.6), channel_id=1, source_target_pairs={{0,4},{1,5},{2,6},{3,7},{4,0},{5,1},{6,2},{7,3},{8,12},{9,13},{10,... | collective-permute-start | bytes 909320 | tf_op jit(solution)/shard_map/ppermute | solution.py:343
  31.0 12.8 %collective-permute-start.10 = (bf16[2,592,128]{2,1,0:T(8,128)(2,1)S(1)}, bf16[2,592,128]{2,1,0:T(8,128)(2,1)S(1)}, u32[]{:S(2)}, u32[]{:S(2)}) collective-permute-start(bf16[2,592,128]{2,1,0:T(8,128)(2,1)S(1)} %fusion.7), channel_id=1, source_target_pairs={{0,2},{1,3},{2,0},{3,1},{4,6},{5,7},{6,4},{7,5},{8,10},{9,11},{10,... | collective-permute-start | bytes 909320 | tf_op jit(solution)/shard_map/ppermute | solution.py:343
  33.0 14.1 %collective-permute-start.1 = (bf16[2,592,128]{2,1,0:T(8,128)(2,1)S(1)}, bf16[2,592,128]{2,1,0:T(8,128)(2,1)S(1)}, u32[]{:S(2)}, u32[]{:S(2)}) collective-permute-start(bf16[2,592,128]{2,1,0:T(8,128)(2,1)S(1)} %fusion.4), channel_id=1, source_target_pairs={{0,4},{1,5},{2,6},{3,7},{4,0},{5,1},{6,2},{7,3},{8,12},{9,13},{10,... | collective-permute-start | bytes 909320 | tf_op jit(solution)/shard_map/ppermute | solution.py:343
  37.3 11.9 %collective-permute-start.5 = (bf16[592,128]{1,0:T(8,128)(2,1)S(1)}, bf16[592,128]{1,0:T(8,128)(2,1)S(1)}, u32[]{:S(2)}, u32[]{:S(2)}) collective-permute-start(bf16[592,128]{1,0:T(8,128)(2,1)S(1)} %fusion.19), channel_id=1, source_target_pairs={{0,4},{1,5},{2,6},{3,7},{4,0},{5,1},{6,2},{7,3},{8,12},{9,13},{10,... | collective-permute-start | bytes 454664 | tf_op jit(solution)/shard_map/ppermute | solution.py:343
  40.7 13.0 %collective-permute-start.8 = (bf16[592,128]{1,0:T(8,128)(2,1)S(1)}, bf16[592,128]{1,0:T(8,128)(2,1)S(1)}, u32[]{:S(2)}, u32[]{:S(2)}) collective-permute-start(bf16[592,128]{1,0:T(8,128)(2,1)S(1)} %fusion.20), channel_id=1, source_target_pairs={{0,2},{1,3},{2,0},{3,1},{4,6},{5,7},{6,4},{7,5},{8,10},{9,11},{10,... | collective-permute-start | bytes 454664 | tf_op jit(solution)/shard_map/ppermute | solution.py:343
  43.8 10.0 %collective-permute-start.11 = (bf16[592,128]{1,0:T(8,128)(2,1)S(1)}, bf16[592,128]{1,0:T(8,128)(2,1)S(1)}, u32[]{:S(2)}, u32[]{:S(2)}) collective-permute-start(bf16[592,128]{1,0:T(8,128)(2,1)S(1)} %fusion.21), channel_id=1, source_target_pairs={{0,4},{1,5},{2,6},{3,7},{4,0},{5,1},{6,2},{7,3},{8,12},{9,13},{10,... | collective-permute-start | bytes 454664 | tf_op jit(solution)/shard_map/ppermute | solution.py:343
  47.2 7.3 %collective-permute-start.2 = (bf16[592,128]{1,0:T(8,128)(2,1)S(1)}, bf16[592,128]{1,0:T(8,128)(2,1)S(1)}, u32[]{:S(2)}, u32[]{:S(2)}) collective-permute-start(bf16[592,128]{1,0:T(8,128)(2,1)S(1)} %fusion.18), channel_id=1, source_target_pairs={{0,2},{1,3},{2,0},{3,1},{4,6},{5,7},{6,4},{7,5},{8,10},{9,11},{10,... | collective-permute-start | bytes 454664 | tf_op jit(solution)/shard_map/ppermute | solution.py:343
  49.2 9.3 %collective-permute-start.6 = (bf16[592,128]{1,0:T(8,128)(2,1)S(1)}, bf16[592,128]{1,0:T(8,128)(2,1)S(1)}, u32[]{:S(2)}, u32[]{:S(2)}) collective-permute-start(bf16[592,128]{1,0:T(8,128)(2,1)S(1)} %fusion.13), channel_id=1, source_target_pairs={{0,24},{8,16},{16,8},{24,0},{1,25},{9,17},{17,9},{25,1},{2,26},{10... | collective-permute-start | bytes 454664 | tf_op jit(solution)/shard_map/ppermute | solution.py:363
  53.7 11.3 %collective-permute-start.9 = (bf16[592,128]{1,0:T(8,128)(2,1)S(1)}, bf16[592,128]{1,0:T(8,128)(2,1)S(1)}, u32[]{:S(2)}, u32[]{:S(2)}) collective-permute-start(bf16[592,128]{1,0:T(8,128)(2,1)S(1)} %fusion.11), channel_id=1, source_target_pairs={{0,16},{8,24},{16,0},{24,8},{1,17},{9,25},{17,1},{25,9},{2,18},{10... | collective-permute-start | bytes 454664 | tf_op jit(solution)/shard_map/ppermute | solution.py:363
  53.9 11.2 %collective-permute-start.12 = (bf16[592,128]{1,0:T(8,128)(2,1)S(1)}, bf16[592,128]{1,0:T(8,128)(2,1)S(1)}, u32[]{:S(2)}, u32[]{:S(2)}) collective-permute-start(bf16[592,128]{1,0:T(8,128)(2,1)S(1)} %fusion.9), channel_id=1, source_target_pairs={{0,8},{8,0},{16,24},{24,16},{1,9},{9,1},{17,25},{25,17},{2,10},{10... | collective-permute-start | bytes 454664 | tf_op jit(solution)/shard_map/ppermute | solution.py:363
  65.9 7.9 %collective-permute-start.13 = (bf16[128,128]{1,0:T(8,128)(2,1)S(1)}, bf16[128,128]{1,0:T(8,128)(2,1)S(1)}, u32[]{:S(2)}, u32[]{:S(2)}) collective-permute-start(bf16[128,128]{1,0:T(8,128)(2,1)S(1)} %get-tuple-element.30), channel_id=1, source_target_pairs={{0,1},{1,2},{2,3},{3,4},{4,5},{5,6},{6,7},{7,0},{8,9},{9,10},{10,1... | collective-permute-start | bytes 98312 | tf_op jit(solution)/shard_map/ppermute | solution.py:369
  66.0 7.8 %collective-permute-start.14 = (bf16[128,128]{1,0:T(8,128)(2,1)S(1)}, bf16[128,128]{1,0:T(8,128)(2,1)S(1)}, u32[]{:S(2)}, u32[]{:S(2)}) collective-permute-start(bf16[128,128]{1,0:T(8,128)(2,1)S(1)} %get-tuple-element.29), channel_id=1, source_target_pairs={{0,2},{1,3},{2,4},{3,5},{4,6},{5,7},{6,0},{7,1},{8,10},{9,11},{10,... | collective-permute-start | bytes 98312 | tf_op jit(solution)/shard_map/ppermute | solution.py:369
  67.7 6.1 %collective-permute-start.15 = (bf16[128,128]{1,0:T(8,128)(2,1)S(1)}, bf16[128,128]{1,0:T(8,128)(2,1)S(1)}, u32[]{:S(2)}, u32[]{:S(2)}) collective-permute-start(bf16[128,128]{1,0:T(8,128)(2,1)S(1)} %get-tuple-element.28), channel_id=1, source_target_pairs={{0,3},{1,4},{2,5},{3,6},{4,7},{5,0},{6,1},{7,2},{8,11},{9,12},{10,... | collective-permute-start | bytes 98312 | tf_op jit(solution)/shard_map/ppermute | solution.py:369
  70.0 3.7 %collective-permute-start.16 = (bf16[64,128]{1,0:T(8,128)(2,1)S(1)}, bf16[64,128]{1,0:T(8,128)(2,1)S(1)}, u32[]{:S(2)}, u32[]{:S(2)}) collective-permute-start(bf16[64,128]{1,0:T(8,128)(2,1)S(1)} %slice.171), channel_id=1, source_target_pairs={{0,4},{1,5},{2,6},{3,7},{4,0},{5,1},{6,2},{7,3},{8,12},{9,13},{10,... | collective-permute-start | bytes 49160 | tf_op jit(solution)/shard_map/ppermute | solution.py:369
  73.8 0.6 copy-start.12
  73.8 0.6 copy-start.9
  73.8 0.6 copy-start.10
  73.8 0.6 copy-start.11

commit v3 on v2

--- a/solution.py
+++ b/solution.py
@@ -9,6 +9,7 @@
 F32 = jnp.float32
 BF16 = jnp.bfloat16
 GROUP = 8
+PAIR = 2 * GROUP
 DEPTH = 256
 
 NT = (((1,), (1,)), ((), ()))
@@ -58,9 +59,24 @@
 
 
 def prepare_kernel(
-    place_ref, region_ref, count_ref, ld_ref, weight_ref, resid_ref, ids_ref,
+    place_hbm, region_hbm, count_hbm, ld_hbm, weight_hbm, resid_hbm, ids_hbm,
     scaled_ref, lanes_ref, column_ref, table_ref,
+    place_ref, region_ref, count_ref, ld_ref, weight_ref, resid_ref, ids_ref, sems,
 ):
+    copies = [
+        pltpu.make_async_copy(source, target, sems.at[n])
+        for n, (source, target) in enumerate(
+            (
+                (region_hbm, region_ref), (count_hbm, count_ref), (place_hbm, place_ref),
+                (ld_hbm, ld_ref), (weight_hbm, weight_ref), (resid_hbm, resid_ref),
+                (ids_hbm, ids_ref),
+            )
+        )
+    ]
+    for copy in copies:
+        copy.start()
+    for copy in copies:
+        copy.wait()
     tracks = region_ref.shape[1]
     groups, _, depth = scaled_ref.shape
     slots = groups * GROUP
@@ -71,7 +87,7 @@
     before = (iota((tracks, tracks), 0) < iota((tracks, tracks), 1)).astype(F32).astype(BF16)
     rank = jnp.dot(member.astype(BF16), before, preferred_element_type=F32)
     count = jnp.sum(member, axis=1, keepdims=True)
-    room = lax.shift_left(lax.shift_right_logical(count.astype(jnp.int32) + 7, 3), 3)
+    room = (count.astype(jnp.int32) + (PAIR - 1)) & -PAIR
     room = jnp.broadcast_to(room.astype(F32), (rr, slots))
     lower = (iota((rr, rr), 1) < iota((rr, rr), 0)).astype(F32)
     start = jnp.zeros((rr, slots), F32)
@@ -125,13 +141,13 @@
     tracks = region_row.shape[1]
     hits = weight.shape[0]
     rr = -(-regions // 8) * 8
-    slots = -(-(tracks + regions * (GROUP - 1)) // 128) * 128
+    slots = -(-(tracks + regions * (PAIR - 1)) // 128) * 128
     depth = GROUP * hits
-    smem = pl.BlockSpec(memory_space=pltpu.SMEM)
     vmem = pl.BlockSpec(memory_space=pltpu.VMEM)
+    values = (place, region_row, count_row, ld, weight, resid, ids)
     return pl.pallas_call(
         prepare_kernel,
-        in_specs=[smem] + [vmem] * 6,
+        in_specs=[pl.BlockSpec(memory_space=pltpu.HBM)] * 7,
         out_specs=[vmem] * 4,
         out_shape=[
             jax.ShapeDtypeStruct((slots // GROUP, 5 * GROUP, depth), F32),
@@ -139,69 +155,77 @@
             jax.ShapeDtypeStruct((depth, 128), BF16),
             jax.ShapeDtypeStruct((8 + rr, slots), jnp.int32),
         ],
+        scratch_shapes=[pltpu.SMEM(place.shape, place.dtype)]
+        + [pltpu.VMEM(value.shape, value.dtype) for value in values[1:]]
+        + [pltpu.SemaphoreType.DMA((7,))],
         compiler_params=pltpu.CompilerParams(vmem_limit_bytes=24 * 1024 * 1024),
         cost_estimate=pl.CostEstimate(flops=10**9, bytes_accessed=2 * 10**6, transcendentals=0),
         name="prepare",
-    )(place, region_row, count_row, ld, weight, resid, ids)
-
-
-def one_group(group, local, table_ref, g_ref, scaled_ref, lanes_ref, column_ref, g_s, direct_s, spread_s):
+    )(*values)
+
+
+def one_step(step, at, table_ref, g_ref, scaled_ref, lanes_ref, column_ref, g_s, direct_s, spread_s):
     hits, width = g_ref.shape[1:]
     depth = GROUP * hits
     blocks = spread_s.shape[1] // width
-    for i in range(GROUP):
-        g_s[i * hits : (i + 1) * hits, :] = g_ref[table_ref[0, group * GROUP + i]]
-    g = g_s[...]
-    chosen = (iota((128, width), 0) == group).astype(F32).astype(BF16)
-    position = jnp.dot(column_ref[...], chosen, preferred_element_type=F32).astype(BF16)
-    right = jnp.concatenate(
-        [jnp.where(position == jnp.bfloat16(p), g, jnp.bfloat16(0)) for p in range(blocks)], axis=1
-    )
-    weighted = g.astype(F32).T * lanes_ref[0, pl.ds(group, 1), :]
-    factor = jnp.where(iota((8, depth), 0) == 0, lanes_ref[1, pl.ds(group, 1), :], 0.0)
-    scaled = scaled_ref[group]
-    high = scaled.astype(BF16).astype(F32)
-    left = jnp.concatenate(
-        [weighted, factor, high, scaled - high, jnp.zeros((8, depth), F32)], axis=0
-    )
-    total = jnp.dot(left.astype(BF16), right, preferred_element_type=F32)
+    rows = 5 * GROUP
     head = width + 8
-    step = 5 * GROUP
-    direct_s[...] += total[:head]
-    spread_s[pl.ds(pl.multiple_of(local * step, GROUP), step), :] = (
-        total[head : head + step] + total[head + step : head + 2 * step]
-    )
-
-
-ODD = (0, 4, 2, 6)
-EVEN = (0, 2, 4, 6)
+    direct = []
+    for u in range(2):
+        group = step * 2 + u
+        for i in range(GROUP):
+            g_s[u, i * hits : (i + 1) * hits, :] = g_ref[table_ref[0, group * GROUP + i]]
+        g = g_s[u]
+        chosen = (iota((128, width), 0) == group).astype(F32).astype(BF16)
+        position = jnp.dot(column_ref[...], chosen, preferred_element_type=F32).astype(BF16)
+        right = jnp.concatenate(
+            [jnp.where(position == jnp.bfloat16(p), g, jnp.bfloat16(0)) for p in range(blocks)],
+            axis=1,
+        )
+        weighted = g.astype(F32).T * lanes_ref[0, pl.ds(group, 1), :]
+        factor = jnp.where(iota((8, depth), 0) == 0, lanes_ref[1, pl.ds(group, 1), :], 0.0)
+        scaled = scaled_ref[group]
+        high = scaled.astype(BF16).astype(F32)
+        left = jnp.concatenate(
+            [weighted, factor, high, scaled - high, jnp.zeros((8, depth), F32)], axis=0
+        )
+        total = jnp.dot(left.astype(BF16), right, preferred_element_type=F32)
+        direct.append(total[:head])
+        spread_s[pl.ds(pl.multiple_of(at + u * rows, GROUP), rows), :] = (
+            total[head : head + rows] + total[head + rows : head + 2 * rows]
+        )
+    direct_s[...] += direct[0] + direct[1]
+
+
+EVEN = (0, 4, 2, 6)
+ODD = (0, 2, 4, 6)
 
 
 def assemble_kernel(
-    first_k, where_ref, table_ref, scaled_ref, lanes_ref, column_ref, g_ref,
+    first_k, sub, table_ref, scaled_ref, lanes_ref, column_ref, g_ref,
     keep_ref, send_ref, g_s, direct_s, spread_s, wide_s, turned_s, acc_s,
 ):
     k = pl.program_id(0) + first_k
     width = g_ref.shape[2]
     blocks = spread_s.shape[1] // width
     many = blocks // 2
-    region = where_ref[1] ^ k
-    first = table_ref[8 + region, 0] // GROUP
-    groups = table_ref[8 + region, 1] // GROUP - first
+    region = lax.axis_index("region") ^ k
+    block = lax.axis_index("tile") // sub
+    first = table_ref[8 + region, 0] // PAIR
+    steps = table_ref[8 + region, 1] // PAIR - first
     direct_s[...] = jnp.zeros_like(direct_s)
-    acc_s[...] = jnp.zeros_like(acc_s)
-
-    def group_step(local, carry):
-        one_group(
-            first + local, local, table_ref, g_ref, scaled_ref, lanes_ref, column_ref,
+
+    def group_step(n, carry):
+        one_step(
+            first + n, n * (10 * GROUP), table_ref, g_ref, scaled_ref, lanes_ref, column_ref,
             g_s, direct_s, spread_s,
         )
         return carry
 
-    lax.fori_loop(0, groups, group_step, 0)
-    used = groups * 5
+    lax.fori_loop(0, steps, group_step, 0)
+    used = steps * 10
     depth_tiles = DEPTH // 8
-    chunks = (used + depth_tiles - 1) // depth_tiles
+    chunks = jnp.maximum((used + depth_tiles - 1) // depth_tiles, 1)
 
     def clear(tile, carry):
         spread_s[pl.ds(pl.multiple_of(tile * 8, 8), 8), :] = jnp.zeros((8, blocks * width), F32)
@@ -214,26 +238,40 @@
         narrow = spread_s[pl.ds(at, DEPTH), :].astype(BF16)
         wide_s[:, : blocks * width] = narrow
         wide_s[:, blocks * width :] = narrow[:, : many * width]
-        turned_s[...] = narrow.astype(F32).T.astype(BF16)
-        for p in range(blocks):
+        turned_s[...] = -narrow.T
+
+        def product(p):
             columns = (many + (1 if p < many else 0)) * width
-            acc_s[p, :, :columns] += jnp.dot(
+            return columns, jnp.dot(
                 turned_s[p * width : (p + 1) * width],
                 wide_s[:, p * width : p * width + columns],
                 preferred_element_type=F32,
             )
+
+        @pl.when(chunk == 0)
+        def _():
+            for p in range(blocks):
+                columns, value = product(p)
+                acc_s[p, :, :columns] = value
+
+        @pl.when(chunk > 0)
+        def _():
+            for p in range(blocks):
+                columns, value = product(p)
+                acc_s[p, :, :columns] += value
+
         return carry
 
     lax.fori_loop(0, chunks, chunk_step, 0)
     half = width // 2
     for n in range(blocks // 2):
         for odd, out_ref in ((0, keep_ref), (1, send_ref)):
-            p = where_ref[0] ^ (jnp.where(k % 2 == 1, ODD[n], EVEN[n]) + odd)
+            p = block ^ (jnp.where(block % 2 == 1 - odd, ODD[n], EVEN[n]) + odd)
             columns = pl.ds(pl.multiple_of(p * width, width), width)
-            parts = [direct_s[0:width, columns] - acc_s[p, :, 0:width]]
-            parts += [0.0 - acc_s[p, :, d * width : (d + 1) * width] for d in range(1, many)]
+            parts = [direct_s[0:width, columns] + acc_s[p, :, 0:width]]
+            parts += [acc_s[p, :, d * width : (d + 1) * width] for d in range(1, many)]
             upper = pl.multiple_of((p // many) * half, half)
-            parts.append(0.0 - acc_s[p % many, pl.ds(upper, half), many * width :])
+            parts.append(acc_s[p % many, pl.ds(upper, half), many * width :])
             row = direct_s[width : width + 1, columns]
             high = row.astype(BF16).astype(F32)
             sub = iota((16, width), 0)
@@ -241,22 +279,22 @@
             out_ref[n, 0] = jnp.concatenate(parts, axis=0).astype(BF16)
 
 
-def assemble(first_k, number, where, table, scaled, lanes, column, g, blocks):
+def assemble(first_k, number, sub, table, scaled, lanes, column, g, blocks):
     tracks, hits, width = g.shape
     rows = width * (blocks // 2) + width // 2 + 16
-    longest = -(-(-(-tracks // GROUP) * 5 * GROUP) // DEPTH) * DEPTH
+    longest = -(-(-(-tracks // PAIR) * 5 * PAIR) // DEPTH) * DEPTH
     out = jax.ShapeDtypeStruct((blocks // 2, number, rows, width), BF16)
     spec = pl.BlockSpec((blocks // 2, 1, rows, width), lambda k: (0, k, 0, 0))
     smem = pl.BlockSpec(memory_space=pltpu.SMEM)
     vmem = pl.BlockSpec(memory_space=pltpu.VMEM)
     return pl.pallas_call(
-        functools.partial(assemble_kernel, first_k),
+        functools.partial(assemble_kernel, first_k, sub),
         grid=(number,),
-        in_specs=[smem, smem, vmem, vmem, vmem, vmem],
+        in_specs=[smem, vmem, vmem, vmem, vmem],
         out_specs=[spec, spec],
         out_shape=[out, out],
         scratch_shapes=[
-            pltpu.VMEM((GROUP * hits, width), BF16),
+            pltpu.VMEM((2, GROUP * hits, width), BF16),
             pltpu.VMEM((width + 8, blocks * width), F32),
             pltpu.VMEM((longest, blocks * width), F32),
             pltpu.VMEM((DEPTH, (blocks + blocks // 2) * width), BF16),
@@ -270,12 +308,12 @@
             flops=3 * 10**9 * number // 2, bytes_accessed=4 * 10**6, transcendentals=0
         ),
         name="assemble",
-    )(where, table, scaled, lanes, column, g)
-
-
-def finish_kernel(where_ref, own_ref, r1_ref, r2_ref, r3_ref, e_ref, out_ref, vec_ref):
+    )(table, scaled, lanes, column, g)
+
+
+def finish_kernel(sub, own_ref, r1_ref, r2_ref, r3_ref, e_ref, out_ref, vec_ref):
     width = own_ref.shape[1]
-    p = where_ref[0]
+    p = lax.axis_index("tile") // sub
     blocks = out_ref.shape[1] // width
     many = blocks // 2
 
@@ -302,20 +340,19 @@
     vec_ref[...] = own_ref[tail : tail + 1, :] + own_ref[tail + 1 : tail + 2, :]
 
 
-def finish(where, own, r1, r2, r3, ext, blocks):
+def finish(sub, own, r1, r2, r3, ext, blocks):
     width = own.shape[1]
-    smem = pl.BlockSpec(memory_space=pltpu.SMEM)
     vmem = pl.BlockSpec(memory_space=pltpu.VMEM)
     return pl.pallas_call(
-        finish_kernel,
-        in_specs=[smem] + [vmem] * 5,
+        functools.partial(finish_kernel, sub),
+        in_specs=[vmem] * 5,
         out_specs=[vmem, vmem],
         out_shape=[
             jax.ShapeDtypeStruct((width, blocks * width), F32),
             jax.ShapeDtypeStruct((1, width), F32),
         ],
         name="finish",
-    )(where, own, r1, r2, r3, ext)
+    )(own, r1, r2, r3, ext)
 
 
 def local(
@@ -327,7 +364,6 @@
     blocks = block_place.shape[0]
     sub = tiles // blocks
     tile = lax.axis_index("tile")
-    where = jnp.stack([tile // sub, lax.axis_index("region")]).astype(jnp.int32)
     scaled, lanes, column, table = prepare(
         block_place,
         track_region.reshape(1, tracks),
@@ -339,28 +375,33 @@
         regions,
     )
 
-    def swap(value, bit):
-        return lax.ppermute(value, "tile", [(t, t ^ bit) for t in range(tiles)])
+    def swap(value, even, odd):
+        pairs = [(t, t ^ (sub * (odd if t // sub % 2 else even))) for t in range(tiles)]
+        return lax.ppermute(value, "tile", pairs)
+
+    def across(value, k):
+        return lax.ppermute(value.astype(BF16), "region", [(r, r ^ k) for r in range(regions)])
 
     totals = [None] * regions
     for first in range(regions - 2, -1, -2):
-        keep, send = assemble(first, 2, where, table, scaled, lanes, column, global_deriv, blocks)
+        keep, send = assemble(first, 2, sub, table, scaled, lanes, column, global_deriv, blocks)
         bit = 1
         while bit < sub:
-            keep, send = keep + swap(keep, bit), send + swap(send, bit)
+            near = [(t, t ^ bit) for t in range(tiles)]
+            keep, send = (v + lax.ppermute(v, "tile", near) for v in (keep, send))
             bit *= 2
-        got = swap(send, sub)
-        for n in range(2):
-            bits = ((4, 2), (2, 4))[n]
-            total = keep[:, n].astype(F32) + got[:, n].astype(F32)
-            more = swap(total[2:].astype(BF16), sub * bits[0])
-            total = total[:2] + more.astype(F32)
-            more = swap(total[1].astype(BF16), sub * bits[1])
-            totals[first + n] = total[0] + more.astype(F32)
+        total = keep.astype(F32) + swap(send, 1, 1).astype(F32)
+        third = total[2:].astype(BF16)
+        if first:
+            third, table = lax.optimization_barrier((third, table))
+        total = total[:2] + swap(third, 2, 4).astype(F32)
+        total = total[0] + swap(total[1].astype(BF16), 4, 2).astype(F32)
+        totals[first], totals[first + 1] = total[0], total[1]
+    bit = 1
+    for k in range(regions - 1, 0, -1):
+        step = k & -k
+        totals[k - step] = totals[k - step] + across(totals[k], step).astype(F32)
     own = totals[0]
-    for k in range(regions - 1, 0, -1):
-        pairs = [(r, r ^ k) for r in range(regions)]
-        own = own + lax.ppermute(totals[k].astype(BF16), "region", pairs).astype(F32)
 
     def onward(value, d):
         pairs = [
@@ -369,7 +410,7 @@
         return lax.ppermute(value.astype(BF16), "tile", pairs)
 
     matrix, vector = finish(
-        where,
+        sub,
         own,
         *(onward(own[d * width : (d + 1) * width], d) for d in range(1, blocks // 2)),
         onward(own[blocks // 2 * width : blocks // 2 * width + width // 2], blocks // 2),

time: 76.3 us -> 77.1 us (1.010); the launches traced: 76.4 us -> 76.4 us
  waiting for transfers between devices: 22.3 us -> 30.1 us
  starting transfers between devices: 23.8 us -> 17.3 us
  Pallas kernels: 21.6 us -> 20.4 us
    ppermute x13 -> x9, waiting for transfers between devices: 19 us -> 26.4 us  [the longest x6 19.3 us: swap(): return lax.ppermute(value, 'tile', pairs)]
    ppermute x13 -> x9, starting transfers between devices: 19.1 us -> 14.3 us  [the longest x6 7.7 us: swap(): return lax.ppermute(value, 'tile', pairs)]
    ppermute x4, starting transfers between devices: 4.64 us -> 3.02 us  [onward(): return lax.ppermute(value.astype(BF16), 'tile', pairs)]
    pallas_call x4, Pallas kernels: 21.6 us -> 20.4 us  [the longest x2 16.9 us: assemble(): pl.pallas_call(functools.partial(assemble_kernel, first_k, sub), grid=(nu...]
    unnamed x26 -> x24, local copies, waits for them, and re-layouts: 5.71 us -> 5.69 us
  transfers between devices with their start and end apart: 17 -> 13, of which waited for: 6 -> 10; matrix products, arithmetic and copies ran while one was open for 2% -> 1% of each run, Pallas kernels for 10% -> 0%
where the time goes in v3:
time: 77.1 us; the launch traced here: 76.4 us
  waiting for transfers between devices  30.1 us (39%)
  Pallas kernels  20.4 us (26%)
  starting transfers between devices  17.3 us (22%)
  local copies, waits for them, and re-layouts  5.98 us (8%)
  other arithmetic  1.76 us (2%)
  between operations  0.79 us (1%)
    ppermute x6, waiting for transfers between devices, swap(): return lax.ppermute(value, 'tile', pairs)  19.3 us
    pallas_call x2, Pallas kernels, assemble(): pl.pallas_call(functools.partial(assemble_kernel, first_k, sub), grid=(nu...  16.9 us
    ppermute x6, starting transfers between devices, swap(): return lax.ppermute(value, 'tile', pairs)  7.7 us
    ppermute x3, waiting for transfers between devices, across(): lax.ppermute(value.astype(BF16), 'region', [(r, r ^ k) for r in range(reg...  7.12 us
    ppermute x3, starting transfers between devices, across(): lax.ppermute(value.astype(BF16), 'region', [(r, r ^ k) for r in range(reg...  6.57 us
    unnamed x24, local copies, waits for them, and re-layouts  5.69 us
    ppermute x4, waiting for transfers between devices, onward(): return lax.ppermute(value.astype(BF16), 'tile', pairs)  3.69 us
    ppermute x4, starting transfers between devices, onward(): return lax.ppermute(value.astype(BF16), 'tile', pairs)  3.02 us
  transfers between devices with their start and end apart: 13, of which 10 were waited for; matrix products, arithmetic and copies ran while one was open for 1% of the time, Pallas kernels for 0%

profile of v3, /device:TPU:0, one launch (start us, length us, event | category | flops | bytes accessed | tf_op | source)
XLA Modules:
  0.0 76.4 jit_solution(11900001514521228788)
XLA Ops:
  0.6 0.9 %copy-done.1 = bf16[192,5,32]{0,2,1:T(8,128)(2,1)S(1)} copy-done((bf16[192,5,32]{0,2,1:T(8,128)(2,1)S(1)}, bf16[192,5,32]{0,2,1:T(8,128)(2,1)}, u32[]{:S(2)}) %copy-start.1) | copy-done | bytes 61464
  1.5 0.8 copy-done.2
  2.3 0.7 copy-done.3
  3.0 0.7 copy-done.4
  3.7 0.7 copy-done.5
  4.4 0.7 copy-done.6
  5.1 0.7 copy-done.7
  5.7 1.6 %prepare.1 = (f32[32,40,256]{2,1,0:T(8,128)S(1)}, f32[2,32,256]{2,1,0:T(8,128)S(1)}, bf16[256,128]{1,0:T(8,128)(2,1)S(1)}, s32[16,256]{1,0:T(8,128)S(1)}) custom-call(s32[8]{0:T(128)S(1)} %copy-done.7, s32[1,192]{1,0:T(1,128)S(1)} %bitcast.42, s32[1,192]{1,0:T(1,128)S(1)} %bitcast.43, bf16[160,192]{1,0:T(8,128)(2,1)S(1)} %bitcast.38, ...), custom_call_target="tpu_custom_call" | custom-call | flops 1000000000 | bytes 2000000 | tf_op jit(solution)/shard_map/prepare/pallas_call | solution.py:148
  7.4 10.3 %assemble.2 = (bf16[4,2,592,128]{3,2,1,0:T(8,128)(2,1)S(1)}, bf16[4,2,592,128]{3,2,1,0:T(8,128)(2,1)S(1)}) custom-call(s32[16,256]{1,0:T(8,128)S(1)} %get-tuple-element.20.table_ref, f32[32,40,256]{2,1,0:T(8,128)S(1)} %get-tuple-element.15.scaled_ref, f32[2,32,256]{2,1,0:T(8,128)S(1)} %get-tuple-element.16.lanes_ref, ...), custom_call_target="tpu_custom_call" | custom-call | flops 3000000000 | bytes 4000000 | tf_op jit(solution)/shard_map/assemble/pallas_call | solution.py:290
  17.6 0.1 collective-permute-start
  17.7 2.9 %collective-permute-done = bf16[4,2,592,128]{3,2,1,0:T(8,128)(2,1)S(1)} collective-permute-done((bf16[4,2,592,128]{3,2,1,0:T(8,128)(2,1)S(1)}, bf16[4,2,592,128]{3,2,1,0:T(8,128)(2,1)S(1)}, u32[]{:S(2)}, u32[]{:S(2)}) %collective-permute-start) | collective-permute-done | bytes 1212448 | tf_op jit(solution)/shard_map/ppermute | solution.py:380
  20.6 0.3 convert_add_fusion.1
  20.9 0.1 slice.123
  21.0 6.6 %assemble.3 = (bf16[4,2,592,128]{3,2,1,0:T(8,128)(2,1)S(1)}, bf16[4,2,592,128]{3,2,1,0:T(8,128)(2,1)S(1)}) custom-call(s32[16,256]{1,0:T(8,128)S(1)} %get-tuple-element.20.table_ref, f32[32,40,256]{2,1,0:T(8,128)S(1)} %get-tuple-element.15.scaled_ref, f32[2,32,256]{2,1,0:T(8,128)S(1)} %get-tuple-element.16.lanes_ref, ...), custom_call_target="tpu_custom_call" | custom-call | flops 3000000000 | bytes 4000000 | tf_op jit(solution)/shard_map/assemble/pallas_call | solution.py:290
  27.6 0.9 %collective-permute-start.1 = (bf16[4,2,592,128]{3,2,1,0:T(8,128)(2,1)S(1)}, bf16[4,2,592,128]{3,2,1,0:T(8,128)(2,1)S(1)}, u32[]{:S(2)}, u32[]{:S(2)}) collective-permute-start(bf16[4,2,592,128]{3,2,1,0:T(8,128)(2,1)S(1)} %get-tuple-element.22), channel_id=1, source_target_pairs={{0,1},{1,0},{2,3},{3,2},{4,5},{5,4},{6,7},{7,6},{8,9},{9,8},{10,11... | collective-permute-start | bytes 3637256 | tf_op jit(solution)/shard_map/ppermute | solution.py:380
  28.5 3.2 %collective-permute-start.4 = (bf16[2,2,592,128]{3,2,1,0:T(8,128)(2,1)S(1)}, bf16[2,2,592,128]{3,2,1,0:T(8,128)(2,1)S(1)}, u32[]{:S(2)}, u32[]{:S(2)}) collective-permute-start(bf16[2,2,592,128]{3,2,1,0:T(8,128)(2,1)S(1)} %slice.123), channel_id=1, source_target_pairs={{0,2},{1,5},{2,0},{3,7},{4,6},{5,1},{6,4},{7,3},{8,10},{9,13},{10,... | collective-permute-start | bytes 1818632 | tf_op jit(solution)/shard_map/ppermute | solution.py:380
  31.7 8.0 %collective-permute-done.4 = bf16[2,2,592,128]{3,2,1,0:T(8,128)(2,1)S(1)} collective-permute-done((bf16[2,2,592,128]{3,2,1,0:T(8,128)(2,1)S(1)}, bf16[2,2,592,128]{3,2,1,0:T(8,128)(2,1)S(1)}, u32[]{:S(2)}, u32[]{:S(2)}) %collective-permute-start.4) | collective-permute-done | bytes 606240 | tf_op jit(solution)/shard_map/ppermute | solution.py:380
  39.7 0.1 slice_add_fusion
  39.8 2.1 %collective-permute-start.5 = (bf16[2,592,128]{2,1,0:T(8,128)(2,1)S(1)}, bf16[2,592,128]{2,1,0:T(8,128)(2,1)S(1)}, u32[]{:S(2)}, u32[]{:S(2)}) collective-permute-start(bf16[2,592,128]{2,1,0:T(8,128)(2,1)S(1)} %fusion.3), channel_id=1, source_target_pairs={{0,4},{1,3},{2,6},{3,1},{4,0},{5,7},{6,2},{7,5},{8,12},{9,11},{10,... | collective-permute-start | bytes 909320 | tf_op jit(solution)/shard_map/ppermute | solution.py:380
  42.0 0.3 convert_add_fusion
  42.3 0.1 slice.122
  42.3 0.4 collective-permute-start.2
  42.7 6.8 %collective-permute-done.5 = bf16[2,592,128]{2,1,0:T(8,128)(2,1)S(1)} collective-permute-done((bf16[2,592,128]{2,1,0:T(8,128)(2,1)S(1)}, bf16[2,592,128]{2,1,0:T(8,128)(2,1)S(1)}, u32[]{:S(2)}, u32[]{:S(2)}) %collective-permute-start.5) | collective-permute-done | bytes 303136 | tf_op jit(solution)/shard_map/ppermute | solution.py:380
  49.5 0.1 fusion
  49.6 2.6 %collective-permute-start.6 = (bf16[592,128]{1,0:T(8,128)(2,1)S(1)}, bf16[592,128]{1,0:T(8,128)(2,1)S(1)}, u32[]{:S(2)}, u32[]{:S(2)}) collective-permute-start(bf16[592,128]{1,0:T(8,128)(2,1)S(1)} %fusion.8), channel_id=1, source_target_pairs={{0,8},{8,0},{16,24},{24,16},{1,9},{9,1},{17,25},{25,17},{2,10},{10... | collective-permute-start | bytes 454664 | tf_op jit(solution)/shard_map/ppermute | solution.py:383
  52.2 0.2 collective-permute-done.2
  52.5 0.1 slice_add_fusion.1
  52.7 1.1 %collective-permute-start.3 = (bf16[2,592,128]{2,1,0:T(8,128)(2,1)S(1)}, bf16[2,592,128]{2,1,0:T(8,128)(2,1)S(1)}, u32[]{:S(2)}, u32[]{:S(2)}) collective-permute-start(bf16[2,592,128]{2,1,0:T(8,128)(2,1)S(1)} %fusion.2), channel_id=1, source_target_pairs={{0,4},{1,3},{2,6},{3,1},{4,0},{5,7},{6,2},{7,5},{8,12},{9,11},{10,... | collective-permute-start | bytes 909320 | tf_op jit(solution)/shard_map/ppermute | solution.py:380
  53.8 1.6 %collective-permute-done.6 = bf16[592,128]{1,0:T(8,128)(2,1)S(1)} collective-permute-done((bf16[592,128]{1,0:T(8,128)(2,1)S(1)}, bf16[592,128]{1,0:T(8,128)(2,1)S(1)}, u32[]{:S(2)}, u32[]{:S(2)}) %collective-permute-start.6) | collective-permute-done | bytes 151584 | tf_op jit(solution)/shard_map/ppermute | solution.py:383
  55.4 2.8 %collective-permute-start.7 = (bf16[592,128]{1,0:T(8,128)(2,1)S(1)}, bf16[592,128]{1,0:T(8,128)(2,1)S(1)}, u32[]{:S(2)}, u32[]{:S(2)}) collective-permute-start(bf16[592,128]{1,0:T(8,128)(2,1)S(1)} %fusion.5), channel_id=1, source_target_pairs={{0,16},{8,24},{16,0},{24,8},{1,17},{9,25},{17,1},{25,9},{2,18},{10... | collective-permute-start | bytes 454664 | tf_op jit(solution)/shard_map/ppermute | solution.py:383
  58.2 1.3 %collective-permute-done.3 = bf16[2,592,128]{2,1,0:T(8,128)(2,1)S(1)} collective-permute-done((bf16[2,592,128]{2,1,0:T(8,128)(2,1)S(1)}, bf16[2,592,128]{2,1,0:T(8,128)(2,1)S(1)}, u32[]{:S(2)}, u32[]{:S(2)}) %collective-permute-start.3) | collective-permute-done | bytes 303136 | tf_op jit(solution)/shard_map/ppermute | solution.py:380
  59.5 0.1 fusion.1
  59.6 1.2 %collective-permute-start.8 = (bf16[592,128]{1,0:T(8,128)(2,1)S(1)}, bf16[592,128]{1,0:T(8,128)(2,1)S(1)}, u32[]{:S(2)}, u32[]{:S(2)}) collective-permute-start(bf16[592,128]{1,0:T(8,128)(2,1)S(1)} %fusion.9), channel_id=1, source_target_pairs={{0,8},{8,0},{16,24},{24,16},{1,9},{9,1},{17,25},{25,17},{2,10},{10... | collective-permute-start | bytes 454664 | tf_op jit(solution)/shard_map/ppermute | solution.py:383
  60.8 3.5 %collective-permute-done.7 = bf16[592,128]{1,0:T(8,128)(2,1)S(1)} collective-permute-done((bf16[592,128]{1,0:T(8,128)(2,1)S(1)}, bf16[592,128]{1,0:T(8,128)(2,1)S(1)}, u32[]{:S(2)}, u32[]{:S(2)}) %collective-permute-start.7) | collective-permute-done | bytes 151584 | tf_op jit(solution)/shard_map/ppermute | solution.py:383
  64.3 2.0 %collective-permute-done.8 = bf16[592,128]{1,0:T(8,128)(2,1)S(1)} collective-permute-done((bf16[592,128]{1,0:T(8,128)(2,1)S(1)}, bf16[592,128]{1,0:T(8,128)(2,1)S(1)}, u32[]{:S(2)}, u32[]{:S(2)}) %collective-permute-start.8) | collective-permute-done | bytes 151584 | tf_op jit(solution)/shard_map/ppermute | solution.py:383
  66.3 0.8 %fusion.10 = (bf16[592,128]{1,0:T(8,128)(2,1)S(1)}, f32[592,128]{1,0:T(8,128)}) fusion(bf16[592,128]{1,0:T(8,128)(2,1)S(1)} %collective-permute-done.8, bf16[592,128]{1,0:T(8,128)(2,1)S(1)} %collective-permute-done.7, f32[2,592,128]{2,1,0:T(8,128)S(1)} %fusion.1), kind=kLoop, calls=%fused_computation.24 | loop fusion | flops 378880 | bytes 1060864 | tf_op jit(solution)/shard_map/convert.3
  67.1 0.1 collective-permute-start.11
  67.2 2.4 %collective-permute-start.10 = (bf16[128,128]{1,0:T(8,128)(2,1)S(1)}, bf16[128,128]{1,0:T(8,128)(2,1)S(1)}, u32[]{:S(2)}, u32[]{:S(2)}) collective-permute-start(bf16[128,128]{1,0:T(8,128)(2,1)S(1)} %get-tuple-element.29), channel_id=1, source_target_pairs={{0,2},{1,3},{2,4},{3,5},{4,6},{5,7},{6,0},{7,1},{8,10},{9,11},{10,... | collective-permute-start | bytes 98312 | tf_op jit(solution)/shard_map/ppermute | solution.py:410
  69.5 0.0 collective-permute-start.9
  69.5 0.6 collective-permute-start.12
  70.1 3.2 %collective-permute-done.12.e_ref = bf16[64,128]{1,0:T(8,128)(2,1)S(1)} collective-permute-done((bf16[64,128]{1,0:T(8,128)(2,1)S(1)}, bf16[64,128]{1,0:T(8,128)(2,1)S(1)}, u32[]{:S(2)}, u32[]{:S(2)}) %collective-permute-start.12) | collective-permute-done | bytes 16416 | tf_op jit(solution)/shard_map/ppermute | solution.py:410
  73.3 0.0 collective-permute-done.10.r2_ref
  73.3 0.5 collective-permute-done.9.r1_ref
  73.8 0.0 copy-done.11
  73.9 0.0 copy-done.8
  73.9 0.0 copy-done.9
  73.9 0.5 copy-done.10
  74.4 1.9 %finish.1 = (f32[128,1024]{1,0:T(8,128)}, f32[1,128]{1,0:T(1,128)}) custom-call(f32[592,128]{1,0:T(8,128)} %get-tuple-element.27.own_ref, bf16[128,128]{1,0:T(8,128)(2,1)} %copy-done.10, bf16[128,128]{1,0:T(8,128)(2,1)} %copy-done.9, bf16[128,128]{1,0:T(8,128)(2,1)} %copy-done.8, bf16[64,128]{1,0:T(8,128)(2,1)} %copy-done.11), custom_call_target="tpu_custom_call" | custom-call | tf_op jit(solution)/shard_map/finish/pallas_call | solution.py:346
  (22 shorter events, 0.2 us)
Async XLA Ops:
  0.6 0.9 %copy-start.1 = (bf16[192,5,32]{0,2,1:T(8,128)(2,1)S(1)}, bf16[192,5,32]{0,2,1:T(8,128)(2,1)}, u32[]{:S(2)}) copy-start(bf16[192,5,32]{0,2,1:T(8,128)(2,1)} %param.9) | copy-start | bytes 184324
  1.5 0.8 copy-start.2
  2.3 0.7 copy-start.3
  3.0 0.7 copy-start.4
  3.7 0.7 copy-start.5
  4.4 0.7 copy-start.6
  5.1 0.7 copy-start.7
  5.7 1.6 %copy-start = (bf16[192,32,128]{2,1,0:T(8,128)(2,1)S(1)}, bf16[192,32,128]{2,1,0:T(8,128)(2,1)}, u32[]{:S(2)}) copy-start(bf16[192,32,128]{2,1,0:T(8,128)(2,1)} %g_ref.3) | copy-start | bytes 4718596
  17.6 3.0 %collective-permute-start = (bf16[4,2,592,128]{3,2,1,0:T(8,128)(2,1)S(1)}, bf16[4,2,592,128]{3,2,1,0:T(8,128)(2,1)S(1)}, u32[]{:S(2)}, u32[]{:S(2)}) collective-permute-start(bf16[4,2,592,128]{3,2,1,0:T(8,128)(2,1)S(1)} %get-tuple-element.19), channel_id=1, source_target_pairs={{0,1},{1,0},{2,3},{3,2},{4,5},{5,4},{6,7},{7,6},{8,9},{9,8},{10,11... | collective-permute-start | bytes 3637256 | tf_op jit(solution)/shard_map/ppermute | solution.py:380
  27.6 14.3 %collective-permute-start.1 = (bf16[4,2,592,128]{3,2,1,0:T(8,128)(2,1)S(1)}, bf16[4,2,592,128]{3,2,1,0:T(8,128)(2,1)S(1)}, u32[]{:S(2)}, u32[]{:S(2)}) collective-permute-start(bf16[4,2,592,128]{3,2,1,0:T(8,128)(2,1)S(1)} %get-tuple-element.22), channel_id=1, source_target_pairs={{0,1},{1,0},{2,3},{3,2},{4,5},{5,4},{6,7},{7,6},{8,9},{9,8},{10,11... | collective-permute-start | bytes 3637256 | tf_op jit(solution)/shard_map/ppermute | solution.py:380
  28.5 11.2 %collective-permute-start.4 = (bf16[2,2,592,128]{3,2,1,0:T(8,128)(2,1)S(1)}, bf16[2,2,592,128]{3,2,1,0:T(8,128)(2,1)S(1)}, u32[]{:S(2)}, u32[]{:S(2)}) collective-permute-start(bf16[2,2,592,128]{3,2,1,0:T(8,128)(2,1)S(1)} %slice.123), channel_id=1, source_target_pairs={{0,2},{1,5},{2,0},{3,7},{4,6},{5,1},{6,4},{7,3},{8,10},{9,13},{10,... | collective-permute-start | bytes 1818632 | tf_op jit(solution)/shard_map/ppermute | solution.py:380
  39.8 9.7 %collective-permute-start.5 = (bf16[2,592,128]{2,1,0:T(8,128)(2,1)S(1)}, bf16[2,592,128]{2,1,0:T(8,128)(2,1)S(1)}, u32[]{:S(2)}, u32[]{:S(2)}) collective-permute-start(bf16[2,592,128]{2,1,0:T(8,128)(2,1)S(1)} %fusion.3), channel_id=1, source_target_pairs={{0,4},{1,3},{2,6},{3,1},{4,0},{5,7},{6,2},{7,5},{8,12},{9,11},{10,... | collective-permute-start | bytes 909320 | tf_op jit(solution)/shard_map/ppermute | solution.py:380
  42.3 10.1 %collective-permute-start.2 = (bf16[2,2,592,128]{3,2,1,0:T(8,128)(2,1)S(1)}, bf16[2,2,592,128]{3,2,1,0:T(8,128)(2,1)S(1)}, u32[]{:S(2)}, u32[]{:S(2)}) collective-permute-start(bf16[2,2,592,128]{3,2,1,0:T(8,128)(2,1)S(1)} %slice.122), channel_id=1, source_target_pairs={{0,2},{1,5},{2,0},{3,7},{4,6},{5,1},{6,4},{7,3},{8,10},{9,13},{10,... | collective-permute-start | bytes 1818632 | tf_op jit(solution)/shard_map/ppermute | solution.py:380
  49.6 5.8 %collective-permute-start.6 = (bf16[592,128]{1,0:T(8,128)(2,1)S(1)}, bf16[592,128]{1,0:T(8,128)(2,1)S(1)}, u32[]{:S(2)}, u32[]{:S(2)}) collective-permute-start(bf16[592,128]{1,0:T(8,128)(2,1)S(1)} %fusion.8), channel_id=1, source_target_pairs={{0,8},{8,0},{16,24},{24,16},{1,9},{9,1},{17,25},{25,17},{2,10},{10... | collective-permute-start | bytes 454664 | tf_op jit(solution)/shard_map/ppermute | solution.py:383
  52.7 6.9 %collective-permute-start.3 = (bf16[2,592,128]{2,1,0:T(8,128)(2,1)S(1)}, bf16[2,592,128]{2,1,0:T(8,128)(2,1)S(1)}, u32[]{:S(2)}, u32[]{:S(2)}) collective-permute-start(bf16[2,592,128]{2,1,0:T(8,128)(2,1)S(1)} %fusion.2), channel_id=1, source_target_pairs={{0,4},{1,3},{2,6},{3,1},{4,0},{5,7},{6,2},{7,5},{8,12},{9,11},{10,... | collective-permute-start | bytes 909320 | tf_op jit(solution)/shard_map/ppermute | solution.py:380
  55.4 8.8 %collective-permute-start.7 = (bf16[592,128]{1,0:T(8,128)(2,1)S(1)}, bf16[592,128]{1,0:T(8,128)(2,1)S(1)}, u32[]{:S(2)}, u32[]{:S(2)}) collective-permute-start(bf16[592,128]{1,0:T(8,128)(2,1)S(1)} %fusion.5), channel_id=1, source_target_pairs={{0,16},{8,24},{16,0},{24,8},{1,17},{9,25},{17,1},{25,9},{2,18},{10... | collective-permute-start | bytes 454664 | tf_op jit(solution)/shard_map/ppermute | solution.py:383
  59.6 6.7 %collective-permute-start.8 = (bf16[592,128]{1,0:T(8,128)(2,1)S(1)}, bf16[592,128]{1,0:T(8,128)(2,1)S(1)}, u32[]{:S(2)}, u32[]{:S(2)}) collective-permute-start(bf16[592,128]{1,0:T(8,128)(2,1)S(1)} %fusion.9), channel_id=1, source_target_pairs={{0,8},{8,0},{16,24},{24,16},{1,9},{9,1},{17,25},{25,17},{2,10},{10... | collective-permute-start | bytes 454664 | tf_op jit(solution)/shard_map/ppermute | solution.py:383
  67.1 6.2 %collective-permute-start.11 = (bf16[128,128]{1,0:T(8,128)(2,1)S(1)}, bf16[128,128]{1,0:T(8,128)(2,1)S(1)}, u32[]{:S(2)}, u32[]{:S(2)}) collective-permute-start(bf16[128,128]{1,0:T(8,128)(2,1)S(1)} %get-tuple-element.28), channel_id=1, source_target_pairs={{0,3},{1,4},{2,5},{3,6},{4,7},{5,0},{6,1},{7,2},{8,11},{9,12},{10,... | collective-permute-start | bytes 98312 | tf_op jit(solution)/shard_map/ppermute | solution.py:410
  67.2 6.1 %collective-permute-start.10 = (bf16[128,128]{1,0:T(8,128)(2,1)S(1)}, bf16[128,128]{1,0:T(8,128)(2,1)S(1)}, u32[]{:S(2)}, u32[]{:S(2)}) collective-permute-start(bf16[128,128]{1,0:T(8,128)(2,1)S(1)} %get-tuple-element.29), channel_id=1, source_target_pairs={{0,2},{1,3},{2,4},{3,5},{4,6},{5,7},{6,0},{7,1},{8,10},{9,11},{10,... | collective-permute-start | bytes 98312 | tf_op jit(solution)/shard_map/ppermute | solution.py:410
  69.5 4.3 %collective-permute-start.9 = (bf16[128,128]{1,0:T(8,128)(2,1)S(1)}, bf16[128,128]{1,0:T(8,128)(2,1)S(1)}, u32[]{:S(2)}, u32[]{:S(2)}) collective-permute-start(bf16[128,128]{1,0:T(8,128)(2,1)S(1)} %get-tuple-element.30), channel_id=1, source_target_pairs={{0,1},{1,2},{2,3},{3,4},{4,5},{5,6},{6,7},{7,0},{8,9},{9,10},{10,1... | collective-permute-start | bytes 98312 | tf_op jit(solution)/shard_map/ppermute | solution.py:410
  69.5 3.7 %collective-permute-start.12 = (bf16[64,128]{1,0:T(8,128)(2,1)S(1)}, bf16[64,128]{1,0:T(8,128)(2,1)S(1)}, u32[]{:S(2)}, u32[]{:S(2)}) collective-permute-start(bf16[64,128]{1,0:T(8,128)(2,1)S(1)} %slice.89), channel_id=1, source_target_pairs={{0,4},{1,5},{2,6},{3,7},{4,0},{5,1},{6,2},{7,3},{8,12},{9,13},{10,... | collective-permute-start | bytes 49160 | tf_op jit(solution)/shard_map/ppermute | solution.py:410
  73.3 0.6 copy-start.11
  73.3 0.6 copy-start.8
  73.3 0.6 copy-start.9
  73.8 0.6 copy-start.10

commit v4 on v3

--- a/solution.py
+++ b/solution.py
@@ -58,25 +58,10 @@
     return solved, masked_w * resid - projection, masked_w
 
 
-def prepare_kernel(
-    place_hbm, region_hbm, count_hbm, ld_hbm, weight_hbm, resid_hbm, ids_hbm,
+def prepare(
+    place_ref, region_ref, count_ref, ld_ref, weight_ref, resid_ref, ids_ref,
     scaled_ref, lanes_ref, column_ref, table_ref,
-    place_ref, region_ref, count_ref, ld_ref, weight_ref, resid_ref, ids_ref, sems,
 ):
-    copies = [
-        pltpu.make_async_copy(source, target, sems.at[n])
-        for n, (source, target) in enumerate(
-            (
-                (region_hbm, region_ref), (count_hbm, count_ref), (place_hbm, place_ref),
-                (ld_hbm, ld_ref), (weight_hbm, weight_ref), (resid_hbm, resid_ref),
-                (ids_hbm, ids_ref),
-            )
-        )
-    ]
-    for copy in copies:
-        copy.start()
-    for copy in copies:
-        copy.wait()
     tracks = region_ref.shape[1]
     groups, _, depth = scaled_ref.shape
     slots = groups * GROUP
@@ -137,33 +122,6 @@
         )
 
 
-def prepare(place, region_row, count_row, ld, weight, resid, ids, regions):
-    tracks = region_row.shape[1]
-    hits = weight.shape[0]
-    rr = -(-regions // 8) * 8
-    slots = -(-(tracks + regions * (PAIR - 1)) // 128) * 128
-    depth = GROUP * hits
-    vmem = pl.BlockSpec(memory_space=pltpu.VMEM)
-    values = (place, region_row, count_row, ld, weight, resid, ids)
-    return pl.pallas_call(
-        prepare_kernel,
-        in_specs=[pl.BlockSpec(memory_space=pltpu.HBM)] * 7,
-        out_specs=[vmem] * 4,
-        out_shape=[
-            jax.ShapeDtypeStruct((slots // GROUP, 5 * GROUP, depth), F32),
-            jax.ShapeDtypeStruct((2, slots // GROUP, depth), F32),
-            jax.ShapeDtypeStruct((depth, 128), BF16),
-            jax.ShapeDtypeStruct((8 + rr, slots), jnp.int32),
-        ],
-        scratch_shapes=[pltpu.SMEM(place.shape, place.dtype)]
-        + [pltpu.VMEM(value.shape, value.dtype) for value in values[1:]]
-        + [pltpu.SemaphoreType.DMA((7,))],
-        compiler_params=pltpu.CompilerParams(vmem_limit_bytes=24 * 1024 * 1024),
-        cost_estimate=pl.CostEstimate(flops=10**9, bytes_accessed=2 * 10**6, transcendentals=0),
-        name="prepare",
-    )(*values)
-
-
 def one_step(step, at, table_ref, g_ref, scaled_ref, lanes_ref, column_ref, g_s, direct_s, spread_s):
     hits, width = g_ref.shape[1:]
     depth = GROUP * hits
@@ -201,11 +159,52 @@
 ODD = (0, 2, 4, 6)
 
 
-def assemble_kernel(
-    first_k, sub, table_ref, scaled_ref, lanes_ref, column_ref, g_ref,
+def fetch(pairs, sems):
+    copies = [
+        pltpu.make_async_copy(source, target, sems.at[n])
+        for n, (source, target) in enumerate(pairs)
+    ]
+    for copy in copies:
+        copy.start()
+    return copies
+
+
+def lead_kernel(ks, sub, *refs):
+    small, g_hbm, (keep_ref, send_ref), shared = refs[:7], refs[7], refs[8:10], refs[10:14]
+    local_small, g_ref, table_s, sems, scratch = refs[14:21], refs[21], refs[22], refs[23], refs[24:]
+
+    @pl.when(pl.program_id(0) == 0)
+    def _():
+        copies = fetch([*zip(small, local_small), (g_hbm, g_ref)], sems)
+        for copy in copies[:-1]:
+            copy.wait()
+        prepare(*local_small, *shared)
+        copy = pltpu.make_async_copy(shared[3], table_s, sems.at[0])
+        copy.start()
+        copy.wait()
+        copies[-1].wait()
+
+    assemble_region(ks, sub, table_s, *shared[:3], g_ref, keep_ref, send_ref, *scratch)
+
+
+def follow_kernel(ks, sub, *refs):
+    shared, (keep_ref, send_ref), mine, sems, scratch = (
+        refs[:5], refs[5:7], refs[7:12], refs[12], refs[13:]
+    )
+
+    @pl.when(pl.program_id(0) == 0)
+    def _():
+        for copy in fetch(list(zip(shared, mine)), sems):
+            copy.wait()
+
+    assemble_region(ks, sub, mine[3], *mine[:3], mine[4], keep_ref, send_ref, *scratch)
+
+
+def assemble_region(
+    ks, sub, table_ref, scaled_ref, lanes_ref, column_ref, g_ref,
     keep_ref, send_ref, g_s, direct_s, spread_s, wide_s, turned_s, acc_s,
 ):
-    k = pl.program_id(0) + first_k
+    k = jnp.where(pl.program_id(0) == 0, ks[0], ks[1])
     width = g_ref.shape[2]
     blocks = spread_s.shape[1] // width
     many = blocks // 2
@@ -276,24 +275,43 @@
             high = row.astype(BF16).astype(F32)
             sub = iota((16, width), 0)
             parts.append(jnp.where(sub == 0, high, jnp.where(sub == 1, row - high, 0.0)))
-            out_ref[n, 0] = jnp.concatenate(parts, axis=0).astype(BF16)
-
-
-def assemble(first_k, number, sub, table, scaled, lanes, column, g, blocks):
+            out_ref[0, n] = jnp.concatenate(parts, axis=0).astype(BF16)
+
+
+def assemble(ks, sub, inputs, g, blocks, regions):
     tracks, hits, width = g.shape
+    lead = len(inputs) == 7
     rows = width * (blocks // 2) + width // 2 + 16
     longest = -(-(-(-tracks // PAIR) * 5 * PAIR) // DEPTH) * DEPTH
-    out = jax.ShapeDtypeStruct((blocks // 2, number, rows, width), BF16)
-    spec = pl.BlockSpec((blocks // 2, 1, rows, width), lambda k: (0, k, 0, 0))
-    smem = pl.BlockSpec(memory_space=pltpu.SMEM)
+    rr = -(-regions // 8) * 8
+    slots = -(-(tracks + regions * (PAIR - 1)) // 128) * 128
+    shared = [
+        jax.ShapeDtypeStruct((slots // GROUP, 5 * GROUP, GROUP * hits), F32),
+        jax.ShapeDtypeStruct((2, slots // GROUP, GROUP * hits), F32),
+        jax.ShapeDtypeStruct((GROUP * hits, 128), BF16),
+        jax.ShapeDtypeStruct((8 + rr, slots), jnp.int32),
+    ]
+    out = jax.ShapeDtypeStruct((2, blocks // 2, rows, width), BF16)
+    spec = pl.BlockSpec((1, blocks // 2, rows, width), lambda k: (k, 0, 0, 0))
     vmem = pl.BlockSpec(memory_space=pltpu.VMEM)
+    table = pltpu.SMEM(shared[3].shape, jnp.int32)
+    arrived = pltpu.VMEM(g.shape, g.dtype)
+    if lead:
+        copies = [pltpu.SMEM(inputs[0].shape, jnp.int32)]
+        copies += [pltpu.VMEM(value.shape, value.dtype) for value in inputs[1:]]
+        copies += [arrived, table]
+    else:
+        copies = [pltpu.VMEM(value.shape, value.dtype) for value in inputs[:3]]
+        copies += [table, arrived]
     return pl.pallas_call(
-        functools.partial(assemble_kernel, first_k, sub),
-        grid=(number,),
-        in_specs=[smem, vmem, vmem, vmem, vmem],
-        out_specs=[spec, spec],
-        out_shape=[out, out],
-        scratch_shapes=[
+        functools.partial(lead_kernel if lead else follow_kernel, ks, sub),
+        grid=(2,),
+        in_specs=[pl.BlockSpec(memory_space=pltpu.HBM)] * (len(inputs) + 1),
+        out_specs=[spec, spec] + [vmem] * (4 * lead),
+        out_shape=[out, out] + shared * lead,
+        scratch_shapes=copies
+        + [
+            pltpu.SemaphoreType.DMA((8,)),
             pltpu.VMEM((2, GROUP * hits, width), BF16),
             pltpu.VMEM((width + 8, blocks * width), F32),
             pltpu.VMEM((longest, blocks * width), F32),
@@ -302,13 +320,13 @@
             pltpu.VMEM((blocks, width, (blocks // 2 + 1) * width), F32),
         ],
         compiler_params=pltpu.CompilerParams(
-            dimension_semantics=("arbitrary",), vmem_limit_bytes=32 * 1024 * 1024
+            dimension_semantics=("arbitrary",), vmem_limit_bytes=60 * 1024 * 1024
         ),
         cost_estimate=pl.CostEstimate(
-            flops=3 * 10**9 * number // 2, bytes_accessed=4 * 10**6, transcendentals=0
+            flops=8 * 10**9, bytes_accessed=4 * 10**6, transcendentals=0
         ),
         name="assemble",
-    )(table, scaled, lanes, column, g)
+    )(*inputs, g)
 
 
 def finish_kernel(sub, own_ref, r1_ref, r2_ref, r3_ref, e_ref, out_ref, vec_ref):
@@ -364,7 +382,7 @@
     blocks = block_place.shape[0]
     sub = tiles // blocks
     tile = lax.axis_index("tile")
-    scaled, lanes, column, table = prepare(
+    inputs = (
         block_place,
         track_region.reshape(1, tracks),
         hit_count.reshape(1, tracks),
@@ -372,7 +390,6 @@
         hit_weight.T,
         hit_resid.T,
         block_ids.T,
-        regions,
     )
 
     def swap(value, even, odd):
@@ -382,26 +399,52 @@
     def across(value, k):
         return lax.ppermute(value.astype(BF16), "region", [(r, r ^ k) for r in range(regions)])
 
-    totals = [None] * regions
-    for first in range(regions - 2, -1, -2):
-        keep, send = assemble(first, 2, sub, table, scaled, lanes, column, global_deriv, blocks)
+    def near(keep, send):
         bit = 1
         while bit < sub:
-            near = [(t, t ^ bit) for t in range(tiles)]
-            keep, send = (v + lax.ppermute(v, "tile", near) for v in (keep, send))
+            pairs = [(t, t ^ bit) for t in range(tiles)]
+            keep, send = (v + lax.ppermute(v, "tile", pairs) for v in (keep, send))
             bit *= 2
-        total = keep.astype(F32) + swap(send, 1, 1).astype(F32)
-        third = total[2:].astype(BF16)
-        if first:
-            third, table = lax.optimization_barrier((third, table))
-        total = total[:2] + swap(third, 2, 4).astype(F32)
-        total = total[0] + swap(total[1].astype(BF16), 4, 2).astype(F32)
-        totals[first], totals[first + 1] = total[0], total[1]
-    bit = 1
-    for k in range(regions - 1, 0, -1):
-        step = k & -k
-        totals[k - step] = totals[k - step] + across(totals[k], step).astype(F32)
-    own = totals[0]
+        return keep.astype(F32) + swap(send, 1, 1).astype(F32)
+
+    def halve(total, even, odd):
+        half = total.shape[0] // 2
+        return total[:half], swap(total[half:].astype(BF16), even, odd).astype(F32)
+
+    def plane(total):
+        total = sum(halve(total, 2, 4))
+        total = sum(halve(total, 4, 2))
+        return total[0]
+
+    arrived = []
+    for n in range(0, regions, 2):
+        ks = (n + 1, (n + 2) % regions)
+        keep, send, *made = assemble(ks, sub, inputs, global_deriv, blocks, regions)
+        if n == 0:
+            inputs = tuple(made)
+        else:
+            send, *waited = lax.optimization_barrier((send, *waited))
+            if n == 2:
+                early = waited[1]
+            total = kept + waited[0].astype(F32)
+            total = sum(halve(total, 4, 2))[0]
+            arrived.append(across(total, ks[0] - 1))
+        pair = near(keep, send)
+        if n == 0:
+            early, late = across(pair[0, 2:], 1), across(pair[0, :2], 1)
+        else:
+            arrived.append(across(plane(pair[0]), ks[0]))
+        if n + 2 < regions:
+            kept, third = pair[1, :2], pair[1, 2:].astype(BF16)
+            third, rest = lax.optimization_barrier((third, inputs[3]))
+            inputs = inputs[:3] + (rest,)
+            waited = [swap(third, 2, 4)] + [early] * (n == 0)
+    last = pair[1]
+    upper = swap((last[2:] + early.astype(F32)).astype(BF16), 2, 4)
+    last = last[:2] + late.astype(F32) + upper.astype(F32)
+    own = sum(halve(last, 4, 2))[0]
+    for value in arrived:
+        own = own + value.astype(F32)
 
     def onward(value, d):
         pairs = [

time: 77.1 us -> 76.2 us (0.988)
  the two profiles are of different devices: /device:TPU:0 before, /device:TPU:8 now
where the time goes in v4:
time: 76.2 us; the launch traced here: 75.2 us
  waiting for transfers between devices  26 us (34%)
  Pallas kernels  24.4 us (32%)
  starting transfers between devices  19 us (25%)
  other arithmetic  4.27 us (6%)
  local copies, waits for them, and re-layouts  0.77 us (1%)
  between operations  0.77 us (1%)
    pallas_call x2, Pallas kernels, assemble(): pl.pallas_call(functools.partial(lead_kernel if lead else follow_kernel,...  22.4 us
    ppermute x4, waiting for transfers between devices, across(): lax.ppermute(value.astype(BF16), 'region', [(r, r ^ k) for r in range(reg...  13.2 us
    ppermute x8, waiting for transfers between devices, swap(): return lax.ppermute(value, 'tile', pairs)  8.91 us
    ppermute x4, starting transfers between devices, across(): lax.ppermute(value.astype(BF16), 'region', [(r, r ^ k) for r in range(reg...  8.85 us
    ppermute x8, starting transfers between devices, swap(): return lax.ppermute(value, 'tile', pairs)  6.92 us
    ppermute x4, waiting for transfers between devices, onward(): return lax.ppermute(value.astype(BF16), 'tile', pairs)  3.86 us
    ppermute x4, starting transfers between devices, onward(): return lax.ppermute(value.astype(BF16), 'tile', pairs)  3.23 us
    add x2, other arithmetic, near(): return keep.astype(F32) + swap(send, 1, 1).astype(F32)  3.13 us
  transfers between devices with their start and end apart: 16, of which 8 were waited for; matrix products, arithmetic and copies ran while one was open for 3% of the time, Pallas kernels for 14%

profile of v4, /device:TPU:8, one launch (start us, length us, event | category | flops | bytes accessed | tf_op | source)
XLA Modules:
  0.0 75.2 jit_solution(18144031479946871025)
XLA Ops:
  0.6 12.3 %assemble.2 = (bf16[2,4,592,128]{3,2,1,0:T(8,128)(2,1)}, bf16[2,4,592,128]{3,2,1,0:T(8,128)(2,1)}, f32[32,40,256]{2,1,0:T(8,128)}, f32[2,32,256]{2,1,0:T(8,128)}...) custom-call(s32[8]{0:T(128)} %refs_0_.1, s32[1,192]{1,0:T(1,128)} %bitcast.53, s32[1,192]{1,0:T(1,128)} %bitcast.54, ...), custom_call_target="tpu_custom_call" | custom-call | flops 8000000000 | bytes 4000000 | tf_op jit(solution)/shard_map/assemble/pallas_call | solution.py:306
  12.9 0.1 collective-permute-start
  13.0 3.1 %collective-permute-done = bf16[2,4,592,128]{3,2,1,0:T(8,128)(2,1)S(1)} collective-permute-done((bf16[2,4,592,128]{3,2,1,0:T(8,128)(2,1)}, bf16[2,4,592,128]{3,2,1,0:T(8,128)(2,1)S(1)}, u32[]{:S(2)}, u32[]{:S(2)}) %collective-permute-start) | collective-permute-done | bytes 1212448 | tf_op jit(solution)/shard_map/ppermute | solution.py:397
  16.1 1.6 %convert_add_fusion.1 = (f32[2,4,592,128]{3,2,1,0:T(8,128)S(1)}, bf16[2,4,592,128]{3,2,1,0:T(8,128)(2,1)S(1)}) fusion(bf16[2,4,592,128]{3,2,1,0:T(8,128)(2,1)S(1)} %collective-permute-done, bf16[2,4,592,128]{3,2,1,0:T(8,128)(2,1)} %get-tuple-element.20), kind=kLoop, calls=%fused_computation.1 | loop fusion | flops 2424832 | bytes 6062080 | tf_op jit(solution)/shard_map/add | solution.py:408
  17.7 0.1 slice_bitcast_fusion.4
  17.8 1.6 %collective-permute-start.1 = (bf16[2,592,128]{2,1,0:T(8,128)(2,1)S(1)}, bf16[2,592,128]{2,1,0:T(8,128)(2,1)S(1)}, u32[]{:S(2)}, u32[]{:S(2)}) collective-permute-start(bf16[2,592,128]{2,1,0:T(8,128)(2,1)S(1)} %get-tuple-element.26), channel_id=1, source_target_pairs={{0,2},{1,5},{2,0},{3,7},{4,6},{5,1},{6,4},{7,3},{8,10},{9,13},{10,... | collective-permute-start | bytes 909320 | tf_op jit(solution)/shard_map/ppermute | solution.py:397
  19.3 0.0 collective-permute-start.2
  19.3 10.2 %assemble.3 = (bf16[2,4,592,128]{3,2,1,0:T(8,128)(2,1)}, bf16[2,4,592,128]{3,2,1,0:T(8,128)(2,1)}) custom-call(f32[32,40,256]{2,1,0:T(8,128)} %get-tuple-element.17.refs_0_, f32[2,32,256]{2,1,0:T(8,128)} %get-tuple-element.18.refs_1_, bf16[256,128]{1,0:T(8,128)(2,1)} %get-tuple-element.19.refs_2_, s32[16,256]{1,0:T(8,128)} %get-tuple-element.23.refs_3_, ...), custom_call_target="tpu_custom_call" | custom-call | flops 8000000000 | bytes 4000000 | tf_op jit(solution)/shard_map/assemble/pallas_call | solution.py:306
  29.5 0.0 collective-permute-done.1
  29.5 0.0 collective-permute-done.2
  29.5 0.1 collective-permute-start.3
  29.6 3.7 %collective-permute-start.4 = (bf16[2,592,128]{2,1,0:T(8,128)(2,1)S(1)}, bf16[2,592,128]{2,1,0:T(8,128)(2,1)S(1)}, u32[]{:S(2)}, u32[]{:S(2)}) collective-permute-start(bf16[2,592,128]{2,1,0:T(8,128)(2,1)S(1)} %get-tuple-element.38), channel_id=1, source_target_pairs={{0,8},{8,0},{16,24},{24,16},{1,9},{9,1},{17,25},{25,17},{2,10},{10... | collective-permute-start | bytes 909320 | tf_op jit(solution)/shard_map/ppermute | solution.py:400
  33.3 0.0 collective-permute-done.3
  33.3 1.5 %convert_add_fusion = f32[2,4,592,128]{3,2,1,0:T(8,128)S(1)} fusion(bf16[2,4,592,128]{3,2,1,0:T(8,128)(2,1)S(1)} %collective-permute-done.3, bf16[2,4,592,128]{3,2,1,0:T(8,128)(2,1)} %get-tuple-element.24), kind=kLoop, calls=%fused_computation | loop fusion | flops 1818624 | bytes 4849664 | tf_op jit(solution)/shard_map/add | solution.py:408
  34.8 0.1 fusion.3
  34.9 1.3 %collective-permute-start.9 = (bf16[2,592,128]{2,1,0:T(8,128)(2,1)S(1)}, bf16[2,592,128]{2,1,0:T(8,128)(2,1)S(1)}, u32[]{:S(2)}, u32[]{:S(2)}) collective-permute-start(bf16[2,592,128]{2,1,0:T(8,128)(2,1)S(1)} %fusion.6), channel_id=1, source_target_pairs={{0,2},{1,5},{2,0},{3,7},{4,6},{5,1},{6,4},{7,3},{8,10},{9,13},{10,... | collective-permute-start | bytes 909320 | tf_op jit(solution)/shard_map/ppermute | solution.py:397
  36.2 0.8 %collective-permute-start.5 = (bf16[2,592,128]{2,1,0:T(8,128)(2,1)S(1)}, bf16[2,592,128]{2,1,0:T(8,128)(2,1)S(1)}, u32[]{:S(2)}, u32[]{:S(2)}) collective-permute-start(bf16[2,592,128]{2,1,0:T(8,128)(2,1)S(1)} %fusion.3), channel_id=1, source_target_pairs={{0,2},{1,5},{2,0},{3,7},{4,6},{5,1},{6,4},{7,3},{8,10},{9,13},{10,... | collective-permute-start | bytes 909320 | tf_op jit(solution)/shard_map/ppermute | solution.py:397
  37.0 0.1 fusion.1
  37.1 1.5 %collective-permute-start.7 = (bf16[1,592,128]{2,1,0:T(8,128)(2,1)S(1)}, bf16[1,592,128]{2,1,0:T(8,128)(2,1)S(1)}, u32[]{:S(2)}, u32[]{:S(2)}) collective-permute-start(bf16[1,592,128]{2,1,0:T(8,128)(2,1)S(1)} %slice.163), channel_id=1, source_target_pairs={{0,4},{1,3},{2,6},{3,1},{4,0},{5,7},{6,2},{7,5},{8,12},{9,11},{10,... | collective-permute-start | bytes 454664 | tf_op jit(solution)/shard_map/ppermute | solution.py:397
  38.6 2.2 %collective-permute-done.4 = bf16[2,592,128]{2,1,0:T(8,128)(2,1)S(1)} collective-permute-done((bf16[2,592,128]{2,1,0:T(8,128)(2,1)S(1)}, bf16[2,592,128]{2,1,0:T(8,128)(2,1)S(1)}, u32[]{:S(2)}, u32[]{:S(2)}) %collective-permute-start.4) | collective-permute-done | bytes 303136 | tf_op jit(solution)/shard_map/ppermute | solution.py:400
  40.8 2.6 %collective-permute-done.9 = bf16[2,592,128]{2,1,0:T(8,128)(2,1)S(1)} collective-permute-done((bf16[2,592,128]{2,1,0:T(8,128)(2,1)S(1)}, bf16[2,592,128]{2,1,0:T(8,128)(2,1)S(1)}, u32[]{:S(2)}, u32[]{:S(2)}) %collective-permute-start.9) | collective-permute-done | bytes 303136 | tf_op jit(solution)/shard_map/ppermute | solution.py:397
  43.4 3.2 %collective-permute-done.5 = bf16[2,592,128]{2,1,0:T(8,128)(2,1)S(1)} collective-permute-done((bf16[2,592,128]{2,1,0:T(8,128)(2,1)S(1)}, bf16[2,592,128]{2,1,0:T(8,128)(2,1)S(1)}, u32[]{:S(2)}, u32[]{:S(2)}) %collective-permute-start.5) | collective-permute-done | bytes 303136 | tf_op jit(solution)/shard_map/ppermute | solution.py:397
  46.6 0.2 fusion.5
  46.8 1.5 %collective-permute-start.10 = (bf16[1,592,128]{2,1,0:T(8,128)(2,1)S(1)}, bf16[1,592,128]{2,1,0:T(8,128)(2,1)S(1)}, u32[]{:S(2)}, u32[]{:S(2)}) collective-permute-start(bf16[1,592,128]{2,1,0:T(8,128)(2,1)S(1)} %slice.162), channel_id=1, source_target_pairs={{0,4},{1,3},{2,6},{3,1},{4,0},{5,7},{6,2},{7,5},{8,12},{9,11},{10,... | collective-permute-start | bytes 454664 | tf_op jit(solution)/shard_map/ppermute | solution.py:397
  48.4 0.0 collective-permute-done.7
  48.4 4.6 %collective-permute-start.8 = (bf16[592,128]{1,0:T(8,128)(2,1)S(1)}, bf16[592,128]{1,0:T(8,128)(2,1)S(1)}, u32[]{:S(2)}, u32[]{:S(2)}) collective-permute-start(bf16[592,128]{1,0:T(8,128)(2,1)S(1)} %fusion.12), channel_id=1, source_target_pairs={{0,16},{8,24},{16,0},{24,8},{1,17},{9,25},{17,1},{25,9},{2,18},{10... | collective-permute-start | bytes 454664 | tf_op jit(solution)/shard_map/ppermute | solution.py:400
  53.1 0.1 collective-permute-start.6
  53.1 0.0 collective-permute-done.10
  53.2 0.6 collective-permute-start.11
  53.7 7.1 %collective-permute-done.8 = bf16[592,128]{1,0:T(8,128)(2,1)S(1)} collective-permute-done((bf16[592,128]{1,0:T(8,128)(2,1)S(1)}, bf16[592,128]{1,0:T(8,128)(2,1)S(1)}, u32[]{:S(2)}, u32[]{:S(2)}) %collective-permute-start.8) | collective-permute-done | bytes 151584 | tf_op jit(solution)/shard_map/ppermute | solution.py:400
  60.8 0.0 collective-permute-done.6
  60.8 3.9 %collective-permute-done.11 = bf16[592,128]{1,0:T(8,128)(2,1)S(1)} collective-permute-done((bf16[592,128]{1,0:T(8,128)(2,1)S(1)}, bf16[592,128]{1,0:T(8,128)(2,1)S(1)}, u32[]{:S(2)}, u32[]{:S(2)}) %collective-permute-start.11) | collective-permute-done | bytes 151584 | tf_op jit(solution)/shard_map/ppermute | solution.py:400
  64.7 0.8 %fusion.15 = (bf16[592,128]{1,0:T(8,128)(2,1)S(1)}, f32[592,128]{1,0:T(8,128)}) fusion(bf16[592,128]{1,0:T(8,128)(2,1)S(1)} %collective-permute-done.11, bf16[592,128]{1,0:T(8,128)(2,1)S(1)} %collective-permute-done.8, bf16[1,592,128]{2,1,0:T(8,128)(2,1)S(1)} %collective-permute-done.6, f32[2,592,128]{2,1,0:T(8,128)S(1)} %get-tuple-element.34), kind=kLoop, calls=%fused_computation.31 | loop fusion | flops 530432 | bytes 1212416 | tf_op jit(solution)/shard_map/convert.3
  65.5 0.5 collective-permute-start.14
  66.0 2.3 %collective-permute-start.13 = (bf16[128,128]{1,0:T(8,128)(2,1)S(1)}, bf16[128,128]{1,0:T(8,128)(2,1)S(1)}, u32[]{:S(2)}, u32[]{:S(2)}) collective-permute-start(bf16[128,128]{1,0:T(8,128)(2,1)S(1)} %get-tuple-element.42), channel_id=1, source_target_pairs={{0,2},{1,3},{2,4},{3,5},{4,6},{5,7},{6,0},{7,1},{8,10},{9,11},{10,... | collective-permute-start | bytes 98312 | tf_op jit(solution)/shard_map/ppermute | solution.py:453
  68.4 0.0 collective-permute-start.12
  68.4 0.4 collective-permute-start.15
  68.7 3.4 %collective-permute-done.15.e_ref = bf16[64,128]{1,0:T(8,128)(2,1)S(1)} collective-permute-done((bf16[64,128]{1,0:T(8,128)(2,1)S(1)}, bf16[64,128]{1,0:T(8,128)(2,1)S(1)}, u32[]{:S(2)}, u32[]{:S(2)}) %collective-permute-start.15) | collective-permute-done | bytes 16416 | tf_op jit(solution)/shard_map/ppermute | solution.py:453
  72.1 0.0 copy-start.3
  72.1 0.0 collective-permute-done.14.r3_ref
  72.1 0.0 collective-permute-done.13.r2_ref
  72.1 0.0 copy-start.1
  72.1 0.5 collective-permute-done.12.r1_ref
  72.6 0.1 copy-done.3
  72.7 0.0 copy-done
  72.7 0.0 copy-done.1
  72.8 0.5 copy-done.2
  73.2 1.9 %finish.1 = (f32[128,1024]{1,0:T(8,128)}, f32[1,128]{1,0:T(1,128)}) custom-call(f32[592,128]{1,0:T(8,128)} %get-tuple-element.33.own_ref, bf16[128,128]{1,0:T(8,128)(2,1)} %copy-done.2, bf16[128,128]{1,0:T(8,128)(2,1)} %copy-done.1, bf16[128,128]{1,0:T(8,128)(2,1)} %copy-done, bf16[64,128]{1,0:T(8,128)(2,1)} %copy-done.3), custom_call_target="tpu_custom_call" | custom-call | tf_op jit(solution)/shard_map/finish/pallas_call | solution.py:364
  (10 shorter events, 0.2 us)
Async XLA Ops:
  12.9 3.2 %collective-permute-start = (bf16[2,4,592,128]{3,2,1,0:T(8,128)(2,1)}, bf16[2,4,592,128]{3,2,1,0:T(8,128)(2,1)S(1)}, u32[]{:S(2)}, u32[]{:S(2)}) collective-permute-start(bf16[2,4,592,128]{3,2,1,0:T(8,128)(2,1)} %get-tuple-element.21), channel_id=1, source_target_pairs={{0,1},{1,0},{2,3},{3,2},{4,5},{5,4},{6,7},{7,6},{8,9},{9,8},{10,11... | collective-permute-start | bytes 3637256 | tf_op jit(solution)/shard_map/ppermute | solution.py:397
  17.8 11.7 %collective-permute-start.1 = (bf16[2,592,128]{2,1,0:T(8,128)(2,1)S(1)}, bf16[2,592,128]{2,1,0:T(8,128)(2,1)S(1)}, u32[]{:S(2)}, u32[]{:S(2)}) collective-permute-start(bf16[2,592,128]{2,1,0:T(8,128)(2,1)S(1)} %get-tuple-element.26), channel_id=1, source_target_pairs={{0,2},{1,5},{2,0},{3,7},{4,6},{5,1},{6,4},{7,3},{8,10},{9,13},{10,... | collective-permute-start | bytes 909320 | tf_op jit(solution)/shard_map/ppermute | solution.py:397
  19.3 10.2 %collective-permute-start.2 = (bf16[2,592,128]{2,1,0:T(8,128)(2,1)S(1)}, bf16[2,592,128]{2,1,0:T(8,128)(2,1)S(1)}, u32[]{:S(2)}, u32[]{:S(2)}) collective-permute-start(bf16[2,592,128]{2,1,0:T(8,128)(2,1)S(1)} %get-tuple-element.39), channel_id=1, source_target_pairs={{0,8},{8,0},{16,24},{24,16},{1,9},{9,1},{17,25},{25,17},{2,10},{10... | collective-permute-start | bytes 909320 | tf_op jit(solution)/shard_map/ppermute | solution.py:400
  29.5 3.7 %collective-permute-start.3 = (bf16[2,4,592,128]{3,2,1,0:T(8,128)(2,1)}, bf16[2,4,592,128]{3,2,1,0:T(8,128)(2,1)S(1)}, u32[]{:S(2)}, u32[]{:S(2)}) collective-permute-start(bf16[2,4,592,128]{3,2,1,0:T(8,128)(2,1)} %get-tuple-element.27), channel_id=1, source_target_pairs={{0,1},{1,0},{2,3},{3,2},{4,5},{5,4},{6,7},{7,6},{8,9},{9,8},{10,11... | collective-permute-start | bytes 3637256 | tf_op jit(solution)/shard_map/ppermute | solution.py:397
  29.6 11.2 %collective-permute-start.4 = (bf16[2,592,128]{2,1,0:T(8,128)(2,1)S(1)}, bf16[2,592,128]{2,1,0:T(8,128)(2,1)S(1)}, u32[]{:S(2)}, u32[]{:S(2)}) collective-permute-start(bf16[2,592,128]{2,1,0:T(8,128)(2,1)S(1)} %get-tuple-element.38), channel_id=1, source_target_pairs={{0,8},{8,0},{16,24},{24,16},{1,9},{9,1},{17,25},{25,17},{2,10},{10... | collective-permute-start | bytes 909320 | tf_op jit(solution)/shard_map/ppermute | solution.py:400
  34.9 8.5 %collective-permute-start.9 = (bf16[2,592,128]{2,1,0:T(8,128)(2,1)S(1)}, bf16[2,592,128]{2,1,0:T(8,128)(2,1)S(1)}, u32[]{:S(2)}, u32[]{:S(2)}) collective-permute-start(bf16[2,592,128]{2,1,0:T(8,128)(2,1)S(1)} %fusion.6), channel_id=1, source_target_pairs={{0,2},{1,5},{2,0},{3,7},{4,6},{5,1},{6,4},{7,3},{8,10},{9,13},{10,... | collective-permute-start | bytes 909320 | tf_op jit(solution)/shard_map/ppermute | solution.py:397
  36.2 10.5 %collective-permute-start.5 = (bf16[2,592,128]{2,1,0:T(8,128)(2,1)S(1)}, bf16[2,592,128]{2,1,0:T(8,128)(2,1)S(1)}, u32[]{:S(2)}, u32[]{:S(2)}) collective-permute-start(bf16[2,592,128]{2,1,0:T(8,128)(2,1)S(1)} %fusion.3), channel_id=1, source_target_pairs={{0,2},{1,5},{2,0},{3,7},{4,6},{5,1},{6,4},{7,3},{8,10},{9,13},{10,... | collective-permute-start | bytes 909320 | tf_op jit(solution)/shard_map/ppermute | solution.py:397
  37.1 11.3 %collective-permute-start.7 = (bf16[1,592,128]{2,1,0:T(8,128)(2,1)S(1)}, bf16[1,592,128]{2,1,0:T(8,128)(2,1)S(1)}, u32[]{:S(2)}, u32[]{:S(2)}) collective-permute-start(bf16[1,592,128]{2,1,0:T(8,128)(2,1)S(1)} %slice.163), channel_id=1, source_target_pairs={{0,4},{1,3},{2,6},{3,1},{4,0},{5,7},{6,2},{7,5},{8,12},{9,11},{10,... | collective-permute-start | bytes 454664 | tf_op jit(solution)/shard_map/ppermute | solution.py:397
  46.8 6.3 %collective-permute-start.10 = (bf16[1,592,128]{2,1,0:T(8,128)(2,1)S(1)}, bf16[1,592,128]{2,1,0:T(8,128)(2,1)S(1)}, u32[]{:S(2)}, u32[]{:S(2)}) collective-permute-start(bf16[1,592,128]{2,1,0:T(8,128)(2,1)S(1)} %slice.162), channel_id=1, source_target_pairs={{0,4},{1,3},{2,6},{3,1},{4,0},{5,7},{6,2},{7,5},{8,12},{9,11},{10,... | collective-permute-start | bytes 454664 | tf_op jit(solution)/shard_map/ppermute | solution.py:397
  48.4 12.4 %collective-permute-start.8 = (bf16[592,128]{1,0:T(8,128)(2,1)S(1)}, bf16[592,128]{1,0:T(8,128)(2,1)S(1)}, u32[]{:S(2)}, u32[]{:S(2)}) collective-permute-start(bf16[592,128]{1,0:T(8,128)(2,1)S(1)} %fusion.12), channel_id=1, source_target_pairs={{0,16},{8,24},{16,0},{24,8},{1,17},{9,25},{17,1},{25,9},{2,18},{10... | collective-permute-start | bytes 454664 | tf_op jit(solution)/shard_map/ppermute | solution.py:400
  53.1 7.8 %collective-permute-start.6 = (bf16[1,592,128]{2,1,0:T(8,128)(2,1)S(1)}, bf16[1,592,128]{2,1,0:T(8,128)(2,1)S(1)}, u32[]{:S(2)}, u32[]{:S(2)}) collective-permute-start(bf16[1,592,128]{2,1,0:T(8,128)(2,1)S(1)} %slice.164), channel_id=1, source_target_pairs={{0,4},{1,3},{2,6},{3,1},{4,0},{5,7},{6,2},{7,5},{8,12},{9,11},{10,... | collective-permute-start | bytes 454664 | tf_op jit(solution)/shard_map/ppermute | solution.py:397
  53.2 11.5 %collective-permute-start.11 = (bf16[592,128]{1,0:T(8,128)(2,1)S(1)}, bf16[592,128]{1,0:T(8,128)(2,1)S(1)}, u32[]{:S(2)}, u32[]{:S(2)}) collective-permute-start(bf16[592,128]{1,0:T(8,128)(2,1)S(1)} %fusion.13), channel_id=1, source_target_pairs={{0,24},{8,16},{16,8},{24,0},{1,25},{9,17},{17,9},{25,1},{2,26},{10... | collective-permute-start | bytes 454664 | tf_op jit(solution)/shard_map/ppermute | solution.py:400
  65.5 6.6 %collective-permute-start.14 = (bf16[128,128]{1,0:T(8,128)(2,1)S(1)}, bf16[128,128]{1,0:T(8,128)(2,1)S(1)}, u32[]{:S(2)}, u32[]{:S(2)}) collective-permute-start(bf16[128,128]{1,0:T(8,128)(2,1)S(1)} %get-tuple-element.41), channel_id=1, source_target_pairs={{0,3},{1,4},{2,5},{3,6},{4,7},{5,0},{6,1},{7,2},{8,11},{9,12},{10,... | collective-permute-start | bytes 98312 | tf_op jit(solution)/shard_map/ppermute | solution.py:453
  66.0 6.1 %collective-permute-start.13 = (bf16[128,128]{1,0:T(8,128)(2,1)S(1)}, bf16[128,128]{1,0:T(8,128)(2,1)S(1)}, u32[]{:S(2)}, u32[]{:S(2)}) collective-permute-start(bf16[128,128]{1,0:T(8,128)(2,1)S(1)} %get-tuple-element.42), channel_id=1, source_target_pairs={{0,2},{1,3},{2,4},{3,5},{4,6},{5,7},{6,0},{7,1},{8,10},{9,11},{10,... | collective-permute-start | bytes 98312 | tf_op jit(solution)/shard_map/ppermute | solution.py:453
  68.4 4.2 %collective-permute-start.12 = (bf16[128,128]{1,0:T(8,128)(2,1)S(1)}, bf16[128,128]{1,0:T(8,128)(2,1)S(1)}, u32[]{:S(2)}, u32[]{:S(2)}) collective-permute-start(bf16[128,128]{1,0:T(8,128)(2,1)S(1)} %get-tuple-element.43), channel_id=1, source_target_pairs={{0,1},{1,2},{2,3},{3,4},{4,5},{5,6},{6,7},{7,0},{8,9},{9,10},{10,1... | collective-permute-start | bytes 98312 | tf_op jit(solution)/shard_map/ppermute | solution.py:453
  68.4 3.7 %collective-permute-start.15 = (bf16[64,128]{1,0:T(8,128)(2,1)S(1)}, bf16[64,128]{1,0:T(8,128)(2,1)S(1)}, u32[]{:S(2)}, u32[]{:S(2)}) collective-permute-start(bf16[64,128]{1,0:T(8,128)(2,1)S(1)} %slice.119), channel_id=1, source_target_pairs={{0,4},{1,5},{2,6},{3,7},{4,0},{5,1},{6,2},{7,3},{8,12},{9,13},{10,... | collective-permute-start | bytes 49160 | tf_op jit(solution)/shard_map/ppermute | solution.py:453
  72.1 0.6 copy-start.3
  72.1 0.6 copy-start
  72.1 0.6 copy-start.1
  72.6 0.6 copy-start.2

commit v5 on v4

--- a/solution.py
+++ b/solution.py
@@ -128,31 +128,43 @@
     blocks = spread_s.shape[1] // width
     rows = 5 * GROUP
     head = width + 8
-    direct = []
+    unit = (iota((width, width), 0) == iota((width, width), 1)).astype(F32).astype(BF16)
+    lefts, values, positions = [], [], []
     for u in range(2):
         group = step * 2 + u
         for i in range(GROUP):
             g_s[u, i * hits : (i + 1) * hits, :] = g_ref[table_ref[0, group * GROUP + i]]
         g = g_s[u]
         chosen = (iota((128, width), 0) == group).astype(F32).astype(BF16)
-        position = jnp.dot(column_ref[...], chosen, preferred_element_type=F32).astype(BF16)
-        right = jnp.concatenate(
-            [jnp.where(position == jnp.bfloat16(p), g, jnp.bfloat16(0)) for p in range(blocks)],
-            axis=1,
-        )
-        weighted = g.astype(F32).T * lanes_ref[0, pl.ds(group, 1), :]
+        position = jnp.dot(column_ref[...], chosen, preferred_element_type=F32)
+        turned = lax.dot_general(unit, g, NT, preferred_element_type=F32)
+        weighted = turned * lanes_ref[0, pl.ds(group, 1), :]
         factor = jnp.where(iota((8, depth), 0) == 0, lanes_ref[1, pl.ds(group, 1), :], 0.0)
         scaled = scaled_ref[group]
         high = scaled.astype(BF16).astype(F32)
         left = jnp.concatenate(
             [weighted, factor, high, scaled - high, jnp.zeros((8, depth), F32)], axis=0
         )
-        total = jnp.dot(left.astype(BF16), right, preferred_element_type=F32)
-        direct.append(total[:head])
-        spread_s[pl.ds(pl.multiple_of(at + u * rows, GROUP), rows), :] = (
-            total[head : head + rows] + total[head + rows : head + 2 * rows]
-        )
-    direct_s[...] += direct[0] + direct[1]
+        lefts.append(left.astype(BF16))
+        values.append(g)
+        positions.append(position.astype(BF16))
+    for p in range(0, blocks, 2):
+        columns = slice(p * width, (p + 2) * width)
+        direct = direct_s[:, columns]
+        for u in range(2):
+            right = jnp.concatenate(
+                [
+                    jnp.where(positions[u] == jnp.bfloat16(q), values[u], jnp.bfloat16(0))
+                    for q in (p, p + 1)
+                ],
+                axis=1,
+            )
+            total = jnp.dot(lefts[u], right, preferred_element_type=F32)
+            direct = direct + total[:head]
+            spread_s[pl.ds(pl.multiple_of(at + u * rows, GROUP), rows), columns] = (
+                total[head : head + rows] + total[head + rows : head + 2 * rows]
+            )
+        direct_s[:, columns] = direct
 
 
 EVEN = (0, 4, 2, 6)
@@ -405,43 +417,45 @@
             pairs = [(t, t ^ bit) for t in range(tiles)]
             keep, send = (v + lax.ppermute(v, "tile", pairs) for v in (keep, send))
             bit *= 2
-        return keep.astype(F32) + swap(send, 1, 1).astype(F32)
+        return keep, swap(send, 1, 1)
+
+    def both(pair, n, part):
+        return pair[0][n, part].astype(F32) + pair[1][n, part].astype(F32)
 
     def halve(total, even, odd):
         half = total.shape[0] // 2
         return total[:half], swap(total[half:].astype(BF16), even, odd).astype(F32)
 
-    def plane(total):
-        total = sum(halve(total, 2, 4))
-        total = sum(halve(total, 4, 2))
-        return total[0]
-
+    low, top = slice(0, blocks // 4), slice(blocks // 4, blocks // 2)
     arrived = []
     for n in range(0, regions, 2):
         ks = (n + 1, (n + 2) % regions)
         keep, send, *made = assemble(ks, sub, inputs, global_deriv, blocks, regions)
         if n == 0:
             inputs = tuple(made)
+            pair = near(keep, send)
+            early, late = across(both(pair, 0, top), 1), across(both(pair, 0, low), 1)
         else:
-            send, *waited = lax.optimization_barrier((send, *waited))
+            send, pair, waited = lax.optimization_barrier((send, pair, waited))
             if n == 2:
                 early = waited[1]
-            total = kept + waited[0].astype(F32)
-            total = sum(halve(total, 4, 2))[0]
-            arrived.append(across(total, ks[0] - 1))
-        pair = near(keep, send)
-        if n == 0:
-            early, late = across(pair[0, 2:], 1), across(pair[0, :2], 1)
-        else:
-            arrived.append(across(plane(pair[0]), ks[0]))
-        if n + 2 < regions:
-            kept, third = pair[1, :2], pair[1, 2:].astype(BF16)
+            half, more = halve(both(pair, 1, low) + waited[0].astype(F32), 4, 2)
+            pair, more = lax.optimization_barrier((near(keep, send), more))
+            value = across((half + more)[0], ks[0] - 1)
+            more = swap(both(pair, 0, top).astype(BF16), 2, 4)
+            if not ks[1]:
+                upper = swap((both(pair, 1, top) + early.astype(F32)).astype(BF16), 2, 4)
+                more, late, value = lax.optimization_barrier((more, late, value))
+            half, more = halve(both(pair, 0, low) + more.astype(F32), 4, 2)
+            if not ks[1]:
+                more, upper, pair = lax.optimization_barrier((more, upper, pair))
+            arrived += [value, across((half + more)[0], ks[0])]
+        if ks[1]:
+            third = both(pair, 1, top).astype(BF16)
             third, rest = lax.optimization_barrier((third, inputs[3]))
             inputs = inputs[:3] + (rest,)
             waited = [swap(third, 2, 4)] + [early] * (n == 0)
-    last = pair[1]
-    upper = swap((last[2:] + early.astype(F32)).astype(BF16), 2, 4)
-    last = last[:2] + late.astype(F32) + upper.astype(F32)
+    last = both(pair, 1, low) + late.astype(F32) + upper.astype(F32)
     own = sum(halve(last, 4, 2))[0]
     for value in arrived:
         own = own + value.astype(F32)

time: 76.2 us -> 77.7 us (1.020)
  the two profiles are of different devices: /device:TPU:8 before, /device:TPU:0 now
where the time goes in v5:
time: 77.7 us; the launch traced here: 77.4 us
  waiting for transfers between devices  27.5 us (35%)
  starting transfers between devices  23.8 us (31%)
  Pallas kernels  20.8 us (27%)
  other arithmetic  3.83 us (5%)
  between operations  0.79 us (1%)
    pallas_call x2, Pallas kernels, assemble(): pl.pallas_call(functools.partial(lead_kernel if lead else follow_kernel,...  18.9 us
    ppermute x4, starting transfers between devices, across(): lax.ppermute(value.astype(BF16), 'region', [(r, r ^ k) for r in range(reg...  13.8 us
    ppermute x8, waiting for transfers between devices, swap(): return lax.ppermute(value, 'tile', pairs)  12.8 us
    ppermute x4, waiting for transfers between devices, across(): lax.ppermute(value.astype(BF16), 'region', [(r, r ^ k) for r in range(reg...  10.8 us
    ppermute x8, starting transfers between devices, swap(): return lax.ppermute(value, 'tile', pairs)  7.58 us
    ppermute x4, waiting for transfers between devices, onward(): return lax.ppermute(value.astype(BF16), 'tile', pairs)  3.97 us
    ppermute x4, starting transfers between devices, onward(): return lax.ppermute(value.astype(BF16), 'tile', pairs)  2.41 us
    pallas_call x1, Pallas kernels, finish(): pl.pallas_call(functools.partial(finish_kernel, sub), in_specs=[vmem] * 5...  1.95 us
  transfers between devices with their start and end apart: 16, of which 8 were waited for; matrix products, arithmetic and copies ran while one was open for 2% of the time, Pallas kernels for 9%

profile of v5, /device:TPU:0, one launch (start us, length us, event | category | flops | bytes accessed | tf_op | source)
XLA Modules:
  0.0 77.4 jit_solution(1798769566528760423)
XLA Ops:
  0.6 11.6 %assemble.2 = (bf16[2,4,592,128]{3,2,1,0:T(8,128)(2,1)}, bf16[2,4,592,128]{3,2,1,0:T(8,128)(2,1)}, f32[32,40,256]{2,1,0:T(8,128)}, f32[2,32,256]{2,1,0:T(8,128)}...) custom-call(s32[8]{0:T(128)} %refs_0_.1, s32[1,192]{1,0:T(1,128)} %bitcast.45, s32[1,192]{1,0:T(1,128)} %bitcast.46, ...), custom_call_target="tpu_custom_call" | custom-call | flops 8000000000 | bytes 4000000 | tf_op jit(solution)/shard_map/assemble/pallas_call | solution.py:318
  12.2 0.5 collective-permute-start
  12.7 2.7 %collective-permute-done = bf16[2,4,592,128]{3,2,1,0:T(8,128)(2,1)S(1)} collective-permute-done((bf16[2,4,592,128]{3,2,1,0:T(8,128)(2,1)}, bf16[2,4,592,128]{3,2,1,0:T(8,128)(2,1)S(1)}, u32[]{:S(2)}, u32[]{:S(2)}) %collective-permute-start) | collective-permute-done | bytes 1212448 | tf_op jit(solution)/shard_map/ppermute | solution.py:409
  15.5 1.4 %fusion.5 = (bf16[2,592,128]{2,1,0:T(8,128)(2,1)S(1)}, bf16[2,592,128]{2,1,0:T(8,128)(2,1)S(1)}, bf16[2,592,128]{2,1,0:T(8,128)(2,1)S(1)}) fusion(bf16[2,4,592,128]{3,2,1,0:T(8,128)(2,1)S(1)} %collective-permute-done, bf16[2,4,592,128]{3,2,1,0:T(8,128)(2,1)} %get-tuple-element.40), kind=kLoop, calls=%fused_computation.13 | loop fusion | flops 1818624 | bytes 2727936 | tf_op jit(solution)/shard_map/convert_element_type | solution.py:412
  16.8 2.9 %collective-permute-start.1 = (bf16[2,592,128]{2,1,0:T(8,128)(2,1)S(1)}, bf16[2,592,128]{2,1,0:T(8,128)(2,1)S(1)}, u32[]{:S(2)}, u32[]{:S(2)}) collective-permute-start(bf16[2,592,128]{2,1,0:T(8,128)(2,1)S(1)} %get-tuple-element.38), channel_id=1, source_target_pairs={{0,2},{1,5},{2,0},{3,7},{4,6},{5,1},{6,4},{7,3},{8,10},{9,13},{10,... | collective-permute-start | bytes 909320 | tf_op jit(solution)/shard_map/ppermute | solution.py:409
  19.8 0.0 collective-permute-start.2
  19.8 7.3 %assemble.3 = (bf16[2,4,592,128]{3,2,1,0:T(8,128)(2,1)}, bf16[2,4,592,128]{3,2,1,0:T(8,128)(2,1)}) custom-call(f32[32,40,256]{2,1,0:T(8,128)} %get-tuple-element.29.refs_0_, f32[2,32,256]{2,1,0:T(8,128)} %get-tuple-element.30.refs_1_, bf16[256,128]{1,0:T(8,128)(2,1)} %get-tuple-element.31.refs_2_, s32[16,256]{1,0:T(8,128)} %get-tuple-element.35.refs_3_, ...), custom_call_target="tpu_custom_call" | custom-call | flops 8000000000 | bytes 4000000 | tf_op jit(solution)/shard_map/assemble/pallas_call | solution.py:318
  27.1 0.0 copy-start
  27.1 0.0 collective-permute-done.1
  27.1 1.7 %collective-permute-done.2 = bf16[2,592,128]{2,1,0:T(8,128)(2,1)S(1)} collective-permute-done((bf16[2,592,128]{2,1,0:T(8,128)(2,1)S(1)}, bf16[2,592,128]{2,1,0:T(8,128)(2,1)S(1)}, u32[]{:S(2)}, u32[]{:S(2)}) %collective-permute-start.2) | collective-permute-done | bytes 303136 | tf_op jit(solution)/shard_map/ppermute | solution.py:412
  28.8 0.0 collective-permute-start.3
  28.8 1.1 %bitcast_add_fusion.3 = f32[2,592,128]{2,1,0:T(8,128)S(1)} fusion(bf16[2,592,128]{2,1,0:T(8,128)(2,1)S(1)} %collective-permute-done.1, bf16[2,4,592,128]{3,2,1,0:T(8,128)(2,1)S(1)} %collective-permute-done, bf16[2,4,592,128]{3,2,1,0:T(8,128)(2,1)} %get-tuple-element.40), kind=kLoop, calls=%fused_computation.5 | loop fusion | flops 757760 | bytes 1515520 | tf_op jit(solution)/shard_map/add | solution.py:442
  29.9 1.5 %collective-permute-start.4 = (bf16[1,592,128]{2,1,0:T(8,128)(2,1)S(1)}, bf16[1,592,128]{2,1,0:T(8,128)(2,1)S(1)}, u32[]{:S(2)}, u32[]{:S(2)}) collective-permute-start(bf16[1,592,128]{2,1,0:T(8,128)(2,1)S(1)} %slice.162), channel_id=1, source_target_pairs={{0,4},{1,3},{2,6},{3,1},{4,0},{5,7},{6,2},{7,5},{8,12},{9,11},{10,... | collective-permute-start | bytes 454664 | tf_op jit(solution)/shard_map/ppermute | solution.py:409
  31.3 7.0 %collective-permute-start.6 = (bf16[2,592,128]{2,1,0:T(8,128)(2,1)S(1)}, bf16[2,592,128]{2,1,0:T(8,128)(2,1)S(1)}, u32[]{:S(2)}, u32[]{:S(2)}) collective-permute-start(bf16[2,592,128]{2,1,0:T(8,128)(2,1)S(1)} %get-tuple-element.60), channel_id=1, source_target_pairs={{0,8},{8,0},{16,24},{24,16},{1,9},{9,1},{17,25},{25,17},{2,10},{10... | collective-permute-start | bytes 909320 | tf_op jit(solution)/shard_map/ppermute | solution.py:412
  38.3 0.0 collective-permute-done.4
  38.4 0.0 collective-permute-done.3
  38.4 0.0 copy-done
  38.4 0.1 fusion.4
  38.5 0.1 collective-permute-start.5
  38.6 5.8 %collective-permute-start.7 = (bf16[592,128]{1,0:T(8,128)(2,1)S(1)}, bf16[592,128]{1,0:T(8,128)(2,1)S(1)}, u32[]{:S(2)}, u32[]{:S(2)}) collective-permute-start(bf16[592,128]{1,0:T(8,128)(2,1)S(1)} %fusion.11), channel_id=1, source_target_pairs={{0,16},{8,24},{16,0},{24,8},{1,17},{9,25},{17,1},{25,9},{2,18},{10... | collective-permute-start | bytes 454664 | tf_op jit(solution)/shard_map/ppermute | solution.py:412
  44.5 0.0 collective-permute-done.6
  44.5 6.9 %collective-permute-done.7 = bf16[592,128]{1,0:T(8,128)(2,1)S(1)} collective-permute-done((bf16[592,128]{1,0:T(8,128)(2,1)S(1)}, bf16[592,128]{1,0:T(8,128)(2,1)S(1)}, u32[]{:S(2)}, u32[]{:S(2)}) %collective-permute-start.7) | collective-permute-done | bytes 151584 | tf_op jit(solution)/shard_map/ppermute | solution.py:412
  51.4 0.0 collective-permute-done.5
  51.4 0.2 fusion.1
  51.6 1.5 %collective-permute-start.9 = (bf16[2,592,128]{2,1,0:T(8,128)(2,1)S(1)}, bf16[2,592,128]{2,1,0:T(8,128)(2,1)S(1)}, u32[]{:S(2)}, u32[]{:S(2)}) collective-permute-start(bf16[2,592,128]{2,1,0:T(8,128)(2,1)S(1)} %get-tuple-element.58), channel_id=1, source_target_pairs={{0,2},{1,5},{2,0},{3,7},{4,6},{5,1},{6,4},{7,3},{8,10},{9,13},{10,... | collective-permute-start | bytes 909320 | tf_op jit(solution)/shard_map/ppermute | solution.py:409
  53.1 0.7 collective-permute-start.8
  53.8 4.7 %collective-permute-done.8 = bf16[1,592,128]{2,1,0:T(8,128)(2,1)S(1)} collective-permute-done((bf16[1,592,128]{2,1,0:T(8,128)(2,1)S(1)}, bf16[1,592,128]{2,1,0:T(8,128)(2,1)S(1)}, u32[]{:S(2)}, u32[]{:S(2)}) %collective-permute-start.8) | collective-permute-done | bytes 151584 | tf_op jit(solution)/shard_map/ppermute | solution.py:409
  58.5 1.5 %collective-permute-done.9 = bf16[2,592,128]{2,1,0:T(8,128)(2,1)S(1)} collective-permute-done((bf16[2,592,128]{2,1,0:T(8,128)(2,1)S(1)}, bf16[2,592,128]{2,1,0:T(8,128)(2,1)S(1)}, u32[]{:S(2)}, u32[]{:S(2)}) %collective-permute-start.9) | collective-permute-done | bytes 303136 | tf_op jit(solution)/shard_map/ppermute | solution.py:409
  60.0 0.1 fusion
  60.2 0.4 collective-permute-start.10
  60.6 1.1 %collective-permute-start.11 = (bf16[592,128]{1,0:T(8,128)(2,1)S(1)}, bf16[592,128]{1,0:T(8,128)(2,1)S(1)}, u32[]{:S(2)}, u32[]{:S(2)}) collective-permute-start(bf16[592,128]{1,0:T(8,128)(2,1)S(1)} %fusion.12), channel_id=1, source_target_pairs={{0,24},{8,16},{16,8},{24,0},{1,25},{9,17},{17,9},{25,1},{2,26},{10... | collective-permute-start | bytes 454664 | tf_op jit(solution)/shard_map/ppermute | solution.py:412
  61.6 3.8 %collective-permute-done.10 = bf16[1,592,128]{2,1,0:T(8,128)(2,1)S(1)} collective-permute-done((bf16[1,592,128]{2,1,0:T(8,128)(2,1)S(1)}, bf16[1,592,128]{2,1,0:T(8,128)(2,1)S(1)}, u32[]{:S(2)}, u32[]{:S(2)}) %collective-permute-start.10) | collective-permute-done | bytes 151584 | tf_op jit(solution)/shard_map/ppermute | solution.py:409
  65.5 2.2 %collective-permute-done.11 = bf16[592,128]{1,0:T(8,128)(2,1)S(1)} collective-permute-done((bf16[592,128]{1,0:T(8,128)(2,1)S(1)}, bf16[592,128]{1,0:T(8,128)(2,1)S(1)}, u32[]{:S(2)}, u32[]{:S(2)}) %collective-permute-start.11) | collective-permute-done | bytes 151584 | tf_op jit(solution)/shard_map/ppermute | solution.py:412
  67.7 0.8 %fusion.13 = (bf16[592,128]{1,0:T(8,128)(2,1)S(1)}, f32[592,128]{1,0:T(8,128)}) fusion(bf16[592,128]{1,0:T(8,128)(2,1)S(1)} %collective-permute-done.11, bf16[592,128]{1,0:T(8,128)(2,1)S(1)} %collective-permute-done.7, bf16[1,592,128]{2,1,0:T(8,128)(2,1)S(1)} %collective-permute-done.10, f32[2,592,128]{2,1,0:T(8,128)S(1)} %fusion), kind=kLoop, calls=%fused_computation.27 | loop fusion | flops 530432 | bytes 1212416 | tf_op jit(solution)/shard_map/convert.3
  68.5 0.1 collective-permute-start.14
  68.5 0.6 collective-permute-start.13
  69.1 1.3 %collective-permute-start.12 = (bf16[128,128]{1,0:T(8,128)(2,1)S(1)}, bf16[128,128]{1,0:T(8,128)(2,1)S(1)}, u32[]{:S(2)}, u32[]{:S(2)}) collective-permute-start(bf16[128,128]{1,0:T(8,128)(2,1)S(1)} %get-tuple-element.65), channel_id=1, source_target_pairs={{0,1},{1,2},{2,3},{3,4},{4,5},{5,6},{6,7},{7,0},{8,9},{9,10},{10,1... | collective-permute-start | bytes 98312 | tf_op jit(solution)/shard_map/ppermute | solution.py:467
  70.4 0.5 collective-permute-start.15
  70.9 4.0 %collective-permute-done.15.e_ref = bf16[64,128]{1,0:T(8,128)(2,1)S(1)} collective-permute-done((bf16[64,128]{1,0:T(8,128)(2,1)S(1)}, bf16[64,128]{1,0:T(8,128)(2,1)S(1)}, u32[]{:S(2)}, u32[]{:S(2)}) %collective-permute-start.15) | collective-permute-done | bytes 16416 | tf_op jit(solution)/shard_map/ppermute | solution.py:467
  74.9 0.0 collective-permute-done.14.r3_ref
  74.9 0.0 collective-permute-done.13.r2_ref
  74.9 0.0 copy-start.2
  74.9 0.0 collective-permute-done.12.r1_ref
  74.9 0.0 copy-start.3
  74.9 0.6 copy-done.4
  75.4 0.0 copy-done.1
  75.5 0.0 copy-done.2
  75.5 1.9 %finish.1 = (f32[128,1024]{1,0:T(8,128)}, f32[1,128]{1,0:T(1,128)}) custom-call(f32[592,128]{1,0:T(8,128)} %get-tuple-element.57.own_ref, bf16[128,128]{1,0:T(8,128)(2,1)} %copy-done.3, bf16[128,128]{1,0:T(8,128)(2,1)} %copy-done.2, bf16[128,128]{1,0:T(8,128)(2,1)} %copy-done.1, bf16[64,128]{1,0:T(8,128)(2,1)} %copy-done.4), custom_call_target="tpu_custom_call" | custom-call | tf_op jit(solution)/shard_map/finish/pallas_call | solution.py:376
  (12 shorter events, 0.2 us)
Async XLA Ops:
  12.2 3.2 %collective-permute-start = (bf16[2,4,592,128]{3,2,1,0:T(8,128)(2,1)}, bf16[2,4,592,128]{3,2,1,0:T(8,128)(2,1)S(1)}, u32[]{:S(2)}, u32[]{:S(2)}) collective-permute-start(bf16[2,4,592,128]{3,2,1,0:T(8,128)(2,1)} %get-tuple-element.33), channel_id=1, source_target_pairs={{0,1},{1,0},{2,3},{3,2},{4,5},{5,4},{6,7},{7,6},{8,9},{9,8},{10,11... | collective-permute-start | bytes 3637256 | tf_op jit(solution)/shard_map/ppermute | solution.py:409
  16.8 10.2 %collective-permute-start.1 = (bf16[2,592,128]{2,1,0:T(8,128)(2,1)S(1)}, bf16[2,592,128]{2,1,0:T(8,128)(2,1)S(1)}, u32[]{:S(2)}, u32[]{:S(2)}) collective-permute-start(bf16[2,592,128]{2,1,0:T(8,128)(2,1)S(1)} %get-tuple-element.38), channel_id=1, source_target_pairs={{0,2},{1,5},{2,0},{3,7},{4,6},{5,1},{6,4},{7,3},{8,10},{9,13},{10,... | collective-permute-start | bytes 909320 | tf_op jit(solution)/shard_map/ppermute | solution.py:409
  19.8 9.0 %collective-permute-start.2 = (bf16[2,592,128]{2,1,0:T(8,128)(2,1)S(1)}, bf16[2,592,128]{2,1,0:T(8,128)(2,1)S(1)}, u32[]{:S(2)}, u32[]{:S(2)}) collective-permute-start(bf16[2,592,128]{2,1,0:T(8,128)(2,1)S(1)} %get-tuple-element.61), channel_id=1, source_target_pairs={{0,8},{8,0},{16,24},{24,16},{1,9},{9,1},{17,25},{25,17},{2,10},{10... | collective-permute-start | bytes 909320 | tf_op jit(solution)/shard_map/ppermute | solution.py:412
  27.1 11.3 %copy-start = (bf16[2,4,592,128]{3,2,1,0:T(8,128)(2,1)S(1)}, bf16[2,4,592,128]{3,2,1,0:T(8,128)(2,1)}, u32[]{:S(2)}) copy-start(bf16[2,4,592,128]{3,2,1,0:T(8,128)(2,1)} %get-tuple-element.48) | copy-start | bytes 3637252
  28.8 9.6 %collective-permute-start.3 = (bf16[2,4,592,128]{3,2,1,0:T(8,128)(2,1)}, bf16[2,4,592,128]{3,2,1,0:T(8,128)(2,1)S(1)}, u32[]{:S(2)}, u32[]{:S(2)}) collective-permute-start(bf16[2,4,592,128]{3,2,1,0:T(8,128)(2,1)} %get-tuple-element.39), channel_id=1, source_target_pairs={{0,1},{1,0},{2,3},{3,2},{4,5},{5,4},{6,7},{7,6},{8,9},{9,8},{10,11... | collective-permute-start | bytes 3637256 | tf_op jit(solution)/shard_map/ppermute | solution.py:409
  29.9 8.5 %collective-permute-start.4 = (bf16[1,592,128]{2,1,0:T(8,128)(2,1)S(1)}, bf16[1,592,128]{2,1,0:T(8,128)(2,1)S(1)}, u32[]{:S(2)}, u32[]{:S(2)}) collective-permute-start(bf16[1,592,128]{2,1,0:T(8,128)(2,1)S(1)} %slice.162), channel_id=1, source_target_pairs={{0,4},{1,3},{2,6},{3,1},{4,0},{5,7},{6,2},{7,5},{8,12},{9,11},{10,... | collective-permute-start | bytes 454664 | tf_op jit(solution)/shard_map/ppermute | solution.py:409
  31.3 13.1 %collective-permute-start.6 = (bf16[2,592,128]{2,1,0:T(8,128)(2,1)S(1)}, bf16[2,592,128]{2,1,0:T(8,128)(2,1)S(1)}, u32[]{:S(2)}, u32[]{:S(2)}) collective-permute-start(bf16[2,592,128]{2,1,0:T(8,128)(2,1)S(1)} %get-tuple-element.60), channel_id=1, source_target_pairs={{0,8},{8,0},{16,24},{24,16},{1,9},{9,1},{17,25},{25,17},{2,10},{10... | collective-permute-start | bytes 909320 | tf_op jit(solution)/shard_map/ppermute | solution.py:412
  38.5 12.9 %collective-permute-start.5 = (bf16[2,592,128]{2,1,0:T(8,128)(2,1)S(1)}, bf16[2,592,128]{2,1,0:T(8,128)(2,1)S(1)}, u32[]{:S(2)}, u32[]{:S(2)}) collective-permute-start(bf16[2,592,128]{2,1,0:T(8,128)(2,1)S(1)} %fusion.4), channel_id=1, source_target_pairs={{0,2},{1,5},{2,0},{3,7},{4,6},{5,1},{6,4},{7,3},{8,10},{9,13},{10,... | collective-permute-start | bytes 909320 | tf_op jit(solution)/shard_map/ppermute | solution.py:409
  38.6 12.7 %collective-permute-start.7 = (bf16[592,128]{1,0:T(8,128)(2,1)S(1)}, bf16[592,128]{1,0:T(8,128)(2,1)S(1)}, u32[]{:S(2)}, u32[]{:S(2)}) collective-permute-start(bf16[592,128]{1,0:T(8,128)(2,1)S(1)} %fusion.11), channel_id=1, source_target_pairs={{0,16},{8,24},{16,0},{24,8},{1,17},{9,25},{17,1},{25,9},{2,18},{10... | collective-permute-start | bytes 454664 | tf_op jit(solution)/shard_map/ppermute | solution.py:412
  51.6 8.4 %collective-permute-start.9 = (bf16[2,592,128]{2,1,0:T(8,128)(2,1)S(1)}, bf16[2,592,128]{2,1,0:T(8,128)(2,1)S(1)}, u32[]{:S(2)}, u32[]{:S(2)}) collective-permute-start(bf16[2,592,128]{2,1,0:T(8,128)(2,1)S(1)} %get-tuple-element.58), channel_id=1, source_target_pairs={{0,2},{1,5},{2,0},{3,7},{4,6},{5,1},{6,4},{7,3},{8,10},{9,13},{10,... | collective-permute-start | bytes 909320 | tf_op jit(solution)/shard_map/ppermute | solution.py:409
  53.1 5.3 %collective-permute-start.8 = (bf16[1,592,128]{2,1,0:T(8,128)(2,1)S(1)}, bf16[1,592,128]{2,1,0:T(8,128)(2,1)S(1)}, u32[]{:S(2)}, u32[]{:S(2)}) collective-permute-start(bf16[1,592,128]{2,1,0:T(8,128)(2,1)S(1)} %slice.161), channel_id=1, source_target_pairs={{0,4},{1,3},{2,6},{3,1},{4,0},{5,7},{6,2},{7,5},{8,12},{9,11},{10,... | collective-permute-start | bytes 454664 | tf_op jit(solution)/shard_map/ppermute | solution.py:409
  60.2 5.3 %collective-permute-start.10 = (bf16[1,592,128]{2,1,0:T(8,128)(2,1)S(1)}, bf16[1,592,128]{2,1,0:T(8,128)(2,1)S(1)}, u32[]{:S(2)}, u32[]{:S(2)}) collective-permute-start(bf16[1,592,128]{2,1,0:T(8,128)(2,1)S(1)} %slice.160), channel_id=1, source_target_pairs={{0,4},{1,3},{2,6},{3,1},{4,0},{5,7},{6,2},{7,5},{8,12},{9,11},{10,... | collective-permute-start | bytes 454664 | tf_op jit(solution)/shard_map/ppermute | solution.py:409
  60.6 7.1 %collective-permute-start.11 = (bf16[592,128]{1,0:T(8,128)(2,1)S(1)}, bf16[592,128]{1,0:T(8,128)(2,1)S(1)}, u32[]{:S(2)}, u32[]{:S(2)}) collective-permute-start(bf16[592,128]{1,0:T(8,128)(2,1)S(1)} %fusion.12), channel_id=1, source_target_pairs={{0,24},{8,16},{16,8},{24,0},{1,25},{9,17},{17,9},{25,1},{2,26},{10... | collective-permute-start | bytes 454664 | tf_op jit(solution)/shard_map/ppermute | solution.py:412
  68.5 6.4 %collective-permute-start.14 = (bf16[128,128]{1,0:T(8,128)(2,1)S(1)}, bf16[128,128]{1,0:T(8,128)(2,1)S(1)}, u32[]{:S(2)}, u32[]{:S(2)}) collective-permute-start(bf16[128,128]{1,0:T(8,128)(2,1)S(1)} %get-tuple-element.63), channel_id=1, source_target_pairs={{0,3},{1,4},{2,5},{3,6},{4,7},{5,0},{6,1},{7,2},{8,11},{9,12},{10,... | collective-permute-start | bytes 98312 | tf_op jit(solution)/shard_map/ppermute | solution.py:467
  68.5 6.3 %collective-permute-start.13 = (bf16[128,128]{1,0:T(8,128)(2,1)S(1)}, bf16[128,128]{1,0:T(8,128)(2,1)S(1)}, u32[]{:S(2)}, u32[]{:S(2)}) collective-permute-start(bf16[128,128]{1,0:T(8,128)(2,1)S(1)} %get-tuple-element.64), channel_id=1, source_target_pairs={{0,2},{1,3},{2,4},{3,5},{4,6},{5,7},{6,0},{7,1},{8,10},{9,11},{10,... | collective-permute-start | bytes 98312 | tf_op jit(solution)/shard_map/ppermute | solution.py:467
  69.1 5.8 %collective-permute-start.12 = (bf16[128,128]{1,0:T(8,128)(2,1)S(1)}, bf16[128,128]{1,0:T(8,128)(2,1)S(1)}, u32[]{:S(2)}, u32[]{:S(2)}) collective-permute-start(bf16[128,128]{1,0:T(8,128)(2,1)S(1)} %get-tuple-element.65), channel_id=1, source_target_pairs={{0,1},{1,2},{2,3},{3,4},{4,5},{5,6},{6,7},{7,0},{8,9},{9,10},{10,1... | collective-permute-start | bytes 98312 | tf_op jit(solution)/shard_map/ppermute | solution.py:467
  70.4 4.5 %collective-permute-start.15 = (bf16[64,128]{1,0:T(8,128)(2,1)S(1)}, bf16[64,128]{1,0:T(8,128)(2,1)S(1)}, u32[]{:S(2)}, u32[]{:S(2)}) collective-permute-start(bf16[64,128]{1,0:T(8,128)(2,1)S(1)} %slice.123), channel_id=1, source_target_pairs={{0,4},{1,5},{2,6},{3,7},{4,0},{5,1},{6,2},{7,3},{8,12},{9,13},{10,... | collective-permute-start | bytes 49160 | tf_op jit(solution)/shard_map/ppermute | solution.py:467
  74.8 0.6 copy-start.4
  74.9 0.6 copy-start.1
  74.9 0.6 copy-start.2
  74.9 0.6 copy-start.3

commit v6 on v5

--- a/solution.py
+++ b/solution.py
@@ -244,32 +244,44 @@
 
     lax.fori_loop(used, chunks * depth_tiles, clear, 0)
 
+    unit = (iota((width, width), 0) == iota((width, width), 1)).astype(F32).astype(BF16)
+
     def chunk_step(chunk, carry):
         at = pl.multiple_of(chunk * DEPTH, DEPTH)
-        narrow = spread_s[pl.ds(at, DEPTH), :].astype(BF16)
-        wide_s[:, : blocks * width] = narrow
-        wide_s[:, blocks * width :] = narrow[:, : many * width]
-        turned_s[...] = -narrow.T
-
-        def product(p):
-            columns = (many + (1 if p < many else 0)) * width
-            return columns, jnp.dot(
-                turned_s[p * width : (p + 1) * width],
-                wide_s[:, p * width : p * width + columns],
-                preferred_element_type=F32,
+        wide_s[...] = spread_s[pl.ds(at, DEPTH), :].astype(BF16)
+        for p in range(blocks):
+            turned = lax.dot_general(
+                unit, wide_s[:, p * width : (p + 1) * width], NT, preferred_element_type=F32
             )
+            turned = (0.0 - turned).astype(BF16)
+            turned_s[p * width : (p + 1) * width] = turned
+            if p < many:
+                turned_s[(blocks + p) * width : (blocks + p + 1) * width] = turned
+
+        def products(add):
+            for q in range(0, blocks, 2):
+                upper = (q + blocks - many) % blocks
+                value = jnp.dot(
+                    turned_s[upper * width : (upper + many + 2) * width],
+                    wide_s[:, q * width : (q + 2) * width],
+                    preferred_element_type=F32,
+                )
+                for r in range(many + 2):
+                    p = (upper + r) % blocks
+                    for c in range(2):
+                        d = many - r + c
+                        if 0 <= d <= many and (d < many or p < many):
+                            part = value[r * width : (r + 1) * width, c * width : (c + 1) * width]
+                            columns = slice(d * width, (d + 1) * width)
+                            acc_s[p, :, columns] = acc_s[p, :, columns] + part if add else part
 
         @pl.when(chunk == 0)
         def _():
-            for p in range(blocks):
-                columns, value = product(p)
-                acc_s[p, :, :columns] = value
+            products(False)
 
         @pl.when(chunk > 0)
         def _():
-            for p in range(blocks):
-                columns, value = product(p)
-                acc_s[p, :, :columns] += value
+            products(True)
 
         return carry
 
@@ -287,7 +299,7 @@
             high = row.astype(BF16).astype(F32)
             sub = iota((16, width), 0)
             parts.append(jnp.where(sub == 0, high, jnp.where(sub == 1, row - high, 0.0)))
-            out_ref[0, n] = jnp.concatenate(parts, axis=0).astype(BF16)
+            out_ref[n, 0] = jnp.concatenate(parts, axis=0).astype(BF16)
 
 
 def assemble(ks, sub, inputs, g, blocks, regions):
@@ -303,8 +315,8 @@
         jax.ShapeDtypeStruct((GROUP * hits, 128), BF16),
         jax.ShapeDtypeStruct((8 + rr, slots), jnp.int32),
     ]
-    out = jax.ShapeDtypeStruct((2, blocks // 2, rows, width), BF16)
-    spec = pl.BlockSpec((1, blocks // 2, rows, width), lambda k: (k, 0, 0, 0))
+    out = jax.ShapeDtypeStruct((blocks // 2, 2, rows, width), BF16)
+    spec = pl.BlockSpec((blocks // 2, 1, rows, width), lambda k: (0, k, 0, 0))
     vmem = pl.BlockSpec(memory_space=pltpu.VMEM)
     table = pltpu.SMEM(shared[3].shape, jnp.int32)
     arrived = pltpu.VMEM(g.shape, g.dtype)
@@ -327,12 +339,12 @@
             pltpu.VMEM((2, GROUP * hits, width), BF16),
             pltpu.VMEM((width + 8, blocks * width), F32),
             pltpu.VMEM((longest, blocks * width), F32),
-            pltpu.VMEM((DEPTH, (blocks + blocks // 2) * width), BF16),
-            pltpu.VMEM((blocks * width, DEPTH), BF16),
+            pltpu.VMEM((DEPTH, blocks * width), BF16),
+            pltpu.VMEM(((blocks + blocks // 2) * width, DEPTH), BF16),
             pltpu.VMEM((blocks, width, (blocks // 2 + 1) * width), F32),
         ],
         compiler_params=pltpu.CompilerParams(
-            dimension_semantics=("arbitrary",), vmem_limit_bytes=60 * 1024 * 1024
+            dimension_semantics=("arbitrary",), vmem_limit_bytes=(60 if lead else 32) * 1024 * 1024
         ),
         cost_estimate=pl.CostEstimate(
             flops=8 * 10**9, bytes_accessed=4 * 10**6, transcendentals=0
@@ -419,46 +431,37 @@
             bit *= 2
         return keep, swap(send, 1, 1)
 
-    def both(pair, n, part):
-        return pair[0][n, part].astype(F32) + pair[1][n, part].astype(F32)
-
-    def halve(total, even, odd):
-        half = total.shape[0] // 2
-        return total[:half], swap(total[half:].astype(BF16), even, odd).astype(F32)
+    def both(pair, part):
+        return pair[0][part].astype(F32) + pair[1][part].astype(F32)
 
     low, top = slice(0, blocks // 4), slice(blocks // 4, blocks // 2)
-    arrived = []
-    for n in range(0, regions, 2):
-        ks = (n + 1, (n + 2) % regions)
+    totals, more, second = [None] * regions, None, None
+    for first in range(regions - 2, -1, -2):
+        ks = (first, first + 1)
         keep, send, *made = assemble(ks, sub, inputs, global_deriv, blocks, regions)
-        if n == 0:
+        if made:
             inputs = tuple(made)
-            pair = near(keep, send)
-            early, late = across(both(pair, 0, top), 1), across(both(pair, 0, low), 1)
         else:
-            send, pair, waited = lax.optimization_barrier((send, pair, waited))
-            if n == 2:
-                early = waited[1]
-            half, more = halve(both(pair, 1, low) + waited[0].astype(F32), 4, 2)
-            pair, more = lax.optimization_barrier((near(keep, send), more))
-            value = across((half + more)[0], ks[0] - 1)
-            more = swap(both(pair, 0, top).astype(BF16), 2, 4)
-            if not ks[1]:
-                upper = swap((both(pair, 1, top) + early.astype(F32)).astype(BF16), 2, 4)
-                more, late, value = lax.optimization_barrier((more, late, value))
-            half, more = halve(both(pair, 0, low) + more.astype(F32), 4, 2)
-            if not ks[1]:
-                more, upper, pair = lax.optimization_barrier((more, upper, pair))
-            arrived += [value, across((half + more)[0], ks[0])]
-        if ks[1]:
-            third = both(pair, 1, top).astype(BF16)
-            third, rest = lax.optimization_barrier((third, inputs[3]))
+            send, pair, more = lax.optimization_barrier((send, pair, more))
+            value = both(pair, low) + more.astype(F32)
+            second = value[0], swap(value[1].astype(BF16), 4, 2)
+        pair = near(keep, send)
+        if second is not None:
+            pair, arrived = lax.optimization_barrier((pair, second[1]))
+            value = second[0] + arrived.astype(F32)
+            totals[first + 2], totals[first + 3] = value[0], value[1]
+        more = both(pair, top).astype(BF16)
+        if first:
+            more, rest = lax.optimization_barrier((more, inputs[3]))
             inputs = inputs[:3] + (rest,)
-            waited = [swap(third, 2, 4)] + [early] * (n == 0)
-    last = both(pair, 1, low) + late.astype(F32) + upper.astype(F32)
-    own = sum(halve(last, 4, 2))[0]
-    for value in arrived:
-        own = own + value.astype(F32)
+        more = swap(more, 2, 4)
+    value = both(pair, low) + more.astype(F32)
+    value = value[0] + swap(value[1].astype(BF16), 4, 2).astype(F32)
+    totals[0], totals[1] = value[0], value[1]
+    for k in range(regions - 1, 0, -1):
+        step = k & -k
+        totals[k - step] = totals[k - step] + across(totals[k], step).astype(F32)
+    own = totals[0]
 
     def onward(value, d):
         pairs = [

time: 77.7 us -> 70.5 us (0.907)
  starting transfers between devices: 23.8 us -> 15 us
  local copies, waits for them, and re-layouts: 0.67 us -> 2.07 us
  waiting for transfers between devices: 27.5 us -> 28.8 us
  other arithmetic: 3.83 us -> 2.72 us
    ppermute x4 -> x3, starting transfers between devices: 13.8 us -> 4.16 us  [across(): lax.ppermute(value.astype(BF16), 'region', [(r, r ^ k) for r in range(reg...]
    ppermute x8 -> x6, waiting for transfers between devices: 12.8 us -> 20.8 us  [swap(): return lax.ppermute(value, 'tile', pairs)]
    ppermute x4 -> x3, waiting for transfers between devices: 10.8 us -> 4.37 us  [across(): lax.ppermute(value.astype(BF16), 'region', [(r, r ^ k) for r in range(reg...]
    convert_element_type x3 -> x1, other arithmetic: 1.46 us -> 0.04 us  [across(): value.astype(BF16)]
    unnamed x10 -> x20, local copies, waits for them, and re-layouts: 0.61 us -> 1.94 us
    convert_element_type x4 -> x2, other arithmetic: 0.36 us -> 1.39 us  [local(): more = both(pair, top).astype(BF16)]
    ppermute x4, starting transfers between devices: 2.41 us -> 3.25 us  [onward(): return lax.ppermute(value.astype(BF16), 'tile', pairs)]
    ppermute x8 -> x6, starting transfers between devices: 7.58 us -> 7.63 us  [swap(): return lax.ppermute(value, 'tile', pairs)]
  transfers between devices with their start and end apart: 16 -> 13, of which waited for: 8 -> 8; matrix products, arithmetic and copies ran while one was open for 2% -> 1% of each run, Pallas kernels for 9% -> 9%
where the time goes in v6:
time: 70.5 us; the launch traced here: 69.6 us
  waiting for transfers between devices  28.8 us (41%)
  Pallas kernels  20.2 us (29%)
  starting transfers between devices  15 us (21%)
  other arithmetic  2.72 us (4%)
  local copies, waits for them, and re-layouts  2.07 us (3%)
  between operations  0.81 us (1%)
    ppermute x6, waiting for transfers between devices, swap(): return lax.ppermute(value, 'tile', pairs)  20.8 us
    pallas_call x2, Pallas kernels, assemble(): pl.pallas_call(functools.partial(lead_kernel if lead else follow_kernel,...  18.2 us
    ppermute x6, starting transfers between devices, swap(): return lax.ppermute(value, 'tile', pairs)  7.63 us
    ppermute x3, waiting for transfers between devices, across(): lax.ppermute(value.astype(BF16), 'region', [(r, r ^ k) for r in range(reg...  4.37 us
    ppermute x3, starting transfers between devices, across(): lax.ppermute(value.astype(BF16), 'region', [(r, r ^ k) for r in range(reg...  4.16 us
    ppermute x4, waiting for transfers between devices, onward(): return lax.ppermute(value.astype(BF16), 'tile', pairs)  3.64 us
    ppermute x4, starting transfers between devices, onward(): return lax.ppermute(value.astype(BF16), 'tile', pairs)  3.25 us
    pallas_call x1, Pallas kernels, finish(): pl.pallas_call(functools.partial(finish_kernel, sub), in_specs=[vmem] * 5...  1.95 us
  transfers between devices with their start and end apart: 13, of which 8 were waited for; matrix products, arithmetic and copies ran while one was open for 1% of the time, Pallas kernels for 9%

profile of v6, /device:TPU:0, one launch (start us, length us, event | category | flops | bytes accessed | tf_op | source)
XLA Modules:
  0.0 69.6 jit_solution(16351624020907928982)
XLA Ops:
  0.6 12.2 %assemble.2 = (bf16[4,2,592,128]{3,2,1,0:T(8,128)(2,1)}, bf16[4,2,592,128]{3,2,1,0:T(8,128)(2,1)}, f32[32,40,256]{2,1,0:T(8,128)}, f32[2,32,256]{2,1,0:T(8,128)}...) custom-call(s32[8]{0:T(128)} %refs_0_.1, s32[1,192]{1,0:T(1,128)} %bitcast.43, s32[1,192]{1,0:T(1,128)} %bitcast.44, ...), custom_call_target="tpu_custom_call" | custom-call | flops 8000000000 | bytes 4000000 | tf_op jit(solution)/shard_map/assemble/pallas_call | solution.py:330
  12.8 0.0 copy-start
  12.8 0.0 copy-start.2
  12.8 0.0 copy-start.3
  12.8 0.0 copy-start.4
  12.9 0.1 collective-permute-start
  12.9 3.1 %collective-permute-done = bf16[4,2,592,128]{3,2,1,0:T(8,128)(2,1)S(1)} collective-permute-done((bf16[4,2,592,128]{3,2,1,0:T(8,128)(2,1)}, bf16[4,2,592,128]{3,2,1,0:T(8,128)(2,1)S(1)}, u32[]{:S(2)}, u32[]{:S(2)}) %collective-permute-start) | collective-permute-done | bytes 1212448 | tf_op jit(solution)/shard_map/ppermute | solution.py:421
  16.0 1.2 %add_convert_fusion.1 = bf16[2,2,592,128]{3,2,1,0:T(8,128)(2,1)S(1)} fusion(bf16[4,2,592,128]{3,2,1,0:T(8,128)(2,1)S(1)} %collective-permute-done, bf16[4,2,592,128]{3,2,1,0:T(8,128)(2,1)} %get-tuple-element.32), kind=kLoop, calls=%fused_computation.3 | loop fusion | flops 1212416 | bytes 1818624 | tf_op jit(solution)/shard_map/convert_element_type | solution.py:453
  17.3 2.5 %collective-permute-start.1 = (bf16[2,2,592,128]{3,2,1,0:T(8,128)(2,1)S(1)}, bf16[2,2,592,128]{3,2,1,0:T(8,128)(2,1)S(1)}, u32[]{:S(2)}, u32[]{:S(2)}) collective-permute-start(bf16[2,2,592,128]{3,2,1,0:T(8,128)(2,1)S(1)} %add_convert_fusion.1), channel_id=1, source_target_pairs={{0,2},{1,5},{2,0},{3,7},{4,6},{5,1},{6,4},{7,3},{8,10},{9,13},{10,... | collective-permute-start | bytes 1818632 | tf_op jit(solution)/shard_map/ppermute | solution.py:421
  19.7 0.0 copy-done
  19.7 0.0 copy-done.2
  19.7 0.0 copy-done.3
  19.7 0.0 copy-done.4
  19.7 1.3 %copy-done.1 = f32[32,40,256]{2,1,0:T(8,128)S(1)} copy-done((f32[32,40,256]{2,1,0:T(8,128)S(1)}, f32[32,40,256]{2,1,0:T(8,128)}, u32[]{:S(2)}) %copy-start.1) | copy-done | bytes 1310744
  21.1 6.0 %assemble.3 = (bf16[4,2,592,128]{3,2,1,0:T(8,128)(2,1)S(1)}, bf16[4,2,592,128]{3,2,1,0:T(8,128)(2,1)S(1)}) custom-call(f32[32,40,256]{2,1,0:T(8,128)S(1)} %copy-done.1, f32[2,32,256]{2,1,0:T(8,128)S(1)} %copy-done.2, bf16[256,128]{1,0:T(8,128)(2,1)S(1)} %copy-done.3, s32[16,256]{1,0:T(8,128)S(1)} %copy-done.4, bf16[192,32,128]{2,1,0:T(8,128)(2,1)S(1)} %copy-done), custom_call_target="tpu_custom_call" | custom-call | flops 8000000000 | bytes 4000000 | tf_op jit(solution)/shard_map/assemble/pallas_call | solution.py:330
  27.1 0.7 collective-permute-done.1
  27.8 1.6 %collective-permute-start.2 = (bf16[4,2,592,128]{3,2,1,0:T(8,128)(2,1)S(1)}, bf16[4,2,592,128]{3,2,1,0:T(8,128)(2,1)S(1)}, u32[]{:S(2)}, u32[]{:S(2)}) collective-permute-start(bf16[4,2,592,128]{3,2,1,0:T(8,128)(2,1)S(1)} %get-tuple-element.31), channel_id=1, source_target_pairs={{0,1},{1,0},{2,3},{3,2},{4,5},{5,4},{6,7},{7,6},{8,9},{9,8},{10,11... | collective-permute-start | bytes 3637256 | tf_op jit(solution)/shard_map/ppermute | solution.py:421
  29.4 0.2 convert_add_fusion.1
  29.7 1.5 %collective-permute-start.3 = (bf16[2,592,128]{2,1,0:T(8,128)(2,1)S(1)}, bf16[2,592,128]{2,1,0:T(8,128)(2,1)S(1)}, u32[]{:S(2)}, u32[]{:S(2)}) collective-permute-start(bf16[2,592,128]{2,1,0:T(8,128)(2,1)S(1)} %fusion.2), channel_id=1, source_target_pairs={{0,4},{1,3},{2,6},{3,1},{4,0},{5,7},{6,2},{7,5},{8,12},{9,11},{10,... | collective-permute-start | bytes 909320 | tf_op jit(solution)/shard_map/ppermute | solution.py:421
  31.2 5.4 %collective-permute-done.3 = bf16[2,592,128]{2,1,0:T(8,128)(2,1)S(1)} collective-permute-done((bf16[2,592,128]{2,1,0:T(8,128)(2,1)S(1)}, bf16[2,592,128]{2,1,0:T(8,128)(2,1)S(1)}, u32[]{:S(2)}, u32[]{:S(2)}) %collective-permute-start.3) | collective-permute-done | bytes 303136 | tf_op jit(solution)/shard_map/ppermute | solution.py:421
  36.5 0.0 collective-permute-done.2
  36.5 0.2 add_convert_fusion
  36.7 0.4 collective-permute-start.4
  37.1 0.1 fusion
  37.2 1.7 %collective-permute-start.6 = (bf16[592,128]{1,0:T(8,128)(2,1)S(1)}, bf16[592,128]{1,0:T(8,128)(2,1)S(1)}, u32[]{:S(2)}, u32[]{:S(2)}) collective-permute-start(bf16[592,128]{1,0:T(8,128)(2,1)S(1)} %fusion.8), channel_id=1, source_target_pairs={{0,8},{8,0},{16,24},{24,16},{1,9},{9,1},{17,25},{25,17},{2,10},{10... | collective-permute-start | bytes 454664 | tf_op jit(solution)/shard_map/ppermute | solution.py:424
  38.9 7.9 %collective-permute-done.4 = bf16[2,2,592,128]{3,2,1,0:T(8,128)(2,1)S(1)} collective-permute-done((bf16[2,2,592,128]{3,2,1,0:T(8,128)(2,1)S(1)}, bf16[2,2,592,128]{3,2,1,0:T(8,128)(2,1)S(1)}, u32[]{:S(2)}, u32[]{:S(2)}) %collective-permute-start.4) | collective-permute-done | bytes 606240 | tf_op jit(solution)/shard_map/ppermute | solution.py:421
  46.8 0.2 convert_add_fusion
  47.1 1.5 %collective-permute-start.5 = (bf16[2,592,128]{2,1,0:T(8,128)(2,1)S(1)}, bf16[2,592,128]{2,1,0:T(8,128)(2,1)S(1)}, u32[]{:S(2)}, u32[]{:S(2)}) collective-permute-start(bf16[2,592,128]{2,1,0:T(8,128)(2,1)S(1)} %fusion.3), channel_id=1, source_target_pairs={{0,4},{1,3},{2,6},{3,1},{4,0},{5,7},{6,2},{7,5},{8,12},{9,11},{10,... | collective-permute-start | bytes 909320 | tf_op jit(solution)/shard_map/ppermute | solution.py:421
  48.6 0.0 collective-permute-done.6
  48.6 1.6 %collective-permute-start.7 = (bf16[592,128]{1,0:T(8,128)(2,1)S(1)}, bf16[592,128]{1,0:T(8,128)(2,1)S(1)}, u32[]{:S(2)}, u32[]{:S(2)}) collective-permute-start(bf16[592,128]{1,0:T(8,128)(2,1)S(1)} %fusion.5), channel_id=1, source_target_pairs={{0,16},{8,24},{16,0},{24,8},{1,17},{9,25},{17,1},{25,9},{2,18},{10... | collective-permute-start | bytes 454664 | tf_op jit(solution)/shard_map/ppermute | solution.py:424
  50.2 3.7 %collective-permute-done.5 = bf16[2,592,128]{2,1,0:T(8,128)(2,1)S(1)} collective-permute-done((bf16[2,592,128]{2,1,0:T(8,128)(2,1)S(1)}, bf16[2,592,128]{2,1,0:T(8,128)(2,1)S(1)}, u32[]{:S(2)}, u32[]{:S(2)}) %collective-permute-start.5) | collective-permute-done | bytes 303136 | tf_op jit(solution)/shard_map/ppermute | solution.py:421
  54.0 0.1 fusion.1
  54.1 0.9 %collective-permute-start.8 = (bf16[592,128]{1,0:T(8,128)(2,1)S(1)}, bf16[592,128]{1,0:T(8,128)(2,1)S(1)}, u32[]{:S(2)}, u32[]{:S(2)}) collective-permute-start(bf16[592,128]{1,0:T(8,128)(2,1)S(1)} %fusion.9), channel_id=1, source_target_pairs={{0,8},{8,0},{16,24},{24,16},{1,9},{9,1},{17,25},{25,17},{2,10},{10... | collective-permute-start | bytes 454664 | tf_op jit(solution)/shard_map/ppermute | solution.py:424
  54.9 1.8 %collective-permute-done.7 = bf16[592,128]{1,0:T(8,128)(2,1)S(1)} collective-permute-done((bf16[592,128]{1,0:T(8,128)(2,1)S(1)}, bf16[592,128]{1,0:T(8,128)(2,1)S(1)}, u32[]{:S(2)}, u32[]{:S(2)}) %collective-permute-start.7) | collective-permute-done | bytes 151584 | tf_op jit(solution)/shard_map/ppermute | solution.py:424
  56.8 2.5 %collective-permute-done.8 = bf16[592,128]{1,0:T(8,128)(2,1)S(1)} collective-permute-done((bf16[592,128]{1,0:T(8,128)(2,1)S(1)}, bf16[592,128]{1,0:T(8,128)(2,1)S(1)}, u32[]{:S(2)}, u32[]{:S(2)}) %collective-permute-start.8) | collective-permute-done | bytes 151584 | tf_op jit(solution)/shard_map/ppermute | solution.py:424
  59.3 0.8 %fusion.10 = (bf16[592,128]{1,0:T(8,128)(2,1)S(1)}, f32[592,128]{1,0:T(8,128)}) fusion(bf16[592,128]{1,0:T(8,128)(2,1)S(1)} %collective-permute-done.8, bf16[592,128]{1,0:T(8,128)(2,1)S(1)} %collective-permute-done.7, f32[2,592,128]{2,1,0:T(8,128)S(1)} %fusion.1), kind=kLoop, calls=%fused_computation.22 | loop fusion | flops 378880 | bytes 1060864 | tf_op jit(solution)/shard_map/convert.3
  60.1 0.1 collective-permute-start.11
  60.2 1.2 %collective-permute-start.10 = (bf16[128,128]{1,0:T(8,128)(2,1)S(1)}, bf16[128,128]{1,0:T(8,128)(2,1)S(1)}, u32[]{:S(2)}, u32[]{:S(2)}) collective-permute-start(bf16[128,128]{1,0:T(8,128)(2,1)S(1)} %get-tuple-element.43), channel_id=1, source_target_pairs={{0,2},{1,3},{2,4},{3,5},{4,6},{5,7},{6,0},{7,1},{8,10},{9,11},{10,... | collective-permute-start | bytes 98312 | tf_op jit(solution)/shard_map/ppermute | solution.py:470
  61.4 1.7 %collective-permute-start.9 = (bf16[128,128]{1,0:T(8,128)(2,1)S(1)}, bf16[128,128]{1,0:T(8,128)(2,1)S(1)}, u32[]{:S(2)}, u32[]{:S(2)}) collective-permute-start(bf16[128,128]{1,0:T(8,128)(2,1)S(1)} %get-tuple-element.44), channel_id=1, source_target_pairs={{0,1},{1,2},{2,3},{3,4},{4,5},{5,6},{6,7},{7,0},{8,9},{9,10},{10,1... | collective-permute-start | bytes 98312 | tf_op jit(solution)/shard_map/ppermute | solution.py:470
  63.1 0.2 collective-permute-start.12
  63.4 3.6 %collective-permute-done.12.e_ref = bf16[64,128]{1,0:T(8,128)(2,1)S(1)} collective-permute-done((bf16[64,128]{1,0:T(8,128)(2,1)S(1)}, bf16[64,128]{1,0:T(8,128)(2,1)S(1)}, u32[]{:S(2)}, u32[]{:S(2)}) %collective-permute-start.12) | collective-permute-done | bytes 16416 | tf_op jit(solution)/shard_map/ppermute | solution.py:470
  67.0 0.0 collective-permute-done.11.r3_ref
  67.0 0.0 collective-permute-done.10.r2_ref
  67.0 0.0 collective-permute-done.9.r1_ref
  67.0 0.6 copy-done.9
  67.6 0.0 copy-done.6
  67.6 0.0 copy-done.7
  67.6 1.9 %finish.1 = (f32[128,1024]{1,0:T(8,128)}, f32[1,128]{1,0:T(1,128)}) custom-call(f32[592,128]{1,0:T(8,128)} %get-tuple-element.41.own_ref, bf16[128,128]{1,0:T(8,128)(2,1)} %copy-done.8, bf16[128,128]{1,0:T(8,128)(2,1)} %copy-done.7, bf16[128,128]{1,0:T(8,128)(2,1)} %copy-done.6, bf16[64,128]{1,0:T(8,128)(2,1)} %copy-done.9), custom_call_target="tpu_custom_call" | custom-call | tf_op jit(solution)/shard_map/finish/pallas_call | solution.py:388
  (15 shorter events, 0.2 us)
Async XLA Ops:
  12.8 6.9 %copy-start = (bf16[192,32,128]{2,1,0:T(8,128)(2,1)S(1)}, bf16[192,32,128]{2,1,0:T(8,128)(2,1)}, u32[]{:S(2)}) copy-start(bf16[192,32,128]{2,1,0:T(8,128)(2,1)} %refs_4_.1) | copy-start | bytes 4718596
  12.8 6.9 %copy-start.2 = (f32[2,32,256]{2,1,0:T(8,128)S(1)}, f32[2,32,256]{2,1,0:T(8,128)}, u32[]{:S(2)}) copy-start(f32[2,32,256]{2,1,0:T(8,128)} %get-tuple-element.22.refs_1_) | copy-start | bytes 196612
  12.8 6.9 %copy-start.3 = (bf16[256,128]{1,0:T(8,128)(2,1)S(1)}, bf16[256,128]{1,0:T(8,128)(2,1)}, u32[]{:S(2)}) copy-start(bf16[256,128]{1,0:T(8,128)(2,1)} %get-tuple-element.23.refs_2_) | copy-start | bytes 196612
  12.8 6.9 %copy-start.4 = (s32[16,256]{1,0:T(8,128)S(1)}, s32[16,256]{1,0:T(8,128)}, u32[]{:S(2)}) copy-start(s32[16,256]{1,0:T(8,128)} %get-tuple-element.27.refs_3_) | copy-start | bytes 49156
  12.9 3.2 %collective-permute-start = (bf16[4,2,592,128]{3,2,1,0:T(8,128)(2,1)}, bf16[4,2,592,128]{3,2,1,0:T(8,128)(2,1)S(1)}, u32[]{:S(2)}, u32[]{:S(2)}) collective-permute-start(bf16[4,2,592,128]{3,2,1,0:T(8,128)(2,1)} %get-tuple-element.25), channel_id=1, source_target_pairs={{0,1},{1,0},{2,3},{3,2},{4,5},{5,4},{6,7},{7,6},{8,9},{9,8},{10,11... | collective-permute-start | bytes 3637256 | tf_op jit(solution)/shard_map/ppermute | solution.py:421
  17.3 10.5 %collective-permute-start.1 = (bf16[2,2,592,128]{3,2,1,0:T(8,128)(2,1)S(1)}, bf16[2,2,592,128]{3,2,1,0:T(8,128)(2,1)S(1)}, u32[]{:S(2)}, u32[]{:S(2)}) collective-permute-start(bf16[2,2,592,128]{3,2,1,0:T(8,128)(2,1)S(1)} %add_convert_fusion.1), channel_id=1, source_target_pairs={{0,2},{1,5},{2,0},{3,7},{4,6},{5,1},{6,4},{7,3},{8,10},{9,13},{10,... | collective-permute-start | bytes 1818632 | tf_op jit(solution)/shard_map/ppermute | solution.py:421
  19.7 1.3 %copy-start.1 = (f32[32,40,256]{2,1,0:T(8,128)S(1)}, f32[32,40,256]{2,1,0:T(8,128)}, u32[]{:S(2)}) copy-start(f32[32,40,256]{2,1,0:T(8,128)} %get-tuple-element.21.refs_0_) | copy-start | bytes 3932164
  21.1 8.4 %copy-start.5 = (bf16[4,2,592,128]{3,2,1,0:T(8,128)(2,1)S(1)}, bf16[4,2,592,128]{3,2,1,0:T(8,128)(2,1)}, u32[]{:S(2)}) copy-start(bf16[4,2,592,128]{3,2,1,0:T(8,128)(2,1)} %get-tuple-element.32) | copy-start | bytes 3637252
  27.8 8.8 %collective-permute-start.2 = (bf16[4,2,592,128]{3,2,1,0:T(8,128)(2,1)S(1)}, bf16[4,2,592,128]{3,2,1,0:T(8,128)(2,1)S(1)}, u32[]{:S(2)}, u32[]{:S(2)}) collective-permute-start(bf16[4,2,592,128]{3,2,1,0:T(8,128)(2,1)S(1)} %get-tuple-element.31), channel_id=1, source_target_pairs={{0,1},{1,0},{2,3},{3,2},{4,5},{5,4},{6,7},{7,6},{8,9},{9,8},{10,11... | collective-permute-start | bytes 3637256 | tf_op jit(solution)/shard_map/ppermute | solution.py:421
  29.7 6.9 %collective-permute-start.3 = (bf16[2,592,128]{2,1,0:T(8,128)(2,1)S(1)}, bf16[2,592,128]{2,1,0:T(8,128)(2,1)S(1)}, u32[]{:S(2)}, u32[]{:S(2)}) collective-permute-start(bf16[2,592,128]{2,1,0:T(8,128)(2,1)S(1)} %fusion.2), channel_id=1, source_target_pairs={{0,4},{1,3},{2,6},{3,1},{4,0},{5,7},{6,2},{7,5},{8,12},{9,11},{10,... | collective-permute-start | bytes 909320 | tf_op jit(solution)/shard_map/ppermute | solution.py:421
  36.7 10.1 %collective-permute-start.4 = (bf16[2,2,592,128]{3,2,1,0:T(8,128)(2,1)S(1)}, bf16[2,2,592,128]{3,2,1,0:T(8,128)(2,1)S(1)}, u32[]{:S(2)}, u32[]{:S(2)}) collective-permute-start(bf16[2,2,592,128]{3,2,1,0:T(8,128)(2,1)S(1)} %add_convert_fusion), channel_id=1, source_target_pairs={{0,2},{1,5},{2,0},{3,7},{4,6},{5,1},{6,4},{7,3},{8,10},{9,13},{10,... | collective-permute-start | bytes 1818632 | tf_op jit(solution)/shard_map/ppermute | solution.py:421
  37.2 11.4 %collective-permute-start.6 = (bf16[592,128]{1,0:T(8,128)(2,1)S(1)}, bf16[592,128]{1,0:T(8,128)(2,1)S(1)}, u32[]{:S(2)}, u32[]{:S(2)}) collective-permute-start(bf16[592,128]{1,0:T(8,128)(2,1)S(1)} %fusion.8), channel_id=1, source_target_pairs={{0,8},{8,0},{16,24},{24,16},{1,9},{9,1},{17,25},{25,17},{2,10},{10... | collective-permute-start | bytes 454664 | tf_op jit(solution)/shard_map/ppermute | solution.py:424
  47.1 6.9 %collective-permute-start.5 = (bf16[2,592,128]{2,1,0:T(8,128)(2,1)S(1)}, bf16[2,592,128]{2,1,0:T(8,128)(2,1)S(1)}, u32[]{:S(2)}, u32[]{:S(2)}) collective-permute-start(bf16[2,592,128]{2,1,0:T(8,128)(2,1)S(1)} %fusion.3), channel_id=1, source_target_pairs={{0,4},{1,3},{2,6},{3,1},{4,0},{5,7},{6,2},{7,5},{8,12},{9,11},{10,... | collective-permute-start | bytes 909320 | tf_op jit(solution)/shard_map/ppermute | solution.py:421
  48.6 8.2 %collective-permute-start.7 = (bf16[592,128]{1,0:T(8,128)(2,1)S(1)}, bf16[592,128]{1,0:T(8,128)(2,1)S(1)}, u32[]{:S(2)}, u32[]{:S(2)}) collective-permute-start(bf16[592,128]{1,0:T(8,128)(2,1)S(1)} %fusion.5), channel_id=1, source_target_pairs={{0,16},{8,24},{16,0},{24,8},{1,17},{9,25},{17,1},{25,9},{2,18},{10... | collective-permute-start | bytes 454664 | tf_op jit(solution)/shard_map/ppermute | solution.py:424
  54.1 5.3 %collective-permute-start.8 = (bf16[592,128]{1,0:T(8,128)(2,1)S(1)}, bf16[592,128]{1,0:T(8,128)(2,1)S(1)}, u32[]{:S(2)}, u32[]{:S(2)}) collective-permute-start(bf16[592,128]{1,0:T(8,128)(2,1)S(1)} %fusion.9), channel_id=1, source_target_pairs={{0,8},{8,0},{16,24},{24,16},{1,9},{9,1},{17,25},{25,17},{2,10},{10... | collective-permute-start | bytes 454664 | tf_op jit(solution)/shard_map/ppermute | solution.py:424
  60.1 6.9 %collective-permute-start.11 = (bf16[128,128]{1,0:T(8,128)(2,1)S(1)}, bf16[128,128]{1,0:T(8,128)(2,1)S(1)}, u32[]{:S(2)}, u32[]{:S(2)}) collective-permute-start(bf16[128,128]{1,0:T(8,128)(2,1)S(1)} %get-tuple-element.42), channel_id=1, source_target_pairs={{0,3},{1,4},{2,5},{3,6},{4,7},{5,0},{6,1},{7,2},{8,11},{9,12},{10,... | collective-permute-start | bytes 98312 | tf_op jit(solution)/shard_map/ppermute | solution.py:470
  60.2 6.8 %collective-permute-start.10 = (bf16[128,128]{1,0:T(8,128)(2,1)S(1)}, bf16[128,128]{1,0:T(8,128)(2,1)S(1)}, u32[]{:S(2)}, u32[]{:S(2)}) collective-permute-start(bf16[128,128]{1,0:T(8,128)(2,1)S(1)} %get-tuple-element.43), channel_id=1, source_target_pairs={{0,2},{1,3},{2,4},{3,5},{4,6},{5,7},{6,0},{7,1},{8,10},{9,11},{10,... | collective-permute-start | bytes 98312 | tf_op jit(solution)/shard_map/ppermute | solution.py:470
  61.4 5.6 %collective-permute-start.9 = (bf16[128,128]{1,0:T(8,128)(2,1)S(1)}, bf16[128,128]{1,0:T(8,128)(2,1)S(1)}, u32[]{:S(2)}, u32[]{:S(2)}) collective-permute-start(bf16[128,128]{1,0:T(8,128)(2,1)S(1)} %get-tuple-element.44), channel_id=1, source_target_pairs={{0,1},{1,2},{2,3},{3,4},{4,5},{5,6},{6,7},{7,0},{8,9},{9,10},{10,1... | collective-permute-start | bytes 98312 | tf_op jit(solution)/shard_map/ppermute | solution.py:470
  63.1 3.9 %collective-permute-start.12 = (bf16[64,128]{1,0:T(8,128)(2,1)S(1)}, bf16[64,128]{1,0:T(8,128)(2,1)S(1)}, u32[]{:S(2)}, u32[]{:S(2)}) collective-permute-start(bf16[64,128]{1,0:T(8,128)(2,1)S(1)} %slice.100), channel_id=1, source_target_pairs={{0,4},{1,5},{2,6},{3,7},{4,0},{5,1},{6,2},{7,3},{8,12},{9,13},{10,... | collective-permute-start | bytes 49160 | tf_op jit(solution)/shard_map/ppermute | solution.py:470
  67.0 0.6 copy-start.9
  67.0 0.6 copy-start.6
  67.0 0.6 copy-start.7
  67.0 0.6 copy-start.8

commit v7 on v6

--- a/solution.py
+++ b/solution.py
@@ -10,7 +10,6 @@
 BF16 = jnp.bfloat16
 GROUP = 8
 PAIR = 2 * GROUP
-DEPTH = 256
 
 NT = (((1,), (1,)), ((), ()))
 
@@ -60,7 +59,7 @@
 
 def prepare(
     place_ref, region_ref, count_ref, ld_ref, weight_ref, resid_ref, ids_ref,
-    scaled_ref, lanes_ref, column_ref, table_ref,
+    scaled_ref, lanes_ref, table_ref,
 ):
     tracks = region_ref.shape[1]
     groups, _, depth = scaled_ref.shape
@@ -107,64 +106,61 @@
         return jnp.where(own, jnp.concatenate([value] * GROUP, axis=0), 0.0)
 
     grouping = (iota((groups, slots), 1) // GROUP == iota((groups, slots), 0)).astype(F32)
-    for n, value in enumerate((masked_w, hit_factor)):
+    for n, value in enumerate((masked_w, hit_factor, position)):
         lanes_ref[n] = lax.dot_general(
             grouping.astype(BF16), spread_out(value).astype(BF16), NT, preferred_element_type=F32
         )
-    columns = column_ref.shape[1]
-    grouping = (iota((columns, slots), 1) // GROUP == iota((columns, slots), 0)).astype(F32)
-    column_ref[...] = lax.dot_general(
-        spread_out(position).astype(BF16), grouping.astype(BF16), NT, preferred_element_type=F32
-    ).astype(BF16)
     for c in range(5):
         scaled_ref[:, c * GROUP : (c + 1) * GROUP, :] = spread_out(solved[c]).T.reshape(
             groups, GROUP, depth
         )
 
 
-def one_step(step, at, table_ref, g_ref, scaled_ref, lanes_ref, column_ref, g_s, direct_s, spread_s):
+def one_step(step, n, table_ref, g_ref, scaled_ref, lanes_ref, g_s, direct_s, vector_s, spread_s):
     hits, width = g_ref.shape[1:]
     depth = GROUP * hits
-    blocks = spread_s.shape[1] // width
+    blocks = direct_s.shape[0] // width
     rows = 5 * GROUP
-    head = width + 8
-    unit = (iota((width, width), 0) == iota((width, width), 1)).astype(F32).astype(BF16)
-    lefts, values, positions = [], [], []
+    sub = iota((16, depth), 0).astype(F32)
+    totals, vector = [], vector_s[...]
     for u in range(2):
         group = step * 2 + u
         for i in range(GROUP):
             g_s[u, i * hits : (i + 1) * hits, :] = g_ref[table_ref[0, group * GROUP + i]]
         g = g_s[u]
-        chosen = (iota((128, width), 0) == group).astype(F32).astype(BF16)
-        position = jnp.dot(column_ref[...], chosen, preferred_element_type=F32)
-        turned = lax.dot_general(unit, g, NT, preferred_element_type=F32)
-        weighted = turned * lanes_ref[0, pl.ds(group, 1), :]
-        factor = jnp.where(iota((8, depth), 0) == 0, lanes_ref[1, pl.ds(group, 1), :], 0.0)
+        turned = g.T
+        position = jnp.broadcast_to(lanes_ref[2, pl.ds(group, 1), :], (16, depth))
+        masks = [jnp.where(position == float(p), 1.0, 0.0).astype(BF16) for p in range(blocks)]
+        streamed = jnp.concatenate(
+            [turned * jnp.concatenate([mask] * (width // 16), axis=0) for mask in masks], axis=0
+        )
+        weighted = turned.astype(F32) * lanes_ref[0, pl.ds(group, 1), :]
         scaled = scaled_ref[group]
         high = scaled.astype(BF16).astype(F32)
-        left = jnp.concatenate(
-            [weighted, factor, high, scaled - high, jnp.zeros((8, depth), F32)], axis=0
-        )
-        lefts.append(left.astype(BF16))
-        values.append(g)
-        positions.append(position.astype(BF16))
-    for p in range(0, blocks, 2):
-        columns = slice(p * width, (p + 2) * width)
-        direct = direct_s[:, columns]
-        for u in range(2):
-            right = jnp.concatenate(
-                [
-                    jnp.where(positions[u] == jnp.bfloat16(q), values[u], jnp.bfloat16(0))
-                    for q in (p, p + 1)
-                ],
-                axis=1,
-            )
-            total = jnp.dot(lefts[u], right, preferred_element_type=F32)
-            direct = direct + total[:head]
-            spread_s[pl.ds(pl.multiple_of(at + u * rows, GROUP), rows), columns] = (
-                total[head : head + rows] + total[head + rows : head + 2 * rows]
-            )
-        direct_s[:, columns] = direct
+        low = scaled - high
+        if u == 0:
+            parts = [high, jnp.zeros((rows, depth), F32), low, jnp.zeros((8, depth), F32)]
+        else:
+            parts = [low[8:], jnp.zeros((8, depth), F32), high, jnp.zeros((rows, depth), F32), low[:8]]
+        held = jnp.concatenate([weighted] + parts, axis=0).astype(BF16)
+        totals.append(lax.dot_general(streamed, held, NT, preferred_element_type=F32))
+        factor = jnp.where(sub == position, lanes_ref[1, pl.ds(group, 1), :], 0.0).astype(BF16)
+        vector = vector + jnp.dot(factor, g, preferred_element_type=F32)
+    vector_s[...] = vector
+    lane = iota((width, width), 1)
+    at = pl.ds(pl.multiple_of((n % 2) * width, width), width)
+    many = blocks // 2
+    for p in range(blocks):
+        part = slice(p * width, (p + 1) * width)
+        direct_s[part] = direct_s[part] + (totals[0][part, :width] + totals[1][part, :width])
+        first, second = totals[0][part, width:], totals[1][part, width:]
+        near = jnp.where(lane < rows, first, second)
+        far = jnp.where((lane >= 2 * rows) & (lane < 3 * rows), first, second)
+        far = pltpu.roll(far, width - 2 * rows, 1)
+        value = jnp.where(lane < 2 * rows, near + far, 0.0).astype(BF16)
+        spread_s[n // 2, part, at] = value
+        if p < many:
+            spread_s[n // 2, (blocks + p) * width : (blocks + p + 1) * width, at] = value
 
 
 EVEN = (0, 4, 2, 6)
@@ -182,8 +178,8 @@
 
 
 def lead_kernel(ks, sub, *refs):
-    small, g_hbm, (keep_ref, send_ref), shared = refs[:7], refs[7], refs[8:10], refs[10:14]
-    local_small, g_ref, table_s, sems, scratch = refs[14:21], refs[21], refs[22], refs[23], refs[24:]
+    small, g_hbm, (keep_ref, send_ref), shared = refs[:7], refs[7], refs[8:10], refs[10:13]
+    local_small, g_ref, table_s, sems, scratch = refs[13:20], refs[20], refs[21], refs[22], refs[23:]
 
     @pl.when(pl.program_id(0) == 0)
     def _():
@@ -191,17 +187,17 @@
         for copy in copies[:-1]:
             copy.wait()
         prepare(*local_small, *shared)
-        copy = pltpu.make_async_copy(shared[3], table_s, sems.at[0])
+        copy = pltpu.make_async_copy(shared[2], table_s, sems.at[0])
         copy.start()
         copy.wait()
         copies[-1].wait()
 
-    assemble_region(ks, sub, table_s, *shared[:3], g_ref, keep_ref, send_ref, *scratch)
+    assemble_region(ks, sub, table_s, *shared[:2], g_ref, keep_ref, send_ref, *scratch)
 
 
 def follow_kernel(ks, sub, *refs):
     shared, (keep_ref, send_ref), mine, sems, scratch = (
-        refs[:5], refs[5:7], refs[7:12], refs[12], refs[13:]
+        refs[:4], refs[4:6], refs[6:10], refs[10], refs[11:]
     )
 
     @pl.when(pl.program_id(0) == 0)
@@ -209,61 +205,49 @@
         for copy in fetch(list(zip(shared, mine)), sems):
             copy.wait()
 
-    assemble_region(ks, sub, mine[3], *mine[:3], mine[4], keep_ref, send_ref, *scratch)
+    assemble_region(ks, sub, mine[2], *mine[:2], mine[3], keep_ref, send_ref, *scratch)
 
 
 def assemble_region(
-    ks, sub, table_ref, scaled_ref, lanes_ref, column_ref, g_ref,
-    keep_ref, send_ref, g_s, direct_s, spread_s, wide_s, turned_s, acc_s,
+    ks, sub, table_ref, scaled_ref, lanes_ref, g_ref,
+    keep_ref, send_ref, g_s, direct_s, vector_s, spread_s, acc_s,
 ):
     k = jnp.where(pl.program_id(0) == 0, ks[0], ks[1])
     width = g_ref.shape[2]
-    blocks = spread_s.shape[1] // width
+    blocks = direct_s.shape[0] // width
     many = blocks // 2
     region = lax.axis_index("region") ^ k
     block = lax.axis_index("tile") // sub
     first = table_ref[8 + region, 0] // PAIR
     steps = table_ref[8 + region, 1] // PAIR - first
+    chunks = jnp.maximum((steps + 1) // 2, 1)
     direct_s[...] = jnp.zeros_like(direct_s)
+    vector_s[...] = jnp.zeros_like(vector_s)
+
+    @pl.when(steps % 2 == 1)
+    def _():
+        spread_s[chunks - 1, :, width:] = jnp.zeros((spread_s.shape[1], width), BF16)
+
+    @pl.when(steps == 0)
+    def _():
+        spread_s[0] = jnp.zeros(spread_s.shape[1:], BF16)
 
     def group_step(n, carry):
         one_step(
-            first + n, n * (10 * GROUP), table_ref, g_ref, scaled_ref, lanes_ref, column_ref,
-            g_s, direct_s, spread_s,
+            first + n, n, table_ref, g_ref, scaled_ref, lanes_ref, g_s, direct_s, vector_s, spread_s
         )
         return carry
 
     lax.fori_loop(0, steps, group_step, 0)
-    used = steps * 10
-    depth_tiles = DEPTH // 8
-    chunks = jnp.maximum((used + depth_tiles - 1) // depth_tiles, 1)
-
-    def clear(tile, carry):
-        spread_s[pl.ds(pl.multiple_of(tile * 8, 8), 8), :] = jnp.zeros((8, blocks * width), F32)
-        return carry
-
-    lax.fori_loop(used, chunks * depth_tiles, clear, 0)
-
-    unit = (iota((width, width), 0) == iota((width, width), 1)).astype(F32).astype(BF16)
 
     def chunk_step(chunk, carry):
-        at = pl.multiple_of(chunk * DEPTH, DEPTH)
-        wide_s[...] = spread_s[pl.ds(at, DEPTH), :].astype(BF16)
-        for p in range(blocks):
-            turned = lax.dot_general(
-                unit, wide_s[:, p * width : (p + 1) * width], NT, preferred_element_type=F32
-            )
-            turned = (0.0 - turned).astype(BF16)
-            turned_s[p * width : (p + 1) * width] = turned
-            if p < many:
-                turned_s[(blocks + p) * width : (blocks + p + 1) * width] = turned
-
         def products(add):
             for q in range(0, blocks, 2):
                 upper = (q + blocks - many) % blocks
-                value = jnp.dot(
-                    turned_s[upper * width : (upper + many + 2) * width],
-                    wide_s[:, q * width : (q + 2) * width],
+                value = lax.dot_general(
+                    spread_s[chunk, upper * width : (upper + many + 2) * width, :],
+                    spread_s[chunk, q * width : (q + 2) * width, :],
+                    NT,
                     preferred_element_type=F32,
                 )
                 for r in range(many + 2):
@@ -273,7 +257,7 @@
                         if 0 <= d <= many and (d < many or p < many):
                             part = value[r * width : (r + 1) * width, c * width : (c + 1) * width]
                             columns = slice(d * width, (d + 1) * width)
-                            acc_s[p, :, columns] = acc_s[p, :, columns] + part if add else part
+                            acc_s[p, :, columns] = acc_s[p, :, columns] - part if add else 0.0 - part
 
         @pl.when(chunk == 0)
         def _():
@@ -290,12 +274,12 @@
     for n in range(blocks // 2):
         for odd, out_ref in ((0, keep_ref), (1, send_ref)):
             p = block ^ (jnp.where(block % 2 == 1 - odd, ODD[n], EVEN[n]) + odd)
-            columns = pl.ds(pl.multiple_of(p * width, width), width)
-            parts = [direct_s[0:width, columns] + acc_s[p, :, 0:width]]
+            at = pl.ds(pl.multiple_of(p * width, width), width)
+            parts = [direct_s[at, :] + acc_s[p, :, 0:width]]
             parts += [acc_s[p, :, d * width : (d + 1) * width] for d in range(1, many)]
             upper = pl.multiple_of((p // many) * half, half)
             parts.append(acc_s[p % many, pl.ds(upper, half), many * width :])
-            row = direct_s[width : width + 1, columns]
+            row = vector_s[pl.ds(p, 1), :]
             high = row.astype(BF16).astype(F32)
             sub = iota((16, width), 0)
             parts.append(jnp.where(sub == 0, high, jnp.where(sub == 1, row - high, 0.0)))
@@ -306,41 +290,39 @@
     tracks, hits, width = g.shape
     lead = len(inputs) == 7
     rows = width * (blocks // 2) + width // 2 + 16
-    longest = -(-(-(-tracks // PAIR) * 5 * PAIR) // DEPTH) * DEPTH
+    longest = -(-tracks // (2 * PAIR))
     rr = -(-regions // 8) * 8
     slots = -(-(tracks + regions * (PAIR - 1)) // 128) * 128
     shared = [
         jax.ShapeDtypeStruct((slots // GROUP, 5 * GROUP, GROUP * hits), F32),
-        jax.ShapeDtypeStruct((2, slots // GROUP, GROUP * hits), F32),
-        jax.ShapeDtypeStruct((GROUP * hits, 128), BF16),
+        jax.ShapeDtypeStruct((3, slots // GROUP, GROUP * hits), F32),
         jax.ShapeDtypeStruct((8 + rr, slots), jnp.int32),
     ]
     out = jax.ShapeDtypeStruct((blocks // 2, 2, rows, width), BF16)
     spec = pl.BlockSpec((blocks // 2, 1, rows, width), lambda k: (0, k, 0, 0))
     vmem = pl.BlockSpec(memory_space=pltpu.VMEM)
-    table = pltpu.SMEM(shared[3].shape, jnp.int32)
+    table = pltpu.SMEM(shared[2].shape, jnp.int32)
     arrived = pltpu.VMEM(g.shape, g.dtype)
     if lead:
         copies = [pltpu.SMEM(inputs[0].shape, jnp.int32)]
         copies += [pltpu.VMEM(value.shape, value.dtype) for value in inputs[1:]]
         copies += [arrived, table]
     else:
-        copies = [pltpu.VMEM(value.shape, value.dtype) for value in inputs[:3]]
+        copies = [pltpu.VMEM(value.shape, value.dtype) for value in inputs[:2]]
         copies += [table, arrived]
     return pl.pallas_call(
         functools.partial(lead_kernel if lead else follow_kernel, ks, sub),
         grid=(2,),
         in_specs=[pl.BlockSpec(memory_space=pltpu.HBM)] * (len(inputs) + 1),
-        out_specs=[spec, spec] + [vmem] * (4 * lead),
+        out_specs=[spec, spec] + [vmem] * (3 * lead),
         out_shape=[out, out] + shared * lead,
         scratch_shapes=copies
         + [
             pltpu.SemaphoreType.DMA((8,)),
             pltpu.VMEM((2, GROUP * hits, width), BF16),
-            pltpu.VMEM((width + 8, blocks * width), F32),
-            pltpu.VMEM((longest, blocks * width), F32),
-            pltpu.VMEM((DEPTH, blocks * width), BF16),
-            pltpu.VMEM(((blocks + blocks // 2) * width, DEPTH), BF16),
+            pltpu.VMEM((blocks * width, width), F32),
+            pltpu.VMEM((16, width), F32),
+            pltpu.VMEM((longest, (blocks + blocks // 2) * width, 2 * width), BF16),
             pltpu.VMEM((blocks, width, (blocks // 2 + 1) * width), F32),
         ],
         compiler_params=pltpu.CompilerParams(
@@ -363,7 +345,8 @@
         column = pl.multiple_of(((column + blocks) % blocks) * width, width)
         out_ref[:, pl.ds(column, width)] = value
 
-    for d in range(many):
+    put(p, own_ref[0:width, :].T)
+    for d in range(1, many):
         put(p + d, own_ref[d * width : (d + 1) * width, :])
     for d, ref in ((1, r1_ref), (2, r2_ref), (3, r3_ref)):
         put(p - d, ref[...].astype(F32).T)
@@ -452,8 +435,8 @@
             totals[first + 2], totals[first + 3] = value[0], value[1]
         more = both(pair, top).astype(BF16)
         if first:
-            more, rest = lax.optimization_barrier((more, inputs[3]))
-            inputs = inputs[:3] + (rest,)
+            more, rest = lax.optimization_barrier((more, inputs[2]))
+            inputs = inputs[:2] + (rest,)
         more = swap(more, 2, 4)
     value = both(pair, low) + more.astype(F32)
     value = value[0] + swap(value[1].astype(BF16), 4, 2).astype(F32)

time: 70.5 us -> 71.1 us (level)
  starting transfers between devices: 15 us -> 17.4 us
  waiting for transfers between devices: 28.8 us -> 26.9 us
    ppermute x6, starting transfers between devices: 7.63 us -> 9.71 us  [swap(): return lax.ppermute(value, 'tile', pairs)]
    ppermute x3, waiting for transfers between devices: 4.37 us -> 3.33 us  [across(): lax.ppermute(value.astype(BF16), 'region', [(r, r ^ k) for r in range(reg...]
    unnamed x20 -> x18, local copies, waits for them, and re-layouts: 1.94 us -> 1.93 us
  transfers between devices with their start and end apart: 13 -> 13, of which waited for: 8 -> 8; matrix products, arithmetic and copies ran while one was open for 1% -> 1% of each run, Pallas kernels for 9% -> 8%
where the time goes in v7:
time: 71.1 us; the launch traced here: 70.6 us
  waiting for transfers between devices  26.9 us (38%)
  Pallas kernels  20.7 us (29%)
  starting transfers between devices  17.4 us (24%)
  other arithmetic  2.73 us (4%)
  local copies, waits for them, and re-layouts  2.06 us (3%)
  between operations  0.78 us (1%)
    ppermute x6, waiting for transfers between devices, swap(): return lax.ppermute(value, 'tile', pairs)  20.1 us
    pallas_call x2, Pallas kernels, assemble(): pl.pallas_call(functools.partial(lead_kernel if lead else follow_kernel,...  18.7 us
    ppermute x6, starting transfers between devices, swap(): return lax.ppermute(value, 'tile', pairs)  9.71 us
    ppermute x3, starting transfers between devices, across(): lax.ppermute(value.astype(BF16), 'region', [(r, r ^ k) for r in range(reg...  4.06 us
    ppermute x4, starting transfers between devices, onward(): return lax.ppermute(value.astype(BF16), 'tile', pairs)  3.64 us
    ppermute x4, waiting for transfers between devices, onward(): return lax.ppermute(value.astype(BF16), 'tile', pairs)  3.51 us
    ppermute x3, waiting for transfers between devices, across(): lax.ppermute(value.astype(BF16), 'region', [(r, r ^ k) for r in range(reg...  3.33 us
    pallas_call x1, Pallas kernels, finish(): pl.pallas_call(functools.partial(finish_kernel, sub), in_specs=[vmem] * 5...  1.97 us
  transfers between devices with their start and end apart: 13, of which 8 were waited for; matrix products, arithmetic and copies ran while one was open for 1% of the time, Pallas kernels for 8%

profile of v7, /device:TPU:0, one launch (start us, length us, event | category | flops | bytes accessed | tf_op | source)
XLA Modules:
  0.0 70.6 jit_solution(6357046024582768141)
XLA Ops:
  0.6 13.2 %assemble.2 = (bf16[4,2,592,128]{3,2,1,0:T(8,128)(2,1)}, bf16[4,2,592,128]{3,2,1,0:T(8,128)(2,1)}, f32[32,40,256]{2,1,0:T(8,128)}, f32[3,32,256]{2,1,0:T(8,128)}, s32[16,256]{1,0:T(8,128)}) custom-call(s32[8]{0:T(128)} %refs_0_.1, s32[1,192]{1,0:T(1,128)} %bitcast.43, s32[1,192]{1,0:T(1,128)} %bitcast.44, bf16[160,192]{1,0:T(8,128)(2,1)} %bitcast.39, ...), custom_call_target="tpu_custom_call" | custom-call | flops 8000000000 | bytes 4000000 | tf_op jit(solution)/shard_map/assemble/pallas_call | solution.py:313
  13.8 0.0 copy-start
  13.8 0.0 copy-start.2
  13.8 0.0 copy-start.3
  13.8 0.5 collective-permute-start
  14.4 2.7 %collective-permute-done = bf16[4,2,592,128]{3,2,1,0:T(8,128)(2,1)S(1)} collective-permute-done((bf16[4,2,592,128]{3,2,1,0:T(8,128)(2,1)}, bf16[4,2,592,128]{3,2,1,0:T(8,128)(2,1)S(1)}, u32[]{:S(2)}, u32[]{:S(2)}) %collective-permute-start) | collective-permute-done | bytes 1212448 | tf_op jit(solution)/shard_map/ppermute | solution.py:404
  17.1 1.2 %add_convert_fusion.1 = bf16[2,2,592,128]{3,2,1,0:T(8,128)(2,1)S(1)} fusion(bf16[4,2,592,128]{3,2,1,0:T(8,128)(2,1)S(1)} %collective-permute-done, bf16[4,2,592,128]{3,2,1,0:T(8,128)(2,1)} %get-tuple-element.30), kind=kLoop, calls=%fused_computation.3 | loop fusion | flops 1212416 | bytes 1818624 | tf_op jit(solution)/shard_map/convert_element_type | solution.py:436
  18.3 2.9 %collective-permute-start.1 = (bf16[2,2,592,128]{3,2,1,0:T(8,128)(2,1)S(1)}, bf16[2,2,592,128]{3,2,1,0:T(8,128)(2,1)S(1)}, u32[]{:S(2)}, u32[]{:S(2)}) collective-permute-start(bf16[2,2,592,128]{3,2,1,0:T(8,128)(2,1)S(1)} %add_convert_fusion.1), channel_id=1, source_target_pairs={{0,2},{1,5},{2,0},{3,7},{4,6},{5,1},{6,4},{7,3},{8,10},{9,13},{10,... | collective-permute-start | bytes 1818632 | tf_op jit(solution)/shard_map/ppermute | solution.py:404
  21.2 0.0 copy-done
  21.2 0.0 copy-done.2
  21.2 0.0 copy-done.3
  21.3 1.3 %copy-done.1 = f32[32,40,256]{2,1,0:T(8,128)S(1)} copy-done((f32[32,40,256]{2,1,0:T(8,128)S(1)}, f32[32,40,256]{2,1,0:T(8,128)}, u32[]{:S(2)}) %copy-start.1) | copy-done | bytes 1310744
  22.6 5.5 %assemble.3 = (bf16[4,2,592,128]{3,2,1,0:T(8,128)(2,1)S(1)}, bf16[4,2,592,128]{3,2,1,0:T(8,128)(2,1)S(1)}) custom-call(f32[32,40,256]{2,1,0:T(8,128)S(1)} %copy-done.1, f32[3,32,256]{2,1,0:T(8,128)S(1)} %copy-done.2, s32[16,256]{1,0:T(8,128)S(1)} %copy-done.3, bf16[192,32,128]{2,1,0:T(8,128)(2,1)S(1)} %copy-done), custom_call_target="tpu_custom_call" | custom-call | flops 8000000000 | bytes 4000000 | tf_op jit(solution)/shard_map/assemble/pallas_call | solution.py:313
  28.1 1.2 %collective-permute-done.1 = bf16[2,2,592,128]{3,2,1,0:T(8,128)(2,1)S(1)} collective-permute-done((bf16[2,2,592,128]{3,2,1,0:T(8,128)(2,1)S(1)}, bf16[2,2,592,128]{3,2,1,0:T(8,128)(2,1)S(1)}, u32[]{:S(2)}, u32[]{:S(2)}) %collective-permute-start.1) | collective-permute-done | bytes 606240 | tf_op jit(solution)/shard_map/ppermute | solution.py:404
  29.3 0.1 collective-permute-start.2
  29.4 0.0 copy-done.4
  29.4 0.2 convert_add_fusion.1
  29.6 2.6 %collective-permute-start.3 = (bf16[2,592,128]{2,1,0:T(8,128)(2,1)S(1)}, bf16[2,592,128]{2,1,0:T(8,128)(2,1)S(1)}, u32[]{:S(2)}, u32[]{:S(2)}) collective-permute-start(bf16[2,592,128]{2,1,0:T(8,128)(2,1)S(1)} %fusion.2), channel_id=1, source_target_pairs={{0,4},{1,3},{2,6},{3,1},{4,0},{5,7},{6,2},{7,5},{8,12},{9,11},{10,... | collective-permute-start | bytes 909320 | tf_op jit(solution)/shard_map/ppermute | solution.py:404
  32.2 4.8 %collective-permute-done.3 = bf16[2,592,128]{2,1,0:T(8,128)(2,1)S(1)} collective-permute-done((bf16[2,592,128]{2,1,0:T(8,128)(2,1)S(1)}, bf16[2,592,128]{2,1,0:T(8,128)(2,1)S(1)}, u32[]{:S(2)}, u32[]{:S(2)}) %collective-permute-start.3) | collective-permute-done | bytes 303136 | tf_op jit(solution)/shard_map/ppermute | solution.py:404
  37.0 0.0 collective-permute-done.2
  37.0 0.2 add_convert_fusion
  37.2 1.5 %collective-permute-start.4 = (bf16[2,2,592,128]{3,2,1,0:T(8,128)(2,1)S(1)}, bf16[2,2,592,128]{3,2,1,0:T(8,128)(2,1)S(1)}, u32[]{:S(2)}, u32[]{:S(2)}) collective-permute-start(bf16[2,2,592,128]{3,2,1,0:T(8,128)(2,1)S(1)} %add_convert_fusion), channel_id=1, source_target_pairs={{0,2},{1,5},{2,0},{3,7},{4,6},{5,1},{6,4},{7,3},{8,10},{9,13},{10,... | collective-permute-start | bytes 1818632 | tf_op jit(solution)/shard_map/ppermute | solution.py:404
  38.7 0.1 fusion
  38.7 1.0 %collective-permute-start.6 = (bf16[592,128]{1,0:T(8,128)(2,1)S(1)}, bf16[592,128]{1,0:T(8,128)(2,1)S(1)}, u32[]{:S(2)}, u32[]{:S(2)}) collective-permute-start(bf16[592,128]{1,0:T(8,128)(2,1)S(1)} %fusion.8), channel_id=1, source_target_pairs={{0,8},{8,0},{16,24},{24,16},{1,9},{9,1},{17,25},{25,17},{2,10},{10... | collective-permute-start | bytes 454664 | tf_op jit(solution)/shard_map/ppermute | solution.py:407
  39.8 7.6 %collective-permute-done.4 = bf16[2,2,592,128]{3,2,1,0:T(8,128)(2,1)S(1)} collective-permute-done((bf16[2,2,592,128]{3,2,1,0:T(8,128)(2,1)S(1)}, bf16[2,2,592,128]{3,2,1,0:T(8,128)(2,1)S(1)}, u32[]{:S(2)}, u32[]{:S(2)}) %collective-permute-start.4) | collective-permute-done | bytes 606240 | tf_op jit(solution)/shard_map/ppermute | solution.py:404
  47.3 0.2 convert_add_fusion
  47.6 2.1 %collective-permute-start.5 = (bf16[2,592,128]{2,1,0:T(8,128)(2,1)S(1)}, bf16[2,592,128]{2,1,0:T(8,128)(2,1)S(1)}, u32[]{:S(2)}, u32[]{:S(2)}) collective-permute-start(bf16[2,592,128]{2,1,0:T(8,128)(2,1)S(1)} %fusion.3), channel_id=1, source_target_pairs={{0,4},{1,3},{2,6},{3,1},{4,0},{5,7},{6,2},{7,5},{8,12},{9,11},{10,... | collective-permute-start | bytes 909320 | tf_op jit(solution)/shard_map/ppermute | solution.py:404
  49.7 0.0 collective-permute-done.6
  49.7 0.9 %collective-permute-start.7 = (bf16[592,128]{1,0:T(8,128)(2,1)S(1)}, bf16[592,128]{1,0:T(8,128)(2,1)S(1)}, u32[]{:S(2)}, u32[]{:S(2)}) collective-permute-start(bf16[592,128]{1,0:T(8,128)(2,1)S(1)} %fusion.5), channel_id=1, source_target_pairs={{0,16},{8,24},{16,0},{24,8},{1,17},{9,25},{17,1},{25,9},{2,18},{10... | collective-permute-start | bytes 454664 | tf_op jit(solution)/shard_map/ppermute | solution.py:407
  50.6 3.8 %collective-permute-done.5 = bf16[2,592,128]{2,1,0:T(8,128)(2,1)S(1)} collective-permute-done((bf16[2,592,128]{2,1,0:T(8,128)(2,1)S(1)}, bf16[2,592,128]{2,1,0:T(8,128)(2,1)S(1)}, u32[]{:S(2)}, u32[]{:S(2)}) %collective-permute-start.5) | collective-permute-done | bytes 303136 | tf_op jit(solution)/shard_map/ppermute | solution.py:404
  54.4 0.1 fusion.1
  54.5 2.1 %collective-permute-start.8 = (bf16[592,128]{1,0:T(8,128)(2,1)S(1)}, bf16[592,128]{1,0:T(8,128)(2,1)S(1)}, u32[]{:S(2)}, u32[]{:S(2)}) collective-permute-start(bf16[592,128]{1,0:T(8,128)(2,1)S(1)} %fusion.9), channel_id=1, source_target_pairs={{0,8},{8,0},{16,24},{24,16},{1,9},{9,1},{17,25},{25,17},{2,10},{10... | collective-permute-start | bytes 454664 | tf_op jit(solution)/shard_map/ppermute | solution.py:407
  56.7 1.1 %collective-permute-done.7 = bf16[592,128]{1,0:T(8,128)(2,1)S(1)} collective-permute-done((bf16[592,128]{1,0:T(8,128)(2,1)S(1)}, bf16[592,128]{1,0:T(8,128)(2,1)S(1)}, u32[]{:S(2)}, u32[]{:S(2)}) %collective-permute-start.7) | collective-permute-done | bytes 151584 | tf_op jit(solution)/shard_map/ppermute | solution.py:407
  57.8 2.2 %collective-permute-done.8 = bf16[592,128]{1,0:T(8,128)(2,1)S(1)} collective-permute-done((bf16[592,128]{1,0:T(8,128)(2,1)S(1)}, bf16[592,128]{1,0:T(8,128)(2,1)S(1)}, u32[]{:S(2)}, u32[]{:S(2)}) %collective-permute-start.8) | collective-permute-done | bytes 151584 | tf_op jit(solution)/shard_map/ppermute | solution.py:407
  60.0 0.8 %fusion.10 = (bf16[592,128]{1,0:T(8,128)(2,1)S(1)}, f32[592,128]{1,0:T(8,128)}) fusion(bf16[592,128]{1,0:T(8,128)(2,1)S(1)} %collective-permute-done.8, bf16[592,128]{1,0:T(8,128)(2,1)S(1)} %collective-permute-done.7, f32[2,592,128]{2,1,0:T(8,128)S(1)} %fusion.1), kind=kLoop, calls=%fused_computation.22 | loop fusion | flops 378880 | bytes 1060864 | tf_op jit(solution)/shard_map/convert.3
  60.8 0.1 collective-permute-start.11
  60.9 1.9 %collective-permute-start.10 = (bf16[128,128]{1,0:T(8,128)(2,1)S(1)}, bf16[128,128]{1,0:T(8,128)(2,1)S(1)}, u32[]{:S(2)}, u32[]{:S(2)}) collective-permute-start(bf16[128,128]{1,0:T(8,128)(2,1)S(1)} %get-tuple-element.41), channel_id=1, source_target_pairs={{0,2},{1,3},{2,4},{3,5},{4,6},{5,7},{6,0},{7,1},{8,10},{9,11},{10,... | collective-permute-start | bytes 98312 | tf_op jit(solution)/shard_map/ppermute | solution.py:453
  62.7 1.5 %collective-permute-start.9 = (bf16[128,128]{1,0:T(8,128)(2,1)S(1)}, bf16[128,128]{1,0:T(8,128)(2,1)S(1)}, u32[]{:S(2)}, u32[]{:S(2)}) collective-permute-start(bf16[128,128]{1,0:T(8,128)(2,1)S(1)} %get-tuple-element.42), channel_id=1, source_target_pairs={{0,1},{1,2},{2,3},{3,4},{4,5},{5,6},{6,7},{7,0},{8,9},{9,10},{10,1... | collective-permute-start | bytes 98312 | tf_op jit(solution)/shard_map/ppermute | solution.py:453
  64.2 0.2 collective-permute-start.12
  64.5 3.5 %collective-permute-done.12.e_ref = bf16[64,128]{1,0:T(8,128)(2,1)S(1)} collective-permute-done((bf16[64,128]{1,0:T(8,128)(2,1)S(1)}, bf16[64,128]{1,0:T(8,128)(2,1)S(1)}, u32[]{:S(2)}, u32[]{:S(2)}) %collective-permute-start.12) | collective-permute-done | bytes 16416 | tf_op jit(solution)/shard_map/ppermute | solution.py:453
  68.0 0.0 collective-permute-done.11.r3_ref
  68.0 0.0 collective-permute-done.10.r2_ref
  68.0 0.0 collective-permute-done.9.r1_ref
  68.0 0.6 copy-done.8
  68.6 0.0 copy-done.5
  68.6 0.0 copy-done.6
  68.6 0.0 copy-done.7
  68.6 2.0 %finish.1 = (f32[128,1024]{1,0:T(8,128)}, f32[1,128]{1,0:T(1,128)}) custom-call(f32[592,128]{1,0:T(8,128)} %get-tuple-element.39.own_ref, bf16[128,128]{1,0:T(8,128)(2,1)} %copy-done.7, bf16[128,128]{1,0:T(8,128)(2,1)} %copy-done.6, bf16[128,128]{1,0:T(8,128)(2,1)} %copy-done.5, bf16[64,128]{1,0:T(8,128)(2,1)} %copy-done.8), custom_call_target="tpu_custom_call" | custom-call | tf_op jit(solution)/shard_map/finish/pallas_call | solution.py:371
  (13 shorter events, 0.2 us)
Async XLA Ops:
  13.8 7.5 %copy-start = (bf16[192,32,128]{2,1,0:T(8,128)(2,1)S(1)}, bf16[192,32,128]{2,1,0:T(8,128)(2,1)}, u32[]{:S(2)}) copy-start(bf16[192,32,128]{2,1,0:T(8,128)(2,1)} %refs_3_.1) | copy-start | bytes 4718596
  13.8 7.4 %copy-start.2 = (f32[3,32,256]{2,1,0:T(8,128)S(1)}, f32[3,32,256]{2,1,0:T(8,128)}, u32[]{:S(2)}) copy-start(f32[3,32,256]{2,1,0:T(8,128)} %get-tuple-element.21.refs_1_) | copy-start | bytes 294916
  13.8 7.4 %copy-start.3 = (s32[16,256]{1,0:T(8,128)S(1)}, s32[16,256]{1,0:T(8,128)}, u32[]{:S(2)}) copy-start(s32[16,256]{1,0:T(8,128)} %get-tuple-element.25.refs_2_) | copy-start | bytes 49156
  13.8 3.3 %collective-permute-start = (bf16[4,2,592,128]{3,2,1,0:T(8,128)(2,1)}, bf16[4,2,592,128]{3,2,1,0:T(8,128)(2,1)S(1)}, u32[]{:S(2)}, u32[]{:S(2)}) collective-permute-start(bf16[4,2,592,128]{3,2,1,0:T(8,128)(2,1)} %get-tuple-element.23), channel_id=1, source_target_pairs={{0,1},{1,0},{2,3},{3,2},{4,5},{5,4},{6,7},{7,6},{8,9},{9,8},{10,11... | collective-permute-start | bytes 3637256 | tf_op jit(solution)/shard_map/ppermute | solution.py:404
  18.3 11.0 %collective-permute-start.1 = (bf16[2,2,592,128]{3,2,1,0:T(8,128)(2,1)S(1)}, bf16[2,2,592,128]{3,2,1,0:T(8,128)(2,1)S(1)}, u32[]{:S(2)}, u32[]{:S(2)}) collective-permute-start(bf16[2,2,592,128]{3,2,1,0:T(8,128)(2,1)S(1)} %add_convert_fusion.1), channel_id=1, source_target_pairs={{0,2},{1,5},{2,0},{3,7},{4,6},{5,1},{6,4},{7,3},{8,10},{9,13},{10,... | collective-permute-start | bytes 1818632 | tf_op jit(solution)/shard_map/ppermute | solution.py:404
  21.2 1.3 %copy-start.1 = (f32[32,40,256]{2,1,0:T(8,128)S(1)}, f32[32,40,256]{2,1,0:T(8,128)}, u32[]{:S(2)}) copy-start(f32[32,40,256]{2,1,0:T(8,128)} %get-tuple-element.20.refs_0_) | copy-start | bytes 3932164
  22.6 6.8 %copy-start.4 = (bf16[4,2,592,128]{3,2,1,0:T(8,128)(2,1)S(1)}, bf16[4,2,592,128]{3,2,1,0:T(8,128)(2,1)}, u32[]{:S(2)}) copy-start(bf16[4,2,592,128]{3,2,1,0:T(8,128)(2,1)} %get-tuple-element.30) | copy-start | bytes 3637252
  29.3 7.8 %collective-permute-start.2 = (bf16[4,2,592,128]{3,2,1,0:T(8,128)(2,1)S(1)}, bf16[4,2,592,128]{3,2,1,0:T(8,128)(2,1)S(1)}, u32[]{:S(2)}, u32[]{:S(2)}) collective-permute-start(bf16[4,2,592,128]{3,2,1,0:T(8,128)(2,1)S(1)} %get-tuple-element.29), channel_id=1, source_target_pairs={{0,1},{1,0},{2,3},{3,2},{4,5},{5,4},{6,7},{7,6},{8,9},{9,8},{10,11... | collective-permute-start | bytes 3637256 | tf_op jit(solution)/shard_map/ppermute | solution.py:404
  29.6 7.4 %collective-permute-start.3 = (bf16[2,592,128]{2,1,0:T(8,128)(2,1)S(1)}, bf16[2,592,128]{2,1,0:T(8,128)(2,1)S(1)}, u32[]{:S(2)}, u32[]{:S(2)}) collective-permute-start(bf16[2,592,128]{2,1,0:T(8,128)(2,1)S(1)} %fusion.2), channel_id=1, source_target_pairs={{0,4},{1,3},{2,6},{3,1},{4,0},{5,7},{6,2},{7,5},{8,12},{9,11},{10,... | collective-permute-start | bytes 909320 | tf_op jit(solution)/shard_map/ppermute | solution.py:404
  37.2 10.1 %collective-permute-start.4 = (bf16[2,2,592,128]{3,2,1,0:T(8,128)(2,1)S(1)}, bf16[2,2,592,128]{3,2,1,0:T(8,128)(2,1)S(1)}, u32[]{:S(2)}, u32[]{:S(2)}) collective-permute-start(bf16[2,2,592,128]{3,2,1,0:T(8,128)(2,1)S(1)} %add_convert_fusion), channel_id=1, source_target_pairs={{0,2},{1,5},{2,0},{3,7},{4,6},{5,1},{6,4},{7,3},{8,10},{9,13},{10,... | collective-permute-start | bytes 1818632 | tf_op jit(solution)/shard_map/ppermute | solution.py:404
  38.7 10.9 %collective-permute-start.6 = (bf16[592,128]{1,0:T(8,128)(2,1)S(1)}, bf16[592,128]{1,0:T(8,128)(2,1)S(1)}, u32[]{:S(2)}, u32[]{:S(2)}) collective-permute-start(bf16[592,128]{1,0:T(8,128)(2,1)S(1)} %fusion.8), channel_id=1, source_target_pairs={{0,8},{8,0},{16,24},{24,16},{1,9},{9,1},{17,25},{25,17},{2,10},{10... | collective-permute-start | bytes 454664 | tf_op jit(solution)/shard_map/ppermute | solution.py:407
  47.6 6.9 %collective-permute-start.5 = (bf16[2,592,128]{2,1,0:T(8,128)(2,1)S(1)}, bf16[2,592,128]{2,1,0:T(8,128)(2,1)S(1)}, u32[]{:S(2)}, u32[]{:S(2)}) collective-permute-start(bf16[2,592,128]{2,1,0:T(8,128)(2,1)S(1)} %fusion.3), channel_id=1, source_target_pairs={{0,4},{1,3},{2,6},{3,1},{4,0},{5,7},{6,2},{7,5},{8,12},{9,11},{10,... | collective-permute-start | bytes 909320 | tf_op jit(solution)/shard_map/ppermute | solution.py:404
  49.7 8.1 %collective-permute-start.7 = (bf16[592,128]{1,0:T(8,128)(2,1)S(1)}, bf16[592,128]{1,0:T(8,128)(2,1)S(1)}, u32[]{:S(2)}, u32[]{:S(2)}) collective-permute-start(bf16[592,128]{1,0:T(8,128)(2,1)S(1)} %fusion.5), channel_id=1, source_target_pairs={{0,16},{8,24},{16,0},{24,8},{1,17},{9,25},{17,1},{25,9},{2,18},{10... | collective-permute-start | bytes 454664 | tf_op jit(solution)/shard_map/ppermute | solution.py:407
  54.5 5.5 %collective-permute-start.8 = (bf16[592,128]{1,0:T(8,128)(2,1)S(1)}, bf16[592,128]{1,0:T(8,128)(2,1)S(1)}, u32[]{:S(2)}, u32[]{:S(2)}) collective-permute-start(bf16[592,128]{1,0:T(8,128)(2,1)S(1)} %fusion.9), channel_id=1, source_target_pairs={{0,8},{8,0},{16,24},{24,16},{1,9},{9,1},{17,25},{25,17},{2,10},{10... | collective-permute-start | bytes 454664 | tf_op jit(solution)/shard_map/ppermute | solution.py:407
  60.8 7.2 %collective-permute-start.11 = (bf16[128,128]{1,0:T(8,128)(2,1)S(1)}, bf16[128,128]{1,0:T(8,128)(2,1)S(1)}, u32[]{:S(2)}, u32[]{:S(2)}) collective-permute-start(bf16[128,128]{1,0:T(8,128)(2,1)S(1)} %get-tuple-element.40), channel_id=1, source_target_pairs={{0,3},{1,4},{2,5},{3,6},{4,7},{5,0},{6,1},{7,2},{8,11},{9,12},{10,... | collective-permute-start | bytes 98312 | tf_op jit(solution)/shard_map/ppermute | solution.py:453
  60.9 7.1 %collective-permute-start.10 = (bf16[128,128]{1,0:T(8,128)(2,1)S(1)}, bf16[128,128]{1,0:T(8,128)(2,1)S(1)}, u32[]{:S(2)}, u32[]{:S(2)}) collective-permute-start(bf16[128,128]{1,0:T(8,128)(2,1)S(1)} %get-tuple-element.41), channel_id=1, source_target_pairs={{0,2},{1,3},{2,4},{3,5},{4,6},{5,7},{6,0},{7,1},{8,10},{9,11},{10,... | collective-permute-start | bytes 98312 | tf_op jit(solution)/shard_map/ppermute | solution.py:453
  62.7 5.2 %collective-permute-start.9 = (bf16[128,128]{1,0:T(8,128)(2,1)S(1)}, bf16[128,128]{1,0:T(8,128)(2,1)S(1)}, u32[]{:S(2)}, u32[]{:S(2)}) collective-permute-start(bf16[128,128]{1,0:T(8,128)(2,1)S(1)} %get-tuple-element.42), channel_id=1, source_target_pairs={{0,1},{1,2},{2,3},{3,4},{4,5},{5,6},{6,7},{7,0},{8,9},{9,10},{10,1... | collective-permute-start | bytes 98312 | tf_op jit(solution)/shard_map/ppermute | solution.py:453
  64.2 3.7 %collective-permute-start.12 = (bf16[64,128]{1,0:T(8,128)(2,1)S(1)}, bf16[64,128]{1,0:T(8,128)(2,1)S(1)}, u32[]{:S(2)}, u32[]{:S(2)}) collective-permute-start(bf16[64,128]{1,0:T(8,128)(2,1)S(1)} %slice.100), channel_id=1, source_target_pairs={{0,4},{1,5},{2,6},{3,7},{4,0},{5,1},{6,2},{7,3},{8,12},{9,13},{10,... | collective-permute-start | bytes 49160 | tf_op jit(solution)/shard_map/ppermute | solution.py:453
  68.0 0.6 copy-start.8
  68.0 0.6 copy-start.5
  68.0 0.6 copy-start.6
  68.0 0.6 copy-start.7

commit v8 on v7

--- a/solution.py
+++ b/solution.py
@@ -118,46 +118,47 @@
 
 def one_step(step, n, table_ref, g_ref, scaled_ref, lanes_ref, g_s, direct_s, vector_s, spread_s):
     hits, width = g_ref.shape[1:]
-    depth = GROUP * hits
+    depth = PAIR * hits
     blocks = direct_s.shape[0] // width
+    many = blocks // 2
     rows = 5 * GROUP
-    sub = iota((16, depth), 0).astype(F32)
-    totals, vector = [], vector_s[...]
-    for u in range(2):
-        group = step * 2 + u
-        for i in range(GROUP):
-            g_s[u, i * hits : (i + 1) * hits, :] = g_ref[table_ref[0, group * GROUP + i]]
-        g = g_s[u]
-        turned = g.T
-        position = jnp.broadcast_to(lanes_ref[2, pl.ds(group, 1), :], (16, depth))
-        masks = [jnp.where(position == float(p), 1.0, 0.0).astype(BF16) for p in range(blocks)]
-        streamed = jnp.concatenate(
-            [turned * jnp.concatenate([mask] * (width // 16), axis=0) for mask in masks], axis=0
+
+    def lanes(which):
+        return jnp.concatenate(
+            [lanes_ref[which, pl.ds(step * 2 + u, 1), :] for u in range(2)], axis=1
         )
-        weighted = turned.astype(F32) * lanes_ref[0, pl.ds(group, 1), :]
-        scaled = scaled_ref[group]
-        high = scaled.astype(BF16).astype(F32)
-        low = scaled - high
-        if u == 0:
-            parts = [high, jnp.zeros((rows, depth), F32), low, jnp.zeros((8, depth), F32)]
-        else:
-            parts = [low[8:], jnp.zeros((8, depth), F32), high, jnp.zeros((rows, depth), F32), low[:8]]
-        held = jnp.concatenate([weighted] + parts, axis=0).astype(BF16)
-        totals.append(lax.dot_general(streamed, held, NT, preferred_element_type=F32))
-        factor = jnp.where(sub == position, lanes_ref[1, pl.ds(group, 1), :], 0.0).astype(BF16)
-        vector = vector + jnp.dot(factor, g, preferred_element_type=F32)
-    vector_s[...] = vector
-    lane = iota((width, width), 1)
+
+    for i in range(PAIR):
+        g_s[i * hits : (i + 1) * hits, :] = g_ref[table_ref[0, step * PAIR + i]]
+    g = g_s[...]
+    turned = g.T
+    position = jnp.broadcast_to(lanes(2), (16, depth))
+    masks = [jnp.where(position == float(p), 1.0, 0.0).astype(BF16) for p in range(blocks)]
+    streamed = jnp.concatenate(
+        [turned * jnp.concatenate([mask] * (width // 16), axis=0) for mask in masks], axis=0
+    )
+    weighted = turned.astype(F32) * lanes(0)
+    none = jnp.zeros((rows, depth // 2), F32)
+    rest = jnp.zeros((width - 2 * rows, depth), F32)
+    scaled = [scaled_ref[step * 2 + u] for u in range(2)]
+    high = [value.astype(BF16).astype(F32) for value in scaled]
+    low = [value - part for value, part in zip(scaled, high)]
+    held = [weighted]
+    for part in (high, low):
+        held += [
+            jnp.concatenate([part[0], none], axis=1),
+            jnp.concatenate([none, part[1]], axis=1),
+            rest,
+        ]
+    held = jnp.concatenate(held, axis=0).astype(BF16)
+    total = lax.dot_general(streamed, held, NT, preferred_element_type=F32)
+    factor = jnp.where(iota((16, depth), 0).astype(F32) == position, lanes(1), 0.0).astype(BF16)
+    vector_s[...] += jnp.dot(factor, g, preferred_element_type=F32)
     at = pl.ds(pl.multiple_of((n % 2) * width, width), width)
-    many = blocks // 2
     for p in range(blocks):
         part = slice(p * width, (p + 1) * width)
-        direct_s[part] = direct_s[part] + (totals[0][part, :width] + totals[1][part, :width])
-        first, second = totals[0][part, width:], totals[1][part, width:]
-        near = jnp.where(lane < rows, first, second)
-        far = jnp.where((lane >= 2 * rows) & (lane < 3 * rows), first, second)
-        far = pltpu.roll(far, width - 2 * rows, 1)
-        value = jnp.where(lane < 2 * rows, near + far, 0.0).astype(BF16)
+        direct_s[part] += total[part, :width]
+        value = (total[part, width : 2 * width] + total[part, 2 * width :]).astype(BF16)
         spread_s[n // 2, part, at] = value
         if p < many:
             spread_s[n // 2, (blocks + p) * width : (blocks + p + 1) * width, at] = value
@@ -177,7 +178,7 @@
     return copies
 
 
-def lead_kernel(ks, sub, *refs):
+def lead_kernel(ks, sub, apart, *refs):
     small, g_hbm, (keep_ref, send_ref), shared = refs[:7], refs[7], refs[8:10], refs[10:13]
     local_small, g_ref, table_s, sems, scratch = refs[13:20], refs[20], refs[21], refs[22], refs[23:]
 
@@ -192,10 +193,10 @@
         copy.wait()
         copies[-1].wait()
 
-    assemble_region(ks, sub, table_s, *shared[:2], g_ref, keep_ref, send_ref, *scratch)
-
-
-def follow_kernel(ks, sub, *refs):
+    assemble_region(ks, sub, False, table_s, *shared[:2], g_ref, keep_ref, send_ref, *scratch)
+
+
+def follow_kernel(ks, sub, apart, *refs):
     shared, (keep_ref, send_ref), mine, sems, scratch = (
         refs[:4], refs[4:6], refs[6:10], refs[10], refs[11:]
     )
@@ -205,11 +206,11 @@
         for copy in fetch(list(zip(shared, mine)), sems):
             copy.wait()
 
-    assemble_region(ks, sub, mine[2], *mine[:2], mine[3], keep_ref, send_ref, *scratch)
+    assemble_region(ks, sub, apart, mine[2], *mine[:2], mine[3], keep_ref, send_ref, *scratch)
 
 
 def assemble_region(
-    ks, sub, table_ref, scaled_ref, lanes_ref, g_ref,
+    ks, sub, apart, table_ref, scaled_ref, lanes_ref, g_ref,
     keep_ref, send_ref, g_s, direct_s, vector_s, spread_s, acc_s,
 ):
     k = jnp.where(pl.program_id(0) == 0, ks[0], ks[1])
@@ -283,10 +284,11 @@
             high = row.astype(BF16).astype(F32)
             sub = iota((16, width), 0)
             parts.append(jnp.where(sub == 0, high, jnp.where(sub == 1, row - high, 0.0)))
-            out_ref[n, 0] = jnp.concatenate(parts, axis=0).astype(BF16)
-
-
-def assemble(ks, sub, inputs, g, blocks, regions):
+            place = (0, n) if apart else (n, 0)
+            out_ref[place] = jnp.concatenate(parts, axis=0).astype(BF16)
+
+
+def assemble(ks, sub, apart, inputs, g, blocks, regions):
     tracks, hits, width = g.shape
     lead = len(inputs) == 7
     rows = width * (blocks // 2) + width // 2 + 16
@@ -298,8 +300,12 @@
         jax.ShapeDtypeStruct((3, slots // GROUP, GROUP * hits), F32),
         jax.ShapeDtypeStruct((8 + rr, slots), jnp.int32),
     ]
-    out = jax.ShapeDtypeStruct((blocks // 2, 2, rows, width), BF16)
-    spec = pl.BlockSpec((blocks // 2, 1, rows, width), lambda k: (0, k, 0, 0))
+    if apart:
+        out = jax.ShapeDtypeStruct((2, blocks // 2, rows, width), BF16)
+        spec = pl.BlockSpec((1, blocks // 2, rows, width), lambda k: (k, 0, 0, 0))
+    else:
+        out = jax.ShapeDtypeStruct((blocks // 2, 2, rows, width), BF16)
+        spec = pl.BlockSpec((blocks // 2, 1, rows, width), lambda k: (0, k, 0, 0))
     vmem = pl.BlockSpec(memory_space=pltpu.VMEM)
     table = pltpu.SMEM(shared[2].shape, jnp.int32)
     arrived = pltpu.VMEM(g.shape, g.dtype)
@@ -311,7 +317,7 @@
         copies = [pltpu.VMEM(value.shape, value.dtype) for value in inputs[:2]]
         copies += [table, arrived]
     return pl.pallas_call(
-        functools.partial(lead_kernel if lead else follow_kernel, ks, sub),
+        functools.partial(lead_kernel if lead else follow_kernel, ks, sub, apart),
         grid=(2,),
         in_specs=[pl.BlockSpec(memory_space=pltpu.HBM)] * (len(inputs) + 1),
         out_specs=[spec, spec] + [vmem] * (3 * lead),
@@ -319,7 +325,7 @@
         scratch_shapes=copies
         + [
             pltpu.SemaphoreType.DMA((8,)),
-            pltpu.VMEM((2, GROUP * hits, width), BF16),
+            pltpu.VMEM((PAIR * hits, width), BF16),
             pltpu.VMEM((blocks * width, width), F32),
             pltpu.VMEM((16, width), F32),
             pltpu.VMEM((longest, (blocks + blocks // 2) * width, 2 * width), BF16),
@@ -421,7 +427,7 @@
     totals, more, second = [None] * regions, None, None
     for first in range(regions - 2, -1, -2):
         ks = (first, first + 1)
-        keep, send, *made = assemble(ks, sub, inputs, global_deriv, blocks, regions)
+        keep, send, *made = assemble(ks, sub, not first, inputs, global_deriv, blocks, regions)
         if made:
             inputs = tuple(made)
         else:
@@ -433,14 +439,19 @@
             pair, arrived = lax.optimization_barrier((pair, second[1]))
             value = second[0] + arrived.astype(F32)
             totals[first + 2], totals[first + 3] = value[0], value[1]
-        more = both(pair, top).astype(BF16)
         if first:
+            more = both(pair, top).astype(BF16)
             more, rest = lax.optimization_barrier((more, inputs[2]))
             inputs = inputs[:2] + (rest,)
-        more = swap(more, 2, 4)
-    value = both(pair, low) + more.astype(F32)
-    value = value[0] + swap(value[1].astype(BF16), 4, 2).astype(F32)
-    totals[0], totals[1] = value[0], value[1]
+            more = swap(more, 2, 4)
+    uppers = [swap(both(pair, (n, top)).astype(BF16), 2, 4) for n in (1, 0)]
+    for n in (1, 0):
+        value = both(pair, (n, low)) + uppers[1 - n].astype(F32)
+        value = value[0], swap(value[1].astype(BF16), 4, 2)
+        if n:
+            pair, uppers[1], more = lax.optimization_barrier((pair, uppers[1], value[1]))
+            value = value[0], more
+        totals[n] = value[0] + value[1].astype(F32)
     for k in range(regions - 1, 0, -1):
         step = k & -k
         totals[k - step] = totals[k - step] + across(totals[k], step).astype(F32)

time: 71.1 us -> 69.6 us (0.979)
  waiting for transfers between devices: 26.9 us -> 21.4 us
  Pallas kernels: 20.7 us -> 23.9 us
  starting transfers between devices: 17.4 us -> 18.5 us
    ppermute x6 -> x8, waiting for transfers between devices: 20.1 us -> 12.2 us  [swap(): return lax.ppermute(value, 'tile', pairs)]
    pallas_call x2, Pallas kernels: 18.7 us -> 21.9 us  [assemble(): pl.pallas_call(functools.partial(lead_kernel if lead else follow_kernel,...]
    ppermute x3, waiting for transfers between devices: 3.33 us -> 5.3 us  [across(): lax.ppermute(value.astype(BF16), 'region', [(r, r ^ k) for r in range(reg...]
    ppermute x6 -> x8, starting transfers between devices: 9.71 us -> 11.4 us  [swap(): return lax.ppermute(value, 'tile', pairs)]
  transfers between devices with their start and end apart: 13 -> 15, of which waited for: 8 -> 10; matrix products, arithmetic and copies ran while one was open for 1% -> 1% of each run, Pallas kernels for 8% -> 13%
where the time goes in v8:
time: 69.6 us; the launch traced here: 69.4 us
  Pallas kernels  23.9 us (34%)
  waiting for transfers between devices  21.4 us (31%)
  starting transfers between devices  18.5 us (27%)
  other arithmetic  2.71 us (4%)
  local copies, waits for them, and re-layouts  2.05 us (3%)
  between operations  0.8 us (1%)
    pallas_call x2, Pallas kernels, assemble(): pl.pallas_call(functools.partial(lead_kernel if lead else follow_kernel,...  21.9 us
    ppermute x8, waiting for transfers between devices, swap(): return lax.ppermute(value, 'tile', pairs)  12.2 us
    ppermute x8, starting transfers between devices, swap(): return lax.ppermute(value, 'tile', pairs)  11.4 us
    ppermute x3, waiting for transfers between devices, across(): lax.ppermute(value.astype(BF16), 'region', [(r, r ^ k) for r in range(reg...  5.3 us
    ppermute x4, waiting for transfers between devices, onward(): return lax.ppermute(value.astype(BF16), 'tile', pairs)  3.86 us
    ppermute x3, starting transfers between devices, across(): lax.ppermute(value.astype(BF16), 'region', [(r, r ^ k) for r in range(reg...  3.73 us
    ppermute x4, starting transfers between devices, onward(): return lax.ppermute(value.astype(BF16), 'tile', pairs)  3.45 us
    pallas_call x1, Pallas kernels, finish(): pl.pallas_call(functools.partial(finish_kernel, sub), in_specs=[vmem] * 5...  1.97 us
  transfers between devices with their start and end apart: 15, of which 10 were waited for; matrix products, arithmetic and copies ran while one was open for 1% of the time, Pallas kernels for 13%

profile of v8, /device:TPU:0, one launch (start us, length us, event | category | flops | bytes accessed | tf_op | source)
XLA Modules:
  0.0 69.4 jit_solution(16237398747814075973)
XLA Ops:
  0.6 13.0 %assemble.2 = (bf16[4,2,592,128]{3,2,1,0:T(8,128)(2,1)}, bf16[4,2,592,128]{3,2,1,0:T(8,128)(2,1)}, f32[32,40,256]{2,1,0:T(8,128)}, f32[3,32,256]{2,1,0:T(8,128)}, s32[16,256]{1,0:T(8,128)}) custom-call(s32[8]{0:T(128)} %refs_0_.1, s32[1,192]{1,0:T(1,128)} %bitcast.55, s32[1,192]{1,0:T(1,128)} %bitcast.56, bf16[160,192]{1,0:T(8,128)(2,1)} %bitcast.51, ...), custom_call_target="tpu_custom_call" | custom-call | flops 8000000000 | bytes 4000000 | tf_op jit(solution)/shard_map/assemble/pallas_call | solution.py:319
  13.6 0.0 copy-start
  13.7 0.0 copy-start.2
  13.7 0.0 copy-start.3
  13.7 0.5 collective-permute-start
  14.2 2.7 %collective-permute-done = bf16[4,2,592,128]{3,2,1,0:T(8,128)(2,1)S(1)} collective-permute-done((bf16[4,2,592,128]{3,2,1,0:T(8,128)(2,1)}, bf16[4,2,592,128]{3,2,1,0:T(8,128)(2,1)S(1)}, u32[]{:S(2)}, u32[]{:S(2)}) %collective-permute-start) | collective-permute-done | bytes 1212448 | tf_op jit(solution)/shard_map/ppermute | solution.py:410
  16.9 1.2 %add_convert_fusion = bf16[2,2,592,128]{3,2,1,0:T(8,128)(2,1)S(1)} fusion(bf16[4,2,592,128]{3,2,1,0:T(8,128)(2,1)S(1)} %collective-permute-done, bf16[4,2,592,128]{3,2,1,0:T(8,128)(2,1)} %get-tuple-element.34), kind=kLoop, calls=%fused_computation.1 | loop fusion | flops 1212416 | bytes 1818624 | tf_op jit(solution)/shard_map/convert_element_type | solution.py:443
  18.2 2.9 %collective-permute-start.1 = (bf16[2,2,592,128]{3,2,1,0:T(8,128)(2,1)S(1)}, bf16[2,2,592,128]{3,2,1,0:T(8,128)(2,1)S(1)}, u32[]{:S(2)}, u32[]{:S(2)}) collective-permute-start(bf16[2,2,592,128]{3,2,1,0:T(8,128)(2,1)S(1)} %add_convert_fusion), channel_id=1, source_target_pairs={{0,2},{1,5},{2,0},{3,7},{4,6},{5,1},{6,4},{7,3},{8,10},{9,13},{10,... | collective-permute-start | bytes 1818632 | tf_op jit(solution)/shard_map/ppermute | solution.py:410
  21.1 1.3 %copy-done.1 = f32[32,40,256]{2,1,0:T(8,128)S(1)} copy-done((f32[32,40,256]{2,1,0:T(8,128)S(1)}, f32[32,40,256]{2,1,0:T(8,128)}, u32[]{:S(2)}) %copy-start.1) | copy-done | bytes 1310744
  22.4 8.9 %assemble.3 = (bf16[2,4,592,128]{3,2,1,0:T(8,128)(2,1)S(1)}, bf16[2,4,592,128]{3,2,1,0:T(8,128)(2,1)S(1)}) custom-call(f32[32,40,256]{2,1,0:T(8,128)S(1)} %copy-done.1, f32[3,32,256]{2,1,0:T(8,128)S(1)} %copy-done.2, s32[16,256]{1,0:T(8,128)S(1)} %copy-done.3, bf16[192,32,128]{2,1,0:T(8,128)(2,1)S(1)} %copy-done), custom_call_target="tpu_custom_call" | custom-call | flops 8000000000 | bytes 4000000 | tf_op jit(solution)/shard_map/assemble/pallas_call | solution.py:319
  31.3 0.0 collective-permute-done.1
  31.4 0.1 collective-permute-start.2
  31.4 0.2 convert_add_fusion
  31.7 1.8 %collective-permute-start.3 = (bf16[2,592,128]{2,1,0:T(8,128)(2,1)S(1)}, bf16[2,592,128]{2,1,0:T(8,128)(2,1)S(1)}, u32[]{:S(2)}, u32[]{:S(2)}) collective-permute-start(bf16[2,592,128]{2,1,0:T(8,128)(2,1)S(1)} %fusion.3), channel_id=1, source_target_pairs={{0,4},{1,3},{2,6},{3,1},{4,0},{5,7},{6,2},{7,5},{8,12},{9,11},{10,... | collective-permute-start | bytes 909320 | tf_op jit(solution)/shard_map/ppermute | solution.py:410
  33.5 5.1 %collective-permute-done.3 = bf16[2,592,128]{2,1,0:T(8,128)(2,1)S(1)} collective-permute-done((bf16[2,592,128]{2,1,0:T(8,128)(2,1)S(1)}, bf16[2,592,128]{2,1,0:T(8,128)(2,1)S(1)}, u32[]{:S(2)}, u32[]{:S(2)}) %collective-permute-start.3) | collective-permute-done | bytes 303136 | tf_op jit(solution)/shard_map/ppermute | solution.py:410
  38.6 0.0 collective-permute-done.2
  38.6 0.2 fusion.1
  38.7 1.8 %collective-permute-start.5 = (bf16[2,592,128]{2,1,0:T(8,128)(2,1)S(1)}, bf16[2,592,128]{2,1,0:T(8,128)(2,1)S(1)}, u32[]{:S(2)}, u32[]{:S(2)}) collective-permute-start(bf16[2,592,128]{2,1,0:T(8,128)(2,1)S(1)} %get-tuple-element.49), channel_id=1, source_target_pairs={{0,2},{1,5},{2,0},{3,7},{4,6},{5,1},{6,4},{7,3},{8,10},{9,13},{10,... | collective-permute-start | bytes 909320 | tf_op jit(solution)/shard_map/ppermute | solution.py:410
  40.6 0.1 fusion
  40.7 1.2 %collective-permute-start.8 = (bf16[592,128]{1,0:T(8,128)(2,1)S(1)}, bf16[592,128]{1,0:T(8,128)(2,1)S(1)}, u32[]{:S(2)}, u32[]{:S(2)}) collective-permute-start(bf16[592,128]{1,0:T(8,128)(2,1)S(1)} %fusion.13), channel_id=1, source_target_pairs={{0,8},{8,0},{16,24},{24,16},{1,9},{9,1},{17,25},{25,17},{2,10},{10... | collective-permute-start | bytes 454664 | tf_op jit(solution)/shard_map/ppermute | solution.py:413
  41.9 0.7 collective-permute-start.4
  42.6 3.1 %collective-permute-done.5 = bf16[2,592,128]{2,1,0:T(8,128)(2,1)S(1)} collective-permute-done((bf16[2,592,128]{2,1,0:T(8,128)(2,1)S(1)}, bf16[2,592,128]{2,1,0:T(8,128)(2,1)S(1)}, u32[]{:S(2)}, u32[]{:S(2)}) %collective-permute-start.5) | collective-permute-done | bytes 303136 | tf_op jit(solution)/shard_map/ppermute | solution.py:410
  45.6 0.1 bitcast_add_fusion.1
  45.8 1.8 %collective-permute-start.6 = (bf16[592,128]{1,0:T(8,128)(2,1)S(1)}, bf16[592,128]{1,0:T(8,128)(2,1)S(1)}, u32[]{:S(2)}, u32[]{:S(2)}) collective-permute-start(bf16[592,128]{1,0:T(8,128)(2,1)S(1)} %fusion.11), channel_id=1, source_target_pairs={{0,4},{1,3},{2,6},{3,1},{4,0},{5,7},{6,2},{7,5},{8,12},{9,11},{10,... | collective-permute-start | bytes 454664 | tf_op jit(solution)/shard_map/ppermute | solution.py:410
  47.5 0.0 collective-permute-done.8
  47.6 2.5 %collective-permute-start.9 = (bf16[592,128]{1,0:T(8,128)(2,1)S(1)}, bf16[592,128]{1,0:T(8,128)(2,1)S(1)}, u32[]{:S(2)}, u32[]{:S(2)}) collective-permute-start(bf16[592,128]{1,0:T(8,128)(2,1)S(1)} %fusion.7), channel_id=1, source_target_pairs={{0,16},{8,24},{16,0},{24,8},{1,17},{9,25},{17,1},{25,9},{2,18},{10... | collective-permute-start | bytes 454664 | tf_op jit(solution)/shard_map/ppermute | solution.py:413
  50.0 0.4 collective-permute-done.4
  50.5 0.5 collective-permute-done.6
  51.0 0.1 bitcast_add_fusion
  51.2 1.8 %collective-permute-start.7 = (bf16[592,128]{1,0:T(8,128)(2,1)S(1)}, bf16[592,128]{1,0:T(8,128)(2,1)S(1)}, u32[]{:S(2)}, u32[]{:S(2)}) collective-permute-start(bf16[592,128]{1,0:T(8,128)(2,1)S(1)} %fusion.12), channel_id=1, source_target_pairs={{0,4},{1,3},{2,6},{3,1},{4,0},{5,7},{6,2},{7,5},{8,12},{9,11},{10,... | collective-permute-start | bytes 454664 | tf_op jit(solution)/shard_map/ppermute | solution.py:410
  53.0 0.0 collective-permute-start.10
  53.0 3.1 %collective-permute-done.9 = bf16[592,128]{1,0:T(8,128)(2,1)S(1)} collective-permute-done((bf16[592,128]{1,0:T(8,128)(2,1)S(1)}, bf16[592,128]{1,0:T(8,128)(2,1)S(1)}, u32[]{:S(2)}, u32[]{:S(2)}) %collective-permute-start.9) | collective-permute-done | bytes 151584 | tf_op jit(solution)/shard_map/ppermute | solution.py:413
  56.1 0.4 collective-permute-done.7
  56.4 2.2 %collective-permute-done.10 = bf16[592,128]{1,0:T(8,128)(2,1)S(1)} collective-permute-done((bf16[592,128]{1,0:T(8,128)(2,1)S(1)}, bf16[592,128]{1,0:T(8,128)(2,1)S(1)}, u32[]{:S(2)}, u32[]{:S(2)}) %collective-permute-start.10) | collective-permute-done | bytes 151584 | tf_op jit(solution)/shard_map/ppermute | solution.py:413
  58.6 0.8 %fusion.14 = (bf16[592,128]{1,0:T(8,128)(2,1)S(1)}, f32[592,128]{1,0:T(8,128)}) fusion(bf16[592,128]{1,0:T(8,128)(2,1)S(1)} %collective-permute-done.10, bf16[592,128]{1,0:T(8,128)(2,1)S(1)} %collective-permute-done.9, bf16[592,128]{1,0:T(8,128)(2,1)S(1)} %collective-permute-done.7, f32[2,592,128]{2,1,0:T(8,128)S(1)} %bitcast_add_fusion), kind=kLoop, calls=%fused_computation.28 | loop fusion | flops 530432 | bytes 1212416 | tf_op jit(solution)/shard_map/convert.3
  59.5 1.2 %collective-permute-start.13 = (bf16[128,128]{1,0:T(8,128)(2,1)S(1)}, bf16[128,128]{1,0:T(8,128)(2,1)S(1)}, u32[]{:S(2)}, u32[]{:S(2)}) collective-permute-start(bf16[128,128]{1,0:T(8,128)(2,1)S(1)} %get-tuple-element.50), channel_id=1, source_target_pairs={{0,3},{1,4},{2,5},{3,6},{4,7},{5,0},{6,1},{7,2},{8,11},{9,12},{10,... | collective-permute-start | bytes 98312 | tf_op jit(solution)/shard_map/ppermute | solution.py:464
  60.7 1.9 %collective-permute-start.12 = (bf16[128,128]{1,0:T(8,128)(2,1)S(1)}, bf16[128,128]{1,0:T(8,128)(2,1)S(1)}, u32[]{:S(2)}, u32[]{:S(2)}) collective-permute-start(bf16[128,128]{1,0:T(8,128)(2,1)S(1)} %get-tuple-element.51), channel_id=1, source_target_pairs={{0,2},{1,3},{2,4},{3,5},{4,6},{5,7},{6,0},{7,1},{8,10},{9,11},{10,... | collective-permute-start | bytes 98312 | tf_op jit(solution)/shard_map/ppermute | solution.py:464
  62.5 0.0 collective-permute-start.11
  62.6 0.4 collective-permute-start.14
  62.9 3.4 %collective-permute-done.14.e_ref = bf16[64,128]{1,0:T(8,128)(2,1)S(1)} collective-permute-done((bf16[64,128]{1,0:T(8,128)(2,1)S(1)}, bf16[64,128]{1,0:T(8,128)(2,1)S(1)}, u32[]{:S(2)}, u32[]{:S(2)}) %collective-permute-start.14) | collective-permute-done | bytes 16416 | tf_op jit(solution)/shard_map/ppermute | solution.py:464
  66.3 0.0 collective-permute-done.13.r3_ref
  66.3 0.0 collective-permute-done.12.r2_ref
  66.3 0.5 collective-permute-done.11.r1_ref
  66.8 0.1 copy-done.8
  66.9 0.0 copy-done.5
  66.9 0.0 copy-done.6
  66.9 0.5 copy-done.7
  67.4 2.0 %finish.1 = (f32[128,1024]{1,0:T(8,128)}, f32[1,128]{1,0:T(1,128)}) custom-call(f32[592,128]{1,0:T(8,128)} %get-tuple-element.47.own_ref, bf16[128,128]{1,0:T(8,128)(2,1)} %copy-done.7, bf16[128,128]{1,0:T(8,128)(2,1)} %copy-done.6, bf16[128,128]{1,0:T(8,128)(2,1)} %copy-done.5, bf16[64,128]{1,0:T(8,128)(2,1)} %copy-done.8), custom_call_target="tpu_custom_call" | custom-call | tf_op jit(solution)/shard_map/finish/pallas_call | solution.py:377
  (18 shorter events, 0.2 us)
Async XLA Ops:
  13.6 7.4 %copy-start = (bf16[192,32,128]{2,1,0:T(8,128)(2,1)S(1)}, bf16[192,32,128]{2,1,0:T(8,128)(2,1)}, u32[]{:S(2)}) copy-start(bf16[192,32,128]{2,1,0:T(8,128)(2,1)} %refs_3_.1) | copy-start | bytes 4718596
  13.7 7.4 %copy-start.2 = (f32[3,32,256]{2,1,0:T(8,128)S(1)}, f32[3,32,256]{2,1,0:T(8,128)}, u32[]{:S(2)}) copy-start(f32[3,32,256]{2,1,0:T(8,128)} %get-tuple-element.25.refs_1_) | copy-start | bytes 294916
  13.7 7.4 %copy-start.3 = (s32[16,256]{1,0:T(8,128)S(1)}, s32[16,256]{1,0:T(8,128)}, u32[]{:S(2)}) copy-start(s32[16,256]{1,0:T(8,128)} %get-tuple-element.29.refs_2_) | copy-start | bytes 49156
  13.7 3.2 %collective-permute-start = (bf16[4,2,592,128]{3,2,1,0:T(8,128)(2,1)}, bf16[4,2,592,128]{3,2,1,0:T(8,128)(2,1)S(1)}, u32[]{:S(2)}, u32[]{:S(2)}) collective-permute-start(bf16[4,2,592,128]{3,2,1,0:T(8,128)(2,1)} %get-tuple-element.27), channel_id=1, source_target_pairs={{0,1},{1,0},{2,3},{3,2},{4,5},{5,4},{6,7},{7,6},{8,9},{9,8},{10,11... | collective-permute-start | bytes 3637256 | tf_op jit(solution)/shard_map/ppermute | solution.py:410
  18.2 13.2 %collective-permute-start.1 = (bf16[2,2,592,128]{3,2,1,0:T(8,128)(2,1)S(1)}, bf16[2,2,592,128]{3,2,1,0:T(8,128)(2,1)S(1)}, u32[]{:S(2)}, u32[]{:S(2)}) collective-permute-start(bf16[2,2,592,128]{3,2,1,0:T(8,128)(2,1)S(1)} %add_convert_fusion), channel_id=1, source_target_pairs={{0,2},{1,5},{2,0},{3,7},{4,6},{5,1},{6,4},{7,3},{8,10},{9,13},{10,... | collective-permute-start | bytes 1818632 | tf_op jit(solution)/shard_map/ppermute | solution.py:410
  21.1 1.3 %copy-start.1 = (f32[32,40,256]{2,1,0:T(8,128)S(1)}, f32[32,40,256]{2,1,0:T(8,128)}, u32[]{:S(2)}) copy-start(f32[32,40,256]{2,1,0:T(8,128)} %get-tuple-element.24.refs_0_) | copy-start | bytes 3932164
  22.4 9.0 %copy-start.4 = (bf16[4,2,592,128]{3,2,1,0:T(8,128)(2,1)S(1)}, bf16[4,2,592,128]{3,2,1,0:T(8,128)(2,1)}, u32[]{:S(2)}) copy-start(bf16[4,2,592,128]{3,2,1,0:T(8,128)(2,1)} %get-tuple-element.34) | copy-start | bytes 3637252
  31.4 7.2 %collective-permute-start.2 = (bf16[2,4,592,128]{3,2,1,0:T(8,128)(2,1)S(1)}, bf16[2,4,592,128]{3,2,1,0:T(8,128)(2,1)S(1)}, u32[]{:S(2)}, u32[]{:S(2)}) collective-permute-start(bf16[2,4,592,128]{3,2,1,0:T(8,128)(2,1)S(1)} %get-tuple-element.33), channel_id=1, source_target_pairs={{0,1},{1,0},{2,3},{3,2},{4,5},{5,4},{6,7},{7,6},{8,9},{9,8},{10,11... | collective-permute-start | bytes 3637256 | tf_op jit(solution)/shard_map/ppermute | solution.py:410
  31.7 6.9 %collective-permute-start.3 = (bf16[2,592,128]{2,1,0:T(8,128)(2,1)S(1)}, bf16[2,592,128]{2,1,0:T(8,128)(2,1)S(1)}, u32[]{:S(2)}, u32[]{:S(2)}) collective-permute-start(bf16[2,592,128]{2,1,0:T(8,128)(2,1)S(1)} %fusion.3), channel_id=1, source_target_pairs={{0,4},{1,3},{2,6},{3,1},{4,0},{5,7},{6,2},{7,5},{8,12},{9,11},{10,... | collective-permute-start | bytes 909320 | tf_op jit(solution)/shard_map/ppermute | solution.py:410
  38.7 6.9 %collective-permute-start.5 = (bf16[2,592,128]{2,1,0:T(8,128)(2,1)S(1)}, bf16[2,592,128]{2,1,0:T(8,128)(2,1)S(1)}, u32[]{:S(2)}, u32[]{:S(2)}) collective-permute-start(bf16[2,592,128]{2,1,0:T(8,128)(2,1)S(1)} %get-tuple-element.49), channel_id=1, source_target_pairs={{0,2},{1,5},{2,0},{3,7},{4,6},{5,1},{6,4},{7,3},{8,10},{9,13},{10,... | collective-permute-start | bytes 909320 | tf_op jit(solution)/shard_map/ppermute | solution.py:410
  40.7 6.9 %collective-permute-start.8 = (bf16[592,128]{1,0:T(8,128)(2,1)S(1)}, bf16[592,128]{1,0:T(8,128)(2,1)S(1)}, u32[]{:S(2)}, u32[]{:S(2)}) collective-permute-start(bf16[592,128]{1,0:T(8,128)(2,1)S(1)} %fusion.13), channel_id=1, source_target_pairs={{0,8},{8,0},{16,24},{24,16},{1,9},{9,1},{17,25},{25,17},{2,10},{10... | collective-permute-start | bytes 454664 | tf_op jit(solution)/shard_map/ppermute | solution.py:413
  41.9 8.6 %collective-permute-start.4 = (bf16[2,592,128]{2,1,0:T(8,128)(2,1)S(1)}, bf16[2,592,128]{2,1,0:T(8,128)(2,1)S(1)}, u32[]{:S(2)}, u32[]{:S(2)}) collective-permute-start(bf16[2,592,128]{2,1,0:T(8,128)(2,1)S(1)} %get-tuple-element.48), channel_id=1, source_target_pairs={{0,2},{1,5},{2,0},{3,7},{4,6},{5,1},{6,4},{7,3},{8,10},{9,13},{10,... | collective-permute-start | bytes 909320 | tf_op jit(solution)/shard_map/ppermute | solution.py:410
  45.8 5.3 %collective-permute-start.6 = (bf16[592,128]{1,0:T(8,128)(2,1)S(1)}, bf16[592,128]{1,0:T(8,128)(2,1)S(1)}, u32[]{:S(2)}, u32[]{:S(2)}) collective-permute-start(bf16[592,128]{1,0:T(8,128)(2,1)S(1)} %fusion.11), channel_id=1, source_target_pairs={{0,4},{1,3},{2,6},{3,1},{4,0},{5,7},{6,2},{7,5},{8,12},{9,11},{10,... | collective-permute-start | bytes 454664 | tf_op jit(solution)/shard_map/ppermute | solution.py:410
  47.6 8.5 %collective-permute-start.9 = (bf16[592,128]{1,0:T(8,128)(2,1)S(1)}, bf16[592,128]{1,0:T(8,128)(2,1)S(1)}, u32[]{:S(2)}, u32[]{:S(2)}) collective-permute-start(bf16[592,128]{1,0:T(8,128)(2,1)S(1)} %fusion.7), channel_id=1, source_target_pairs={{0,16},{8,24},{16,0},{24,8},{1,17},{9,25},{17,1},{25,9},{2,18},{10... | collective-permute-start | bytes 454664 | tf_op jit(solution)/shard_map/ppermute | solution.py:413
  51.2 5.3 %collective-permute-start.7 = (bf16[592,128]{1,0:T(8,128)(2,1)S(1)}, bf16[592,128]{1,0:T(8,128)(2,1)S(1)}, u32[]{:S(2)}, u32[]{:S(2)}) collective-permute-start(bf16[592,128]{1,0:T(8,128)(2,1)S(1)} %fusion.12), channel_id=1, source_target_pairs={{0,4},{1,3},{2,6},{3,1},{4,0},{5,7},{6,2},{7,5},{8,12},{9,11},{10,... | collective-permute-start | bytes 454664 | tf_op jit(solution)/shard_map/ppermute | solution.py:410
  53.0 5.7 %collective-permute-start.10 = (bf16[592,128]{1,0:T(8,128)(2,1)S(1)}, bf16[592,128]{1,0:T(8,128)(2,1)S(1)}, u32[]{:S(2)}, u32[]{:S(2)}) collective-permute-start(bf16[592,128]{1,0:T(8,128)(2,1)S(1)} %fusion.5), channel_id=1, source_target_pairs={{0,8},{8,0},{16,24},{24,16},{1,9},{9,1},{17,25},{25,17},{2,10},{10... | collective-permute-start | bytes 454664 | tf_op jit(solution)/shard_map/ppermute | solution.py:413
  59.5 6.8 %collective-permute-start.13 = (bf16[128,128]{1,0:T(8,128)(2,1)S(1)}, bf16[128,128]{1,0:T(8,128)(2,1)S(1)}, u32[]{:S(2)}, u32[]{:S(2)}) collective-permute-start(bf16[128,128]{1,0:T(8,128)(2,1)S(1)} %get-tuple-element.50), channel_id=1, source_target_pairs={{0,3},{1,4},{2,5},{3,6},{4,7},{5,0},{6,1},{7,2},{8,11},{9,12},{10,... | collective-permute-start | bytes 98312 | tf_op jit(solution)/shard_map/ppermute | solution.py:464
  60.7 5.6 %collective-permute-start.12 = (bf16[128,128]{1,0:T(8,128)(2,1)S(1)}, bf16[128,128]{1,0:T(8,128)(2,1)S(1)}, u32[]{:S(2)}, u32[]{:S(2)}) collective-permute-start(bf16[128,128]{1,0:T(8,128)(2,1)S(1)} %get-tuple-element.51), channel_id=1, source_target_pairs={{0,2},{1,3},{2,4},{3,5},{4,6},{5,7},{6,0},{7,1},{8,10},{9,11},{10,... | collective-permute-start | bytes 98312 | tf_op jit(solution)/shard_map/ppermute | solution.py:464
  62.5 4.2 %collective-permute-start.11 = (bf16[128,128]{1,0:T(8,128)(2,1)S(1)}, bf16[128,128]{1,0:T(8,128)(2,1)S(1)}, u32[]{:S(2)}, u32[]{:S(2)}) collective-permute-start(bf16[128,128]{1,0:T(8,128)(2,1)S(1)} %get-tuple-element.52), channel_id=1, source_target_pairs={{0,1},{1,2},{2,3},{3,4},{4,5},{5,6},{6,7},{7,0},{8,9},{9,10},{10,1... | collective-permute-start | bytes 98312 | tf_op jit(solution)/shard_map/ppermute | solution.py:464
  62.6 3.7 %collective-permute-start.14 = (bf16[64,128]{1,0:T(8,128)(2,1)S(1)}, bf16[64,128]{1,0:T(8,128)(2,1)S(1)}, u32[]{:S(2)}, u32[]{:S(2)}) collective-permute-start(bf16[64,128]{1,0:T(8,128)(2,1)S(1)} %slice.116), channel_id=1, source_target_pairs={{0,4},{1,5},{2,6},{3,7},{4,0},{5,1},{6,2},{7,3},{8,12},{9,13},{10,... | collective-permute-start | bytes 49160 | tf_op jit(solution)/shard_map/ppermute | solution.py:464
  66.3 0.6 copy-start.8
  66.3 0.6 copy-start.5
  66.3 0.6 copy-start.6
  66.8 0.6 copy-start.7

commit v9 on v6

--- a/solution.py
+++ b/solution.py
@@ -115,7 +115,7 @@
     grouping = (iota((columns, slots), 1) // GROUP == iota((columns, slots), 0)).astype(F32)
     column_ref[...] = lax.dot_general(
         spread_out(position).astype(BF16), grouping.astype(BF16), NT, preferred_element_type=F32
-    ).astype(BF16)
+    )
     for c in range(5):
         scaled_ref[:, c * GROUP : (c + 1) * GROUP, :] = spread_out(solved[c]).T.reshape(
             groups, GROUP, depth
@@ -135,8 +135,8 @@
         for i in range(GROUP):
             g_s[u, i * hits : (i + 1) * hits, :] = g_ref[table_ref[0, group * GROUP + i]]
         g = g_s[u]
-        chosen = (iota((128, width), 0) == group).astype(F32).astype(BF16)
-        position = jnp.dot(column_ref[...], chosen, preferred_element_type=F32)
+        chosen = jnp.full(column_ref.shape, group, jnp.int32)
+        position = jnp.take_along_axis(column_ref[...], chosen, axis=1, mode="promise_in_bounds")
         turned = lax.dot_general(unit, g, NT, preferred_element_type=F32)
         weighted = turned * lanes_ref[0, pl.ds(group, 1), :]
         factor = jnp.where(iota((8, depth), 0) == 0, lanes_ref[1, pl.ds(group, 1), :], 0.0)
@@ -199,24 +199,15 @@
     assemble_region(ks, sub, table_s, *shared[:3], g_ref, keep_ref, send_ref, *scratch)
 
 
-def follow_kernel(ks, sub, *refs):
-    shared, (keep_ref, send_ref), mine, sems, scratch = (
-        refs[:5], refs[5:7], refs[7:12], refs[12], refs[13:]
-    )
-
-    @pl.when(pl.program_id(0) == 0)
-    def _():
-        for copy in fetch(list(zip(shared, mine)), sems):
-            copy.wait()
-
-    assemble_region(ks, sub, mine[3], *mine[:3], mine[4], keep_ref, send_ref, *scratch)
+def follow_kernel(ks, sub, scaled_ref, lanes_ref, column_ref, table_ref, g_ref, *refs):
+    assemble_region(ks, sub, table_ref, scaled_ref, lanes_ref, column_ref, g_ref, *refs)
 
 
 def assemble_region(
     ks, sub, table_ref, scaled_ref, lanes_ref, column_ref, g_ref,
     keep_ref, send_ref, g_s, direct_s, spread_s, wide_s, turned_s, acc_s,
 ):
-    k = jnp.where(pl.program_id(0) == 0, ks[0], ks[1])
+    k = jnp.where(pl.program_id(0) == 0, ks[0], ks[-1])
     width = g_ref.shape[2]
     blocks = spread_s.shape[1] // width
     many = blocks // 2
@@ -312,10 +303,10 @@
     shared = [
         jax.ShapeDtypeStruct((slots // GROUP, 5 * GROUP, GROUP * hits), F32),
         jax.ShapeDtypeStruct((2, slots // GROUP, GROUP * hits), F32),
-        jax.ShapeDtypeStruct((GROUP * hits, 128), BF16),
+        jax.ShapeDtypeStruct((GROUP * hits, 128), F32),
         jax.ShapeDtypeStruct((8 + rr, slots), jnp.int32),
     ]
-    out = jax.ShapeDtypeStruct((blocks // 2, 2, rows, width), BF16)
+    out = jax.ShapeDtypeStruct((blocks // 2, len(ks), rows, width), BF16)
     spec = pl.BlockSpec((blocks // 2, 1, rows, width), lambda k: (0, k, 0, 0))
     vmem = pl.BlockSpec(memory_space=pltpu.VMEM)
     table = pltpu.SMEM(shared[3].shape, jnp.int32)
@@ -323,19 +314,19 @@
     if lead:
         copies = [pltpu.SMEM(inputs[0].shape, jnp.int32)]
         copies += [pltpu.VMEM(value.shape, value.dtype) for value in inputs[1:]]
-        copies += [arrived, table]
+        copies += [arrived, table, pltpu.SemaphoreType.DMA((8,))]
+        in_specs = [pl.BlockSpec(memory_space=pltpu.HBM)] * 8
     else:
-        copies = [pltpu.VMEM(value.shape, value.dtype) for value in inputs[:3]]
-        copies += [table, arrived]
+        copies = []
+        in_specs = [vmem, vmem, vmem, pl.BlockSpec(memory_space=pltpu.SMEM), vmem]
     return pl.pallas_call(
         functools.partial(lead_kernel if lead else follow_kernel, ks, sub),
-        grid=(2,),
-        in_specs=[pl.BlockSpec(memory_space=pltpu.HBM)] * (len(inputs) + 1),
+        grid=(len(ks),),
+        in_specs=in_specs,
         out_specs=[spec, spec] + [vmem] * (4 * lead),
         out_shape=[out, out] + shared * lead,
         scratch_shapes=copies
         + [
-            pltpu.SemaphoreType.DMA((8,)),
             pltpu.VMEM((2, GROUP * hits, width), BF16),
             pltpu.VMEM((width + 8, blocks * width), F32),
             pltpu.VMEM((longest, blocks * width), F32),
@@ -347,7 +338,7 @@
             dimension_semantics=("arbitrary",), vmem_limit_bytes=(60 if lead else 32) * 1024 * 1024
         ),
         cost_estimate=pl.CostEstimate(
-            flops=8 * 10**9, bytes_accessed=4 * 10**6, transcendentals=0
+            flops=4 * 10**9 * len(ks), bytes_accessed=4 * 10**6, transcendentals=0
         ),
         name="assemble",
     )(*inputs, g)
@@ -435,29 +426,45 @@
         return pair[0][part].astype(F32) + pair[1][part].astype(F32)
 
     low, top = slice(0, blocks // 4), slice(blocks // 4, blocks // 2)
-    totals, more, second = [None] * regions, None, None
-    for first in range(regions - 2, -1, -2):
-        ks = (first, first + 1)
+    def upper(pair):
+        return swap(both(pair, top).astype(BF16), 2, 4)
+
+    def lower(pair, more):
+        value = both(pair, low) + more.astype(F32)
+        return value[0], swap(value[1].astype(BF16), 4, 2)
+
+    groups = [(k + 1, k) for k in range(regions - 2, 0, -2)] + [(1,), (0,)]
+    cores, firsts, seconds = [], [], []
+    for n, ks in enumerate(groups):
         keep, send, *made = assemble(ks, sub, inputs, global_deriv, blocks, regions)
-        if made:
+        if n == 0:
+            cores.append(near(keep, send))
+            made[3], more = lax.optimization_barrier((made[3], both(cores[0], top).astype(BF16)))
             inputs = tuple(made)
+            firsts.append(swap(more, 2, 4))
+            continue
+        if n > 1:
+            send, cores[-1], firsts[-1] = lax.optimization_barrier((send, cores[-1], firsts[-1]))
+            seconds.append(lower(cores[-2], firsts[-1]))
+            firsts.append(upper(cores[-1]))
         else:
-            send, pair, more = lax.optimization_barrier((send, pair, more))
-            value = both(pair, low) + more.astype(F32)
-            second = value[0], swap(value[1].astype(BF16), 4, 2)
-        pair = near(keep, send)
-        if second is not None:
-            pair, arrived = lax.optimization_barrier((pair, second[1]))
-            value = second[0] + arrived.astype(F32)
-            totals[first + 2], totals[first + 3] = value[0], value[1]
-        more = both(pair, top).astype(BF16)
-        if first:
-            more, rest = lax.optimization_barrier((more, inputs[3]))
+            rest, send = lax.optimization_barrier((inputs[3], send))
             inputs = inputs[:3] + (rest,)
-        more = swap(more, 2, 4)
-    value = both(pair, low) + more.astype(F32)
-    value = value[0] + swap(value[1].astype(BF16), 4, 2).astype(F32)
-    totals[0], totals[1] = value[0], value[1]
+        core = near(keep, send)
+        if n > 1:
+            core, firsts[-1], value = lax.optimization_barrier((core, firsts[-1], seconds[-1][1]))
+            seconds[-1] = seconds[-1][0], value
+        cores.append(core)
+    seconds.append(lower(cores[-2], firsts[-1]))
+    firsts.append(upper(cores[-1]))
+    firsts[-1], value = lax.optimization_barrier((firsts[-1], seconds[-1][1]))
+    seconds[-1] = seconds[-1][0], value
+    seconds.append(lower(cores[-1], firsts[-1]))
+    totals = [None] * regions
+    for ks, (own, value) in zip(groups, seconds):
+        value = own + value.astype(F32)
+        for n, k in enumerate(ks):
+            totals[k] = value[n]
     for k in range(regions - 1, 0, -1):
         step = k & -k
         totals[k - step] = totals[k - step] + across(totals[k], step).astype(F32)

time: 70.5 us -> 68.7 us (0.974); the launches traced: 69.6 us -> 68.6 us
  waiting for transfers between devices: 28.8 us -> 25 us
  starting transfers between devices: 15 us -> 17.8 us
    ppermute x6 -> x9, waiting for transfers between devices: 20.8 us -> 12.6 us  [swap(): return lax.ppermute(value, 'tile', pairs)]
    ppermute x3, waiting for transfers between devices: 4.37 us -> 9.37 us  [across(): lax.ppermute(value.astype(BF16), 'region', [(r, r ^ k) for r in range(reg...]
    ppermute x3, starting transfers between devices: 4.16 us -> 5.75 us  [across(): lax.ppermute(value.astype(BF16), 'region', [(r, r ^ k) for r in range(reg...]
    ppermute x6 -> x9, starting transfers between devices: 7.63 us -> 8.22 us  [swap(): return lax.ppermute(value, 'tile', pairs)]
    pallas_call x2 -> x3, Pallas kernels: 18.2 us -> 18.2 us  [assemble(): pl.pallas_call(functools.partial(lead_kernel if lead else follow_kernel,...]
  transfers between devices with their start and end apart: 13 -> 16, of which waited for: 8 -> 8; matrix products, arithmetic and copies ran while one was open for 1% -> 1% of each run, Pallas kernels for 9% -> 14%
where the time goes in v9:
time: 68.7 us; the launch traced here: 68.6 us
  waiting for transfers between devices  25 us (36%)
  Pallas kernels  20.1 us (29%)
  starting transfers between devices  17.8 us (26%)
  other arithmetic  2.76 us (4%)
  local copies, waits for them, and re-layouts  2.05 us (3%)
  between operations  0.87 us (1%)
    pallas_call x3, Pallas kernels, assemble(): pl.pallas_call(functools.partial(lead_kernel if lead else follow_kernel,...  18.2 us
    ppermute x9, waiting for transfers between devices, swap(): return lax.ppermute(value, 'tile', pairs)  12.6 us
    ppermute x3, waiting for transfers between devices, across(): lax.ppermute(value.astype(BF16), 'region', [(r, r ^ k) for r in range(reg...  9.37 us
    ppermute x9, starting transfers between devices, swap(): return lax.ppermute(value, 'tile', pairs)  8.22 us
    ppermute x3, starting transfers between devices, across(): lax.ppermute(value.astype(BF16), 'region', [(r, r ^ k) for r in range(reg...  5.75 us
    ppermute x4, starting transfers between devices, onward(): return lax.ppermute(value.astype(BF16), 'tile', pairs)  3.79 us
    ppermute x4, waiting for transfers between devices, onward(): return lax.ppermute(value.astype(BF16), 'tile', pairs)  3.07 us
    pallas_call x1, Pallas kernels, finish(): pl.pallas_call(functools.partial(finish_kernel, sub), in_specs=[vmem] * 5...  1.95 us
  transfers between devices with their start and end apart: 16, of which 8 were waited for; matrix products, arithmetic and copies ran while one was open for 1% of the time, Pallas kernels for 14%

profile of v9, /device:TPU:0, one launch (start us, length us, event | category | flops | bytes accessed | tf_op | source)
XLA Modules:
  0.0 68.6 jit_solution(6886269607959397301)
XLA Ops:
  0.6 8.4 %assemble.3 = (bf16[4,2,592,128]{3,2,1,0:T(8,128)(2,1)}, bf16[4,2,592,128]{3,2,1,0:T(8,128)(2,1)}, f32[32,40,256]{2,1,0:T(8,128)}, f32[2,32,256]{2,1,0:T(8,128)}, f32[256,128]{1,0:T(8,128)}, /*index=5*/s32[16,256]{1,0:T(8,128)}) custom-call(s32[8]{0:T(128)} %refs_0_.1, s32[1,192]{1,0:T(1,128)} %bitcast.60, s32[1,192]{1,0:T(1,128)} %bitcast.61, ...), custom_call_target="tpu_custom_call" | custom-call | flops 8000000000 | bytes 4000000 | tf_op jit(solution)/shard_map/assemble/pallas_call | solution.py:322
  9.0 0.0 copy-start
  9.0 0.0 copy-start.2
  9.1 1.0 %collective-permute-start = (bf16[4,2,592,128]{3,2,1,0:T(8,128)(2,1)}, bf16[4,2,592,128]{3,2,1,0:T(8,128)(2,1)S(1)}, u32[]{:S(2)}, u32[]{:S(2)}) collective-permute-start(bf16[4,2,592,128]{3,2,1,0:T(8,128)(2,1)} %get-tuple-element.33), channel_id=1, source_target_pairs={{0,1},{1,0},{2,3},{3,2},{4,5},{5,4},{6,7},{7,6},{8,9},{9,8},{10,11... | collective-permute-start | bytes 3637256 | tf_op jit(solution)/shard_map/ppermute | solution.py:412
  10.1 2.7 %collective-permute-done = bf16[4,2,592,128]{3,2,1,0:T(8,128)(2,1)S(1)} collective-permute-done((bf16[4,2,592,128]{3,2,1,0:T(8,128)(2,1)}, bf16[4,2,592,128]{3,2,1,0:T(8,128)(2,1)S(1)}, u32[]{:S(2)}, u32[]{:S(2)}) %collective-permute-start) | collective-permute-done | bytes 1212448 | tf_op jit(solution)/shard_map/ppermute | solution.py:412
  12.8 1.2 %add_convert_fusion = bf16[2,2,592,128]{3,2,1,0:T(8,128)(2,1)S(1)} fusion(bf16[4,2,592,128]{3,2,1,0:T(8,128)(2,1)S(1)} %collective-permute-done, bf16[4,2,592,128]{3,2,1,0:T(8,128)(2,1)} %get-tuple-element.32), kind=kLoop, calls=%fused_computation.1 | loop fusion | flops 1212416 | bytes 1818624 | tf_op jit(solution)/shard_map/convert_element_type | solution.py:442
  14.0 2.9 %collective-permute-start.2 = (bf16[2,2,592,128]{3,2,1,0:T(8,128)(2,1)S(1)}, bf16[2,2,592,128]{3,2,1,0:T(8,128)(2,1)S(1)}, u32[]{:S(2)}, u32[]{:S(2)}) collective-permute-start(bf16[2,2,592,128]{3,2,1,0:T(8,128)(2,1)S(1)} %add_convert_fusion), channel_id=1, source_target_pairs={{0,2},{1,5},{2,0},{3,7},{4,6},{5,1},{6,4},{7,3},{8,10},{9,13},{10,... | collective-permute-start | bytes 1818632 | tf_op jit(solution)/shard_map/ppermute | solution.py:412
  17.0 1.3 %copy-done.1 = f32[32,40,256]{2,1,0:T(8,128)S(1)} copy-done((f32[32,40,256]{2,1,0:T(8,128)S(1)}, f32[32,40,256]{2,1,0:T(8,128)}, u32[]{:S(2)}) %copy-start.1) | copy-done | bytes 1310744
  18.3 6.2 %assemble.4 = (bf16[4,1,592,128]{3,2,1,0:T(8,128)(2,1)S(1)}, bf16[4,1,592,128]{3,2,1,0:T(8,128)(2,1)S(1)}) custom-call(f32[32,40,256]{2,1,0:T(8,128)S(1)} %copy-done.1, f32[2,32,256]{2,1,0:T(8,128)S(1)} %copy-done.3, f32[256,128]{1,0:T(8,128)S(1)} %copy-done.2, s32[16,256]{1,0:T(8,128)S(1)} %copy-done.4, bf16[192,32,128]{2,1,0:T(8,128)(2,1)S(1)} %copy-done), custom_call_target="tpu_custom_call" | custom-call | flops 4000000000 | bytes 4000000 | tf_op jit(solution)/shard_map/assemble/pallas_call | solution.py:322
  24.5 0.1 collective-permute-start.1
  24.6 3.6 %assemble.5 = (bf16[4,1,592,128]{3,2,1,0:T(8,128)(2,1)S(1)}, bf16[4,1,592,128]{3,2,1,0:T(8,128)(2,1)S(1)}) custom-call(f32[32,40,256]{2,1,0:T(8,128)S(1)} %copy-done.1, f32[2,32,256]{2,1,0:T(8,128)S(1)} %copy-done.3, f32[256,128]{1,0:T(8,128)S(1)} %copy-done.2, s32[16,256]{1,0:T(8,128)S(1)} %copy-done.4, bf16[192,32,128]{2,1,0:T(8,128)(2,1)S(1)} %copy-done), custom_call_target="tpu_custom_call" | custom-call | flops 4000000000 | bytes 4000000 | tf_op jit(solution)/shard_map/assemble/pallas_call | solution.py:322
  28.2 0.0 collective-permute-done.2
  28.2 0.0 collective-permute-done.1
  28.2 0.1 collective-permute-start.3
  28.3 0.2 convert_add_fusion
  28.6 0.1 add_convert_fusion.2
  28.7 0.9 %collective-permute-start.4 = (bf16[2,1,592,128]{3,2,1,0:T(8,128)(2,1)S(1)}, bf16[2,1,592,128]{3,2,1,0:T(8,128)(2,1)S(1)}, u32[]{:S(2)}, u32[]{:S(2)}) collective-permute-start(bf16[2,1,592,128]{3,2,1,0:T(8,128)(2,1)S(1)} %add_convert_fusion.2), channel_id=1, source_target_pairs={{0,2},{1,5},{2,0},{3,7},{4,6},{5,1},{6,4},{7,3},{8,10},{9,13},{10,... | collective-permute-start | bytes 909320 | tf_op jit(solution)/shard_map/ppermute | solution.py:412
  29.6 1.1 %collective-permute-start.5 = (bf16[2,592,128]{2,1,0:T(8,128)(2,1)S(1)}, bf16[2,592,128]{2,1,0:T(8,128)(2,1)S(1)}, u32[]{:S(2)}, u32[]{:S(2)}) collective-permute-start(bf16[2,592,128]{2,1,0:T(8,128)(2,1)S(1)} %fusion.1), channel_id=1, source_target_pairs={{0,4},{1,3},{2,6},{3,1},{4,0},{5,7},{6,2},{7,5},{8,12},{9,11},{10,... | collective-permute-start | bytes 909320 | tf_op jit(solution)/shard_map/ppermute | solution.py:412
  30.7 7.8 %collective-permute-done.4 = bf16[2,1,592,128]{3,2,1,0:T(8,128)(2,1)S(1)} collective-permute-done((bf16[2,1,592,128]{3,2,1,0:T(8,128)(2,1)S(1)}, bf16[2,1,592,128]{3,2,1,0:T(8,128)(2,1)S(1)}, u32[]{:S(2)}, u32[]{:S(2)}) %collective-permute-start.4) | collective-permute-done | bytes 303136 | tf_op jit(solution)/shard_map/ppermute | solution.py:412
  38.5 0.0 collective-permute-done.5
  38.5 0.0 collective-permute-done.3
  38.5 0.1 fusion
  38.6 0.1 convert_add_fusion.2
  38.7 4.5 %collective-permute-start.9 = (bf16[592,128]{1,0:T(8,128)(2,1)S(1)}, bf16[592,128]{1,0:T(8,128)(2,1)S(1)}, u32[]{:S(2)}, u32[]{:S(2)}) collective-permute-start(bf16[592,128]{1,0:T(8,128)(2,1)S(1)} %fusion.12), channel_id=1, source_target_pairs={{0,8},{8,0},{16,24},{24,16},{1,9},{9,1},{17,25},{25,17},{2,10},{10... | collective-permute-start | bytes 454664 | tf_op jit(solution)/shard_map/ppermute | solution.py:415
  43.3 0.1 add_convert_fusion.1
  43.3 0.4 collective-permute-start.6
  43.7 0.1 collective-permute-start.7
  43.8 3.4 %collective-permute-done.9 = bf16[592,128]{1,0:T(8,128)(2,1)S(1)} collective-permute-done((bf16[592,128]{1,0:T(8,128)(2,1)S(1)}, bf16[592,128]{1,0:T(8,128)(2,1)S(1)}, u32[]{:S(2)}, u32[]{:S(2)}) %collective-permute-start.9) | collective-permute-done | bytes 151584 | tf_op jit(solution)/shard_map/ppermute | solution.py:415
  47.2 1.2 %collective-permute-start.10 = (bf16[592,128]{1,0:T(8,128)(2,1)S(1)}, bf16[592,128]{1,0:T(8,128)(2,1)S(1)}, u32[]{:S(2)}, u32[]{:S(2)}) collective-permute-start(bf16[592,128]{1,0:T(8,128)(2,1)S(1)} %fusion.5), channel_id=1, source_target_pairs={{0,16},{8,24},{16,0},{24,8},{1,17},{9,25},{17,1},{25,9},{2,18},{10... | collective-permute-start | bytes 454664 | tf_op jit(solution)/shard_map/ppermute | solution.py:415
  48.4 2.0 %collective-permute-done.7 = bf16[1,592,128]{2,1,0:T(8,128)(2,1)S(1)} collective-permute-done((bf16[1,592,128]{2,1,0:T(8,128)(2,1)S(1)}, bf16[1,592,128]{2,1,0:T(8,128)(2,1)S(1)}, u32[]{:S(2)}, u32[]{:S(2)}) %collective-permute-start.7) | collective-permute-done | bytes 151584 | tf_op jit(solution)/shard_map/ppermute | solution.py:412
  50.4 0.1 collective-permute-done.6
  50.5 0.1 convert_add_fusion.1
  50.7 1.6 %collective-permute-start.8 = (bf16[1,592,128]{2,1,0:T(8,128)(2,1)S(1)}, bf16[1,592,128]{2,1,0:T(8,128)(2,1)S(1)}, u32[]{:S(2)}, u32[]{:S(2)}) collective-permute-start(bf16[1,592,128]{2,1,0:T(8,128)(2,1)S(1)} %fusion.11), channel_id=1, source_target_pairs={{0,4},{1,3},{2,6},{3,1},{4,0},{5,7},{6,2},{7,5},{8,12},{9,11},{10,... | collective-permute-start | bytes 454664 | tf_op jit(solution)/shard_map/ppermute | solution.py:412
  52.3 0.0 collective-permute-start.11
  52.3 4.2 %collective-permute-done.10 = bf16[592,128]{1,0:T(8,128)(2,1)S(1)} collective-permute-done((bf16[592,128]{1,0:T(8,128)(2,1)S(1)}, bf16[592,128]{1,0:T(8,128)(2,1)S(1)}, u32[]{:S(2)}, u32[]{:S(2)}) %collective-permute-start.10) | collective-permute-done | bytes 151584 | tf_op jit(solution)/shard_map/ppermute | solution.py:415
  56.5 1.8 %collective-permute-done.11 = bf16[592,128]{1,0:T(8,128)(2,1)S(1)} collective-permute-done((bf16[592,128]{1,0:T(8,128)(2,1)S(1)}, bf16[592,128]{1,0:T(8,128)(2,1)S(1)}, u32[]{:S(2)}, u32[]{:S(2)}) %collective-permute-start.11) | collective-permute-done | bytes 151584 | tf_op jit(solution)/shard_map/ppermute | solution.py:415
  58.3 0.8 %fusion.14 = (bf16[592,128]{1,0:T(8,128)(2,1)S(1)}, f32[592,128]{1,0:T(8,128)}) fusion(bf16[592,128]{1,0:T(8,128)(2,1)S(1)} %collective-permute-done.11, bf16[592,128]{1,0:T(8,128)(2,1)S(1)} %collective-permute-done.10, bf16[1,592,128]{2,1,0:T(8,128)(2,1)S(1)} %collective-permute-done.8, f32[2,1,592,128]{3,2,1,0:T(8,128)S(1)} %convert_add_fusion.1), kind=kLoop, calls=%fused_computation.28 | loop fusion | flops 530432 | bytes 1212416 | tf_op jit(solution)/shard_map/convert.3
  59.1 1.3 %collective-permute-start.14 = (bf16[128,128]{1,0:T(8,128)(2,1)S(1)}, bf16[128,128]{1,0:T(8,128)(2,1)S(1)}, u32[]{:S(2)}, u32[]{:S(2)}) collective-permute-start(bf16[128,128]{1,0:T(8,128)(2,1)S(1)} %get-tuple-element.56), channel_id=1, source_target_pairs={{0,3},{1,4},{2,5},{3,6},{4,7},{5,0},{6,1},{7,2},{8,11},{9,12},{10,... | collective-permute-start | bytes 98312 | tf_op jit(solution)/shard_map/ppermute | solution.py:477
  60.5 0.7 collective-permute-start.13
  61.1 0.3 collective-permute-start.12
  61.4 1.5 %collective-permute-start.15 = (bf16[64,128]{1,0:T(8,128)(2,1)S(1)}, bf16[64,128]{1,0:T(8,128)(2,1)S(1)}, u32[]{:S(2)}, u32[]{:S(2)}) collective-permute-start(bf16[64,128]{1,0:T(8,128)(2,1)S(1)} %slice.117), channel_id=1, source_target_pairs={{0,4},{1,5},{2,6},{3,7},{4,0},{5,1},{6,2},{7,3},{8,12},{9,13},{10,... | collective-permute-start | bytes 49160 | tf_op jit(solution)/shard_map/ppermute | solution.py:477
  62.9 3.1 %collective-permute-done.15.e_ref = bf16[64,128]{1,0:T(8,128)(2,1)S(1)} collective-permute-done((bf16[64,128]{1,0:T(8,128)(2,1)S(1)}, bf16[64,128]{1,0:T(8,128)(2,1)S(1)}, u32[]{:S(2)}, u32[]{:S(2)}) %collective-permute-start.15) | collective-permute-done | bytes 16416 | tf_op jit(solution)/shard_map/ppermute | solution.py:477
  66.0 0.0 collective-permute-done.12.r1_ref
  66.0 0.6 copy-done.9
  66.6 0.0 copy-done.6
  66.6 0.0 copy-done.7
  66.6 0.0 copy-done.8
  66.7 1.9 %finish.1 = (f32[128,1024]{1,0:T(8,128)}, f32[1,128]{1,0:T(1,128)}) custom-call(f32[592,128]{1,0:T(8,128)} %get-tuple-element.55.own_ref, bf16[128,128]{1,0:T(8,128)(2,1)} %copy-done.8, bf16[128,128]{1,0:T(8,128)(2,1)} %copy-done.7, bf16[128,128]{1,0:T(8,128)(2,1)} %copy-done.6, bf16[64,128]{1,0:T(8,128)(2,1)} %copy-done.9), custom_call_target="tpu_custom_call" | custom-call | tf_op jit(solution)/shard_map/finish/pallas_call | solution.py:379
  (24 shorter events, 0.2 us)
Async XLA Ops:
  9.0 8.0 %copy-start = (bf16[192,32,128]{2,1,0:T(8,128)(2,1)S(1)}, bf16[192,32,128]{2,1,0:T(8,128)(2,1)}, u32[]{:S(2)}) copy-start(bf16[192,32,128]{2,1,0:T(8,128)(2,1)} %g_ref.3) | copy-start | bytes 4718596
  9.0 8.0 %copy-start.2 = (f32[256,128]{1,0:T(8,128)S(1)}, f32[256,128]{1,0:T(8,128)}, u32[]{:S(2)}) copy-start(f32[256,128]{1,0:T(8,128)} %get-tuple-element.30.column_ref) | copy-start | bytes 393220
  9.0 7.9 %copy-start.3 = (f32[2,32,256]{2,1,0:T(8,128)S(1)}, f32[2,32,256]{2,1,0:T(8,128)}, u32[]{:S(2)}) copy-start(f32[2,32,256]{2,1,0:T(8,128)} %get-tuple-element.29.lanes_ref) | copy-start | bytes 196612
  9.0 7.9 %copy-start.4 = (s32[16,256]{1,0:T(8,128)S(1)}, s32[16,256]{1,0:T(8,128)}, u32[]{:S(2)}) copy-start(s32[16,256]{1,0:T(8,128)} %get-tuple-element.36.table_ref) | copy-start | bytes 49156
  9.1 3.8 %collective-permute-start = (bf16[4,2,592,128]{3,2,1,0:T(8,128)(2,1)}, bf16[4,2,592,128]{3,2,1,0:T(8,128)(2,1)S(1)}, u32[]{:S(2)}, u32[]{:S(2)}) collective-permute-start(bf16[4,2,592,128]{3,2,1,0:T(8,128)(2,1)} %get-tuple-element.33), channel_id=1, source_target_pairs={{0,1},{1,0},{2,3},{3,2},{4,5},{5,4},{6,7},{7,6},{8,9},{9,8},{10,11... | collective-permute-start | bytes 3637256 | tf_op jit(solution)/shard_map/ppermute | solution.py:412
  14.0 14.2 %collective-permute-start.2 = (bf16[2,2,592,128]{3,2,1,0:T(8,128)(2,1)S(1)}, bf16[2,2,592,128]{3,2,1,0:T(8,128)(2,1)S(1)}, u32[]{:S(2)}, u32[]{:S(2)}) collective-permute-start(bf16[2,2,592,128]{3,2,1,0:T(8,128)(2,1)S(1)} %add_convert_fusion), channel_id=1, source_target_pairs={{0,2},{1,5},{2,0},{3,7},{4,6},{5,1},{6,4},{7,3},{8,10},{9,13},{10,... | collective-permute-start | bytes 1818632 | tf_op jit(solution)/shard_map/ppermute | solution.py:412
  17.0 1.3 %copy-start.1 = (f32[32,40,256]{2,1,0:T(8,128)S(1)}, f32[32,40,256]{2,1,0:T(8,128)}, u32[]{:S(2)}) copy-start(f32[32,40,256]{2,1,0:T(8,128)} %get-tuple-element.28.scaled_ref) | copy-start | bytes 3932164
  24.5 3.8 %copy-start.5 = (bf16[4,2,592,128]{3,2,1,0:T(8,128)(2,1)S(1)}, bf16[4,2,592,128]{3,2,1,0:T(8,128)(2,1)}, u32[]{:S(2)}) copy-start(bf16[4,2,592,128]{3,2,1,0:T(8,128)(2,1)} %get-tuple-element.32) | copy-start | bytes 3637252
  24.5 3.7 %collective-permute-start.1 = (bf16[4,1,592,128]{3,2,1,0:T(8,128)(2,1)S(1)}, bf16[4,1,592,128]{3,2,1,0:T(8,128)(2,1)S(1)}, u32[]{:S(2)}, u32[]{:S(2)}) collective-permute-start(bf16[4,1,592,128]{3,2,1,0:T(8,128)(2,1)S(1)} %get-tuple-element.40), channel_id=1, source_target_pairs={{0,1},{1,0},{2,3},{3,2},{4,5},{5,4},{6,7},{7,6},{8,9},{9,8},{10,11... | collective-permute-start | bytes 1818632 | tf_op jit(solution)/shard_map/ppermute | solution.py:412
  28.2 10.3 %collective-permute-start.3 = (bf16[4,1,592,128]{3,2,1,0:T(8,128)(2,1)S(1)}, bf16[4,1,592,128]{3,2,1,0:T(8,128)(2,1)S(1)}, u32[]{:S(2)}, u32[]{:S(2)}) collective-permute-start(bf16[4,1,592,128]{3,2,1,0:T(8,128)(2,1)S(1)} %get-tuple-element.42), channel_id=1, source_target_pairs={{0,1},{1,0},{2,3},{3,2},{4,5},{5,4},{6,7},{7,6},{8,9},{9,8},{10,11... | collective-permute-start | bytes 1818632 | tf_op jit(solution)/shard_map/ppermute | solution.py:412
  28.7 9.9 %collective-permute-start.4 = (bf16[2,1,592,128]{3,2,1,0:T(8,128)(2,1)S(1)}, bf16[2,1,592,128]{3,2,1,0:T(8,128)(2,1)S(1)}, u32[]{:S(2)}, u32[]{:S(2)}) collective-permute-start(bf16[2,1,592,128]{3,2,1,0:T(8,128)(2,1)S(1)} %add_convert_fusion.2), channel_id=1, source_target_pairs={{0,2},{1,5},{2,0},{3,7},{4,6},{5,1},{6,4},{7,3},{8,10},{9,13},{10,... | collective-permute-start | bytes 909320 | tf_op jit(solution)/shard_map/ppermute | solution.py:412
  29.6 8.9 %collective-permute-start.5 = (bf16[2,592,128]{2,1,0:T(8,128)(2,1)S(1)}, bf16[2,592,128]{2,1,0:T(8,128)(2,1)S(1)}, u32[]{:S(2)}, u32[]{:S(2)}) collective-permute-start(bf16[2,592,128]{2,1,0:T(8,128)(2,1)S(1)} %fusion.1), channel_id=1, source_target_pairs={{0,4},{1,3},{2,6},{3,1},{4,0},{5,7},{6,2},{7,5},{8,12},{9,11},{10,... | collective-permute-start | bytes 909320 | tf_op jit(solution)/shard_map/ppermute | solution.py:412
  38.7 8.4 %collective-permute-start.9 = (bf16[592,128]{1,0:T(8,128)(2,1)S(1)}, bf16[592,128]{1,0:T(8,128)(2,1)S(1)}, u32[]{:S(2)}, u32[]{:S(2)}) collective-permute-start(bf16[592,128]{1,0:T(8,128)(2,1)S(1)} %fusion.12), channel_id=1, source_target_pairs={{0,8},{8,0},{16,24},{24,16},{1,9},{9,1},{17,25},{25,17},{2,10},{10... | collective-permute-start | bytes 454664 | tf_op jit(solution)/shard_map/ppermute | solution.py:415
  43.3 7.1 %collective-permute-start.6 = (bf16[2,1,592,128]{3,2,1,0:T(8,128)(2,1)S(1)}, bf16[2,1,592,128]{3,2,1,0:T(8,128)(2,1)S(1)}, u32[]{:S(2)}, u32[]{:S(2)}) collective-permute-start(bf16[2,1,592,128]{3,2,1,0:T(8,128)(2,1)S(1)} %add_convert_fusion.1), channel_id=1, source_target_pairs={{0,2},{1,5},{2,0},{3,7},{4,6},{5,1},{6,4},{7,3},{8,10},{9,13},{10,... | collective-permute-start | bytes 909320 | tf_op jit(solution)/shard_map/ppermute | solution.py:412
  43.7 6.7 %collective-permute-start.7 = (bf16[1,592,128]{2,1,0:T(8,128)(2,1)S(1)}, bf16[1,592,128]{2,1,0:T(8,128)(2,1)S(1)}, u32[]{:S(2)}, u32[]{:S(2)}) collective-permute-start(bf16[1,592,128]{2,1,0:T(8,128)(2,1)S(1)} %fusion.10), channel_id=1, source_target_pairs={{0,4},{1,3},{2,6},{3,1},{4,0},{5,7},{6,2},{7,5},{8,12},{9,11},{10,... | collective-permute-start | bytes 454664 | tf_op jit(solution)/shard_map/ppermute | solution.py:412
  47.2 9.3 %collective-permute-start.10 = (bf16[592,128]{1,0:T(8,128)(2,1)S(1)}, bf16[592,128]{1,0:T(8,128)(2,1)S(1)}, u32[]{:S(2)}, u32[]{:S(2)}) collective-permute-start(bf16[592,128]{1,0:T(8,128)(2,1)S(1)} %fusion.5), channel_id=1, source_target_pairs={{0,16},{8,24},{16,0},{24,8},{1,17},{9,25},{17,1},{25,9},{2,18},{10... | collective-permute-start | bytes 454664 | tf_op jit(solution)/shard_map/ppermute | solution.py:415
  50.7 5.9 %collective-permute-start.8 = (bf16[1,592,128]{2,1,0:T(8,128)(2,1)S(1)}, bf16[1,592,128]{2,1,0:T(8,128)(2,1)S(1)}, u32[]{:S(2)}, u32[]{:S(2)}) collective-permute-start(bf16[1,592,128]{2,1,0:T(8,128)(2,1)S(1)} %fusion.11), channel_id=1, source_target_pairs={{0,4},{1,3},{2,6},{3,1},{4,0},{5,7},{6,2},{7,5},{8,12},{9,11},{10,... | collective-permute-start | bytes 454664 | tf_op jit(solution)/shard_map/ppermute | solution.py:412
  52.3 6.0 %collective-permute-start.11 = (bf16[592,128]{1,0:T(8,128)(2,1)S(1)}, bf16[592,128]{1,0:T(8,128)(2,1)S(1)}, u32[]{:S(2)}, u32[]{:S(2)}) collective-permute-start(bf16[592,128]{1,0:T(8,128)(2,1)S(1)} %fusion.13), channel_id=1, source_target_pairs={{0,8},{8,0},{16,24},{24,16},{1,9},{9,1},{17,25},{25,17},{2,10},{10... | collective-permute-start | bytes 454664 | tf_op jit(solution)/shard_map/ppermute | solution.py:415
  59.1 6.9 %collective-permute-start.14 = (bf16[128,128]{1,0:T(8,128)(2,1)S(1)}, bf16[128,128]{1,0:T(8,128)(2,1)S(1)}, u32[]{:S(2)}, u32[]{:S(2)}) collective-permute-start(bf16[128,128]{1,0:T(8,128)(2,1)S(1)} %get-tuple-element.56), channel_id=1, source_target_pairs={{0,3},{1,4},{2,5},{3,6},{4,7},{5,0},{6,1},{7,2},{8,11},{9,12},{10,... | collective-permute-start | bytes 98312 | tf_op jit(solution)/shard_map/ppermute | solution.py:477
  60.5 5.5 %collective-permute-start.13 = (bf16[128,128]{1,0:T(8,128)(2,1)S(1)}, bf16[128,128]{1,0:T(8,128)(2,1)S(1)}, u32[]{:S(2)}, u32[]{:S(2)}) collective-permute-start(bf16[128,128]{1,0:T(8,128)(2,1)S(1)} %get-tuple-element.57), channel_id=1, source_target_pairs={{0,2},{1,3},{2,4},{3,5},{4,6},{5,7},{6,0},{7,1},{8,10},{9,11},{10,... | collective-permute-start | bytes 98312 | tf_op jit(solution)/shard_map/ppermute | solution.py:477
  61.1 4.9 %collective-permute-start.12 = (bf16[128,128]{1,0:T(8,128)(2,1)S(1)}, bf16[128,128]{1,0:T(8,128)(2,1)S(1)}, u32[]{:S(2)}, u32[]{:S(2)}) collective-permute-start(bf16[128,128]{1,0:T(8,128)(2,1)S(1)} %get-tuple-element.58), channel_id=1, source_target_pairs={{0,1},{1,2},{2,3},{3,4},{4,5},{5,6},{6,7},{7,0},{8,9},{9,10},{10,1... | collective-permute-start | bytes 98312 | tf_op jit(solution)/shard_map/ppermute | solution.py:477
  61.4 4.6 %collective-permute-start.15 = (bf16[64,128]{1,0:T(8,128)(2,1)S(1)}, bf16[64,128]{1,0:T(8,128)(2,1)S(1)}, u32[]{:S(2)}, u32[]{:S(2)}) collective-permute-start(bf16[64,128]{1,0:T(8,128)(2,1)S(1)} %slice.117), channel_id=1, source_target_pairs={{0,4},{1,5},{2,6},{3,7},{4,0},{5,1},{6,2},{7,3},{8,12},{9,13},{10,... | collective-permute-start | bytes 49160 | tf_op jit(solution)/shard_map/ppermute | solution.py:477
  66.0 0.6 copy-start.9
  66.0 0.6 copy-start.6
  66.0 0.6 copy-start.7
  66.0 0.6 copy-start.8

commit v10 on v9

--- a/solution.py
+++ b/solution.py
@@ -58,17 +58,16 @@
     return solved, masked_w * resid - projection, masked_w
 
 
-def prepare(
-    place_ref, region_ref, count_ref, ld_ref, weight_ref, resid_ref, ids_ref,
-    scaled_ref, lanes_ref, column_ref, table_ref,
-):
-    tracks = region_ref.shape[1]
+def prepare(blocks, floats_ref, numbers_ref, scaled_ref, lanes_ref, column_ref, table_ref):
+    tracks = floats_ref.shape[1]
     groups, _, depth = scaled_ref.shape
     slots = groups * GROUP
     hits = depth // GROUP
-    blocks = place_ref.shape[0]
+    count_row, region_row, place_row = (
+        numbers_ref[hits + n : hits + n + 1, :] for n in range(3)
+    )
     rr = table_ref.shape[0] - 8
-    member = (iota((rr, tracks), 0) == region_ref[...]).astype(F32)
+    member = (iota((rr, tracks), 0) == region_row).astype(F32)
     before = (iota((tracks, tracks), 0) < iota((tracks, tracks), 1)).astype(F32).astype(BF16)
     rank = jnp.dot(member.astype(BF16), before, preferred_element_type=F32)
     count = jnp.sum(member, axis=1, keepdims=True)
@@ -81,7 +80,7 @@
     slot = jnp.sum(member * (rank + start[:, 0:1]), axis=0, keepdims=True)
     perm = (iota((slots, tracks), 0) == slot.astype(jnp.int32)).astype(F32).astype(BF16)
     numbers = jnp.where(
-        iota((8, tracks), 0) == 0, iota((8, tracks), 1), jnp.broadcast_to(count_ref[...], (8, tracks))
+        iota((8, tracks), 0) == 0, iota((8, tracks), 1), jnp.broadcast_to(count_row, (8, tracks))
     )
 
     def sort(value):
@@ -92,15 +91,13 @@
     table_ref[8:, :] = jnp.where(
         iota((rr, slots), 1) == 0, start.astype(jnp.int32), (start + room).astype(jnp.int32)
     )
-    flat = sort(ld_ref[...])
-    ld = [flat[c * hits : (c + 1) * hits] for c in range(5)]
-    solved, hit_factor, masked_w = fit(
-        ld, sort(weight_ref[...]), sort(resid_ref[...]), numbers[1:2]
-    )
-    ids = sort(ids_ref[...].astype(F32).astype(BF16))
+    flat = sort(floats_ref[...])
+    flat = [flat[c * hits : (c + 1) * hits] for c in range(7)]
+    solved, hit_factor, masked_w = fit(flat[:5], flat[5], flat[6], numbers[1:2])
+    ids = sort(numbers_ref[:hits, :].astype(F32).astype(BF16))
     position = jnp.zeros_like(ids)
     for b in range(blocks):
-        position = jnp.where(ids == float(b), place_ref[b].astype(F32), position)
+        position = jnp.where(ids == float(b), place_row[:, b : b + 1].astype(F32), position)
     own = (iota((depth, slots), 0) // hits) == (iota((depth, slots), 1) % GROUP)
 
     def spread_out(value):
@@ -171,43 +168,41 @@
 ODD = (0, 2, 4, 6)
 
 
-def fetch(pairs, sems):
-    copies = [
-        pltpu.make_async_copy(source, target, sems.at[n])
-        for n, (source, target) in enumerate(pairs)
-    ]
-    for copy in copies:
-        copy.start()
-    return copies
-
-
-def lead_kernel(ks, sub, *refs):
-    small, g_hbm, (keep_ref, send_ref), shared = refs[:7], refs[7], refs[8:10], refs[10:14]
-    local_small, g_ref, table_s, sems, scratch = refs[14:21], refs[21], refs[22], refs[23], refs[24:]
-
-    @pl.when(pl.program_id(0) == 0)
-    def _():
-        copies = fetch([*zip(small, local_small), (g_hbm, g_ref)], sems)
-        for copy in copies[:-1]:
-            copy.wait()
-        prepare(*local_small, *shared)
-        copy = pltpu.make_async_copy(shared[3], table_s, sems.at[0])
-        copy.start()
-        copy.wait()
-        copies[-1].wait()
-
-    assemble_region(ks, sub, table_s, *shared[:3], g_ref, keep_ref, send_ref, *scratch)
-
-
-def follow_kernel(ks, sub, scaled_ref, lanes_ref, column_ref, table_ref, g_ref, *refs):
-    assemble_region(ks, sub, table_ref, scaled_ref, lanes_ref, column_ref, g_ref, *refs)
+def lead_kernel(
+    ks, sub, blocks, floats_ref, numbers_ref, g_ref,
+    keep_ref, send_ref, scaled_ref, lanes_ref, column_ref, table_ref, table_s, sem, *scratch,
+):
+    prepare(blocks, floats_ref, numbers_ref, scaled_ref, lanes_ref, column_ref, table_ref)
+    copy = pltpu.make_async_copy(table_ref, table_s, sem)
+    copy.start()
+    copy.wait()
+
+    def region(n, carry):
+        assemble_region(
+            n, ks, sub, table_s, scaled_ref, lanes_ref, column_ref, g_ref, keep_ref, send_ref,
+            *scratch,
+        )
+        return carry
+
+    lax.fori_loop(0, len(ks), region, 0)
+
+
+def follow_kernel(ks, sub, blocks, scaled_ref, lanes_ref, column_ref, table_ref, g_ref, *refs):
+    def region(n, carry):
+        assemble_region(n, ks, sub, table_ref, scaled_ref, lanes_ref, column_ref, g_ref, *refs)
+        return carry
+
+    if len(ks) == 1:
+        region(0, 0)
+    else:
+        lax.fori_loop(0, len(ks), region, 0)
 
 
 def assemble_region(
-    ks, sub, table_ref, scaled_ref, lanes_ref, column_ref, g_ref,
+    number, ks, sub, table_ref, scaled_ref, lanes_ref, column_ref, g_ref,
     keep_ref, send_ref, g_s, direct_s, spread_s, wide_s, turned_s, acc_s,
 ):
-    k = jnp.where(pl.program_id(0) == 0, ks[0], ks[-1])
+    k = jnp.where(number == 0, ks[0], ks[-1])
     width = g_ref.shape[2]
     blocks = spread_s.shape[1] // width
     many = blocks // 2
@@ -290,12 +285,12 @@
             high = row.astype(BF16).astype(F32)
             sub = iota((16, width), 0)
             parts.append(jnp.where(sub == 0, high, jnp.where(sub == 1, row - high, 0.0)))
-            out_ref[n, 0] = jnp.concatenate(parts, axis=0).astype(BF16)
+            out_ref[n, number] = jnp.concatenate(parts, axis=0).astype(BF16)
 
 
 def assemble(ks, sub, inputs, g, blocks, regions):
     tracks, hits, width = g.shape
-    lead = len(inputs) == 7
+    lead = len(inputs) == 2
     rows = width * (blocks // 2) + width // 2 + 16
     longest = -(-(-(-tracks // PAIR) * 5 * PAIR) // DEPTH) * DEPTH
     rr = -(-regions // 8) * 8
@@ -307,25 +302,15 @@
         jax.ShapeDtypeStruct((8 + rr, slots), jnp.int32),
     ]
     out = jax.ShapeDtypeStruct((blocks // 2, len(ks), rows, width), BF16)
-    spec = pl.BlockSpec((blocks // 2, 1, rows, width), lambda k: (0, k, 0, 0))
     vmem = pl.BlockSpec(memory_space=pltpu.VMEM)
-    table = pltpu.SMEM(shared[3].shape, jnp.int32)
-    arrived = pltpu.VMEM(g.shape, g.dtype)
-    if lead:
-        copies = [pltpu.SMEM(inputs[0].shape, jnp.int32)]
-        copies += [pltpu.VMEM(value.shape, value.dtype) for value in inputs[1:]]
-        copies += [arrived, table, pltpu.SemaphoreType.DMA((8,))]
-        in_specs = [pl.BlockSpec(memory_space=pltpu.HBM)] * 8
-    else:
-        copies = []
-        in_specs = [vmem, vmem, vmem, pl.BlockSpec(memory_space=pltpu.SMEM), vmem]
+    smem = pl.BlockSpec(memory_space=pltpu.SMEM)
+    local_table = [pltpu.SMEM(shared[3].shape, jnp.int32), pltpu.SemaphoreType.DMA]
     return pl.pallas_call(
-        functools.partial(lead_kernel if lead else follow_kernel, ks, sub),
-        grid=(len(ks),),
-        in_specs=in_specs,
-        out_specs=[spec, spec] + [vmem] * (4 * lead),
+        functools.partial(lead_kernel if lead else follow_kernel, ks, sub, blocks),
+        in_specs=[vmem] * 3 if lead else [vmem, vmem, vmem, smem, vmem],
+        out_specs=[vmem] * (6 if lead else 2),
         out_shape=[out, out] + shared * lead,
-        scratch_shapes=copies
+        scratch_shapes=local_table * lead
         + [
             pltpu.VMEM((2, GROUP * hits, width), BF16),
             pltpu.VMEM((width + 8, blocks * width), F32),
@@ -334,9 +319,7 @@
             pltpu.VMEM(((blocks + blocks // 2) * width, DEPTH), BF16),
             pltpu.VMEM((blocks, width, (blocks // 2 + 1) * width), F32),
         ],
-        compiler_params=pltpu.CompilerParams(
-            dimension_semantics=("arbitrary",), vmem_limit_bytes=(60 if lead else 32) * 1024 * 1024
-        ),
+        compiler_params=pltpu.CompilerParams(vmem_limit_bytes=28 * 1024 * 1024),
         cost_estimate=pl.CostEstimate(
             flops=4 * 10**9 * len(ks), bytes_accessed=4 * 10**6, transcendentals=0
         ),
@@ -397,15 +380,14 @@
     blocks = block_place.shape[0]
     sub = tiles // blocks
     tile = lax.axis_index("tile")
-    inputs = (
-        block_place,
+    floats = [local_deriv.transpose(1, 2, 0).reshape(-1, tracks), hit_weight.T, hit_resid.T]
+    numbers = [
+        block_ids.T,
+        hit_count.reshape(1, tracks),
         track_region.reshape(1, tracks),
-        hit_count.reshape(1, tracks),
-        local_deriv.transpose(1, 2, 0).reshape(-1, tracks),
-        hit_weight.T,
-        hit_resid.T,
-        block_ids.T,
-    )
+        jnp.pad(block_place, (0, tracks - blocks)).reshape(1, tracks),
+    ]
+    inputs = (jnp.concatenate(floats, axis=0), jnp.concatenate(numbers, axis=0))
 
     def swap(value, even, odd):
         pairs = [(t, t ^ (sub * (odd if t // sub % 2 else even))) for t in range(tiles)]
@@ -434,7 +416,16 @@
         return value[0], swap(value[1].astype(BF16), 4, 2)
 
     groups = [(k + 1, k) for k in range(regions - 2, 0, -2)] + [(1,), (0,)]
-    cores, firsts, seconds = [], [], []
+    totals, cores, firsts, seconds = [None] * regions, [], [], []
+
+    def after(value, other):
+        return lax.optimization_barrier((value, other))[0]
+
+    def settle(n):
+        value = seconds[n][0] + seconds[n][1].astype(F32)
+        for place, k in enumerate(groups[n]):
+            totals[k] = value[place]
+
     for n, ks in enumerate(groups):
         keep, send, *made = assemble(ks, sub, inputs, global_deriv, blocks, regions)
         if n == 0:
@@ -444,31 +435,36 @@
             firsts.append(swap(more, 2, 4))
             continue
         if n > 1:
-            send, cores[-1], firsts[-1] = lax.optimization_barrier((send, cores[-1], firsts[-1]))
-            seconds.append(lower(cores[-2], firsts[-1]))
-            firsts.append(upper(cores[-1]))
+            send = after(send, firsts[n - 2])
+        rest, send = lax.optimization_barrier((inputs[3], send))
+        inputs = inputs[:3] + (rest,)
+        cores.append(near(keep, send))
+        if n > 1:
+            seconds.append(lower(cores[n - 2], firsts[n - 2]))
+            firsts.append(upper(cores[n - 1]))
+            settle(n - 2)
+    last = len(groups) - 1
+    firsts[last - 1] = after(firsts[last - 1], cores[last])
+    half, more = lower(cores[last - 1], firsts[last - 1])
+    firsts.append(upper(cores[last]))
+    seconds.append((half, after(more, firsts[last])))
+    settle(last - 1)
+    crossed = []
+    for k in range(regions - 1, 1, -1):
+        step = k & -k
+        value = across(totals[k], step)
+        if k == 3:
+            value = after(value, cores[last])
+            firsts[last] = after(firsts[last], value)
+        if k == step:
+            crossed.append(value)
         else:
-            rest, send = lax.optimization_barrier((inputs[3], send))
-            inputs = inputs[:3] + (rest,)
-        core = near(keep, send)
-        if n > 1:
-            core, firsts[-1], value = lax.optimization_barrier((core, firsts[-1], seconds[-1][1]))
-            seconds[-1] = seconds[-1][0], value
-        cores.append(core)
-    seconds.append(lower(cores[-2], firsts[-1]))
-    firsts.append(upper(cores[-1]))
-    firsts[-1], value = lax.optimization_barrier((firsts[-1], seconds[-1][1]))
-    seconds[-1] = seconds[-1][0], value
-    seconds.append(lower(cores[-1], firsts[-1]))
-    totals = [None] * regions
-    for ks, (own, value) in zip(groups, seconds):
-        value = own + value.astype(F32)
-        for n, k in enumerate(ks):
-            totals[k] = value[n]
-    for k in range(regions - 1, 0, -1):
-        step = k & -k
-        totals[k - step] = totals[k - step] + across(totals[k], step).astype(F32)
+            totals[k - step] = totals[k - step] + value.astype(F32)
+    seconds.append(lower(cores[last], firsts[last]))
+    settle(last)
     own = totals[0]
+    for value in crossed + [across(totals[1], 1)]:
+        own = own + value.astype(F32)
 
     def onward(value, d):
         pairs = [

time: 68.7 us -> 67.6 us (0.984)
  waiting for transfers between devices: 25 us -> 22.3 us
  starting transfers between devices: 17.8 us -> 19.8 us
  Pallas kernels: 20.1 us -> 18.6 us
  local copies, waits for them, and re-layouts: 2.05 us -> 2.78 us
    ppermute x3, waiting for transfers between devices: 9.37 us -> 4.45 us  [across(): lax.ppermute(value.astype(BF16), 'region', [(r, r ^ k) for r in range(reg...]
    ppermute x9, waiting for transfers between devices: 12.6 us -> 15.2 us  [swap(): return lax.ppermute(value, 'tile', pairs)]
    ppermute x9, starting transfers between devices: 8.22 us -> 10.6 us  [swap(): return lax.ppermute(value, 'tile', pairs)]
    concatenate x0 -> x2, other arithmetic: none -> 1.74 us  [local(): inputs = (jnp.concatenate(floats, axis=0), jnp.concatenate(numbers, axis=0))]
    pallas_call x3, Pallas kernels: 18.2 us -> 16.6 us  [assemble(): pl.pallas_call(functools.partial(lead_kernel if lead else follow_kernel,...]
    convert_element_type x1, other arithmetic: 1.23 us -> 0.17 us  [local(): both(cores[0], top).astype(BF16)]
    unnamed x20 -> x12, local copies, waits for them, and re-layouts: 1.95 us -> 2.01 us
  transfers between devices with their start and end apart: 16 -> 16, of which waited for: 8 -> 7; matrix products, arithmetic and copies ran while one was open for 1% -> 1% of each run, Pallas kernels for 14% -> 12%
where the time goes in v10:
time: 67.6 us; the launch traced here: 67.7 us
  waiting for transfers between devices  22.3 us (33%)
  starting transfers between devices  19.8 us (29%)
  Pallas kernels  18.6 us (28%)
  other arithmetic  3.43 us (5%)
  local copies, waits for them, and re-layouts  2.78 us (4%)
  between operations  0.81 us (1%)
    pallas_call x3, Pallas kernels, assemble(): pl.pallas_call(functools.partial(lead_kernel if lead else follow_kernel,...  16.6 us
    ppermute x9, waiting for transfers between devices, swap(): return lax.ppermute(value, 'tile', pairs)  15.2 us
    ppermute x9, starting transfers between devices, swap(): return lax.ppermute(value, 'tile', pairs)  10.6 us
    ppermute x3, starting transfers between devices, across(): lax.ppermute(value.astype(BF16), 'region', [(r, r ^ k) for r in range(reg...  5.94 us
    ppermute x3, waiting for transfers between devices, across(): lax.ppermute(value.astype(BF16), 'region', [(r, r ^ k) for r in range(reg...  4.45 us
    ppermute x4, starting transfers between devices, onward(): return lax.ppermute(value.astype(BF16), 'tile', pairs)  3.28 us
    ppermute x4, waiting for transfers between devices, onward(): return lax.ppermute(value.astype(BF16), 'tile', pairs)  2.62 us
    unnamed x12, local copies, waits for them, and re-layouts  2.01 us
  transfers between devices with their start and end apart: 16, of which 7 were waited for; matrix products, arithmetic and copies ran while one was open for 1% of the time, Pallas kernels for 12%

profile of v10, /device:TPU:0, one launch (start us, length us, event | category | flops | bytes accessed | tf_op | source)
XLA Modules:
  0.0 67.7 jit_solution(11838185891789810030)
XLA Ops:
  0.6 0.7 pad.4
  1.3 0.9 %pad_maximum_fusion.floats_ref = bf16[224,192]{1,0:T(8,128)(2,1)S(1)} fusion(bf16[32,192]{1,0:T(8,128)(2,1)} %bitcast.58, bf16[32,192]{1,0:T(8,128)(2,1)} %bitcast.59, bf16[160,192]{1,0:T(8,128)(2,1)} %bitcast.56), kind=kLoop, calls=%fused_computation.28 | loop fusion | flops 258048 | bytes 172032 | tf_op jit(solution)/shard_map/concatenate | solution.py:390
  2.2 0.8 %pad_add_fusion.numbers_ref = s32[35,192]{1,0:T(8,128)S(1)} fusion(s32[1,192]{1,0:T(1,128)S(1)} %bitcast.60, s32[1,192]{1,0:T(1,128)} %bitcast.61, s32[1,192]{1,0:T(1,128)} %bitcast.62, s32[32,192]{1,0:T(8,128)} %bitcast.57), kind=kLoop, calls=%fused_computation.29 | loop fusion | flops 20160 | bytes 53760 | tf_op jit(solution)/shard_map/concatenate | solution.py:390
  3.0 0.0 copy-start
  3.0 1.4 %copy-done = bf16[192,32,128]{2,1,0:T(8,128)(2,1)S(1)} copy-done((bf16[192,32,128]{2,1,0:T(8,128)(2,1)S(1)}, bf16[192,32,128]{2,1,0:T(8,128)(2,1)}, u32[]{:S(2)}) %copy-start) | copy-done | bytes 1572888
  4.4 8.3 %assemble.3 = (bf16[4,2,592,128]{3,2,1,0:T(8,128)(2,1)S(1)}, bf16[4,2,592,128]{3,2,1,0:T(8,128)(2,1)S(1)}, f32[32,40,256]{2,1,0:T(8,128)S(1)}, f32[2,32,256]{2,1...) custom-call(bf16[224,192]{1,0:T(8,128)(2,1)S(1)} %pad_maximum_fusion.floats_ref, ...), custom_call_target="tpu_custom_call" | custom-call | flops 8000000000 | bytes 4000000 | tf_op jit(solution)/shard_map/assemble/pallas_call | solution.py:308
  12.8 0.0 copy-start.1
  12.8 0.5 collective-permute-start
  13.3 2.5 %collective-permute-done = bf16[4,2,592,128]{3,2,1,0:T(8,128)(2,1)S(1)} collective-permute-done((bf16[4,2,592,128]{3,2,1,0:T(8,128)(2,1)S(1)}, bf16[4,2,592,128]{3,2,1,0:T(8,128)(2,1)S(1)}, u32[]{:S(2)}, u32[]{:S(2)}) %collective-permute-start) | collective-permute-done | bytes 1212448 | tf_op jit(solution)/shard_map/ppermute | solution.py:394
  15.8 0.2 add_convert_fusion
  16.0 3.4 %collective-permute-start.1 = (bf16[2,2,592,128]{3,2,1,0:T(8,128)(2,1)S(1)}, bf16[2,2,592,128]{3,2,1,0:T(8,128)(2,1)S(1)}, u32[]{:S(2)}, u32[]{:S(2)}) collective-permute-start(bf16[2,2,592,128]{3,2,1,0:T(8,128)(2,1)S(1)} %add_convert_fusion), channel_id=1, source_target_pairs={{0,2},{1,5},{2,0},{3,7},{4,6},{5,1},{6,4},{7,3},{8,10},{9,13},{10,... | collective-permute-start | bytes 1818632 | tf_op jit(solution)/shard_map/ppermute | solution.py:394
  19.4 3.1 %assemble.4 = (bf16[4,1,592,128]{3,2,1,0:T(8,128)(2,1)S(1)}, bf16[4,1,592,128]{3,2,1,0:T(8,128)(2,1)S(1)}) custom-call(f32[32,40,256]{2,1,0:T(8,128)S(1)} %get-tuple-element.24.scaled_ref, f32[2,32,256]{2,1,0:T(8,128)S(1)} %get-tuple-element.25.lanes_ref, f32[256,128]{1,0:T(8,128)S(1)} %get-tuple-element.26.column_ref, ...), custom_call_target="tpu_custom_call" | custom-call | flops 4000000000 | bytes 4000000 | tf_op jit(solution)/shard_map/assemble/pallas_call | solution.py:308
  22.6 0.1 collective-permute-start.8
  22.6 4.8 %collective-permute-done.1 = bf16[2,2,592,128]{3,2,1,0:T(8,128)(2,1)S(1)} collective-permute-done((bf16[2,2,592,128]{3,2,1,0:T(8,128)(2,1)S(1)}, bf16[2,2,592,128]{3,2,1,0:T(8,128)(2,1)S(1)}, u32[]{:S(2)}, u32[]{:S(2)}) %collective-permute-start.1) | collective-permute-done | bytes 606240 | tf_op jit(solution)/shard_map/ppermute | solution.py:394
  27.5 0.2 convert_add_fusion
  27.8 2.1 %collective-permute-start.4 = (bf16[2,592,128]{2,1,0:T(8,128)(2,1)S(1)}, bf16[2,592,128]{2,1,0:T(8,128)(2,1)S(1)}, u32[]{:S(2)}, u32[]{:S(2)}) collective-permute-start(bf16[2,592,128]{2,1,0:T(8,128)(2,1)S(1)} %fusion.1), channel_id=1, source_target_pairs={{0,4},{1,3},{2,6},{3,1},{4,0},{5,7},{6,2},{7,5},{8,12},{9,11},{10,... | collective-permute-start | bytes 909320 | tf_op jit(solution)/shard_map/ppermute | solution.py:394
  29.9 5.2 %assemble.5 = (bf16[4,1,592,128]{3,2,1,0:T(8,128)(2,1)S(1)}, bf16[4,1,592,128]{3,2,1,0:T(8,128)(2,1)S(1)}) custom-call(f32[32,40,256]{2,1,0:T(8,128)S(1)} %get-tuple-element.24.scaled_ref, f32[2,32,256]{2,1,0:T(8,128)S(1)} %get-tuple-element.25.lanes_ref, f32[256,128]{1,0:T(8,128)S(1)} %get-tuple-element.26.column_ref, ...), custom_call_target="tpu_custom_call" | custom-call | flops 4000000000 | bytes 4000000 | tf_op jit(solution)/shard_map/assemble/pallas_call | solution.py:308
  35.1 0.1 collective-permute-start.2
  35.2 0.0 collective-permute-done.4
  35.2 0.1 fusion
  35.3 1.6 %collective-permute-start.5 = (bf16[592,128]{1,0:T(8,128)(2,1)S(1)}, bf16[592,128]{1,0:T(8,128)(2,1)S(1)}, u32[]{:S(2)}, u32[]{:S(2)}) collective-permute-start(bf16[592,128]{1,0:T(8,128)(2,1)S(1)} %fusion.10), channel_id=1, source_target_pairs={{0,8},{8,0},{16,24},{24,16},{1,9},{9,1},{17,25},{25,17},{2,10},{10... | collective-permute-start | bytes 454664 | tf_op jit(solution)/shard_map/ppermute | solution.py:397
  36.9 0.0 collective-permute-done.8
  36.9 0.1 add_convert_fusion.1
  37.0 1.6 %collective-permute-start.9 = (bf16[2,1,592,128]{3,2,1,0:T(8,128)(2,1)S(1)}, bf16[2,1,592,128]{3,2,1,0:T(8,128)(2,1)S(1)}, u32[]{:S(2)}, u32[]{:S(2)}) collective-permute-start(bf16[2,1,592,128]{3,2,1,0:T(8,128)(2,1)S(1)} %add_convert_fusion.1), channel_id=1, source_target_pairs={{0,2},{1,5},{2,0},{3,7},{4,6},{5,1},{6,4},{7,3},{8,10},{9,13},{10,... | collective-permute-start | bytes 909320 | tf_op jit(solution)/shard_map/ppermute | solution.py:394
  38.5 3.1 %collective-permute-done.5 = bf16[592,128]{1,0:T(8,128)(2,1)S(1)} collective-permute-done((bf16[592,128]{1,0:T(8,128)(2,1)S(1)}, bf16[592,128]{1,0:T(8,128)(2,1)S(1)}, u32[]{:S(2)}, u32[]{:S(2)}) %collective-permute-start.5) | collective-permute-done | bytes 151584 | tf_op jit(solution)/shard_map/ppermute | solution.py:397
  41.7 2.5 %collective-permute-start.7 = (bf16[592,128]{1,0:T(8,128)(2,1)S(1)}, bf16[592,128]{1,0:T(8,128)(2,1)S(1)}, u32[]{:S(2)}, u32[]{:S(2)}) collective-permute-start(bf16[592,128]{1,0:T(8,128)(2,1)S(1)} %fusion.5), channel_id=1, source_target_pairs={{0,16},{8,24},{16,0},{24,8},{1,17},{9,25},{17,1},{25,9},{2,18},{10... | collective-permute-start | bytes 454664 | tf_op jit(solution)/shard_map/ppermute | solution.py:397
  44.2 0.1 add_convert_fusion.2
  44.3 1.6 %collective-permute-start.3 = (bf16[2,1,592,128]{3,2,1,0:T(8,128)(2,1)S(1)}, bf16[2,1,592,128]{3,2,1,0:T(8,128)(2,1)S(1)}, u32[]{:S(2)}, u32[]{:S(2)}) collective-permute-start(bf16[2,1,592,128]{3,2,1,0:T(8,128)(2,1)S(1)} %add_convert_fusion.2), channel_id=1, source_target_pairs={{0,2},{1,5},{2,0},{3,7},{4,6},{5,1},{6,4},{7,3},{8,10},{9,13},{10,... | collective-permute-start | bytes 909320 | tf_op jit(solution)/shard_map/ppermute | solution.py:394
  45.8 0.0 collective-permute-done.9
  45.8 0.1 convert_add_fusion.1
  46.0 0.1 collective-permute-start.10
  46.0 5.6 %collective-permute-done.3 = bf16[2,1,592,128]{3,2,1,0:T(8,128)(2,1)S(1)} collective-permute-done((bf16[2,1,592,128]{3,2,1,0:T(8,128)(2,1)S(1)}, bf16[2,1,592,128]{3,2,1,0:T(8,128)(2,1)S(1)}, u32[]{:S(2)}, u32[]{:S(2)}) %collective-permute-start.3) | collective-permute-done | bytes 303136 | tf_op jit(solution)/shard_map/ppermute | solution.py:394
  51.7 0.1 convert_add_fusion.2
  51.8 1.2 %collective-permute-start.6 = (bf16[1,592,128]{2,1,0:T(8,128)(2,1)S(1)}, bf16[1,592,128]{2,1,0:T(8,128)(2,1)S(1)}, u32[]{:S(2)}, u32[]{:S(2)}) collective-permute-start(bf16[1,592,128]{2,1,0:T(8,128)(2,1)S(1)} %fusion.11), channel_id=1, source_target_pairs={{0,4},{1,3},{2,6},{3,1},{4,0},{5,7},{6,2},{7,5},{8,12},{9,11},{10,... | collective-permute-start | bytes 454664 | tf_op jit(solution)/shard_map/ppermute | solution.py:394
  53.0 0.0 collective-permute-done.10
  53.0 1.8 %collective-permute-start.11 = (bf16[592,128]{1,0:T(8,128)(2,1)S(1)}, bf16[592,128]{1,0:T(8,128)(2,1)S(1)}, u32[]{:S(2)}, u32[]{:S(2)}) collective-permute-start(bf16[592,128]{1,0:T(8,128)(2,1)S(1)} %fusion.12), channel_id=1, source_target_pairs={{0,8},{8,0},{16,24},{24,16},{1,9},{9,1},{17,25},{25,17},{2,10},{10... | collective-permute-start | bytes 454664 | tf_op jit(solution)/shard_map/ppermute | solution.py:397
  54.8 2.2 %collective-permute-done.6 = bf16[1,592,128]{2,1,0:T(8,128)(2,1)S(1)} collective-permute-done((bf16[1,592,128]{2,1,0:T(8,128)(2,1)S(1)}, bf16[1,592,128]{2,1,0:T(8,128)(2,1)S(1)}, u32[]{:S(2)}, u32[]{:S(2)}) %collective-permute-start.6) | collective-permute-done | bytes 151584 | tf_op jit(solution)/shard_map/ppermute | solution.py:394
  57.0 1.3 %collective-permute-done.11 = bf16[592,128]{1,0:T(8,128)(2,1)S(1)} collective-permute-done((bf16[592,128]{1,0:T(8,128)(2,1)S(1)}, bf16[592,128]{1,0:T(8,128)(2,1)S(1)}, u32[]{:S(2)}, u32[]{:S(2)}) %collective-permute-start.11) | collective-permute-done | bytes 151584 | tf_op jit(solution)/shard_map/ppermute | solution.py:397
  58.4 0.8 %fusion.14 = (bf16[592,128]{1,0:T(8,128)(2,1)S(1)}, f32[592,128]{1,0:T(8,128)}) fusion(bf16[592,128]{1,0:T(8,128)(2,1)S(1)} %collective-permute-done.11, bf16[592,128]{1,0:T(8,128)(2,1)S(1)} %collective-permute-done.7, bf16[1,592,128]{2,1,0:T(8,128)(2,1)S(1)} %collective-permute-done.6, f32[2,1,592,128]{3,2,1,0:T(8,128)S(1)} %convert_add_fusion.2), kind=kLoop, calls=%fused_computation.30 | loop fusion | flops 530432 | bytes 1212416 | tf_op jit(solution)/shard_map/convert.3
  59.2 0.1 collective-permute-start.14
  59.2 1.4 %collective-permute-start.13 = (bf16[128,128]{1,0:T(8,128)(2,1)S(1)}, bf16[128,128]{1,0:T(8,128)(2,1)S(1)}, u32[]{:S(2)}, u32[]{:S(2)}) collective-permute-start(bf16[128,128]{1,0:T(8,128)(2,1)S(1)} %get-tuple-element.49), channel_id=1, source_target_pairs={{0,2},{1,3},{2,4},{3,5},{4,6},{5,7},{6,0},{7,1},{8,10},{9,11},{10,... | collective-permute-start | bytes 98312 | tf_op jit(solution)/shard_map/ppermute | solution.py:473
  60.7 0.7 collective-permute-start.12
  61.3 1.1 %collective-permute-start.15 = (bf16[64,128]{1,0:T(8,128)(2,1)S(1)}, bf16[64,128]{1,0:T(8,128)(2,1)S(1)}, u32[]{:S(2)}, u32[]{:S(2)}) collective-permute-start(bf16[64,128]{1,0:T(8,128)(2,1)S(1)} %slice.121), channel_id=1, source_target_pairs={{0,4},{1,5},{2,6},{3,7},{4,0},{5,1},{6,2},{7,3},{8,12},{9,13},{10,... | collective-permute-start | bytes 49160 | tf_op jit(solution)/shard_map/ppermute | solution.py:473
  62.5 2.6 %collective-permute-done.15.e_ref = bf16[64,128]{1,0:T(8,128)(2,1)S(1)} collective-permute-done((bf16[64,128]{1,0:T(8,128)(2,1)S(1)}, bf16[64,128]{1,0:T(8,128)(2,1)S(1)}, u32[]{:S(2)}, u32[]{:S(2)}) %collective-permute-start.15) | collective-permute-done | bytes 16416 | tf_op jit(solution)/shard_map/ppermute | solution.py:473
  65.1 0.6 copy-done.5
  65.7 0.0 copy-done.2
  65.7 0.0 copy-done.3
  65.7 1.9 %finish.1 = (f32[128,1024]{1,0:T(8,128)}, f32[1,128]{1,0:T(1,128)}) custom-call(f32[592,128]{1,0:T(8,128)} %get-tuple-element.47.own_ref, bf16[128,128]{1,0:T(8,128)(2,1)} %copy-done.4, bf16[128,128]{1,0:T(8,128)(2,1)} %copy-done.3, bf16[128,128]{1,0:T(8,128)(2,1)} %copy-done.2, bf16[64,128]{1,0:T(8,128)(2,1)} %copy-done.5), custom_call_target="tpu_custom_call" | custom-call | tf_op jit(solution)/shard_map/finish/pallas_call | solution.py:362
  (19 shorter events, 0.2 us)
Async XLA Ops:
  3.0 1.4 %copy-start = (bf16[192,32,128]{2,1,0:T(8,128)(2,1)S(1)}, bf16[192,32,128]{2,1,0:T(8,128)(2,1)}, u32[]{:S(2)}) copy-start(bf16[192,32,128]{2,1,0:T(8,128)(2,1)} %g_ref.5) | copy-start | bytes 4718596
  12.8 6.6 %copy-start.1 = (bf16[192,32,128]{2,1,0:T(8,128)(2,1)S(1)}, bf16[192,32,128]{2,1,0:T(8,128)(2,1)}, u32[]{:S(2)}) copy-start(bf16[192,32,128]{2,1,0:T(8,128)(2,1)} %g_ref.5) | copy-start | bytes 4718596
  12.8 3.0 %collective-permute-start = (bf16[4,2,592,128]{3,2,1,0:T(8,128)(2,1)S(1)}, bf16[4,2,592,128]{3,2,1,0:T(8,128)(2,1)S(1)}, u32[]{:S(2)}, u32[]{:S(2)}) collective-permute-start(bf16[4,2,592,128]{3,2,1,0:T(8,128)(2,1)S(1)} %get-tuple-element.29), channel_id=1, source_target_pairs={{0,1},{1,0},{2,3},{3,2},{4,5},{5,4},{6,7},{7,6},{8,9},{9,8},{10,11... | collective-permute-start | bytes 3637256 | tf_op jit(solution)/shard_map/ppermute | solution.py:394
  16.0 11.5 %collective-permute-start.1 = (bf16[2,2,592,128]{3,2,1,0:T(8,128)(2,1)S(1)}, bf16[2,2,592,128]{3,2,1,0:T(8,128)(2,1)S(1)}, u32[]{:S(2)}, u32[]{:S(2)}) collective-permute-start(bf16[2,2,592,128]{3,2,1,0:T(8,128)(2,1)S(1)} %add_convert_fusion), channel_id=1, source_target_pairs={{0,2},{1,5},{2,0},{3,7},{4,6},{5,1},{6,4},{7,3},{8,10},{9,13},{10,... | collective-permute-start | bytes 1818632 | tf_op jit(solution)/shard_map/ppermute | solution.py:394
  22.6 14.3 %collective-permute-start.8 = (bf16[4,1,592,128]{3,2,1,0:T(8,128)(2,1)S(1)}, bf16[4,1,592,128]{3,2,1,0:T(8,128)(2,1)S(1)}, u32[]{:S(2)}, u32[]{:S(2)}) collective-permute-start(bf16[4,1,592,128]{3,2,1,0:T(8,128)(2,1)S(1)} %get-tuple-element.41), channel_id=1, source_target_pairs={{0,1},{1,0},{2,3},{3,2},{4,5},{5,4},{6,7},{7,6},{8,9},{9,8},{10,11... | collective-permute-start | bytes 1818632 | tf_op jit(solution)/shard_map/ppermute | solution.py:394
  27.8 7.4 %collective-permute-start.4 = (bf16[2,592,128]{2,1,0:T(8,128)(2,1)S(1)}, bf16[2,592,128]{2,1,0:T(8,128)(2,1)S(1)}, u32[]{:S(2)}, u32[]{:S(2)}) collective-permute-start(bf16[2,592,128]{2,1,0:T(8,128)(2,1)S(1)} %fusion.1), channel_id=1, source_target_pairs={{0,4},{1,3},{2,6},{3,1},{4,0},{5,7},{6,2},{7,5},{8,12},{9,11},{10,... | collective-permute-start | bytes 909320 | tf_op jit(solution)/shard_map/ppermute | solution.py:394
  35.1 6.6 %collective-permute-start.2 = (bf16[4,1,592,128]{3,2,1,0:T(8,128)(2,1)S(1)}, bf16[4,1,592,128]{3,2,1,0:T(8,128)(2,1)S(1)}, u32[]{:S(2)}, u32[]{:S(2)}) collective-permute-start(bf16[4,1,592,128]{3,2,1,0:T(8,128)(2,1)S(1)} %get-tuple-element.37), channel_id=1, source_target_pairs={{0,1},{1,0},{2,3},{3,2},{4,5},{5,4},{6,7},{7,6},{8,9},{9,8},{10,11... | collective-permute-start | bytes 1818632 | tf_op jit(solution)/shard_map/ppermute | solution.py:394
  35.3 6.4 %collective-permute-start.5 = (bf16[592,128]{1,0:T(8,128)(2,1)S(1)}, bf16[592,128]{1,0:T(8,128)(2,1)S(1)}, u32[]{:S(2)}, u32[]{:S(2)}) collective-permute-start(bf16[592,128]{1,0:T(8,128)(2,1)S(1)} %fusion.10), channel_id=1, source_target_pairs={{0,8},{8,0},{16,24},{24,16},{1,9},{9,1},{17,25},{25,17},{2,10},{10... | collective-permute-start | bytes 454664 | tf_op jit(solution)/shard_map/ppermute | solution.py:397
  37.0 8.8 %collective-permute-start.9 = (bf16[2,1,592,128]{3,2,1,0:T(8,128)(2,1)S(1)}, bf16[2,1,592,128]{3,2,1,0:T(8,128)(2,1)S(1)}, u32[]{:S(2)}, u32[]{:S(2)}) collective-permute-start(bf16[2,1,592,128]{3,2,1,0:T(8,128)(2,1)S(1)} %add_convert_fusion.1), channel_id=1, source_target_pairs={{0,2},{1,5},{2,0},{3,7},{4,6},{5,1},{6,4},{7,3},{8,10},{9,13},{10,... | collective-permute-start | bytes 909320 | tf_op jit(solution)/shard_map/ppermute | solution.py:394
  41.7 13.1 %collective-permute-start.7 = (bf16[592,128]{1,0:T(8,128)(2,1)S(1)}, bf16[592,128]{1,0:T(8,128)(2,1)S(1)}, u32[]{:S(2)}, u32[]{:S(2)}) collective-permute-start(bf16[592,128]{1,0:T(8,128)(2,1)S(1)} %fusion.5), channel_id=1, source_target_pairs={{0,16},{8,24},{16,0},{24,8},{1,17},{9,25},{17,1},{25,9},{2,18},{10... | collective-permute-start | bytes 454664 | tf_op jit(solution)/shard_map/ppermute | solution.py:397
  44.3 7.4 %collective-permute-start.3 = (bf16[2,1,592,128]{3,2,1,0:T(8,128)(2,1)S(1)}, bf16[2,1,592,128]{3,2,1,0:T(8,128)(2,1)S(1)}, u32[]{:S(2)}, u32[]{:S(2)}) collective-permute-start(bf16[2,1,592,128]{3,2,1,0:T(8,128)(2,1)S(1)} %add_convert_fusion.2), channel_id=1, source_target_pairs={{0,2},{1,5},{2,0},{3,7},{4,6},{5,1},{6,4},{7,3},{8,10},{9,13},{10,... | collective-permute-start | bytes 909320 | tf_op jit(solution)/shard_map/ppermute | solution.py:394
  46.0 7.0 %collective-permute-start.10 = (bf16[1,592,128]{2,1,0:T(8,128)(2,1)S(1)}, bf16[1,592,128]{2,1,0:T(8,128)(2,1)S(1)}, u32[]{:S(2)}, u32[]{:S(2)}) collective-permute-start(bf16[1,592,128]{2,1,0:T(8,128)(2,1)S(1)} %fusion.13), channel_id=1, source_target_pairs={{0,4},{1,3},{2,6},{3,1},{4,0},{5,7},{6,2},{7,5},{8,12},{9,11},{10,... | collective-permute-start | bytes 454664 | tf_op jit(solution)/shard_map/ppermute | solution.py:394
  51.8 5.3 %collective-permute-start.6 = (bf16[1,592,128]{2,1,0:T(8,128)(2,1)S(1)}, bf16[1,592,128]{2,1,0:T(8,128)(2,1)S(1)}, u32[]{:S(2)}, u32[]{:S(2)}) collective-permute-start(bf16[1,592,128]{2,1,0:T(8,128)(2,1)S(1)} %fusion.11), channel_id=1, source_target_pairs={{0,4},{1,3},{2,6},{3,1},{4,0},{5,7},{6,2},{7,5},{8,12},{9,11},{10,... | collective-permute-start | bytes 454664 | tf_op jit(solution)/shard_map/ppermute | solution.py:394
  53.0 5.4 %collective-permute-start.11 = (bf16[592,128]{1,0:T(8,128)(2,1)S(1)}, bf16[592,128]{1,0:T(8,128)(2,1)S(1)}, u32[]{:S(2)}, u32[]{:S(2)}) collective-permute-start(bf16[592,128]{1,0:T(8,128)(2,1)S(1)} %fusion.12), channel_id=1, source_target_pairs={{0,8},{8,0},{16,24},{24,16},{1,9},{9,1},{17,25},{25,17},{2,10},{10... | collective-permute-start | bytes 454664 | tf_op jit(solution)/shard_map/ppermute | solution.py:397
  59.2 5.9 %collective-permute-start.14 = (bf16[128,128]{1,0:T(8,128)(2,1)S(1)}, bf16[128,128]{1,0:T(8,128)(2,1)S(1)}, u32[]{:S(2)}, u32[]{:S(2)}) collective-permute-start(bf16[128,128]{1,0:T(8,128)(2,1)S(1)} %get-tuple-element.48), channel_id=1, source_target_pairs={{0,3},{1,4},{2,5},{3,6},{4,7},{5,0},{6,1},{7,2},{8,11},{9,12},{10,... | collective-permute-start | bytes 98312 | tf_op jit(solution)/shard_map/ppermute | solution.py:473
  59.2 5.9 %collective-permute-start.13 = (bf16[128,128]{1,0:T(8,128)(2,1)S(1)}, bf16[128,128]{1,0:T(8,128)(2,1)S(1)}, u32[]{:S(2)}, u32[]{:S(2)}) collective-permute-start(bf16[128,128]{1,0:T(8,128)(2,1)S(1)} %get-tuple-element.49), channel_id=1, source_target_pairs={{0,2},{1,3},{2,4},{3,5},{4,6},{5,7},{6,0},{7,1},{8,10},{9,11},{10,... | collective-permute-start | bytes 98312 | tf_op jit(solution)/shard_map/ppermute | solution.py:473
  60.7 4.4 %collective-permute-start.12 = (bf16[128,128]{1,0:T(8,128)(2,1)S(1)}, bf16[128,128]{1,0:T(8,128)(2,1)S(1)}, u32[]{:S(2)}, u32[]{:S(2)}) collective-permute-start(bf16[128,128]{1,0:T(8,128)(2,1)S(1)} %get-tuple-element.50), channel_id=1, source_target_pairs={{0,1},{1,2},{2,3},{3,4},{4,5},{5,6},{6,7},{7,0},{8,9},{9,10},{10,1... | collective-permute-start | bytes 98312 | tf_op jit(solution)/shard_map/ppermute | solution.py:473
  61.3 3.7 %collective-permute-start.15 = (bf16[64,128]{1,0:T(8,128)(2,1)S(1)}, bf16[64,128]{1,0:T(8,128)(2,1)S(1)}, u32[]{:S(2)}, u32[]{:S(2)}) collective-permute-start(bf16[64,128]{1,0:T(8,128)(2,1)S(1)} %slice.121), channel_id=1, source_target_pairs={{0,4},{1,5},{2,6},{3,7},{4,0},{5,1},{6,2},{7,3},{8,12},{9,13},{10,... | collective-permute-start | bytes 49160 | tf_op jit(solution)/shard_map/ppermute | solution.py:473
  65.1 0.6 copy-start.5
  65.1 0.6 copy-start.2
  65.1 0.6 copy-start.3
  65.1 0.6 copy-start.4
